TPU v7x, 32 devices: a whole 2x2x4 slice. The times are simulated.
32 devices in a mesh: dp: 8 (over y, x, core), expert: 4 (over z).
Axes of the slice: x: 2, y: 2, z: 4, core: 2. Of those that a mesh axis runs over, the one named last changes fastest.
Arguments:
- tokens: bfloat16 [2, 8192, 1024], P(None, ('dp', 'expert')), may hold values from -6 to 6
- cotangent: bfloat16 [2, 8192, 1024], P(None, ('dp', 'expert')), may hold values from -6 to 6
- segment_ids: int32 [2, 8192], P(None, ('dp', 'expert')), may hold values from 0 to 3, as said below
- parent_ids: int32 [2, 8192], P(None, ('dp', 'expert')), may hold values from 0 to 3, as said below
- routes: int32 [2, 8192, 2], P(None, ('dp', 'expert')), may hold values from 0 to 3, all different within a row; in each aligned block of 256 rows (0 to 255, 256 to 511, ..., all dimensions but the last counted through in order) at most 160 rows name the same one
- gain_attn: float32 [1024], replicated, may hold values from 0.5 to 1.5
- w_qkv: bfloat16 [1024, 3072], P(('dp', 'expert')), may hold values from -0.25 to 0.25
- w_proj: bfloat16 [1024, 1024], P(('dp', 'expert')), may hold values from -0.5 to 0.5
- rel_bias: float32 [32, 16], replicated, may hold values from -4 to 4
- gain_moe: float32 [1024], replicated, may hold values from 0.5 to 1.5
- w_router: bfloat16 [1024, 4], replicated, may hold values from -0.125 to 0.125
- w_in: bfloat16 [4, 1024, 5632], P('expert', 'dp'), may hold values from -0.1875 to 0.1875
- w_out: bfloat16 [4, 2816, 1024], P('expert', 'dp'), may hold values from -0.4375 to 0.4375
Outputs:
- output: bfloat16 [2, 8192, 1024], P(None, ('dp', 'expert'))
- input_grad: bfloat16 [2, 8192, 1024], P(None, ('dp', 'expert'))
- gain_attn_grad: float32 [1024], replicated
- w_qkv_grad: float32 [1024, 3072], P(('dp', 'expert'))
- w_proj_grad: float32 [1024, 1024], P(('dp', 'expert'))
- rel_bias_grad: float32 [32, 16], replicated
- gain_moe_grad: float32 [1024], replicated
- w_router_grad: float32 [1024, 4], replicated
- w_in_grad: float32 [4, 1024, 5632], P('expert', 'dp')
- w_out_grad: float32 [4, 2816, 1024], P('expert', 'dp')
Inputs may be any that keep to these rules, and one draw needn't show every extreme that they name: `routes`: each token names two different experts; in each micro-batch the 256 tokens of one device (rows of one device) name any expert at most 160 times, a bound that some block reaches. `segment_ids`: within each sequence of 256 tokens segment ids start at 0, never fall and take exactly 4 values. `parent_ids`: tokens of one segment share one parent: the segment itself or one of the two segments before it in the same sequence.
All inputs are finite; a program needn't handle non-finite values.
Results may differ from a plain program's by a relative error of at most 0.017.
The roundings to bfloat16 on the way count: a program that leaves them out, or rounds other values in their place, can miss the bound.
Values may be sent and summed in bfloat16 or wider, within the bound.
No kernel may reach another device: no remote copies, remote signals or barrier semaphores. Data moves between devices by JAX's collectives and lax.ppermute only.
A program may use at most 256 MiB of HBM per device.

v0:
```python
from functools import partial

import jax
import jax.numpy as jnp
from jax import lax
from jax.sharding import PartitionSpec as P

EPSILON = 1e-06
NEG_BIG = -1e30
LIMITS = (12, 16, 23, 32, 46, 64, 91)


def bucket_of(offset):
    distance = jnp.abs(offset)
    far_part = 8 + sum(((distance >= limit).astype(jnp.int32) for limit in LIMITS))
    near_far = jnp.where(distance < 8, distance, far_part)
    return jnp.where(offset > 0, 16, 0) + near_far


def slot_positions(routes, experts):
    order = jnp.concatenate([routes[:, 0], routes[:, 1]])
    chosen = (order[:, None] == jnp.arange(experts, dtype=jnp.int32)[None, :]).astype(jnp.int32)
    before = jnp.cumsum(chosen, axis=0) - chosen
    place = jnp.sum(before * chosen, axis=1)
    return place.reshape(2, -1).T


def tree_mask(segment, parent):
    same = segment[:, None, :] == segment[:, :, None]
    upward = segment[:, None, :] == parent[:, :, None]
    downward = parent[:, None, :] == segment[:, :, None]
    return same | upward | downward


def rms_scale(values):
    return lax.rsqrt(jnp.mean(values * values, axis=-1, keepdims=True) + EPSILON)


def gelu_product(gate_part, up_part):
    return jax.nn.gelu(gate_part, approximate=True) * up_part


def weight_term(lefts, rights):
    total = None
    for left, right in zip(lefts, rights):
        term = jnp.einsum("rd,rf->df", left, right, preferred_element_type=jnp.float32)
        total = term if total is None else total + term
    return total


def on_device(
    tokens,
    cotangent,
    segment_ids,
    parent_ids,
    routes,
    gain_attn,
    w_qkv,
    w_proj,
    rel_bias,
    gain_moe,
    w_router,
    w_in,
    w_out,
):
    batches, length, width = tokens.shape
    total_rows = batches * length
    heads = rel_bias.shape[1]
    head_size = width // heads
    experts = w_router.shape[1]
    inner = w_in.shape[2] // 2
    capacity = (10 * length + 4 * experts - 1) // (4 * experts)
    slot_count = experts * capacity
    scale = head_size ** (-0.5)
    hidden_in = tokens.reshape(total_rows, width).astype(jnp.float32)
    first_scale = rms_scale(hidden_in)
    first_hat = hidden_in * first_scale
    first_norm = (first_hat * gain_attn).astype(jnp.bfloat16)
    full_qkv, full_proj = (
        lax.all_gather(w_qkv, ("dp", "expert"), axis=0, tiled=True),
        lax.all_gather(w_proj, ("dp", "expert"), axis=0, tiled=True),
    )
    projected = jnp.dot(first_norm, full_qkv, preferred_element_type=jnp.float32).astype(
        jnp.bfloat16
    )
    split_heads = projected.reshape(batches, length, 3, heads, head_size).transpose(2, 0, 3, 1, 4)
    queries, keys, values = (split_heads[0], split_heads[1], split_heads[2])
    positions = jnp.arange(length, dtype=jnp.int32)
    buckets = bucket_of(positions[None, :] - positions[:, None])
    bucket_hot = (buckets[:, :, None] == jnp.arange(rel_bias.shape[0], dtype=jnp.int32)).astype(
        jnp.float32
    )
    bias_heads = jnp.einsum("qkc,ch->hqk", bucket_hot, rel_bias, precision=lax.Precision.HIGHEST)
    allowed = tree_mask(segment_ids, parent_ids)[:, None]

    def masked_scores(query_block, key_block):
        raw = (
            jnp.einsum(
                "nhqd,nhkd->nhqk", query_block, key_block, preferred_element_type=jnp.float32
            )
            * scale
            + bias_heads[None]
        )
        return jnp.where(allowed, raw, NEG_BIG)

    scores = masked_scores(queries, keys)
    log_total = jax.nn.logsumexp(scores, axis=-1, keepdims=True)
    attn_weights = jnp.exp(scores - log_total)
    mixed = jnp.einsum(
        "nhqk,nhkd->nhqd",
        attn_weights.astype(jnp.bfloat16),
        values,
        preferred_element_type=jnp.float32,
    )
    mixed_low = mixed.transpose(0, 2, 1, 3).reshape(total_rows, width).astype(jnp.bfloat16)
    attended = jnp.dot(mixed_low, full_proj, preferred_element_type=jnp.float32)
    hidden_mid = hidden_in + attended
    second_scale = rms_scale(hidden_mid)
    second_hat = hidden_mid * second_scale
    second_norm = (second_hat * gain_moe).astype(jnp.bfloat16)
    logits = jnp.dot(second_norm, w_router, preferred_element_type=jnp.float32)
    router_log = jax.nn.logsumexp(logits, axis=-1, keepdims=True)
    router_weights = jnp.exp(logits - router_log)
    flat_routes = routes.reshape(total_rows, 2)
    route_hot = (flat_routes[:, :, None] == jnp.arange(experts, dtype=jnp.int32)).astype(
        jnp.float32
    )
    gates = jnp.sum(router_weights[:, None, :] * route_hot, axis=-1)
    places = jax.vmap(partial(slot_positions, experts=experts))(routes)
    targets = routes * capacity + places
    selectors = (targets[..., None] == jnp.arange(slot_count, dtype=jnp.int32)).astype(jnp.bfloat16)
    gathered_in, gathered_out = (
        lax.all_gather(w_in, "dp", axis=1, tiled=True),
        lax.all_gather(w_out, "dp", axis=1, tiled=True),
    )
    gate_w = gathered_in[0, :, :inner]
    up_w = gathered_in[0, :, inner:]
    down_w = gathered_out[0]
    kept_slots = []
    picked_rows = []
    for batch in range(batches):
        lower, upper = (batch * length, (batch + 1) * length)
        outgoing = jnp.einsum(
            "tjk,td->kd",
            selectors[batch],
            second_norm[lower:upper],
            preferred_element_type=jnp.float32,
        )
        outgoing = outgoing.astype(jnp.bfloat16).reshape(experts, capacity, width)
        received = lax.all_to_all(outgoing, "expert", split_axis=0, concat_axis=0, tiled=True)
        flat_rows = received.reshape(-1, width)
        expert_gate_part = jnp.dot(flat_rows, gate_w, preferred_element_type=jnp.float32)
        expert_up_part = jnp.dot(flat_rows, up_w, preferred_element_type=jnp.float32)
        expert_product = gelu_product(expert_gate_part, expert_up_part).astype(jnp.bfloat16)
        result = (
            jnp.dot(expert_product, down_w, preferred_element_type=jnp.float32)
            .astype(jnp.bfloat16)
            .reshape(received.shape)
        )
        returned = lax.all_to_all(result, "expert", split_axis=0, concat_axis=0, tiled=True)
        received, returned = (received, returned)
        kept_slots.append(received)
        picked_rows.append(
            jnp.einsum(
                "tjk,kd->tjd",
                selectors[batch],
                returned.reshape(slot_count, width),
                preferred_element_type=jnp.float32,
            )
        )
    picked = jnp.concatenate(picked_rows, 0)
    mixture = gates[:, 0, None] * picked[:, 0] + gates[:, 1, None] * picked[:, 1]
    output = (hidden_mid + mixture).astype(jnp.bfloat16).reshape(tokens.shape)
    out_grad = cotangent.reshape(total_rows, width).astype(jnp.float32)
    gate_grads = jnp.sum(out_grad[:, None, :] * picked, axis=-1)
    slot_grads = (gates[:, :, None] * out_grad[:, None, :]).astype(jnp.bfloat16)
    again_in, again_out = (
        lax.all_gather(w_in, "dp", axis=1, tiled=True),
        lax.all_gather(w_out, "dp", axis=1, tiled=True),
    )
    back_in = again_in[0]
    back_down = again_out[0]
    held_inputs, held_joined, held_products, held_arriving = ([], [], [], [])
    dispatch_grads = []
    for batch in range(batches):
        lower, upper = (batch * length, (batch + 1) * length)
        outgoing_grad = jnp.einsum(
            "tjk,tjd->kd",
            selectors[batch],
            slot_grads[lower:upper],
            preferred_element_type=jnp.float32,
        )
        outgoing_grad = outgoing_grad.astype(jnp.bfloat16).reshape(experts, capacity, width)
        arriving = lax.all_to_all(
            outgoing_grad, "expert", split_axis=0, concat_axis=0, tiled=True
        ).reshape(-1, width)
        inputs_flat = kept_slots[batch].reshape(-1, width)
        gate_part = jnp.dot(inputs_flat, back_in[:, :inner], preferred_element_type=jnp.float32)
        up_part = jnp.dot(inputs_flat, back_in[:, inner:], preferred_element_type=jnp.float32)
        product, product_vjp = jax.vjp(gelu_product, gate_part, up_part)
        product_low = product.astype(jnp.bfloat16)
        product_grad = jnp.einsum(
            "rd,fd->rf", arriving, back_down, preferred_element_type=jnp.float32
        )
        gate_grad, up_grad = product_vjp(product_grad)
        joined_grad = jnp.concatenate([gate_grad, up_grad], axis=1).astype(jnp.bfloat16)
        slot_input_grad = jnp.einsum(
            "rf,df->rd", joined_grad, back_in, preferred_element_type=jnp.float32
        ).astype(jnp.bfloat16)
        returned_grad = lax.all_to_all(
            slot_input_grad.reshape(experts, capacity, width),
            "expert",
            split_axis=0,
            concat_axis=0,
            tiled=True,
        )
        dispatch_grads.append(
            jnp.einsum(
                "tjk,kd->td",
                selectors[batch],
                returned_grad.reshape(slot_count, width),
                preferred_element_type=jnp.float32,
            )
        )
        held_inputs.append(inputs_flat)
        held_joined.append(joined_grad)
        held_products.append(product_low)
        held_arriving.append(arriving)
    in_total = lax.psum_scatter(
        weight_term(tuple(held_inputs), tuple(held_joined)).astype(jnp.bfloat16),
        "dp",
        scatter_dimension=0,
        tiled=True,
    ).astype(jnp.float32)
    out_total = lax.psum_scatter(
        weight_term(tuple(held_products), tuple(held_arriving)).astype(jnp.bfloat16),
        "dp",
        scatter_dimension=0,
        tiled=True,
    ).astype(jnp.float32)
    dispatch_grad = jnp.concatenate(dispatch_grads, 0)
    weight_grads = jnp.sum(route_hot * gate_grads[:, :, None], axis=1)
    logit_grads = router_weights * (
        weight_grads - jnp.sum(router_weights * weight_grads, axis=-1, keepdims=True)
    )
    logit_grads = logit_grads.astype(jnp.bfloat16)
    norm_grad = dispatch_grad + jnp.einsum(
        "re,de->rd", logit_grads, w_router, preferred_element_type=jnp.float32
    )
    router_grad = jnp.einsum(
        "rd,re->de", second_norm, logit_grads, preferred_element_type=jnp.float32
    )
    gain_moe_grad = jnp.sum(norm_grad * second_hat, axis=0)
    scaled_second = norm_grad * gain_moe
    mid_grad = out_grad + second_scale * (
        scaled_second - second_hat * jnp.mean(scaled_second * second_hat, axis=-1, keepdims=True)
    )
    branch_grad = mid_grad.astype(jnp.bfloat16)
    mixed_grad = jnp.einsum(
        "re,de->rd", branch_grad, full_proj, preferred_element_type=jnp.float32
    ).astype(jnp.bfloat16)
    head_grad = mixed_grad.reshape(batches, length, heads, head_size).transpose(0, 2, 1, 3)
    weights_again = jnp.exp(masked_scores(queries, keys) - log_total)
    value_grad = jnp.einsum(
        "nhqk,nhqd->nhkd",
        weights_again.astype(jnp.bfloat16),
        head_grad,
        preferred_element_type=jnp.float32,
    )
    prob_grad = jnp.einsum("nhqd,nhkd->nhqk", head_grad, values, preferred_element_type=jnp.float32)
    score_grad = weights_again * (
        prob_grad - jnp.sum(weights_again * prob_grad, axis=-1, keepdims=True)
    )
    score_grad = score_grad.astype(jnp.bfloat16)
    query_grad = (
        jnp.einsum("nhqk,nhkd->nhqd", score_grad, keys, preferred_element_type=jnp.float32) * scale
    )
    key_grad = (
        jnp.einsum("nhqk,nhqd->nhkd", score_grad, queries, preferred_element_type=jnp.float32)
        * scale
    )
    table_grad = jnp.einsum(
        "nhqk,qkc->ch",
        score_grad,
        bucket_hot.astype(jnp.bfloat16),
        preferred_element_type=jnp.float32,
    )
    qkv_grad = jnp.stack([query_grad, key_grad, value_grad], 0).transpose(1, 3, 0, 2, 4)
    qkv_grad = qkv_grad.reshape(total_rows, 3 * width).astype(jnp.bfloat16)
    first_grad = jnp.einsum("rf,df->rd", qkv_grad, full_qkv, preferred_element_type=jnp.float32)
    gain_attn_grad = jnp.sum(first_grad * first_hat, axis=0)
    scaled_first = first_grad * gain_attn
    input_grad = mid_grad + first_scale * (
        scaled_first - first_hat * jnp.mean(scaled_first * first_hat, axis=-1, keepdims=True)
    )
    input_grad = input_grad.astype(jnp.bfloat16).reshape(tokens.shape)
    qkv_part = jnp.einsum("rd,rf->df", first_norm, qkv_grad, preferred_element_type=jnp.float32)
    proj_part = jnp.einsum("rd,rf->df", mixed_low, branch_grad, preferred_element_type=jnp.float32)
    attn_grads = lax.psum_scatter(
        jnp.concatenate([qkv_part, proj_part], axis=1),
        ("dp", "expert"),
        scatter_dimension=0,
        tiled=True,
    )
    small = lax.psum((gain_attn_grad, table_grad, gain_moe_grad, router_grad), ("dp", "expert"))
    return (
        output,
        input_grad,
        small[0],
        attn_grads[:, : 3 * width],
        attn_grads[:, 3 * width :],
        small[1],
        small[2],
        small[3],
        in_total[None],
        out_total[None],
    )


def solution(mesh):
    in_specs = (
        P(None, ("dp", "expert"), None),
        P(None, ("dp", "expert"), None),
        P(None, ("dp", "expert")),
        P(None, ("dp", "expert")),
        P(None, ("dp", "expert"), None),
        P(),
        P(("dp", "expert"), None),
        P(("dp", "expert"), None),
        P(),
        P(),
        P(),
        P("expert", "dp", None),
        P("expert", "dp", None),
    )
    out_specs = (
        P(None, ("dp", "expert"), None),
        P(None, ("dp", "expert"), None),
        P(),
        P(("dp", "expert"), None),
        P(("dp", "expert"), None),
        P(),
        P(),
        P(),
        P("expert", "dp", None),
        P("expert", "dp", None),
    )
    return jax.shard_map(
        on_device, mesh=mesh, in_specs=in_specs, out_specs=out_specs, check_vma=False
    )
```

profile of v0, /device:TPU:0, one launch (start us, length us, event | category | flops | bytes accessed | tf_op | source)
XLA Modules:
  0.0 1007.7 jit_solution(18439001783409405728)
XLA Ops:
  12.1 11.5 %copy.78 = pred[256,256,32]{1,2,0:T(32,128)(4,1)S(1)} copy(pred[256,256,32]{0,2,1:T(32,128)(4,1)S(1)} %iota_compare_fusion) | data formatting | bytes 4194304 | tf_op jit(solution)/shard_map/eq | solution.py:90
  23.5 3.7 convolution_bitcast_fusion
  27.2 5.3 copy.79
  41.2 42.0 %all-gather.5.cloned.1.call-done = bf16[1024,3072]{1,0:T(8,128)(2,1)} async-done(((bf16[32,3072]{1,0:T(8,128)(2,1)}), bf16[1024,3072]{1,0:T(8,128)(2,1)}) %all-gather.5.cloned.1.call-update) | async-done | bytes 6291472 | tf_op jit(solution)/shard_map/all_gather | solution.py:80
  83.2 6.5 convolution_convert_fusion
  89.8 6.1 reshape.283
  95.8 7.2 copy.77
  103.1 5.3 fusion.149
  114.6 26.6 %all-gather.7.cloned.1.call-done = bf16[1024,1024]{1,0:T(8,128)(2,1)} async-done(((bf16[32,1024]{1,0:T(8,128)(2,1)}), bf16[1024,1024]{1,0:T(8,128)(2,1)}) %all-gather.7.cloned.1.call-update) | async-done | bytes 2097168 | tf_op jit(solution)/shard_map/all_gather | solution.py:81
  147.3 3.6 all-to-all-start.2
  152.5 30.4 %all-to-all-done.2 = bf16[4,160,1024]{2,1,0:T(8,128)(2,1)S(1)} async-done(((bf16[4,160,1024]{2,1,0:T(8,128)(2,1)}), bf16[4,160,1024]{2,1,0:T(8,128)(2,1)S(1)}, u32[]{:S(2)}, u32[]{:S(2)}) %all-to-all-start.2) | async-done | bytes 1310752 | tf_op jit(solution)/shard_map/all_to_all | solution.py:150
  184.0 3.9 all-to-all-start
  188.0 21.6 %all-gather.9.cloned.1.call-done = bf16[1,1024,5632]{2,1,0:T(8,128)(2,1)} async-done(((bf16[1,128,5632]{2,1,0:T(8,128)(2,1)}), bf16[1,1024,5632]{2,1,0:T(8,128)(2,1)}) %all-gather.9.cloned.1.call-update) | async-done | bytes 11534352 | tf_op jit(solution)/shard_map/all_gather | solution.py:133
  209.6 9.9 fusion.41
  219.5 35.2 %all-gather.11.cloned.1.call-done = bf16[1,2816,1024]{2,1,0:T(8,128)(2,1)} async-done(((bf16[1,352,1024]{2,1,0:T(8,128)(2,1)}), bf16[1,2816,1024]{2,1,0:T(8,128)(2,1)}) %all-gather.11.cloned.1.call-update) | async-done | bytes 5767184 | tf_op jit(solution)/shard_map/all_gather | solution.py:134
  254.7 15.5 %fusion.88 = bf16[640,1024]{1,0:T(8,128)(2,1)} fusion(bf16[1,2816,1024]{2,1,0:T(8,128)(2,1)} %all-gather.11.cloned.1.call-done, f32[640,2816]{1,0:T(8,128)} %fusion.41, bf16[640,1024]{1,0:T(8,128)(2,1)} %bitcast.246, bf16[1,1024,5632]{2,1,0:T(8,128)(2,1)} %all-gather.9.cloned.1.call-done), kind=kOutput, calls=%fused_computation.138 | convolution fusion | flops 7400652800 | bytes 21364736 | tf_op jit(solution)/shard_map/dot_general | solution.py:156
  270.2 4.8 all-to-all-start.3
  275.0 8.6 fusion.42
  283.6 15.0 %fusion.85 = bf16[640,1024]{1,0:T(8,128)(2,1)} fusion(bf16[1,2816,1024]{2,1,0:T(8,128)(2,1)} %all-gather.11.cloned.1.call-done, f32[640,2816]{1,0:T(8,128)} %fusion.42, bf16[640,1024]{1,0:T(8,128)(2,1)S(1)} %bitcast.239, bf16[1,1024,5632]{2,1,0:T(8,128)(2,1)} %all-gather.9.cloned.1.call-done), kind=kOutput, calls=%fused_computation.137 | convolution fusion | flops 7400652800 | bytes 21364736 | tf_op jit(solution)/shard_map/dot_general | solution.py:156
  298.6 8.2 all-to-all-done.3
  306.9 4.7 all-to-all-start.1
  313.5 3.8 fusion.100
  317.4 25.2 %all-to-all-done.1 = bf16[4,160,1024]{2,1,0:T(8,128)(2,1)} async-done(((bf16[4,160,1024]{2,1,0:T(8,128)(2,1)}), bf16[4,160,1024]{2,1,0:T(8,128)(2,1)}, u32[]{:S(2)}, u32[]{:S(2)}) %all-to-all-start.1) | async-done | bytes 1310752 | tf_op jit(solution)/shard_map/all_to_all | solution.py:160
  348.9 4.3 all-to-all-start.4
  353.3 8.7 fusion.47
  361.9 8.7 fusion.49
  372.6 11.5 %all-to-all-done.4 = bf16[4,160,1024]{2,1,0:T(8,128)(2,1)} async-done(((bf16[4,160,1024]{2,1,0:T(8,128)(2,1)}), bf16[4,160,1024]{2,1,0:T(8,128)(2,1)}, u32[]{:S(2)}, u32[]{:S(2)}) %all-to-all-start.4) | async-done | bytes 1310752 | tf_op jit(solution)/shard_map/all_to_all | solution.py:194
  384.1 4.3 all-to-all-start.6
  388.5 10.0 fusion.35
  398.5 16.3 %fusion.6 = (bf16[640,2816]{1,0:T(8,128)(2,1)}, bf16[640,2816]{1,0:T(8,128)(2,1)}, f32[640,2816]{1,0:T(8,128)}) fusion(f32[640,2816]{1,0:T(8,128)} %fusion.35, f32[640,2816]{1,0:T(8,128)} %fusion.49, bf16[640,1024]{1,0:T(8,128)(2,1)S(1)} %bitcast.241, bf16[1024,5632]{1,0:T(8,128)(2,1)} %bitcast.272), kind=kOutput, calls=%fused_computation.23 | convolution fusion | flops 3734241280 | bytes 35913728 | tf_op jit(solution)/shard_map/dot_general | solution.py:198
  414.9 13.7 %fusion.58 = f32[2816,1024]{1,0:T(8,128)} fusion(bf16[640,1024]{1,0:T(8,128)(2,1)} %bitcast.37, f32[640,2816]{1,0:T(8,128)S(1)} %bitcast.277, f32[640,2816]{1,0:T(8,128)} %get-tuple-element.45), kind=kOutput, calls=%fused_computation.93 | convolution fusion | flops 3709009920 | bytes 27262976 | tf_op jit(solution)/shard_map/rd,rf->df/dot_general | solution.py:46
  428.5 10.0 fusion.33
  438.5 16.2 %fusion.13 = (bf16[640,2816]{1,0:T(8,128)(2,1)}, bf16[640,2816]{1,0:T(8,128)(2,1)}, f32[640,2816]{1,0:T(8,128)}) fusion(f32[640,2816]{1,0:T(8,128)} %fusion.33, f32[640,2816]{1,0:T(8,128)} %fusion.47, bf16[640,1024]{1,0:T(8,128)(2,1)S(1)} %bitcast.248, bf16[1024,5632]{1,0:T(8,128)(2,1)} %bitcast.273), kind=kOutput, calls=%fused_computation.30 | convolution fusion | flops 3734241280 | bytes 35913728 | tf_op jit(solution)/shard_map/dot_general | solution.py:198
  454.7 11.3 %add_convert_fusion.1 = bf16[2816,1024]{1,0:T(8,128)(2,1)} fusion(f32[2816,1024]{1,0:T(8,128)S(1)} %bitcast.275, bf16[640,1024]{1,0:T(8,128)(2,1)} %bitcast.43, f32[640,2816]{1,0:T(8,128)} %fusion.47, f32[640,2816]{1,0:T(8,128)} %get-tuple-element.44), kind=kOutput, calls=%fused_computation.2 | convolution fusion | flops 3714777088 | bytes 33030144 | tf_op jit(solution)/shard_map/rd,rf->df/dot_general | solution.py:46
  466.2 18.0 %fusion.52 = f32[1024,5632]{1,0:T(8,128)} fusion(bf16[640,1024]{1,0:T(8,128)(2,1)S(1)} %bitcast.242, bf16[640,2816]{1,0:T(8,128)(2,1)} %get-tuple-element.25, bf16[640,2816]{1,0:T(8,128)(2,1)} %get-tuple-element.24), kind=kOutput, calls=%fused_computation.85 | convolution fusion | flops 7396392960 | bytes 31588352 | tf_op jit(solution)/shard_map/rd,rf->df/dot_general | solution.py:46
  484.1 17.6 %add_convert_fusion = bf16[1024,5632]{1,0:T(8,128)(2,1)} fusion(f32[1024,5632]{1,0:T(8,128)} %fusion.52, bf16[640,1024]{1,0:T(8,128)(2,1)S(1)} %bitcast.249, bf16[640,2816]{1,0:T(8,128)(2,1)S(1)} %copy-done.27, bf16[640,2816]{1,0:T(8,128)(2,1)S(1)} %copy-done.26), kind=kOutput, calls=%fused_computation | convolution fusion | flops 7407927296 | bytes 43122688 | tf_op jit(solution)/shard_map/rd,rf->df/dot_general | solution.py:46
  501.7 13.6 %fusion.84 = bf16[640,1024]{1,0:T(8,128)(2,1)} fusion(bf16[640,2816]{1,0:T(8,128)(2,1)} %get-tuple-element.27, bf16[640,2816]{1,0:T(8,128)(2,1)} %get-tuple-element.26, bf16[1,1024,5632]{2,1,0:T(8,128)(2,1)} %all-gather.9.cloned.1.call-done), kind=kOutput, calls=%fused_computation.136 | convolution fusion | flops 7397048320 | bytes 20054016 | tf_op jit(solution)/shard_map/rf,df->rd/dot_general | solution.py:207
  515.3 5.1 all-to-all-start.7
  520.5 13.7 %fusion.83 = bf16[640,1024]{1,0:T(8,128)(2,1)} fusion(bf16[640,2816]{1,0:T(8,128)(2,1)} %get-tuple-element.25, bf16[640,2816]{1,0:T(8,128)(2,1)} %get-tuple-element.24, bf16[1,1024,5632]{2,1,0:T(8,128)(2,1)} %all-gather.9.cloned.1.call-done), kind=kOutput, calls=%fused_computation.135 | convolution fusion | flops 7397048320 | bytes 20054016 | tf_op jit(solution)/shard_map/rf,df->rd/dot_general | solution.py:207
  534.2 17.0 %all-to-all-done.7 = bf16[4,160,1024]{2,1,0:T(8,128)(2,1)S(1)} async-done(((bf16[4,160,1024]{2,1,0:T(8,128)(2,1)}), bf16[4,160,1024]{2,1,0:T(8,128)(2,1)S(1)}, u32[]{:S(2)}, u32[]{:S(2)}) %all-to-all-start.7) | async-done | bytes 1310752 | tf_op jit(solution)/shard_map/all_to_all | solution.py:210
  552.3 4.3 all-to-all-start.5
  561.1 26.4 %all-to-all-done.5 = bf16[4,160,1024]{2,1,0:T(8,128)(2,1)} async-done(((bf16[4,160,1024]{2,1,0:T(8,128)(2,1)}), bf16[4,160,1024]{2,1,0:T(8,128)(2,1)}, u32[]{:S(2)}, u32[]{:S(2)}) %all-to-all-start.5) | async-done | bytes 1310752 | tf_op jit(solution)/shard_map/all_to_all | solution.py:210
  597.8 6.2 multiply_reduce_fusion
  604.3 4.9 convert_reduce_fusion
  626.5 6.3 pad_maximum_fusion
  637.4 8.3 fusion.79
  645.7 42.9 %all-reduce = (f32[1024]{0:T(1024)}, f32[32,16]{0,1:T(8,128)}, f32[1024]{0:T(1024)}, f32[1024,4]{0,1:T(4,128)}) all-reduce(f32[1024]{0:T(1024)S(1)} %get-tuple-element.12, f32[32,16]{0,1:T(8,128)S(1)} %fusion.92, f32[1024]{0:T(1024)S(1)} %get-tuple-element.10, ...), channel_id=1, replica_groups=mesh['dp'=8,'expert'=4] {'dp','expert'}, use_global_device_ids=true, to_apply=%region_19.20 | all-reduce | flops 6656 | bytes 53248 | tf_op jit(solution)/shard_map/psum | solution.py:305
  697.5 299.6 %reduce-scatter.4.cloned.1.call-done = f32[32,4096]{1,0:T(8,128)} async-done(((f32[1024,4096]{1,0:T(8,128)}), f32[32,4096]{1,0:T(8,128)}) %reduce-scatter.4.cloned.1.call-update) | async-done | bytes 524304 | tf_op jit(solution)/shard_map/reduce_scatter | solution.py:299
  (234 shorter events, 88.5 us)
Async XLA Ops:
  7.2 16.4 %copy-start = (f32[32,16]{0,1:T(8,128)S(1)}, f32[32,16]{0,1:T(8,128)}, u32[]{:S(2)}) copy-start(f32[32,16]{0,1:T(8,128)} %param.21) | copy-start | bytes 6148
  7.2 76.0 %all-gather.5.cloned.1.call-start = ((), (), s32[]{:S(2)}) async-start(), calls=%async_computation.11 | async-start | bytes 6488064 | tf_op jit(solution)/shard_map/all_gather | solution.py:80
  7.9 133.2 %all-gather.7.cloned.1.call-start = ((), (), s32[]{:S(2)}) async-start(), calls=%async_computation.12 | async-start | bytes 2162688 | tf_op jit(solution)/shard_map/all_gather | solution.py:81
  8.7 200.9 %all-gather.9.cloned.1.call-start = ((), (), s32[]{:S(2)}) async-start(), calls=%async_computation.13 | async-start | bytes 12976128 | tf_op jit(solution)/shard_map/all_gather | solution.py:133
  9.4 245.3 %all-gather.11.cloned.1.call-start = ((), (), s32[]{:S(2)}) async-start(), calls=%async_computation.14 | async-start | bytes 6488064 | tf_op jit(solution)/shard_map/all_gather | solution.py:134
  33.5 56.3 %copy-start.58 = (f32[1,2,2,128]{3,1,2,0:T(2,128)}, f32[1,2,2,128]{3,1,2,0:T(2,128)S(1)}, u32[]{:S(2)}) copy-start(f32[1,2,2,128]{3,1,2,0:T(2,128)S(1)} %copy.105) | copy-start | bytes 6148
  39.1 111.9 %copy-start.30 = (bf16[256,640]{1,0:T(8,128)(2,1)}, bf16[256,640]{1,0:T(8,128)(2,1)S(1)}, u32[]{:S(2)}) copy-start(bf16[256,640]{1,0:T(8,128)(2,1)S(1)} %get-tuple-element.15) | copy-start | bytes 983044
  113.2 27.9 %copy-start.7 = (bf16[2,256,1024]{2,1,0:T(8,128)(2,1)S(1)}, bf16[2,256,1024]{2,1,0:T(8,128)(2,1)}, u32[]{:S(2)}) copy-start(bf16[2,256,1024]{2,1,0:T(8,128)(2,1)} %param.13) | copy-start | bytes 3145732
  114.3 31.1 %copy-start.45 = (f32[1024]{0:T(1024)S(1)}, f32[1024]{0:T(1024)}, u32[]{:S(2)}) copy-start(f32[1024]{0:T(1024)} %param.22) | copy-start | bytes 12292
  114.6 31.2 %copy-start.12 = (bf16[128,8,2,256]{3,1,2,0:T(8,128)(2,1)}, bf16[128,8,2,256]{3,1,2,0:T(8,128)(2,1)S(1)}, u32[]{:S(2)}) copy-start(bf16[128,8,2,256]{3,1,2,0:T(8,128)(2,1)S(1)} %copy.106) | copy-start | bytes 3145732
  145.7 167.3 %copy-start.11 = (bf16[512,1024]{1,0:T(8,128)(2,1)}, bf16[512,1024]{1,0:T(8,128)(2,1)S(1)}, u32[]{:S(2)}) copy-start(bf16[512,1024]{1,0:T(8,128)(2,1)S(1)} %multiply_convert_fusion.8) | copy-start | bytes 3145732
  147.3 35.6 %all-to-all-start.2 = ((bf16[4,160,1024]{2,1,0:T(8,128)(2,1)}), bf16[4,160,1024]{2,1,0:T(8,128)(2,1)S(1)}, u32[]{:S(2)}, u32[]{:S(2)}) async-start(bf16[4,160,1024]{2,1,0:T(8,128)(2,1)} %bitcast.24), calls=%async_computation.2 | async-start | bytes 2621440 | tf_op jit(solution)/shard_map/all_to_all | solution.py:150
  184.0 86.2 %all-to-all-start = ((bf16[4,160,1024]{2,1,0:T(8,128)(2,1)}), bf16[4,160,1024]{2,1,0:T(8,128)(2,1)S(1)}, u32[]{:S(2)}, u32[]{:S(2)}) async-start(bf16[4,160,1024]{2,1,0:T(8,128)(2,1)} %bitcast.244), calls=%async_computation | async-start | bytes 2621440 | tf_op jit(solution)/shard_map/all_to_all | solution.py:150
  270.2 13.4 %copy-start.20 = (bf16[4,160,1024]{2,1,0:T(8,128)(2,1)}, bf16[4,160,1024]{2,1,0:T(8,128)(2,1)S(1)}, u32[]{:S(2)}) copy-start(bf16[4,160,1024]{2,1,0:T(8,128)(2,1)S(1)} %all-to-all-done) | copy-start | bytes 3932164
  270.2 36.7 %all-to-all-start.3 = ((bf16[4,160,1024]{2,1,0:T(8,128)(2,1)}), bf16[4,160,1024]{2,1,0:T(8,128)(2,1)}, u32[]{:S(2)}, u32[]{:S(2)}) async-start(bf16[4,160,1024]{2,1,0:T(8,128)(2,1)} %bitcast.257), calls=%async_computation.3 | async-start | bytes 2621440 | tf_op jit(solution)/shard_map/all_to_all | solution.py:160
  298.6 14.4 %copy-start.52 = (bf16[1024,4]{0,1:T(4,128)(2,1)S(1)}, bf16[1024,4]{0,1:T(4,128)(2,1)}, u32[]{:S(2)}) copy-start(bf16[1024,4]{0,1:T(4,128)(2,1)} %param.23) | copy-start | bytes 24580
  306.9 35.7 %all-to-all-start.1 = ((bf16[4,160,1024]{2,1,0:T(8,128)(2,1)}), bf16[4,160,1024]{2,1,0:T(8,128)(2,1)}, u32[]{:S(2)}, u32[]{:S(2)}) async-start(bf16[4,160,1024]{2,1,0:T(8,128)(2,1)} %bitcast.255), calls=%async_computation.1 | async-start | bytes 2621440 | tf_op jit(solution)/shard_map/all_to_all | solution.py:160
  313.4 31.7 %copy-start.42 = (f32[512,4]{0,1:T(4,128)}, f32[512,4]{0,1:T(4,128)S(1)}, u32[]{:S(2)}) copy-start(f32[512,4]{0,1:T(4,128)S(1)} %get-tuple-element.43) | copy-start | bytes 24580
  313.5 31.7 %copy-start.54 = (f32[512]{0:T(512)}, f32[512]{0:T(512)S(1)}, u32[]{:S(2)}) copy-start(f32[512]{0:T(512)S(1)} %log_add_fusion.1) | copy-start | bytes 6148
  348.9 35.2 %all-to-all-start.4 = ((bf16[4,160,1024]{2,1,0:T(8,128)(2,1)}), bf16[4,160,1024]{2,1,0:T(8,128)(2,1)}, u32[]{:S(2)}, u32[]{:S(2)}) async-start(bf16[4,160,1024]{2,1,0:T(8,128)(2,1)} %bitcast.36), calls=%async_computation.4 | async-start | bytes 2621440 | tf_op jit(solution)/shard_map/all_to_all | solution.py:194
  353.2 8.7 copy-start.21
  361.9 8.7 copy-start.34
  384.1 44.4 %all-to-all-start.6 = ((bf16[4,160,1024]{2,1,0:T(8,128)(2,1)}), bf16[4,160,1024]{2,1,0:T(8,128)(2,1)}, u32[]{:S(2)}, u32[]{:S(2)}) async-start(bf16[4,160,1024]{2,1,0:T(8,128)(2,1)} %bitcast.256), calls=%async_computation.6 | async-start | bytes 2621440 | tf_op jit(solution)/shard_map/all_to_all | solution.py:194
  388.5 303.4 %reduce-scatter.8.cloned.1.call-start = ((), (), s32[]{:S(2)}) async-start(), calls=%async_computation.17 | async-start | bytes 6488064 | tf_op jit(solution)/shard_map/reduce_scatter | solution.py:235
  388.5 26.3 %slice-start.5 = ((s8[7208960]{0:T(1024)(128)(4,1)}), s8[4194304]{0:T(1024)(128)(4,1)S(1)}, s32[]{:S(2)}) async-start(s8[7208960]{0:T(1024)(128)(4,1)} %bitcast.276), calls=%async_computation.23 | async-start | bytes 8388608
  398.5 16.3 %slice-start.6 = ((s8[7208960]{0:T(1024)(128)(4,1)}), s8[3014656]{0:T(1024)(128)(4,1)S(1)}, s32[]{:S(2)}) async-start(s8[7208960]{0:T(1024)(128)(4,1)} %bitcast.276), calls=%async_computation.24 | async-start | bytes 6029312
  428.5 26.2 %slice-start.2 = ((s8[11534336]{0:T(1024)(128)(4,1)}), s8[4194304]{0:T(1024)(128)(4,1)S(1)}, s32[]{:S(2)}) async-start(s8[11534336]{0:T(1024)(128)(4,1)} %bitcast.274), calls=%async_computation.20 | async-start | bytes 8388608
  438.5 16.2 %slice-start.3 = ((s8[11534336]{0:T(1024)(128)(4,1)}), s8[4194304]{0:T(1024)(128)(4,1)S(1)}, s32[]{:S(2)}) async-start(s8[11534336]{0:T(1024)(128)(4,1)} %bitcast.274), calls=%async_computation.21 | async-start | bytes 8388608
  438.5 16.2 %slice-start.4 = ((s8[11534336]{0:T(1024)(128)(4,1)}), s8[3145728]{0:T(1024)(128)(4,1)S(1)}, s32[]{:S(2)}) async-start(s8[11534336]{0:T(1024)(128)(4,1)} %bitcast.274), calls=%async_computation.22 | async-start | bytes 6291456
  466.1 228.1 %reduce-scatter.6.cloned.1.call-start = ((), (), s32[]{:S(2)}) async-start(), calls=%async_computation.16 | async-start | bytes 12976128 | tf_op jit(solution)/shard_map/reduce_scatter | solution.py:229
  466.1 18.0 %copy-start.26 = (bf16[640,2816]{1,0:T(8,128)(2,1)S(1)}, bf16[640,2816]{1,0:T(8,128)(2,1)}, u32[]{:S(2)}) copy-start(bf16[640,2816]{1,0:T(8,128)(2,1)} %get-tuple-element.26) | copy-start | bytes 10813444
  466.1 18.0 %copy-start.27 = (bf16[640,2816]{1,0:T(8,128)(2,1)S(1)}, bf16[640,2816]{1,0:T(8,128)(2,1)}, u32[]{:S(2)}) copy-start(bf16[640,2816]{1,0:T(8,128)(2,1)} %get-tuple-element.27) | copy-start | bytes 10813444
  515.3 36.0 %all-to-all-start.7 = ((bf16[4,160,1024]{2,1,0:T(8,128)(2,1)}), bf16[4,160,1024]{2,1,0:T(8,128)(2,1)S(1)}, u32[]{:S(2)}, u32[]{:S(2)}) async-start(bf16[4,160,1024]{2,1,0:T(8,128)(2,1)} %bitcast.44), calls=%async_computation.7 | async-start | bytes 2621440 | tf_op jit(solution)/shard_map/all_to_all | solution.py:210
  520.5 36.3 %copy-start.8 = (bf16[2,256,1024]{2,1,0:T(8,128)(2,1)S(1)}, bf16[2,256,1024]{2,1,0:T(8,128)(2,1)}, u32[]{:S(2)}) copy-start(bf16[2,256,1024]{2,1,0:T(8,128)(2,1)} %param.13) | copy-start | bytes 3145732
  520.5 36.3 %copy-start.48 = (f32[1024]{0:T(1024)S(1)}, f32[1024]{0:T(1024)}, u32[]{:S(2)}) copy-start(f32[1024]{0:T(1024)} %param.18) | copy-start | bytes 12292
  520.5 36.3 %copy-start.60 = (f32[2,256]{1,0:T(2,128)S(1)}, f32[2,256]{1,0:T(2,128)}, u32[]{:S(2)}) copy-start(f32[2,256]{1,0:T(2,128)} %get-tuple-element.36) | copy-start | bytes 6148
  534.2 23.9 %copy-start.43 = (f32[512,4]{0,1:T(4,128)S(1)}, f32[512,4]{0,1:T(4,128)}, u32[]{:S(2)}) copy-start(f32[512,4]{0,1:T(4,128)} %copy-done.42) | copy-start | bytes 24580
  534.2 23.9 %copy-start.44 = (f32[512,4]{0,1:T(4,128)S(1)}, f32[512,4]{0,1:T(4,128)}, u32[]{:S(2)}) copy-start(f32[512,4]{0,1:T(4,128)} %get-tuple-element.16) | copy-start | bytes 24580
  534.2 23.9 %copy-start.55 = (f32[512]{0:T(512)S(1)}, f32[512]{0:T(512)}, u32[]{:S(2)}) copy-start(f32[512]{0:T(512)} %copy-done.54) | copy-start | bytes 6148
  534.2 23.9 %copy-start.50 = (f32[512,2]{0,1:T(2,128)S(1)}, f32[512,2]{0,1:T(2,128)}, u32[]{:S(2)}) copy-start(f32[512,2]{0,1:T(2,128)} %copy-done.49) | copy-start | bytes 12292
  534.2 53.3 %copy-start.31 = (bf16[256,640]{1,0:T(8,128)(2,1)S(1)}, bf16[256,640]{1,0:T(8,128)(2,1)}, u32[]{:S(2)}) copy-start(bf16[256,640]{1,0:T(8,128)(2,1)} %copy-done.30) | copy-start | bytes 983044
  552.3 35.2 %all-to-all-start.5 = ((bf16[4,160,1024]{2,1,0:T(8,128)(2,1)}), bf16[4,160,1024]{2,1,0:T(8,128)(2,1)}, u32[]{:S(2)}, u32[]{:S(2)}) async-start(bf16[4,160,1024]{2,1,0:T(8,128)(2,1)} %bitcast.254), calls=%async_computation.5 | async-start | bytes 2621440 | tf_op jit(solution)/shard_map/all_to_all | solution.py:210
  556.6 33.0 %copy-start.4 = (f32[512,1024]{1,0:T(8,128)S(1)}, f32[512,1024]{1,0:T(8,128)}, u32[]{:S(2)}) copy-start(f32[512,1024]{1,0:T(8,128)} %copy-done.3) | copy-start | bytes 6291460
  556.7 33.0 %copy-start.46 = (f32[1024]{0:T(1024)S(1)}, f32[1024]{0:T(1024)}, u32[]{:S(2)}) copy-start(f32[1024]{0:T(1024)} %param.22) | copy-start | bytes 12292
  556.7 33.0 %copy-start.53 = (bf16[1024,4]{0,1:T(4,128)(2,1)S(1)}, bf16[1024,4]{0,1:T(4,128)(2,1)}, u32[]{:S(2)}) copy-start(bf16[1024,4]{0,1:T(4,128)(2,1)} %param.23) | copy-start | bytes 24580
  556.7 33.0 %copy-start.57 = (f32[512]{0:T(512)S(1)}, f32[512]{0:T(512)}, u32[]{:S(2)}) copy-start(f32[512]{0:T(512)} %copy-done.56) | copy-start | bytes 6148
  556.7 440.4 %reduce-scatter.4.cloned.1.call-start = ((), (), s32[]{:S(2)}) async-start(), calls=%async_computation.15 | async-start | bytes 17301504 | tf_op jit(solution)/shard_map/reduce_scatter | solution.py:299
  688.6 311.8 %copy-start.1 = (f32[32,16]{0,1:T(8,128)S(1)}, f32[32,16]{0,1:T(8,128)}, u32[]{:S(2)}) copy-start(f32[32,16]{0,1:T(8,128)} %param.21) | copy-start | bytes 6148
  (37 other events, 137.6 us)
Sparse Core Ops, SparseCore 0:
  10.9 72.2 all-gather.4
  86.1 54.9 all-gather.6
  143.0 66.5 all-gather.8
  211.4 43.3 all-gather.10
  466.2 59.4 reduce-scatter.7
  529.4 86.7 reduce-scatter.5
  632.9 364.1 reduce-scatter.3
where the time goes:
time: 1020 us; the launch traced here: 1010 us
  waiting for transfers between devices  546 us (54%)
  matrix products  279 us (27%)
  local copies, waits for them, and re-layouts  49.4 us (5%)
  blocking collectives  42.9 us (4%)
  other arithmetic  38.9 us (4%)
  starting transfers between devices  35.3 us (3%)
  between operations  15.6 us (2%)
    reduce_scatter x1, waiting for transfers between devices, on_device(): lax.psum_scatter(jnp.concatenate([qkv_part, proj_part], axis=1), ('dp', '...  300 us
    dot_general x4, matrix products, weight_term(): jnp.einsum('rd,rf->df', left, right, preferred_element_type=jnp.float32)  60.6 us
    all_to_all x2, waiting for transfers between devices, on_device(): lax.all_to_all(slot_input_grad.reshape(experts, capacity, width), 'expert...  43.5 us
    psum x1, blocking collectives, on_device(): lax.psum((gain_attn_grad, table_grad, gain_moe_grad, router_grad), ('dp',...  42.9 us
    all_gather x1, waiting for transfers between devices, on_device(): lax.all_gather(w_qkv, ('dp', 'expert'), axis=0, tiled=True)  42 us
    all_gather x1, waiting for transfers between devices, on_device(): lax.all_gather(w_out, 'dp', axis=1, tiled=True)  35.2 us
    all_to_all x2, waiting for transfers between devices, on_device(): lax.all_to_all(result, 'expert', split_axis=0, concat_axis=0, tiled=True)  33.4 us
    dot_general x2, matrix products, on_device(): jnp.dot(inputs_flat, back_in[:, :inner], preferred_element_type=jnp.float32)  32.5 us
  transfers between devices with their start and end apart: 15, of which 11 were waited for; matrix products, arithmetic and copies ran while one was open for 31% of the time, Pallas kernels for 0%

commit v1 on v0

v1 whole, which is shorter than its diff:
```python
from functools import partial

import jax
import jax.numpy as jnp
from jax import lax
from jax.sharding import PartitionSpec as P

EPSILON = 1e-06
NEG_BIG = -1e30
LIMITS = (12, 16, 23, 32, 46, 64, 91)
F32 = jnp.float32
BF16 = jnp.bfloat16


def bucket_of(offset):
    distance = jnp.abs(offset)
    far_part = 8 + sum(((distance >= limit).astype(jnp.int32) for limit in LIMITS))
    near_far = jnp.where(distance < 8, distance, far_part)
    return jnp.where(offset > 0, 16, 0) + near_far


def slot_positions(routes, experts):
    order = jnp.concatenate([routes[:, 0], routes[:, 1]])
    chosen = (order[:, None] == jnp.arange(experts, dtype=jnp.int32)[None, :]).astype(jnp.int32)
    before = jnp.cumsum(chosen, axis=0) - chosen
    place = jnp.sum(before * chosen, axis=1)
    return place.reshape(2, -1).T


def tree_mask(segment, parent):
    same = segment[None, :] == segment[:, None]
    upward = segment[None, :] == parent[:, None]
    downward = parent[None, :] == segment[:, None]
    return same | upward | downward


def rms_scale(values):
    return lax.rsqrt(jnp.mean(values * values, axis=-1, keepdims=True) + EPSILON)


def gelu_product(gate_part, up_part):
    return jax.nn.gelu(gate_part, approximate=True) * up_part


def flip(value, axis, size, bit):
    return lax.ppermute(value, axis, [(i, i ^ bit) for i in range(size)])


def shift(value, axis, size, step):
    return lax.ppermute(value, axis, [(i, (i + step) % size) for i in range(size)])


def halving_orders(size):
    bits = [1 << k for k in range(1, size.bit_length() - 1)]
    return (bits, bits[::-1])


def gather_pieces(block, size):
    half = block.shape[0] // 2
    found = []
    for part, order in enumerate(halving_orders(size)):
        have = [(0, block[part * half : (part + 1) * half])]
        for bit in order:
            have = have + [(rel ^ bit, flip(piece, "dp", size, bit)) for rel, piece in have]
        have = have + [(rel ^ 1, flip(piece, "dp", size, 1)) for rel, piece in have]
        found += [(rel, part * half, piece) for rel, piece in have]
    return found


def gather_dp(block, size):
    me = lax.axis_index("dp")
    full = jnp.zeros((size,) + block.shape, block.dtype)
    for rel, offset, piece in gather_pieces(block, size):
        full = lax.dynamic_update_slice(full, piece[None], (me ^ rel, offset, 0))
    return full.reshape(size * block.shape[0], block.shape[1])


def gather_expert(block, size):
    me = lax.axis_index("expert")
    full = jnp.zeros((size,) + block.shape, block.dtype)
    for step in range(size):
        piece = shift(block, "expert", size, step) if step else block
        full = lax.dynamic_update_slice(full, piece[None], ((me - step) % size, 0, 0))
    return full.reshape(size * block.shape[0], block.shape[1])


def split_bit(value, me, bit):
    mine = (me // bit) % 2
    kept = lax.dynamic_index_in_dim(value, mine, 0, keepdims=False)
    sent = lax.dynamic_index_in_dim(value, 1 - mine, 0, keepdims=False)
    return kept, sent


def scatter_dp(total, size):
    me = lax.axis_index("dp")
    rows, width = total.shape[0] // size, total.shape[1]
    half = rows // 2
    kept, sent = split_bit(jnp.moveaxis(total.reshape(size // 2, 2, rows, width), 1, 0), me, 1)
    summed = kept.astype(F32) + flip(sent, "dp", size, 1).astype(F32)
    outs = []
    for part, order in enumerate(halving_orders(size)):
        value = summed[:, part * half : (part + 1) * half]
        left = [1 << k for k in range(1, size.bit_length() - 1)]
        for bit in order:
            place = left.index(bit)
            high, low = 1 << (len(left) - 1 - place), 1 << place
            shaped = value.astype(BF16).reshape(high, 2, low, half, width)
            kept, sent = split_bit(jnp.moveaxis(shaped, 1, 0), me, bit)
            value = kept.astype(F32) + flip(sent, "dp", size, bit).astype(F32)
            left.remove(bit)
        outs.append(value.reshape(half, width))
    return jnp.concatenate(outs, axis=0)


def scatter_expert(total, size):
    me = lax.axis_index("expert")
    rows = total.shape[0] // size
    low = total.astype(BF16)
    result = lax.dynamic_slice_in_dim(total, me * rows, rows, 0)
    for step in range(1, size):
        block = lax.dynamic_slice_in_dim(low, ((me + step) % size) * rows, rows, 0)
        result = result + shift(block, "expert", size, step).astype(F32)
    return result


def sum_all(value, sizes):
    for axis in ("dp", "expert"):
        bit = 1
        while bit < sizes[axis]:
            value = value + flip(value, axis, sizes[axis], bit)
            bit *= 2
    return value


def dot(left, right):
    return jnp.dot(left, right, preferred_element_type=F32)


def dot_t(left, right):
    return lax.dot_general(left, right, (((1,), (1,)), ((), ())), preferred_element_type=F32)


def t_dot(left, right):
    return lax.dot_general(left, right, (((0,), (0,)), ((), ())), preferred_element_type=F32)


def on_device(
    sizes,
    tokens,
    cotangent,
    segment_ids,
    parent_ids,
    routes,
    gain_attn,
    w_qkv,
    w_proj,
    rel_bias,
    gain_moe,
    w_router,
    w_in,
    w_out,
):
    dp, experts = sizes["dp"], sizes["expert"]
    batches, length, width = tokens.shape
    heads = rel_bias.shape[1]
    head_size = width // heads
    inner = w_in.shape[2] // 2
    capacity = (10 * length + 4 * experts - 1) // (4 * experts)
    slot_count = experts * capacity
    scale = head_size ** (-0.5)
    me_e = lax.axis_index("expert")

    attn_w = gather_dp(gather_expert(jnp.concatenate([w_qkv, w_proj], axis=1), experts), dp)
    full_qkv, full_proj = attn_w[:, : 3 * width], attn_w[:, 3 * width :]

    relative = (routes - me_e) % experts
    places = jax.vmap(partial(slot_positions, experts=experts))(routes)
    targets = relative * capacity + places
    hot = targets[..., None] == jnp.arange(slot_count, dtype=jnp.int32)
    select = hot.astype(BF16)
    both = select[:, :, 0] + select[:, :, 1]

    def exchange(blocks, sign):
        parts = [blocks[:capacity]]
        for step in range(1, experts):
            parts.append(
                shift(blocks[step * capacity : (step + 1) * capacity], "expert", experts, sign * step)
            )
        return jnp.concatenate(parts, axis=0)

    out_grads = [cotangent[n] for n in range(batches)]
    go_slots = [
        exchange(t_dot(both[n], out_grads[n]).astype(BF16), 1) for n in range(batches)
    ]

    win_full = gather_dp(w_in[0], dp)
    wout_full = gather_dp(w_out[0], dp)

    positions = jnp.arange(length, dtype=jnp.int32)
    buckets = bucket_of(positions[None, :] - positions[:, None])
    bucket_hot = (buckets[:, :, None] == jnp.arange(rel_bias.shape[0], dtype=jnp.int32)).astype(F32)
    bias_heads = jnp.einsum("qkc,ch->hqk", bucket_hot, rel_bias, precision=lax.Precision.HIGHEST)

    saved = []
    for n in range(batches):
        h0 = tokens[n].astype(F32)
        r1 = rms_scale(h0)
        n1_hat = h0 * r1
        n1 = (n1_hat * gain_attn).astype(BF16)
        qkv = dot(n1, full_qkv).astype(BF16).reshape(length, 3, heads, head_size)
        q, k, v = qkv[:, 0], qkv[:, 1], qkv[:, 2]
        allowed = tree_mask(segment_ids[n], parent_ids[n])
        raw = jnp.einsum("qhd,khd->hqk", q, k, preferred_element_type=F32) * scale + bias_heads
        scores = jnp.where(allowed[None], raw, NEG_BIG)
        lse = jax.nn.logsumexp(scores, axis=-1, keepdims=True)
        p = jnp.exp(scores - lse)
        p_low = p.astype(BF16)
        o = jnp.einsum("hqk,khd->qhd", p_low, v, preferred_element_type=F32)
        o = o.reshape(length, width).astype(BF16)
        h1 = h0 + dot(o, full_proj)
        r2 = rms_scale(h1)
        n2_hat = h1 * r2
        n2 = (n2_hat * gain_moe).astype(BF16)
        probs = jax.nn.softmax(dot(n2, w_router), axis=-1)
        x_slots = exchange(t_dot(both[n], n2).astype(BF16), 1)
        saved.append((h0, r1, n1_hat, n1, q, k, v, p, p_low, o, h1, r2, n2_hat, n2, probs, x_slots))

    mine_hot = jnp.arange(experts, dtype=jnp.int32) == me_e
    held = []
    for n in range(batches):
        x = saved[n][-1]
        go = go_slots[n].astype(F32)
        gate = jnp.sum(
            jnp.where(mine_hot, jax.nn.softmax(dot(x, w_router), axis=-1), 0.0), -1, keepdims=True
        )
        dy = (gate * go).astype(BF16)
        a = dot(x, win_full[:, :inner])
        b = dot(x, win_full[:, inner:])
        g, back = jax.vjp(gelu_product, a, b)
        g = g.astype(BF16)
        y = dot(g, wout_full).astype(BF16)
        dgate = jnp.sum(go * y.astype(F32), axis=-1)
        da, db = back(dot_t(dy, wout_full))
        du = jnp.concatenate([da, db], axis=1).astype(BF16)
        dx = dot_t(du, win_full).astype(BF16)
        dgate_back = exchange(dgate, -1)
        dx_back = exchange(dx, -1)
        y_back = exchange(y, -1)
        held.append((x, du, g, dy, dgate_back, dx_back, y_back))

    in_part = sum(t_dot(h[0], h[1]) for h in held).astype(BF16)
    out_part = sum(t_dot(h[2], h[3]) for h in held).astype(BF16)
    in_total = scatter_dp(in_part, dp)
    out_total = scatter_dp(out_part, dp)

    outputs, input_grads = [], []
    qkv_part = proj_part = None
    table_grad = gain_attn_grad = gain_moe_grad = router_grad = 0.0
    for n in range(batches):
        h0, r1, n1_hat, n1, q, k, v, p, p_low, o, h1, r2, n2_hat, n2, probs, _ = saved[n]
        _, _, _, _, dgate_back, dx_back, y_back = held[n]
        go = out_grads[n].astype(F32)
        route_hot = (routes[n][:, :, None] == jnp.arange(experts, dtype=jnp.int32)).astype(F32)
        gates = jnp.sum(probs[:, None, :] * route_hot, axis=-1)
        picked0, picked1 = dot(select[n][:, 0], y_back), dot(select[n][:, 1], y_back)
        moe = gates[:, :1] * picked0 + gates[:, 1:] * picked1
        outputs.append((h1 + moe).astype(BF16))
        dgate = jnp.sum(jnp.where(hot[n], dgate_back, 0.0), axis=-1)
        dprobs = jnp.sum(route_hot * dgate[:, :, None], axis=1)
        dlogits = probs * (dprobs - jnp.sum(probs * dprobs, axis=-1, keepdims=True))
        dlogits = dlogits.astype(BF16)
        dn2 = dot(both[n], dx_back) + dot_t(dlogits, w_router)
        router_grad = router_grad + t_dot(n2, dlogits)
        gain_moe_grad = gain_moe_grad + jnp.sum(dn2 * n2_hat, axis=0)
        scaled = dn2 * gain_moe
        dh1 = go + r2 * (scaled - n2_hat * jnp.mean(scaled * n2_hat, axis=-1, keepdims=True))
        dbranch = dh1.astype(BF16)
        term = t_dot(o, dbranch)
        proj_part = term if proj_part is None else proj_part + term
        do = dot_t(dbranch, full_proj).astype(BF16).reshape(length, heads, head_size)
        dv = jnp.einsum("hqk,qhd->khd", p_low, do, preferred_element_type=F32)
        dp_ = jnp.einsum("qhd,khd->hqk", do, v, preferred_element_type=F32)
        ds = (p * (dp_ - jnp.sum(p * dp_, axis=-1, keepdims=True))).astype(BF16)
        dq = jnp.einsum("hqk,khd->qhd", ds, k, preferred_element_type=F32) * scale
        dk = jnp.einsum("hqk,qhd->khd", ds, q, preferred_element_type=F32) * scale
        table_grad = table_grad + jnp.einsum(
            "hqk,qkc->ch", ds, bucket_hot.astype(BF16), preferred_element_type=F32
        )
        dqkv = jnp.stack([dq, dk, dv], axis=1).reshape(length, 3 * width).astype(BF16)
        term = t_dot(n1, dqkv)
        qkv_part = term if qkv_part is None else qkv_part + term
        dn1 = dot_t(dqkv, full_qkv)
        gain_attn_grad = gain_attn_grad + jnp.sum(dn1 * n1_hat, axis=0)
        scaled = dn1 * gain_attn
        input_grad = dh1 + r1 * (
            scaled - n1_hat * jnp.mean(scaled * n1_hat, axis=-1, keepdims=True)
        )
        input_grads.append(input_grad.astype(BF16))

    proj_total = scatter_expert(scatter_dp(proj_part.astype(BF16), dp), experts)
    qkv_total = scatter_expert(scatter_dp(qkv_part.astype(BF16), dp), experts)
    small = jnp.concatenate(
        [gain_attn_grad, table_grad.reshape(-1), gain_moe_grad, router_grad.reshape(-1)]
    )
    small = sum_all(small.reshape(-1, 128), sizes).reshape(-1)
    cuts = (width, width + table_grad.size, 2 * width + table_grad.size)
    return (
        jnp.stack(outputs),
        jnp.stack(input_grads),
        small[: cuts[0]],
        qkv_total,
        proj_total,
        small[cuts[0] : cuts[1]].reshape(table_grad.shape),
        small[cuts[1] : cuts[2]],
        small[cuts[2] :].reshape(router_grad.shape),
        in_total[None],
        out_total[None],
    )


def solution(mesh):
    rows = P(None, ("dp", "expert"), None)
    in_specs = (
        rows,
        rows,
        P(None, ("dp", "expert")),
        P(None, ("dp", "expert")),
        rows,
        P(),
        P(("dp", "expert"), None),
        P(("dp", "expert"), None),
        P(),
        P(),
        P(),
        P("expert", "dp", None),
        P("expert", "dp", None),
    )
    out_specs = (
        rows,
        rows,
        P(),
        P(("dp", "expert"), None),
        P(("dp", "expert"), None),
        P(),
        P(),
        P(),
        P("expert", "dp", None),
        P("expert", "dp", None),
    )
    return jax.shard_map(
        partial(on_device, dict(mesh.shape)),
        mesh=mesh,
        in_specs=in_specs,
        out_specs=out_specs,
        check_vma=False,
    )
```

time: 1020 us -> 862 us (0.85)
  waiting for transfers between devices: 546 us -> 301 us
  starting transfers between devices: 35.3 us -> 156 us
  local copies, waits for them, and re-layouts: 49.4 us -> 110 us
  blocking collectives: 42.9 us -> 0 us
  matrix products: 279 us -> 246 us
  between operations: 15.6 us -> 3.77 us
    ppermute x0 -> x106, waiting for transfers between devices: none -> 301 us  [the longest x67 232 us: flip(): return lax.ppermute(value, axis, [(i, i ^ bit) for i in range(size)])]
    reduce_scatter x3 -> x0, waiting for transfers between devices: 300 us -> none  [the longest x1 300 us: on_device(): lax.psum_scatter(jnp.concatenate([qkv_part, proj_part], axis=1), ('dp', '...]
    ppermute x0 -> x106, starting transfers between devices: none -> 156 us  [the longest x39 108 us: shift(): lax.ppermute(value, axis, [(i, (i + step) % size) for i in range(size)])]
    all_gather x4 -> x0, waiting for transfers between devices: 125 us -> none  [the longest x1 42 us: on_device(): lax.all_gather(w_qkv, ('dp', 'expert'), axis=0, tiled=True)]
    all_to_all x8 -> x0, waiting for transfers between devices: 119 us -> none  [the longest x2 43.5 us: on_device(): lax.all_to_all(slot_input_grad.reshape(experts, capacity, width), 'expert...]
    psum x1 -> x0, blocking collectives: 42.9 us -> none  [on_device(): lax.psum((gain_attn_grad, table_grad, gain_moe_grad, router_grad), ('dp',...]
    all_to_all x8 -> x0, starting transfers between devices: 35.1 us -> none  [the longest x2 9.47 us: on_device(): lax.all_to_all(result, 'expert', split_axis=0, concat_axis=0, tiled=True)]
    dot_general x40 -> x58, matrix products: 276 us -> 242 us  [the longest x20 85.6 us: dot(): return jnp.dot(left, right, preferred_element_type=F32)]
  transfers between devices with their start and end apart: 15 -> 106, of which waited for: 11 -> 46; matrix products, arithmetic and copies ran while one was open for 31% -> 43% of each run, Pallas kernels for 0% -> 0%
where the time goes in v1:
time: 862 us; the launch traced here: 852 us
  waiting for transfers between devices  301 us (35%)
  matrix products  246 us (29%)
  starting transfers between devices  156 us (18%)
  local copies, waits for them, and re-layouts  110 us (13%)
  other arithmetic  34.5 us (4%)
    ppermute x67, waiting for transfers between devices, flip(): return lax.ppermute(value, axis, [(i, i ^ bit) for i in range(size)])  232 us
    ppermute x39, starting transfers between devices, shift(): lax.ppermute(value, axis, [(i, (i + step) % size) for i in range(size)])  108 us
    dot_general x20, matrix products, dot(): return jnp.dot(left, right, preferred_element_type=F32)  85.6 us
    dot_general x14, matrix products, t_dot(): lax.dot_general(left, right, (((0,), (0,)), ((), ())), preferred_element_...  71.5 us
    ppermute x39, waiting for transfers between devices, shift(): lax.ppermute(value, axis, [(i, (i + step) % size) for i in range(size)])  69.2 us
    dot_general x10, matrix products, dot_t(): lax.dot_general(left, right, (((1,), (1,)), ((), ())), preferred_element_...  53.7 us
    ppermute x67, starting transfers between devices, flip(): return lax.ppermute(value, axis, [(i, i ^ bit) for i in range(size)])  48.1 us
    dynamic_update_slice x46, local copies, waits for them, and re-layouts, gather_dp(): full = lax.dynamic_update_slice(full, piece[None], (me ^ rel, offset, 0))  25.6 us
  transfers between devices with their start and end apart: 106, of which 46 were waited for; matrix products, arithmetic and copies ran while one was open for 43% of the time, Pallas kernels for 0%

profile of v1, /device:TPU:0, one launch (start us, length us, event | category | flops | bytes accessed | tf_op | source)
XLA Modules:
  0.0 851.7 jit_solution(13280595772864688576)
XLA Ops:
  38.8 5.2 broadcast_in_dim.287
  61.8 8.0 collective-permute-done.20
  78.8 6.8 collective-permute-done.36
  91.2 12.3 %collective-permute-done.4 = bf16[64,4096]{1,0:T(8,128)(2,1)S(1)} collective-permute-done((bf16[64,4096]{1,0:T(8,128)(2,1)S(1)}, bf16[64,4096]{1,0:T(8,128)(2,1)S(1)}, u32[]{:S(2)}, u32[]{:S(2)}) %collective-permute-start.4) | collective-permute-done | bytes 524320 | tf_op jit(solution)/shard_map/ppermute | solution.py:46
  108.8 6.9 collective-permute-done.43
  121.9 11.7 %collective-permute-done.5 = bf16[64,4096]{1,0:T(8,128)(2,1)S(1)} collective-permute-done((bf16[64,4096]{1,0:T(8,128)(2,1)S(1)}, bf16[64,4096]{1,0:T(8,128)(2,1)S(1)}, u32[]{:S(2)}, u32[]{:S(2)}) %collective-permute-start.5) | collective-permute-done | bytes 524320 | tf_op jit(solution)/shard_map/ppermute | solution.py:46
  140.9 16.8 %collective-permute-done.22 = bf16[64,5632]{1,0:T(8,128)(2,1)} collective-permute-done((bf16[64,5632]{1,0:T(8,128)(2,1)S(1)}, bf16[64,5632]{1,0:T(8,128)(2,1)}, u32[]{:S(2)}, u32[]{:S(2)}) %collective-permute-start.22) | collective-permute-done | bytes 720928 | tf_op jit(solution)/shard_map/ppermute | solution.py:46
  168.2 12.4 %collective-permute-done.10 = bf16[64,4096]{1,0:T(8,128)(2,1)S(1)} collective-permute-done((bf16[64,4096]{1,0:T(8,128)(2,1)S(1)}, bf16[64,4096]{1,0:T(8,128)(2,1)S(1)}, u32[]{:S(2)}, u32[]{:S(2)}) %collective-permute-start.10) | collective-permute-done | bytes 524320 | tf_op jit(solution)/shard_map/ppermute | solution.py:46
  181.2 12.5 %collective-permute-done.11 = bf16[64,4096]{1,0:T(8,128)(2,1)S(1)} collective-permute-done((bf16[64,4096]{1,0:T(8,128)(2,1)S(1)}, bf16[64,4096]{1,0:T(8,128)(2,1)S(1)}, u32[]{:S(2)}, u32[]{:S(2)}) %collective-permute-start.11) | collective-permute-done | bytes 524320 | tf_op jit(solution)/shard_map/ppermute | solution.py:46
  194.4 11.6 %collective-permute-done.12 = bf16[64,4096]{1,0:T(8,128)(2,1)S(1)} collective-permute-done((bf16[64,4096]{1,0:T(8,128)(2,1)S(1)}, bf16[64,4096]{1,0:T(8,128)(2,1)S(1)}, u32[]{:S(2)}, u32[]{:S(2)}) %collective-permute-start.12) | collective-permute-done | bytes 524320 | tf_op jit(solution)/shard_map/ppermute | solution.py:46
  221.8 5.8 fusion.258
  238.4 5.8 fusion.259
  260.2 14.0 %collective-permute-done.29 = bf16[64,5632]{1,0:T(8,128)(2,1)S(1)} collective-permute-done((bf16[64,5632]{1,0:T(8,128)(2,1)}, bf16[64,5632]{1,0:T(8,128)(2,1)S(1)}, u32[]{:S(2)}, u32[]{:S(2)}) %collective-permute-start.29) | collective-permute-done | bytes 720928 | tf_op jit(solution)/shard_map/ppermute | solution.py:46
  279.6 6.9 collective-permute-done.19
  290.8 17.5 %collective-permute-done.18 = bf16[160,1024]{1,0:T(8,128)(2,1)S(1)} collective-permute-done((bf16[160,1024]{1,0:T(8,128)(2,1)S(1)}, bf16[160,1024]{1,0:T(8,128)(2,1)S(1)}, u32[]{:S(2)}, u32[]{:S(2)}) %collective-permute-start.18) | collective-permute-done | bytes 327712 | tf_op jit(solution)/shard_map/ppermute | solution.py:50
  308.3 13.9 %collective-permute-start.51 = (bf16[160,1024]{1,0:T(8,128)(2,1)S(1)}, bf16[160,1024]{1,0:T(8,128)(2,1)S(1)}, u32[]{:S(2)}, u32[]{:S(2)}) collective-permute-start(bf16[160,1024]{1,0:T(8,128)(2,1)S(1)} %get-tuple-element.98), channel_id=1, source_target_pairs={{0,1},{1,2},{2,3},{3,0},{4,5},{5,6},{6,7},{7,4},{8,9},{9,10},{10,1... | collective-permute-start | bytes 983048 | tf_op jit(solution)/shard_map/ppermute | solution.py:50
  322.1 6.9 fusion.22
  332.5 10.0 %collective-permute-done.52 = bf16[160,1024]{1,0:T(8,128)(2,1)S(1)} collective-permute-done((bf16[160,1024]{1,0:T(8,128)(2,1)S(1)}, bf16[160,1024]{1,0:T(8,128)(2,1)S(1)}, u32[]{:S(2)}, u32[]{:S(2)}) %collective-permute-start.52) | collective-permute-done | bytes 327712 | tf_op jit(solution)/shard_map/ppermute | solution.py:50
  346.2 9.6 %fusion.156 = f32[640,2816]{1,0:T(8,128)} fusion(bf16[2816,1024]{1,0:T(8,128)(2,1)} %bitcast.76, f32[640]{0:T(1024)S(1)} %get-tuple-element.58, bf16[160,1024]{1,0:T(8,128)(2,1)} %collective-permute-done.59, bf16[160,1024]{1,0:T(8,128)(2,1)S(1)} %collective-permute-done.58, bf16[160,1024]{1,0:T(8,128)(2,1)S(1)} %collective-permute-done.57, ...), kind=kOutput, calls=%fused_computation.277 | convolution fusion | flops 3697541120 | bytes 14289408 | tf_op jit(solution)/shard_map/dot_general | solution.py:140
  355.8 16.1 %fusion.8 = (bf16[640,2816]{1,0:T(8,128)(2,1)}, bf16[640,2816]{1,0:T(8,128)(2,1)}, bf16[640,2816]{1,0:T(8,128)(2,1)}) fusion(f32[640,2816]{1,0:T(8,128)} %fusion.156, f32[640,2816]{1,0:T(8,128)} %fusion.22, bf16[1024,5632]{1,0:T(8,128)(2,1)S(1)} %bitcast.521, bf16[160,1024]{1,0:T(8,128)(2,1)S(1)} %collective-permute-done.19, ...), kind=kOutput, calls=%fused_computation.18 | convolution fusion | flops 3743088640 | bytes 32309248 | tf_op jit(solution)/shard_map/dot_general | solution.py:136
  371.9 8.0 fusion.55
  380.0 9.3 %collective-permute-start.65 = (f32[160]{0:T(256)S(1)}, f32[160]{0:T(256)S(1)}, u32[]{:S(2)}, u32[]{:S(2)}) collective-permute-start(f32[160]{0:T(256)S(1)} %get-tuple-element.139), channel_id=1, source_target_pairs={{0,1},{1,2},{2,3},{3,0},{4,5},{5,6},{6,7},{7,4},{8,9},{9,10},{10,1... | collective-permute-start | bytes 1928 | tf_op jit(solution)/shard_map/ppermute | solution.py:50
  391.8 6.9 fusion.20
  401.8 9.8 %fusion.152 = f32[640,2816]{1,0:T(8,128)} fusion(bf16[2816,1024]{1,0:T(8,128)(2,1)} %bitcast.76, f32[640]{0:T(1024)S(1)} %get-tuple-element.59, bf16[160,1024]{1,0:T(8,128)(2,1)} %collective-permute-done.68, bf16[160,1024]{1,0:T(8,128)(2,1)} %collective-permute-done.67, bf16[160,1024]{1,0:T(8,128)(2,1)} %collective-permute-done.66, ...), kind=kOutput, calls=%fused_computation.275 | convolution fusion | flops 3697541120 | bytes 14289408 | tf_op jit(solution)/shard_map/dot_general | solution.py:140
  411.6 14.9 %fusion.15 = (bf16[640,2816]{1,0:T(8,128)(2,1)}, bf16[640,2816]{1,0:T(8,128)(2,1)}, bf16[640,2816]{1,0:T(8,128)(2,1)}) fusion(f32[640,2816]{1,0:T(8,128)} %fusion.152, f32[640,2816]{1,0:T(8,128)} %fusion.20, bf16[1024,5632]{1,0:T(8,128)(2,1)S(1)} %bitcast.523, bf16[160,1024]{1,0:T(8,128)(2,1)S(1)} %copy-done.68, bf16[160,1024]{1,0:T(8,128)(2,1)S(1)} %copy-done.70, ...), kind=kOutput, calls=%fused_computation.25 | convolution fusion | flops 3743088640 | bytes 32309248 | tf_op jit(solution)/shard_map/dot_general | solution.py:136
  426.5 7.9 fusion.57
  437.9 10.7 %fusion.62 = bf16[640,1024]{1,0:T(8,128)(2,1)} fusion(bf16[1024,5632]{1,0:T(8,128)(2,1)S(1)} %bitcast.524, bf16[640,2816]{1,0:T(8,128)(2,1)} %get-tuple-element.64, bf16[640,2816]{1,0:T(8,128)(2,1)} %get-tuple-element.63), kind=kOutput, calls=%fused_computation.110 | convolution fusion | flops 7397048320 | bytes 20054016 | tf_op jit(solution)/shard_map/dot_general | solution.py:140
  451.1 10.7 %fusion.61 = bf16[640,1024]{1,0:T(8,128)(2,1)} fusion(bf16[1024,5632]{1,0:T(8,128)(2,1)S(1)} %bitcast.525, bf16[640,2816]{1,0:T(8,128)(2,1)} %get-tuple-element.61, bf16[640,2816]{1,0:T(8,128)(2,1)} %get-tuple-element.60), kind=kOutput, calls=%fused_computation.109 | convolution fusion | flops 7397048320 | bytes 20054016 | tf_op jit(solution)/shard_map/dot_general | solution.py:140
  464.1 17.2 %fusion.28 = f32[1024,5632]{1,0:T(8,128)} fusion(bf16[640,2816]{1,0:T(8,128)(2,1)} %get-tuple-element.64, bf16[640,2816]{1,0:T(8,128)(2,1)} %get-tuple-element.63, bf16[160,1024]{1,0:T(8,128)(2,1)} %copy-done.67, bf16[160,1024]{1,0:T(8,128)(2,1)} %copy-done.69, bf16[160,1024]{1,0:T(8,128)(2,1)} %copy-done.71, bf16[160,1024]{1,0:T(8,128)(2,1)S(1)} %get-tuple-element.95), kind=kOutput, calls=%fused_computation.49 | convolution fusion | flops 7401635840 | bytes 31588352 | tf_op jit(solution)/shard_map/dot_general | solution.py:144
  481.3 17.7 %add_convert_fusion = bf16[1024,5632]{1,0:T(8,128)(2,1)} fusion(f32[1024,5632]{1,0:T(8,128)} %fusion.28, bf16[640,2816]{1,0:T(8,128)(2,1)S(1)} %copy-done.40, bf16[640,2816]{1,0:T(8,128)(2,1)S(1)} %copy-done.39, bf16[160,1024]{1,0:T(8,128)(2,1)S(1)} %collective-permute-done.19, bf16[160,1024]{1,0:T(8,128)(2,1)} %copy-done.65, ...), kind=kOutput, calls=%fused_computation | convolution fusion | flops 7413170176 | bytes 43122688 | tf_op jit(solution)/shard_map/dot_general | solution.py:144
  499.1 5.6 dynamic-slice_bitcast_fusion
  504.8 5.9 fusion.154
  510.7 7.3 add_convert_fusion.2
  537.4 6.7 collective-permute-start.60
  545.1 13.8 %collective-permute-done.70 = bf16[160,1024]{1,0:T(8,128)(2,1)} collective-permute-done((bf16[160,1024]{1,0:T(8,128)(2,1)S(1)}, bf16[160,1024]{1,0:T(8,128)(2,1)}, u32[]{:S(2)}, u32[]{:S(2)}) %collective-permute-start.70) | collective-permute-done | bytes 327712 | tf_op jit(solution)/shard_map/ppermute | solution.py:50
  558.9 11.6 %collective-permute-start.56 = (bf16[160,1024]{1,0:T(8,128)(2,1)}, bf16[160,1024]{1,0:T(8,128)(2,1)}, u32[]{:S(2)}, u32[]{:S(2)}) collective-permute-start(bf16[160,1024]{1,0:T(8,128)(2,1)} %get-tuple-element.88), channel_id=1, source_target_pairs={{0,1},{1,2},{2,3},{3,0},{4,5},{5,6},{6,7},{7,4},{8,9},{9,10},{10,1... | collective-permute-start | bytes 983048 | tf_op jit(solution)/shard_map/ppermute | solution.py:50
  578.2 12.2 %collective-permute-done.61 = bf16[160,1024]{1,0:T(8,128)(2,1)} collective-permute-done((bf16[160,1024]{1,0:T(8,128)(2,1)}, bf16[160,1024]{1,0:T(8,128)(2,1)}, u32[]{:S(2)}, u32[]{:S(2)}) %collective-permute-start.61) | collective-permute-done | bytes 327712 | tf_op jit(solution)/shard_map/ppermute | solution.py:50
  590.4 12.3 %collective-permute-start.50 = (bf16[160,1024]{1,0:T(8,128)(2,1)}, bf16[160,1024]{1,0:T(8,128)(2,1)}, u32[]{:S(2)}, u32[]{:S(2)}) collective-permute-start(bf16[160,1024]{1,0:T(8,128)(2,1)} %get-tuple-element.84), channel_id=1, source_target_pairs={{0,1},{1,2},{2,3},{3,0},{4,5},{5,6},{6,7},{7,4},{8,9},{9,10},{10,1... | collective-permute-start | bytes 983048 | tf_op jit(solution)/shard_map/ppermute | solution.py:50
  644.6 6.6 fusion.164
  656.6 7.1 add_convert_fusion.1
  730.1 13.2 %collective-permute-done.104 = bf16[1,2,176,1024]{3,2,1,0:T(8,128)(2,1)S(1)} collective-permute-done((bf16[1,2,176,1024]{3,2,1,0:T(8,128)(2,1)S(1)}, bf16[1,2,176,1024]{3,2,1,0:T(8,128)(2,1)S(1)}, u32[]{:S(2)}, u32[]{:S(2)}) %collective-permute-start.104) | collective-permute-done | bytes 720928 | tf_op jit(solution)/shard_map/ppermute | solution.py:46
  747.8 21.3 %collective-permute-done.105 = bf16[1,1,176,1024]{3,2,1,0:T(8,128)(2,1)S(1)} collective-permute-done((bf16[1,1,176,1024]{3,2,1,0:T(8,128)(2,1)S(1)}, bf16[1,1,176,1024]{3,2,1,0:T(8,128)(2,1)S(1)}, u32[]{:S(2)}, u32[]{:S(2)}) %collective-permute-start.105) | collective-permute-done | bytes 360480 | tf_op jit(solution)/shard_map/ppermute | solution.py:46
  773.2 6.9 collective-permute-done.82
  786.1 5.7 fusion
  795.4 5.1 collective-permute-done.86
  803.7 19.2 %collective-permute-done.99 = bf16[1,2,64,5632]{3,2,1,0:T(8,128)(2,1)S(1)} collective-permute-done((bf16[1,2,64,5632]{3,2,1,0:T(8,128)(2,1)S(1)}, bf16[1,2,64,5632]{3,2,1,0:T(8,128)(2,1)S(1)}, u32[]{:S(2)}, u32[]{:S(2)}) %collective-permute-start.99) | collective-permute-done | bytes 1441824 | tf_op jit(solution)/shard_map/ppermute | solution.py:46
  824.7 12.3 %collective-permute-done.97 = bf16[2,1,64,5632]{3,2,0,1:T(8,128)(2,1)S(1)} collective-permute-done((bf16[2,1,64,5632]{3,2,0,1:T(8,128)(2,1)S(1)}, bf16[2,1,64,5632]{3,2,0,1:T(8,128)(2,1)S(1)}, u32[]{:S(2)}, u32[]{:S(2)}) %collective-permute-start.97) | collective-permute-done | bytes 1441824 | tf_op jit(solution)/shard_map/ppermute | solution.py:46
  839.4 9.6 %collective-permute-done.100 = bf16[1,1,64,5632]{3,2,1,0:T(8,128)(2,1)S(1)} collective-permute-done((bf16[1,1,64,5632]{3,2,1,0:T(8,128)(2,1)S(1)}, bf16[1,1,64,5632]{3,2,1,0:T(8,128)(2,1)S(1)}, u32[]{:S(2)}, u32[]{:S(2)}) %collective-permute-start.100) | collective-permute-done | bytes 720928 | tf_op jit(solution)/shard_map/ppermute | solution.py:46
  (721 shorter events, 341.8 us)
Async XLA Ops:
  3.8 43.0 %collective-permute-start = (bf16[32,4096]{1,0:T(8,128)(2,1)}, bf16[32,4096]{1,0:T(8,128)(2,1)}, u32[]{:S(2)}, u32[]{:S(2)}) collective-permute-start(bf16[32,4096]{1,0:T(8,128)(2,1)} %constant_dynamic-update-slice_fusion), channel_id=1, source_target_pairs={{0,1},{1,2},{2,3},{3,0},{4,5},{5,6},{6,7},{7,4},{8,9},{9,10},{10,1... | collective-permute-start | bytes 786440 | tf_op jit(solution)/shard_map/ppermute | solution.py:50
  6.8 41.7 %collective-permute-start.1 = (bf16[32,4096]{1,0:T(8,128)(2,1)}, bf16[32,4096]{1,0:T(8,128)(2,1)}, u32[]{:S(2)}, u32[]{:S(2)}) collective-permute-start(bf16[32,4096]{1,0:T(8,128)(2,1)} %constant_dynamic-update-slice_fusion), channel_id=1, source_target_pairs={{0,2},{1,3},{2,0},{3,1},{4,6},{5,7},{6,4},{7,5},{8,10},{9,11},{10,... | collective-permute-start | bytes 786440 | tf_op jit(solution)/shard_map/ppermute | solution.py:50
  9.4 41.3 %collective-permute-start.2 = (bf16[32,4096]{1,0:T(8,128)(2,1)}, bf16[32,4096]{1,0:T(8,128)(2,1)}, u32[]{:S(2)}, u32[]{:S(2)}) collective-permute-start(bf16[32,4096]{1,0:T(8,128)(2,1)} %constant_dynamic-update-slice_fusion), channel_id=1, source_target_pairs={{0,3},{1,0},{2,1},{3,2},{4,7},{5,4},{6,5},{7,6},{8,11},{9,8},{10,9... | collective-permute-start | bytes 786440 | tf_op jit(solution)/shard_map/ppermute | solution.py:50
  15.0 40.2 %collective-permute-start.34 = (bf16[176,1024]{1,0:T(8,128)(2,1)}, bf16[176,1024]{1,0:T(8,128)(2,1)}, u32[]{:S(2)}, u32[]{:S(2)}) collective-permute-start(bf16[176,1024]{1,0:T(8,128)(2,1)} %get-tuple-element.119), channel_id=1, source_target_pairs={{0,8},{4,12},{8,0},{12,4},{16,24},{20,28},{24,16},{28,20},{1,9},{5... | collective-permute-start | bytes 1081352 | tf_op jit(solution)/shard_map/ppermute | solution.py:46
  16.5 42.0 %collective-permute-start.35 = (bf16[176,1024]{1,0:T(8,128)(2,1)}, bf16[176,1024]{1,0:T(8,128)(2,1)}, u32[]{:S(2)}, u32[]{:S(2)}) collective-permute-start(bf16[176,1024]{1,0:T(8,128)(2,1)} %get-tuple-element.119), channel_id=1, source_target_pairs={{0,16},{4,20},{8,24},{12,28},{16,0},{20,4},{24,8},{28,12},{1,17},{... | collective-permute-start | bytes 1081352 | tf_op jit(solution)/shard_map/ppermute | solution.py:46
  46.8 39.6 %collective-permute-start.37 = (bf16[176,1024]{1,0:T(8,128)(2,1)}, bf16[176,1024]{1,0:T(8,128)(2,1)S(1)}, u32[]{:S(2)}, u32[]{:S(2)}) collective-permute-start(bf16[176,1024]{1,0:T(8,128)(2,1)} %get-tuple-element.119), channel_id=1, source_target_pairs={{0,4},{4,0},{8,12},{12,8},{16,20},{20,16},{24,28},{28,24},{1,5},{5... | collective-permute-start | bytes 1081352 | tf_op jit(solution)/shard_map/ppermute | solution.py:46
  48.5 55.1 %collective-permute-start.41 = (bf16[176,1024]{1,0:T(8,128)(2,1)}, bf16[176,1024]{1,0:T(8,128)(2,1)S(1)}, u32[]{:S(2)}, u32[]{:S(2)}) collective-permute-start(bf16[176,1024]{1,0:T(8,128)(2,1)} %get-tuple-element.118), channel_id=1, source_target_pairs={{0,16},{4,20},{8,24},{12,28},{16,0},{20,4},{24,8},{28,12},{1,17},{... | collective-permute-start | bytes 1081352 | tf_op jit(solution)/shard_map/ppermute | solution.py:46
  55.3 52.7 %collective-permute-start.42 = (bf16[176,1024]{1,0:T(8,128)(2,1)S(1)}, bf16[176,1024]{1,0:T(8,128)(2,1)S(1)}, u32[]{:S(2)}, u32[]{:S(2)}) collective-permute-start(bf16[176,1024]{1,0:T(8,128)(2,1)S(1)} %copy-done.64), channel_id=1, source_target_pairs={{0,8},{4,12},{8,0},{12,4},{16,24},{20,28},{24,16},{28,20},{1,9},{5... | collective-permute-start | bytes 1081352 | tf_op jit(solution)/shard_map/ppermute | solution.py:46
  87.7 28.8 %collective-permute-start.44 = (bf16[176,1024]{1,0:T(8,128)(2,1)S(1)}, bf16[176,1024]{1,0:T(8,128)(2,1)S(1)}, u32[]{:S(2)}, u32[]{:S(2)}) collective-permute-start(bf16[176,1024]{1,0:T(8,128)(2,1)S(1)} %copy-done.64), channel_id=1, source_target_pairs={{0,4},{4,0},{8,12},{12,8},{16,20},{20,16},{24,28},{28,24},{1,5},{5... | collective-permute-start | bytes 1081352 | tf_op jit(solution)/shard_map/ppermute | solution.py:46
  88.4 71.9 %collective-permute-start.23 = (bf16[64,5632]{1,0:T(8,128)(2,1)S(1)}, bf16[64,5632]{1,0:T(8,128)(2,1)S(1)}, u32[]{:S(2)}, u32[]{:S(2)}) collective-permute-start(bf16[64,5632]{1,0:T(8,128)(2,1)S(1)} %copy-done.59), channel_id=1, source_target_pairs={{0,4},{4,0},{8,12},{12,8},{16,20},{20,16},{24,28},{28,24},{1,5},{5... | collective-permute-start | bytes 2162696 | tf_op jit(solution)/shard_map/ppermute | solution.py:46
  103.6 150.4 %collective-permute-start.27 = (bf16[64,5632]{1,0:T(8,128)(2,1)}, bf16[64,5632]{1,0:T(8,128)(2,1)}, u32[]{:S(2)}, u32[]{:S(2)}) collective-permute-start(bf16[64,5632]{1,0:T(8,128)(2,1)} %get-tuple-element.72), channel_id=1, source_target_pairs={{0,16},{4,20},{8,24},{12,28},{16,0},{20,4},{24,8},{28,12},{1,17},{... | collective-permute-start | bytes 2162696 | tf_op jit(solution)/shard_map/ppermute | solution.py:46
  119.9 139.0 %collective-permute-start.28 = (bf16[64,5632]{1,0:T(8,128)(2,1)}, bf16[64,5632]{1,0:T(8,128)(2,1)}, u32[]{:S(2)}, u32[]{:S(2)}) collective-permute-start(bf16[64,5632]{1,0:T(8,128)(2,1)} %get-tuple-element.72), channel_id=1, source_target_pairs={{0,8},{4,12},{8,0},{12,4},{16,24},{20,28},{24,16},{28,20},{1,9},{5... | collective-permute-start | bytes 2162696 | tf_op jit(solution)/shard_map/ppermute | solution.py:46
  121.2 153.0 %collective-permute-start.30 = (bf16[64,5632]{1,0:T(8,128)(2,1)}, bf16[64,5632]{1,0:T(8,128)(2,1)}, u32[]{:S(2)}, u32[]{:S(2)}) collective-permute-start(bf16[64,5632]{1,0:T(8,128)(2,1)} %get-tuple-element.72), channel_id=1, source_target_pairs={{0,4},{4,0},{8,12},{12,8},{16,20},{20,16},{24,28},{28,24},{1,5},{5... | collective-permute-start | bytes 2162696 | tf_op jit(solution)/shard_map/ppermute | solution.py:46
  157.7 185.5 %collective-permute-start.59 = (bf16[160,1024]{1,0:T(8,128)(2,1)}, bf16[160,1024]{1,0:T(8,128)(2,1)}, u32[]{:S(2)}, u32[]{:S(2)}) collective-permute-start(bf16[160,1024]{1,0:T(8,128)(2,1)} %get-tuple-element.100), channel_id=1, source_target_pairs={{0,3},{1,0},{2,1},{3,2},{4,7},{5,4},{6,5},{7,6},{8,11},{9,8},{10,9... | collective-permute-start | bytes 983048 | tf_op jit(solution)/shard_map/ppermute | solution.py:50
  213.6 42.2 %collective-permute-start.26 = (bf16[64,5632]{1,0:T(8,128)(2,1)}, bf16[64,5632]{1,0:T(8,128)(2,1)}, u32[]{:S(2)}, u32[]{:S(2)}) collective-permute-start(bf16[64,5632]{1,0:T(8,128)(2,1)} %collective-permute-done.22), channel_id=1, source_target_pairs={{0,4},{4,0},{8,12},{12,8},{16,20},{20,16},{24,28},{28,24},{1,5},{5... | collective-permute-start | bytes 2162696 | tf_op jit(solution)/shard_map/ppermute | solution.py:46
  254.0 91.3 %collective-permute-start.58 = (bf16[160,1024]{1,0:T(8,128)(2,1)S(1)}, bf16[160,1024]{1,0:T(8,128)(2,1)S(1)}, u32[]{:S(2)}, u32[]{:S(2)}) collective-permute-start(bf16[160,1024]{1,0:T(8,128)(2,1)S(1)} %copy-done.80), channel_id=1, source_target_pairs={{0,2},{1,3},{2,0},{3,1},{4,6},{5,7},{6,4},{7,5},{8,10},{9,11},{10,... | collective-permute-start | bytes 983048 | tf_op jit(solution)/shard_map/ppermute | solution.py:50
  278.3 29.9 %collective-permute-start.18 = (bf16[160,1024]{1,0:T(8,128)(2,1)S(1)}, bf16[160,1024]{1,0:T(8,128)(2,1)S(1)}, u32[]{:S(2)}, u32[]{:S(2)}) collective-permute-start(bf16[160,1024]{1,0:T(8,128)(2,1)S(1)} %get-tuple-element.105), channel_id=1, source_target_pairs={{0,2},{1,3},{2,0},{3,1},{4,6},{5,7},{6,4},{7,5},{8,10},{9,11},{10,... | collective-permute-start | bytes 983048 | tf_op jit(solution)/shard_map/ppermute | solution.py:50
  278.5 29.8 %collective-permute-start.17 = (bf16[160,1024]{1,0:T(8,128)(2,1)S(1)}, bf16[160,1024]{1,0:T(8,128)(2,1)S(1)}, u32[]{:S(2)}, u32[]{:S(2)}) collective-permute-start(bf16[160,1024]{1,0:T(8,128)(2,1)S(1)} %get-tuple-element.106), channel_id=1, source_target_pairs={{0,1},{1,2},{2,3},{3,0},{4,5},{5,6},{6,7},{7,4},{8,9},{9,10},{10,1... | collective-permute-start | bytes 983048 | tf_op jit(solution)/shard_map/ppermute | solution.py:50
  286.4 43.0 %collective-permute-start.53 = (bf16[160,1024]{1,0:T(8,128)(2,1)S(1)}, bf16[160,1024]{1,0:T(8,128)(2,1)S(1)}, u32[]{:S(2)}, u32[]{:S(2)}) collective-permute-start(bf16[160,1024]{1,0:T(8,128)(2,1)S(1)} %get-tuple-element.96), channel_id=1, source_target_pairs={{0,3},{1,0},{2,1},{3,2},{4,7},{5,4},{6,5},{7,6},{8,11},{9,8},{10,9... | collective-permute-start | bytes 983048 | tf_op jit(solution)/shard_map/ppermute | solution.py:50
  308.2 34.2 %collective-permute-start.52 = (bf16[160,1024]{1,0:T(8,128)(2,1)S(1)}, bf16[160,1024]{1,0:T(8,128)(2,1)S(1)}, u32[]{:S(2)}, u32[]{:S(2)}) collective-permute-start(bf16[160,1024]{1,0:T(8,128)(2,1)S(1)} %get-tuple-element.97), channel_id=1, source_target_pairs={{0,2},{1,3},{2,0},{3,1},{4,6},{5,7},{6,4},{7,5},{8,10},{9,11},{10,... | collective-permute-start | bytes 983048 | tf_op jit(solution)/shard_map/ppermute | solution.py:50
  308.3 34.2 %collective-permute-start.51 = (bf16[160,1024]{1,0:T(8,128)(2,1)S(1)}, bf16[160,1024]{1,0:T(8,128)(2,1)S(1)}, u32[]{:S(2)}, u32[]{:S(2)}) collective-permute-start(bf16[160,1024]{1,0:T(8,128)(2,1)S(1)} %get-tuple-element.98), channel_id=1, source_target_pairs={{0,1},{1,2},{2,3},{3,0},{4,5},{5,6},{6,7},{7,4},{8,9},{9,10},{10,1... | collective-permute-start | bytes 983048 | tf_op jit(solution)/shard_map/ppermute | solution.py:50
  342.4 56.3 %collective-permute-start.68 = (bf16[160,1024]{1,0:T(8,128)(2,1)}, bf16[160,1024]{1,0:T(8,128)(2,1)}, u32[]{:S(2)}, u32[]{:S(2)}) collective-permute-start(bf16[160,1024]{1,0:T(8,128)(2,1)} %get-tuple-element.92), channel_id=1, source_target_pairs={{0,3},{1,0},{2,1},{3,2},{4,7},{5,4},{6,5},{7,6},{8,11},{9,8},{10,9... | collective-permute-start | bytes 983048 | tf_op jit(solution)/shard_map/ppermute | solution.py:50
  342.5 59.3 %collective-permute-start.67 = (bf16[160,1024]{1,0:T(8,128)(2,1)}, bf16[160,1024]{1,0:T(8,128)(2,1)}, u32[]{:S(2)}, u32[]{:S(2)}) collective-permute-start(bf16[160,1024]{1,0:T(8,128)(2,1)} %get-tuple-element.93), channel_id=1, source_target_pairs={{0,2},{1,3},{2,0},{3,1},{4,6},{5,7},{6,4},{7,5},{8,10},{9,11},{10,... | collective-permute-start | bytes 983048 | tf_op jit(solution)/shard_map/ppermute | solution.py:50
  343.2 58.6 %collective-permute-start.66 = (bf16[160,1024]{1,0:T(8,128)(2,1)}, bf16[160,1024]{1,0:T(8,128)(2,1)}, u32[]{:S(2)}, u32[]{:S(2)}) collective-permute-start(bf16[160,1024]{1,0:T(8,128)(2,1)} %get-tuple-element.94), channel_id=1, source_target_pairs={{0,1},{1,2},{2,3},{3,0},{4,5},{5,6},{6,7},{7,4},{8,9},{9,10},{10,1... | collective-permute-start | bytes 983048 | tf_op jit(solution)/shard_map/ppermute | solution.py:50
  380.0 141.6 %collective-permute-start.65 = (f32[160]{0:T(256)S(1)}, f32[160]{0:T(256)S(1)}, u32[]{:S(2)}, u32[]{:S(2)}) collective-permute-start(f32[160]{0:T(256)S(1)} %get-tuple-element.139), channel_id=1, source_target_pairs={{0,1},{1,2},{2,3},{3,0},{4,5},{5,6},{6,7},{7,4},{8,9},{9,10},{10,1... | collective-permute-start | bytes 1928 | tf_op jit(solution)/shard_map/ppermute | solution.py:50
  389.3 135.6 %collective-permute-start.64 = (f32[160]{0:T(256)S(1)}, f32[160]{0:T(256)S(1)}, u32[]{:S(2)}, u32[]{:S(2)}) collective-permute-start(f32[160]{0:T(256)S(1)} %get-tuple-element.140), channel_id=1, source_target_pairs={{0,2},{1,3},{2,0},{3,1},{4,6},{5,7},{6,4},{7,5},{8,10},{9,11},{10,... | collective-permute-start | bytes 1928 | tf_op jit(solution)/shard_map/ppermute | solution.py:50
  398.7 126.8 %collective-permute-start.63 = (f32[160]{0:T(256)S(1)}, f32[160]{0:T(256)S(1)}, u32[]{:S(2)}, u32[]{:S(2)}) collective-permute-start(f32[160]{0:T(256)S(1)} %get-tuple-element.141), channel_id=1, source_target_pairs={{0,3},{1,0},{2,1},{3,2},{4,7},{5,4},{6,5},{7,6},{8,11},{9,8},{10,9... | collective-permute-start | bytes 1928 | tf_op jit(solution)/shard_map/ppermute | solution.py:50
  434.5 92.6 %collective-permute-start.74 = (f32[160]{0:T(256)S(1)}, f32[160]{0:T(256)S(1)}, u32[]{:S(2)}, u32[]{:S(2)}) collective-permute-start(f32[160]{0:T(256)S(1)} %get-tuple-element.133), channel_id=1, source_target_pairs={{0,1},{1,2},{2,3},{3,0},{4,5},{5,6},{6,7},{7,4},{8,9},{9,10},{10,1... | collective-permute-start | bytes 1928 | tf_op jit(solution)/shard_map/ppermute | solution.py:50
  435.0 95.0 %collective-permute-start.73 = (f32[160]{0:T(256)S(1)}, f32[160]{0:T(256)S(1)}, u32[]{:S(2)}, u32[]{:S(2)}) collective-permute-start(f32[160]{0:T(256)S(1)} %get-tuple-element.134), channel_id=1, source_target_pairs={{0,2},{1,3},{2,0},{3,1},{4,6},{5,7},{6,4},{7,5},{8,10},{9,11},{10,... | collective-permute-start | bytes 1928 | tf_op jit(solution)/shard_map/ppermute | solution.py:50
  525.5 33.4 %collective-permute-start.70 = (bf16[160,1024]{1,0:T(8,128)(2,1)S(1)}, bf16[160,1024]{1,0:T(8,128)(2,1)}, u32[]{:S(2)}, u32[]{:S(2)}) collective-permute-start(bf16[160,1024]{1,0:T(8,128)(2,1)S(1)} %copy-done.87), channel_id=1, source_target_pairs={{0,2},{1,3},{2,0},{3,1},{4,6},{5,7},{6,4},{7,5},{8,10},{9,11},{10,... | collective-permute-start | bytes 983048 | tf_op jit(solution)/shard_map/ppermute | solution.py:50
  527.1 43.4 %collective-permute-start.69 = (bf16[160,1024]{1,0:T(8,128)(2,1)S(1)}, bf16[160,1024]{1,0:T(8,128)(2,1)}, u32[]{:S(2)}, u32[]{:S(2)}) collective-permute-start(bf16[160,1024]{1,0:T(8,128)(2,1)S(1)} %copy-done.86), channel_id=1, source_target_pairs={{0,3},{1,0},{2,1},{3,2},{4,7},{5,4},{6,5},{7,6},{8,11},{9,8},{10,9... | collective-permute-start | bytes 983048 | tf_op jit(solution)/shard_map/ppermute | solution.py:50
  530.0 46.5 %collective-permute-start.62 = (bf16[160,1024]{1,0:T(8,128)(2,1)}, bf16[160,1024]{1,0:T(8,128)(2,1)}, u32[]{:S(2)}, u32[]{:S(2)}) collective-permute-start(bf16[160,1024]{1,0:T(8,128)(2,1)} %get-tuple-element.76), channel_id=1, source_target_pairs={{0,1},{1,2},{2,3},{3,0},{4,5},{5,6},{6,7},{7,4},{8,9},{9,10},{10,1... | collective-permute-start | bytes 983048 | tf_op jit(solution)/shard_map/ppermute | solution.py:50
  530.0 60.4 %collective-permute-start.61 = (bf16[160,1024]{1,0:T(8,128)(2,1)}, bf16[160,1024]{1,0:T(8,128)(2,1)}, u32[]{:S(2)}, u32[]{:S(2)}) collective-permute-start(bf16[160,1024]{1,0:T(8,128)(2,1)} %get-tuple-element.77), channel_id=1, source_target_pairs={{0,2},{1,3},{2,0},{3,1},{4,6},{5,7},{6,4},{7,5},{8,10},{9,11},{10,... | collective-permute-start | bytes 983048 | tf_op jit(solution)/shard_map/ppermute | solution.py:50
  537.4 65.2 %collective-permute-start.60 = (bf16[160,1024]{1,0:T(8,128)(2,1)}, bf16[160,1024]{1,0:T(8,128)(2,1)}, u32[]{:S(2)}, u32[]{:S(2)}) collective-permute-start(bf16[160,1024]{1,0:T(8,128)(2,1)} %get-tuple-element.78), channel_id=1, source_target_pairs={{0,3},{1,0},{2,1},{3,2},{4,7},{5,4},{6,5},{7,6},{8,11},{9,8},{10,9... | collective-permute-start | bytes 983048 | tf_op jit(solution)/shard_map/ppermute | solution.py:50
  558.9 113.2 %collective-permute-start.56 = (bf16[160,1024]{1,0:T(8,128)(2,1)}, bf16[160,1024]{1,0:T(8,128)(2,1)}, u32[]{:S(2)}, u32[]{:S(2)}) collective-permute-start(bf16[160,1024]{1,0:T(8,128)(2,1)} %get-tuple-element.88), channel_id=1, source_target_pairs={{0,1},{1,2},{2,3},{3,0},{4,5},{5,6},{6,7},{7,4},{8,9},{9,10},{10,1... | collective-permute-start | bytes 983048 | tf_op jit(solution)/shard_map/ppermute | solution.py:50
  570.5 102.2 %collective-permute-start.55 = (bf16[160,1024]{1,0:T(8,128)(2,1)}, bf16[160,1024]{1,0:T(8,128)(2,1)}, u32[]{:S(2)}, u32[]{:S(2)}) collective-permute-start(bf16[160,1024]{1,0:T(8,128)(2,1)} %get-tuple-element.89), channel_id=1, source_target_pairs={{0,2},{1,3},{2,0},{3,1},{4,6},{5,7},{6,4},{7,5},{8,10},{9,11},{10,... | collective-permute-start | bytes 983048 | tf_op jit(solution)/shard_map/ppermute | solution.py:50
  576.5 96.3 %collective-permute-start.54 = (bf16[160,1024]{1,0:T(8,128)(2,1)}, bf16[160,1024]{1,0:T(8,128)(2,1)}, u32[]{:S(2)}, u32[]{:S(2)}) collective-permute-start(bf16[160,1024]{1,0:T(8,128)(2,1)} %get-tuple-element.90), channel_id=1, source_target_pairs={{0,3},{1,0},{2,1},{3,2},{4,7},{5,4},{6,5},{7,6},{8,11},{9,8},{10,9... | collective-permute-start | bytes 983048 | tf_op jit(solution)/shard_map/ppermute | solution.py:50
  590.4 87.7 %collective-permute-start.50 = (bf16[160,1024]{1,0:T(8,128)(2,1)}, bf16[160,1024]{1,0:T(8,128)(2,1)}, u32[]{:S(2)}, u32[]{:S(2)}) collective-permute-start(bf16[160,1024]{1,0:T(8,128)(2,1)} %get-tuple-element.84), channel_id=1, source_target_pairs={{0,1},{1,2},{2,3},{3,0},{4,5},{5,6},{6,7},{7,4},{8,9},{9,10},{10,1... | collective-permute-start | bytes 983048 | tf_op jit(solution)/shard_map/ppermute | solution.py:50
  602.6 75.7 %collective-permute-start.49 = (bf16[160,1024]{1,0:T(8,128)(2,1)S(1)}, bf16[160,1024]{1,0:T(8,128)(2,1)}, u32[]{:S(2)}, u32[]{:S(2)}) collective-permute-start(bf16[160,1024]{1,0:T(8,128)(2,1)S(1)} %copy-done.83), channel_id=1, source_target_pairs={{0,2},{1,3},{2,0},{3,1},{4,6},{5,7},{6,4},{7,5},{8,10},{9,11},{10,... | collective-permute-start | bytes 983048 | tf_op jit(solution)/shard_map/ppermute | solution.py:50
  672.7 47.4 %collective-permute-start.101 = (bf16[4,352,1024]{2,1,0:T(8,128)(2,1)}, bf16[4,352,1024]{2,1,0:T(8,128)(2,1)}, u32[]{:S(2)}, u32[]{:S(2)}) collective-permute-start(bf16[4,352,1024]{2,1,0:T(8,128)(2,1)} %dynamic-slice_bitcast_fusion.2), channel_id=1, source_target_pairs={{0,4},{4,0},{8,12},{12,8},{16,20},{20,16},{24,28},{28,24},{1,5},{5... | collective-permute-start | bytes 8650760 | tf_op jit(solution)/shard_map/ppermute | solution.py:46
  678.1 48.9 %collective-permute-start.80 = (bf16[4,128,3072]{2,1,0:T(8,128)(2,1)}, bf16[4,128,3072]{2,1,0:T(8,128)(2,1)S(1)}, u32[]{:S(2)}, u32[]{:S(2)}) collective-permute-start(bf16[4,128,3072]{2,1,0:T(8,128)(2,1)} %dynamic-slice_bitcast_fusion.1), channel_id=1, source_target_pairs={{0,4},{4,0},{8,12},{12,8},{16,20},{20,16},{24,28},{28,24},{1,5},{5... | collective-permute-start | bytes 9437192 | tf_op jit(solution)/shard_map/ppermute | solution.py:46
  718.5 67.6 %collective-permute-start.96 = (bf16[4,128,5632]{2,1,0:T(8,128)(2,1)}, bf16[4,128,5632]{2,1,0:T(8,128)(2,1)}, u32[]{:S(2)}, u32[]{:S(2)}) collective-permute-start(bf16[4,128,5632]{2,1,0:T(8,128)(2,1)} %dynamic-slice_bitcast_fusion), channel_id=1, source_target_pairs={{0,4},{4,0},{8,12},{12,8},{16,20},{20,16},{24,28},{28,24},{1,5},{5... | collective-permute-start | bytes 17301512 | tf_op jit(solution)/shard_map/ppermute | solution.py:46
  728.6 40.8 %collective-permute-start.81 = (bf16[2,1,64,3072]{3,2,0,1:T(8,128)(2,1)S(1)}, bf16[2,1,64,3072]{3,2,0,1:T(8,128)(2,1)S(1)}, u32[]{:S(2)}, u32[]{:S(2)}) collective-permute-start(bf16[2,1,64,3072]{3,2,0,1:T(8,128)(2,1)S(1)} %dynamic-slice_bitcast_fusion.7), channel_id=1, source_target_pairs={{0,8},{4,12},{8,0},{12,4},{16,24},{20,28},{24,16},{28,20},{1,9},{5... | collective-permute-start | bytes 2359304 | tf_op jit(solution)/shard_map/ppermute | solution.py:46
  743.6 25.6 %collective-permute-start.105 = (bf16[1,1,176,1024]{3,2,1,0:T(8,128)(2,1)S(1)}, bf16[1,1,176,1024]{3,2,1,0:T(8,128)(2,1)S(1)}, u32[]{:S(2)}, u32[]{:S(2)}) collective-permute-start(bf16[1,1,176,1024]{3,2,1,0:T(8,128)(2,1)S(1)} %constant_dynamic-slice_fusion), channel_id=1, source_target_pairs={{0,8},{4,12},{8,0},{12,4},{16,24},{20,28},{24,16},{28,20},{1,9},{5... | collective-permute-start | bytes 1081352 | tf_op jit(solution)/shard_map/ppermute | solution.py:46
  746.3 25.2 %collective-permute-start.83 = (bf16[1,2,64,3072]{3,2,1,0:T(8,128)(2,1)S(1)}, bf16[1,2,64,3072]{3,2,1,0:T(8,128)(2,1)S(1)}, u32[]{:S(2)}, u32[]{:S(2)}) collective-permute-start(bf16[1,2,64,3072]{3,2,1,0:T(8,128)(2,1)S(1)} %dynamic-slice_bitcast_fusion.6), channel_id=1, source_target_pairs={{0,16},{4,20},{8,24},{12,28},{16,0},{20,4},{24,8},{28,12},{1,17},{... | collective-permute-start | bytes 2359304 | tf_op jit(solution)/shard_map/ppermute | solution.py:46
  792.3 30.7 %collective-permute-start.99 = (bf16[1,2,64,5632]{3,2,1,0:T(8,128)(2,1)S(1)}, bf16[1,2,64,5632]{3,2,1,0:T(8,128)(2,1)S(1)}, u32[]{:S(2)}, u32[]{:S(2)}) collective-permute-start(bf16[1,2,64,5632]{3,2,1,0:T(8,128)(2,1)S(1)} %dynamic-slice_bitcast_fusion.3), channel_id=1, source_target_pairs={{0,16},{4,20},{8,24},{12,28},{16,0},{20,4},{24,8},{28,12},{1,17},{... | collective-permute-start | bytes 4325384 | tf_op jit(solution)/shard_map/ppermute | solution.py:46
  802.4 34.6 %collective-permute-start.97 = (bf16[2,1,64,5632]{3,2,0,1:T(8,128)(2,1)S(1)}, bf16[2,1,64,5632]{3,2,0,1:T(8,128)(2,1)S(1)}, u32[]{:S(2)}, u32[]{:S(2)}) collective-permute-start(bf16[2,1,64,5632]{3,2,0,1:T(8,128)(2,1)S(1)} %dynamic-slice_bitcast_fusion.4), channel_id=1, source_target_pairs={{0,8},{4,12},{8,0},{12,4},{16,24},{20,28},{24,16},{28,20},{1,9},{5... | collective-permute-start | bytes 4325384 | tf_op jit(solution)/shard_map/ppermute | solution.py:46
  823.4 25.6 %collective-permute-start.100 = (bf16[1,1,64,5632]{3,2,1,0:T(8,128)(2,1)S(1)}, bf16[1,1,64,5632]{3,2,1,0:T(8,128)(2,1)S(1)}, u32[]{:S(2)}, u32[]{:S(2)}) collective-permute-start(bf16[1,1,64,5632]{3,2,1,0:T(8,128)(2,1)S(1)} %constant_dynamic-slice_fusion.2), channel_id=1, source_target_pairs={{0,8},{4,12},{8,0},{12,4},{16,24},{20,28},{24,16},{28,20},{1,9},{5... | collective-permute-start | bytes 2162696 | tf_op jit(solution)/shard_map/ppermute | solution.py:46
  (202 other events, 2548.3 us)

commit v2 on v1

--- a/solution.py
+++ b/solution.py
@@ -55,24 +55,28 @@
     return (bits, bits[::-1])
 
 
-def gather_pieces(block, size):
-    half = block.shape[0] // 2
-    found = []
-    for part, order in enumerate(halving_orders(size)):
-        have = [(0, block[part * half : (part + 1) * half])]
-        for bit in order:
-            have = have + [(rel ^ bit, flip(piece, "dp", size, bit)) for rel, piece in have]
-        have = have + [(rel ^ 1, flip(piece, "dp", size, 1)) for rel, piece in have]
-        found += [(rel, part * half, piece) for rel, piece in have]
-    return found
-
-
 def gather_dp(block, size):
     me = lax.axis_index("dp")
-    full = jnp.zeros((size,) + block.shape, block.dtype)
-    for rel, offset, piece in gather_pieces(block, size):
-        full = lax.dynamic_update_slice(full, piece[None], (me ^ rel, offset, 0))
-    return full.reshape(size * block.shape[0], block.shape[1])
+    rows, width = block.shape
+    half = rows // 2
+    columns = []
+    for part, order in enumerate(halving_orders(size)):
+        have = block[None, part * half : (part + 1) * half]
+        rels = [0]
+        for bit in order:
+            have = jnp.concatenate([have, flip(have, "dp", size, bit)], axis=0)
+            rels = rels + [rel ^ bit for rel in rels]
+        columns.append((have, rels))
+    near = [columns[0][0], columns[1][0]]
+    far = [flip(have, "dp", size, 1) for have in near]
+    full = jnp.zeros((size, rows, width), block.dtype)
+    for part in range(2):
+        for other, have in ((0, near[part]), (1, far[part])):
+            for place, rel in enumerate(columns[part][1]):
+                full = lax.dynamic_update_slice(
+                    full, have[place : place + 1], (me ^ rel ^ other, part * half, 0)
+                )
+    return full.reshape(size * rows, width)
 
 
 def gather_expert(block, size):
@@ -82,6 +86,10 @@
         piece = shift(block, "expert", size, step) if step else block
         full = lax.dynamic_update_slice(full, piece[None], ((me - step) % size, 0, 0))
     return full.reshape(size * block.shape[0], block.shape[1])
+
+
+def all_to_all(value):
+    return lax.all_to_all(value, "expert", split_axis=0, concat_axis=0, tiled=True)
 
 
 def split_bit(value, me, bit):
@@ -113,14 +121,19 @@
 
 
 def scatter_expert(total, size):
+    rows = total.shape[0] // size
+    low = total.astype(BF16).reshape(size, rows, total.shape[1])
+    return jnp.sum(all_to_all(low).astype(F32), axis=0)
+
+
+def exchange(value, size):
     me = lax.axis_index("expert")
-    rows = total.shape[0] // size
-    low = total.astype(BF16)
-    result = lax.dynamic_slice_in_dim(total, me * rows, rows, 0)
+    full = value
     for step in range(1, size):
-        block = lax.dynamic_slice_in_dim(low, ((me + step) % size) * rows, rows, 0)
-        result = result + shift(block, "expert", size, step).astype(F32)
-    return result
+        sent = lax.dynamic_slice_in_dim(value, (me + step) % size, 1, 0)
+        got = shift(sent, "expert", size, step)
+        full = lax.dynamic_update_slice_in_dim(full, got, (me - step) % size, 0)
+    return full
 
 
 def sum_all(value, sizes):
@@ -170,31 +183,25 @@
     scale = head_size ** (-0.5)
     me_e = lax.axis_index("expert")
 
-    attn_w = gather_dp(gather_expert(jnp.concatenate([w_qkv, w_proj], axis=1), experts), dp)
+    attn_block = gather_expert(jnp.concatenate([w_qkv, w_proj], axis=1), experts)
+    attn_w = gather_dp(attn_block, dp)
     full_qkv, full_proj = attn_w[:, : 3 * width], attn_w[:, 3 * width :]
 
-    relative = (routes - me_e) % experts
     places = jax.vmap(partial(slot_positions, experts=experts))(routes)
-    targets = relative * capacity + places
+    targets = routes * capacity + places
     hot = targets[..., None] == jnp.arange(slot_count, dtype=jnp.int32)
     select = hot.astype(BF16)
     both = select[:, :, 0] + select[:, :, 1]
-
-    def exchange(blocks, sign):
-        parts = [blocks[:capacity]]
-        for step in range(1, experts):
-            parts.append(
-                shift(blocks[step * capacity : (step + 1) * capacity], "expert", experts, sign * step)
-            )
-        return jnp.concatenate(parts, axis=0)
-
     out_grads = [cotangent[n] for n in range(batches)]
-    go_slots = [
-        exchange(t_dot(both[n], out_grads[n]).astype(BF16), 1) for n in range(batches)
+    outgoing = [
+        t_dot(both[n], out_grads[n]).astype(BF16).reshape(experts, capacity, width)
+        for n in range(batches)
     ]
-
-    win_full = gather_dp(w_in[0], dp)
-    wout_full = gather_dp(w_out[0], dp)
+    outgoing, _ = lax.optimization_barrier((jnp.stack(outgoing, axis=1), attn_block))
+    go_slots = all_to_all(outgoing)
+
+    win_full = lax.all_gather(w_in[0], "dp", axis=0, tiled=True)
+    wout_full = lax.all_gather(w_out[0], "dp", axis=0, tiled=True)
 
     positions = jnp.arange(length, dtype=jnp.int32)
     buckets = bucket_of(positions[None, :] - positions[:, None])
@@ -222,14 +229,14 @@
         n2_hat = h1 * r2
         n2 = (n2_hat * gain_moe).astype(BF16)
         probs = jax.nn.softmax(dot(n2, w_router), axis=-1)
-        x_slots = exchange(t_dot(both[n], n2).astype(BF16), 1)
+        x_slots = all_to_all(t_dot(both[n], n2).astype(BF16).reshape(experts, capacity, width))
         saved.append((h0, r1, n1_hat, n1, q, k, v, p, p_low, o, h1, r2, n2_hat, n2, probs, x_slots))
 
     mine_hot = jnp.arange(experts, dtype=jnp.int32) == me_e
     held = []
     for n in range(batches):
-        x = saved[n][-1]
-        go = go_slots[n].astype(F32)
+        x = saved[n][-1].reshape(slot_count, width)
+        go = go_slots[:, n].reshape(slot_count, width).astype(F32)
         gate = jnp.sum(
             jnp.where(mine_hot, jax.nn.softmax(dot(x, w_router), axis=-1), 0.0), -1, keepdims=True
         )
@@ -243,14 +250,17 @@
         da, db = back(dot_t(dy, wout_full))
         du = jnp.concatenate([da, db], axis=1).astype(BF16)
         dx = dot_t(du, win_full).astype(BF16)
-        dgate_back = exchange(dgate, -1)
-        dx_back = exchange(dx, -1)
-        y_back = exchange(y, -1)
-        held.append((x, du, g, dy, dgate_back, dx_back, y_back))
+        dx_back = all_to_all(dx.reshape(experts, capacity, width)).reshape(slot_count, width)
+        held.append((x, du, g, dy, dgate, dx_back, y))
+    dgate_all = jnp.stack([h[4].reshape(experts, capacity) for h in held], axis=1)
+    dgate_back = exchange(dgate_all, experts)
+    y_back = all_to_all(
+        jnp.stack([h[6].reshape(experts, capacity, width) for h in held], axis=1)
+    )
 
     in_part = sum(t_dot(h[0], h[1]) for h in held).astype(BF16)
     out_part = sum(t_dot(h[2], h[3]) for h in held).astype(BF16)
-    in_total = scatter_dp(in_part, dp)
+    in_total = lax.psum_scatter(in_part, "dp", scatter_dimension=0, tiled=True).astype(F32)
     out_total = scatter_dp(out_part, dp)
 
     outputs, input_grads = [], []
@@ -258,14 +268,15 @@
     table_grad = gain_attn_grad = gain_moe_grad = router_grad = 0.0
     for n in range(batches):
         h0, r1, n1_hat, n1, q, k, v, p, p_low, o, h1, r2, n2_hat, n2, probs, _ = saved[n]
-        _, _, _, _, dgate_back, dx_back, y_back = held[n]
+        dx_back = held[n][5]
+        y_n = y_back[:, n].reshape(slot_count, width)
         go = out_grads[n].astype(F32)
         route_hot = (routes[n][:, :, None] == jnp.arange(experts, dtype=jnp.int32)).astype(F32)
         gates = jnp.sum(probs[:, None, :] * route_hot, axis=-1)
-        picked0, picked1 = dot(select[n][:, 0], y_back), dot(select[n][:, 1], y_back)
+        picked0, picked1 = dot(select[n][:, 0], y_n), dot(select[n][:, 1], y_n)
         moe = gates[:, :1] * picked0 + gates[:, 1:] * picked1
         outputs.append((h1 + moe).astype(BF16))
-        dgate = jnp.sum(jnp.where(hot[n], dgate_back, 0.0), axis=-1)
+        dgate = jnp.sum(jnp.where(hot[n], dgate_back[:, n].reshape(-1), 0.0), axis=-1)
         dprobs = jnp.sum(route_hot * dgate[:, :, None], axis=1)
         dlogits = probs * (dprobs - jnp.sum(probs * dprobs, axis=-1, keepdims=True))
         dlogits = dlogits.astype(BF16)

time: 862 us -> 669 us (0.78)
  waiting for transfers between devices: 301 us -> 208 us
  starting transfers between devices: 156 us -> 82.9 us
  local copies, waits for them, and re-layouts: 110 us -> 56.1 us
  other arithmetic: 34.5 us -> 50.3 us
  between operations: 3.77 us -> 16.3 us
    ppermute x67 -> x26, waiting for transfers between devices: 232 us -> 123 us  [flip(): return lax.ppermute(value, axis, [(i, i ^ bit) for i in range(size)])]
    ppermute x39 -> x6, starting transfers between devices: 108 us -> 10.8 us  [shift(): lax.ppermute(value, axis, [(i, (i + step) % size) for i in range(size)])]
    all_to_all x0 -> x8, waiting for transfers between devices: none -> 83 us  [all_to_all(): lax.all_to_all(value, 'expert', split_axis=0, concat_axis=0, tiled=True)]
    ppermute x39 -> x6, waiting for transfers between devices: 69.2 us -> 0.02 us  [shift(): lax.ppermute(value, axis, [(i, (i + step) % size) for i in range(size)])]
    all_to_all x0 -> x8, starting transfers between devices: none -> 47.2 us  [all_to_all(): lax.all_to_all(value, 'expert', split_axis=0, concat_axis=0, tiled=True)]
    dynamic_update_slice x46 -> x19, local copies, waits for them, and re-layouts: 25.6 us -> 0.69 us  [the longest x16 0.65 us: gather_dp(): lax.dynamic_update_slice(full, have[place:place + 1], (me ^ rel ^ other,...]
    ppermute x67 -> x26, starting transfers between devices: 48.1 us -> 24.7 us  [flip(): return lax.ppermute(value, axis, [(i, i ^ bit) for i in range(size)])]
    unnamed x291 -> x245, local copies, waits for them, and re-layouts: 24.8 us -> 19.8 us
  transfers between devices with their start and end apart: 106 -> 43, of which waited for: 46 -> 21; matrix products, arithmetic and copies ran while one was open for 43% -> 40% of each run, Pallas kernels for 0% -> 0%
where the time goes in v2:
time: 669 us; the launch traced here: 664 us
  matrix products  250 us (37%)
  waiting for transfers between devices  208 us (31%)
  starting transfers between devices  82.9 us (12%)
  local copies, waits for them, and re-layouts  56.1 us (8%)
  other arithmetic  50.3 us (8%)
  between operations  16.3 us (2%)
    ppermute x26, waiting for transfers between devices, flip(): return lax.ppermute(value, axis, [(i, i ^ bit) for i in range(size)])  123 us
    dot_general x20, matrix products, dot(): return jnp.dot(left, right, preferred_element_type=F32)  86.4 us
    all_to_all x8, waiting for transfers between devices, all_to_all(): lax.all_to_all(value, 'expert', split_axis=0, concat_axis=0, tiled=True)  83 us
    dot_general x14, matrix products, t_dot(): lax.dot_general(left, right, (((0,), (0,)), ((), ())), preferred_element_...  72.3 us
    dot_general x10, matrix products, dot_t(): lax.dot_general(left, right, (((1,), (1,)), ((), ())), preferred_element_...  55.5 us
    all_to_all x8, starting transfers between devices, all_to_all(): lax.all_to_all(value, 'expert', split_axis=0, concat_axis=0, tiled=True)  47.2 us
    ppermute x26, starting transfers between devices, flip(): return lax.ppermute(value, axis, [(i, i ^ bit) for i in range(size)])  24.7 us
    unnamed x245, local copies, waits for them, and re-layouts  19.8 us
  transfers between devices with their start and end apart: 43, of which 21 were waited for; matrix products, arithmetic and copies ran while one was open for 40% of the time, Pallas kernels for 0%

profile of v2, /device:TPU:0, one launch (start us, length us, event | category | flops | bytes accessed | tf_op | source)
XLA Modules:
  0.0 663.6 jit_solution(17798031656313007551)
XLA Ops:
  26.0 4.7 all-to-all-start.3
  39.5 4.3 fusion
  45.4 17.8 %collective-permute-done.3 = bf16[1,64,4096]{2,1,0:T(8,128)(2,1)S(1)} collective-permute-done((bf16[1,64,4096]{2,1,0:T(8,128)(2,1)S(1)}, bf16[1,64,4096]{2,1,0:T(8,128)(2,1)S(1)}, u32[]{:S(2)}, u32[]{:S(2)}) %collective-permute-start.3) | collective-permute-done | bytes 524320 | tf_op jit(solution)/shard_map/ppermute | solution.py:46
  69.1 27.7 %collective-permute-done.4 = bf16[2,64,4096]{2,1,0:T(8,128)(2,1)S(1)} collective-permute-done((bf16[2,64,4096]{2,1,0:T(8,128)(2,1)S(1)}, bf16[2,64,4096]{2,1,0:T(8,128)(2,1)S(1)}, u32[]{:S(2)}, u32[]{:S(2)}) %collective-permute-start.4) | collective-permute-done | bytes 1048608 | tf_op jit(solution)/shard_map/ppermute | solution.py:46
  97.0 5.5 collective-permute-done.7
  103.3 3.6 collective-permute-done.8
  115.6 5.8 fusion.230
  127.1 3.6 convolution_convert_fusion.5
  143.7 16.2 %all-to-all-start = ((bf16[4,160,1024]{2,1,0:T(8,128)(2,1)}), bf16[4,160,1024]{2,1,0:T(8,128)(2,1)S(1)}, u32[]{:S(2)}, u32[]{:S(2)}) async-start(bf16[4,160,1024]{2,1,0:T(8,128)(2,1)} %bitcast.508), calls=%async_computation | async-start | bytes 2621440 | tf_op jit(solution)/shard_map/all_to_all | solution.py:92
  163.8 27.7 %all-to-all-done = bf16[4,160,1024]{2,1,0:T(8,128)(2,1)S(1)} async-done(((bf16[4,160,1024]{2,1,0:T(8,128)(2,1)}), bf16[4,160,1024]{2,1,0:T(8,128)(2,1)S(1)}, u32[]{:S(2)}, u32[]{:S(2)}) %all-to-all-start) | async-done | bytes 1310752 | tf_op jit(solution)/shard_map/all_to_all | solution.py:92
  191.6 3.9 all-to-all-start.1
  199.1 3.4 fusion.221
  203.0 23.6 %all-to-all-done.1 = bf16[4,160,1024]{2,1,0:T(8,128)(2,1)S(1)} async-done(((bf16[4,160,1024]{2,1,0:T(8,128)(2,1)}), bf16[4,160,1024]{2,1,0:T(8,128)(2,1)S(1)}, u32[]{:S(2)}, u32[]{:S(2)}) %all-to-all-start.1) | async-done | bytes 1310752 | tf_op jit(solution)/shard_map/all_to_all | solution.py:92
  231.3 10.1 %fusion.19 = f32[640,2816]{1,0:T(8,128)} fusion(bf16[640,1024]{1,0:T(8,128)(2,1)} %fusion.62, bf16[1,2816,1024]{2,1,0:T(8,128)(2,1)} %all-gather.7.cloned.1.call-done), kind=kOutput, calls=%fused_computation.38 | convolution fusion | flops 3690987520 | bytes 14286848 | tf_op jit(solution)/shard_map/dot_general | solution.py:153
  241.4 6.1 fusion.21
  247.4 8.7 %fusion.27 = f32[640,2816]{1,0:T(8,128)} fusion(bf16[640,1024]{1,0:T(8,128)(2,1)S(1)} %bitcast.468, bf16[1024,5632]{1,0:T(8,128)(2,1)} %bitcast.537), kind=kOutput, calls=%fused_computation.46 | convolution fusion | flops 3690987520 | bytes 14286848 | tf_op jit(solution)/shard_map/dot_general | solution.py:149
  256.2 6.0 fusion.29
  262.1 15.2 %fusion.14 = (bf16[640,2816]{1,0:T(8,128)(2,1)}, bf16[640,2816]{1,0:T(8,128)(2,1)}, bf16[640,2816]{1,0:T(8,128)(2,1)}) fusion(f32[640,2816]{1,0:T(8,128)} %fusion.19, f32[640,2816]{1,0:T(8,128)} %fusion.27, bf16[640,1024]{1,0:T(8,128)(2,1)S(1)} %bitcast.469, bf16[1024,5632]{1,0:T(8,128)(2,1)S(1)} %bitcast.540), kind=kOutput, calls=%fused_computation.23 | convolution fusion | flops 3737845760 | bytes 32309248 | tf_op jit(solution)/shard_map/dot_general | solution.py:149
  277.4 8.7 %fusion.61 = (f32[640]{0:T(1024)S(1)}, bf16[640,1024]{1,0:T(8,128)(2,1)}) fusion(bf16[4,1,160,1024]{3,2,1,0:T(8,128)(2,1)S(1)} %copy-done.48, bf16[640,2816]{1,0:T(8,128)(2,1)} %get-tuple-element.67, bf16[1,2816,1024]{2,1,0:T(8,128)(2,1)} %all-gather.7.cloned.1.call-done), kind=kOutput, calls=%fused_computation.95 | convolution fusion | flops 3694263808 | bytes 11995648 | tf_op jit(solution)/shard_map/dot_general | solution.py:149
  286.2 15.4 %fusion.7 = (bf16[640,2816]{1,0:T(8,128)(2,1)}, bf16[640,2816]{1,0:T(8,128)(2,1)}, bf16[640,2816]{1,0:T(8,128)(2,1)S(1)}) fusion(f32[640,2816]{1,0:T(8,128)} %fusion.21, f32[640,2816]{1,0:T(8,128)} %fusion.29, bf16[640,1024]{1,0:T(8,128)(2,1)S(1)} %bitcast.461, bf16[1024,5632]{1,0:T(8,128)(2,1)} %bitcast.538), kind=kOutput, calls=%fused_computation.16 | convolution fusion | flops 3737845760 | bytes 32309248 | tf_op jit(solution)/shard_map/dot_general | solution.py:149
  301.7 7.6 %fusion.236 = f32[2816,1024]{1,0:T(8,128)} fusion(bf16[640,2816]{1,0:T(8,128)(2,1)S(1)} %get-tuple-element.64, bf16[640,1024]{1,0:T(8,128)(2,1)S(1)} %copy-done.74), kind=kOutput, calls=%fused_computation.423 | convolution fusion | flops 3690987520 | bytes 16449536 | tf_op jit(solution)/shard_map/dot_general | solution.py:157
  309.3 7.6 %fusion.60 = (f32[640]{0:T(1024)S(1)}, bf16[640,1024]{1,0:T(8,128)(2,1)}) fusion(bf16[4,1,160,1024]{3,2,1,0:T(8,128)(2,1)S(1)} %copy-done.47, bf16[640,2816]{1,0:T(8,128)(2,1)S(1)} %get-tuple-element.64, bf16[1,2816,1024]{2,1,0:T(8,128)(2,1)} %all-gather.7.cloned.1.call-done), kind=kOutput, calls=%fused_computation.94 | convolution fusion | flops 3694263808 | bytes 11995648 | tf_op jit(solution)/shard_map/dot_general | solution.py:149
  320.9 13.5 %fusion.67 = bf16[640,1024]{1,0:T(8,128)(2,1)} fusion(bf16[640,2816]{1,0:T(8,128)(2,1)} %get-tuple-element.66, bf16[640,2816]{1,0:T(8,128)(2,1)} %get-tuple-element.65, bf16[1,1024,5632]{2,1,0:T(8,128)(2,1)} %all-gather.5.cloned.1.call-done), kind=kOutput, calls=%fused_computation.111 | convolution fusion | flops 7397048320 | bytes 20054016 | tf_op jit(solution)/shard_map/dot_general | solution.py:153
  334.4 4.3 all-to-all-start.5
  338.7 17.4 %fusion.36 = f32[1024,5632]{1,0:T(8,128)} fusion(bf16[640,1024]{1,0:T(8,128)(2,1)S(1)} %bitcast.462, bf16[640,2816]{1,0:T(8,128)(2,1)} %get-tuple-element.63, bf16[640,2816]{1,0:T(8,128)(2,1)} %get-tuple-element.62), kind=kOutput, calls=%fused_computation.55 | convolution fusion | flops 7396392960 | bytes 31588352 | tf_op jit(solution)/shard_map/dot_general | solution.py:157
  356.1 17.4 %add_convert_fusion = bf16[1024,5632]{1,0:T(8,128)(2,1)} fusion(f32[1024,5632]{1,0:T(8,128)} %fusion.36, bf16[640,1024]{1,0:T(8,128)(2,1)S(1)} %bitcast.470, bf16[640,2816]{1,0:T(8,128)(2,1)S(1)} %copy-done.55, bf16[640,2816]{1,0:T(8,128)(2,1)S(1)} %copy-done.54), kind=kOutput, calls=%fused_computation | convolution fusion | flops 7407927296 | bytes 43122688 | tf_op jit(solution)/shard_map/dot_general | solution.py:157
  374.8 8.7 %add_convert_fusion.2 = bf16[2816,1024]{1,0:T(8,128)(2,1)S(1)} fusion(f32[2816,1024]{1,0:T(8,128)} %fusion.236, bf16[640,2816]{1,0:T(8,128)(2,1)} %get-tuple-element.67, bf16[640,1024]{1,0:T(8,128)(2,1)S(1)} %copy-done.72), kind=kOutput, calls=%fused_computation.2 | convolution fusion | flops 3696754688 | bytes 22216704 | tf_op jit(solution)/shard_map/dot_general | solution.py:157
  393.1 11.6 %fusion.66 = bf16[640,1024]{1,0:T(8,128)(2,1)} fusion(bf16[640,2816]{1,0:T(8,128)(2,1)S(1)} %copy-done.53, bf16[640,2816]{1,0:T(8,128)(2,1)S(1)} %copy-done.52, bf16[1,1024,5632]{2,1,0:T(8,128)(2,1)} %all-gather.5.cloned.1.call-done), kind=kOutput, calls=%fused_computation.110 | convolution fusion | flops 7397048320 | bytes 20054016 | tf_op jit(solution)/shard_map/dot_general | solution.py:153
  405.0 5.2 all-to-all-start.4
  415.4 25.0 %all-to-all-done.4 = bf16[4,160,1024]{2,1,0:T(8,128)(2,1)} async-done(((bf16[4,160,1024]{2,1,0:T(8,128)(2,1)}), bf16[4,160,1024]{2,1,0:T(8,128)(2,1)}, u32[]{:S(2)}, u32[]{:S(2)}) %all-to-all-start.4) | async-done | bytes 1310752 | tf_op jit(solution)/shard_map/all_to_all | solution.py:92
  449.0 3.9 convolution_bitcast_fusion
  490.0 4.1 collective-permute-done.25
  495.2 3.8 collective-permute-done.23
  501.5 3.7 collective-permute-done.24
  509.3 8.0 %fusion.152 = f32[1024,3072]{1,0:T(8,128)} fusion(bf16[256,3072]{0,1:T(8,128)(2,1)} %bitcast.494, f32[1024]{0:T(1024)S(1)} %copy-done.87, f32[256]{0:T(256)S(1)} %copy-done.104, bf16[2,256,1024]{2,1,0:T(8,128)(2,1)S(1)} %copy-done.25), kind=kOutput, calls=%fused_computation.238 | convolution fusion | flops 1611661312 | bytes 14685184 | tf_op jit(solution)/shard_map/dot_general | solution.py:157
  517.4 5.2 all-to-all-start.2
  522.6 7.1 %add_convert_fusion.1 = bf16[1024,3072]{1,0:T(8,128)(2,1)S(1)} fusion(f32[1024,3072]{1,0:T(8,128)} %fusion.152, bf16[256,3072]{0,1:T(8,128)(2,1)} %bitcast.492, f32[256]{0:T(256)S(1)} %copy-done.112, f32[1024]{0:T(1024)S(1)} %copy-done.87, bf16[2,256,1024]{2,1,0:T(8,128)(2,1)S(1)} %copy-done.25), kind=kOutput, calls=%fused_computation.1 | convolution fusion | flops 1617952768 | bytes 20976640 | tf_op jit(solution)/shard_map/dot_general | solution.py:157
  532.0 3.7 collective-permute-done.13
  541.7 4.1 fusion.18
  549.9 13.6 %collective-permute-done.15 = f32[52,128]{1,0:T(8,128)S(1)} collective-permute-done((f32[52,128]{1,0:T(8,128)S(1)}, f32[52,128]{1,0:T(8,128)S(1)}, u32[]{:S(2)}, u32[]{:S(2)}) %collective-permute-start.15) | collective-permute-done | bytes 26656 | tf_op jit(solution)/shard_map/ppermute | solution.py:46
  563.6 4.9 collective-permute-start.16
  571.2 10.0 %collective-permute-done.16 = f32[52,128]{1,0:T(8,128)S(1)} collective-permute-done((f32[52,128]{1,0:T(8,128)S(1)}, f32[52,128]{1,0:T(8,128)S(1)}, u32[]{:S(2)}, u32[]{:S(2)}) %collective-permute-start.16) | collective-permute-done | bytes 26656 | tf_op jit(solution)/shard_map/ppermute | solution.py:46
  592.7 4.9 fusion.15
  603.3 12.8 %collective-permute-done.20 = bf16[1,2,64,3072]{3,2,1,0:T(8,128)(2,1)S(1)} collective-permute-done((bf16[1,2,64,3072]{3,2,1,0:T(8,128)(2,1)S(1)}, bf16[1,2,64,3072]{3,2,1,0:T(8,128)(2,1)S(1)}, u32[]{:S(2)}, u32[]{:S(2)}) %collective-permute-start.20) | collective-permute-done | bytes 786464 | tf_op jit(solution)/shard_map/ppermute | solution.py:46
  618.0 4.6 collective-permute-done.18
  623.1 5.2 collective-permute-done.21
  631.7 4.2 all-to-all-start.6
  645.0 6.7 %all-to-all-done.6 = bf16[4,32,3072]{2,1,0:T(8,128)(2,1)} async-done(((bf16[4,32,3072]{2,1,0:T(8,128)(2,1)}), bf16[4,32,3072]{2,1,0:T(8,128)(2,1)}, u32[]{:S(2)}, u32[]{:S(2)}) %all-to-all-start.6) | async-done | bytes 786464 | tf_op jit(solution)/shard_map/all_to_all | solution.py:92
  (510 shorter events, 200.4 us)
Async XLA Ops:
  7.2 224.1 %all-gather.7.cloned.1.call-start = ((), (), s32[]{:S(2)}) async-start(), calls=%async_computation.11 | async-start | bytes 6488064 | tf_op jit(solution)/shard_map/all_gather | solution.py:204
  9.7 24.5 %collective-permute-start = (bf16[32,4096]{1,0:T(8,128)(2,1)S(1)}, bf16[32,4096]{1,0:T(8,128)(2,1)S(1)}, u32[]{:S(2)}, u32[]{:S(2)}) collective-permute-start(bf16[32,4096]{1,0:T(8,128)(2,1)S(1)} %constant_dynamic-update-slice_fusion.7), channel_id=1, source_target_pairs={{0,1},{1,2},{2,3},{3,0},{4,5},{5,6},{6,7},{7,4},{8,9},{9,10},{10,1... | collective-permute-start | bytes 786440 | tf_op jit(solution)/shard_map/ppermute | solution.py:50
  12.8 22.2 %collective-permute-start.1 = (bf16[32,4096]{1,0:T(8,128)(2,1)S(1)}, bf16[32,4096]{1,0:T(8,128)(2,1)S(1)}, u32[]{:S(2)}, u32[]{:S(2)}) collective-permute-start(bf16[32,4096]{1,0:T(8,128)(2,1)S(1)} %constant_dynamic-update-slice_fusion.7), channel_id=1, source_target_pairs={{0,2},{1,3},{2,0},{3,1},{4,6},{5,7},{6,4},{7,5},{8,10},{9,11},{10,... | collective-permute-start | bytes 786440 | tf_op jit(solution)/shard_map/ppermute | solution.py:50
  15.3 20.3 %collective-permute-start.2 = (bf16[32,4096]{1,0:T(8,128)(2,1)S(1)}, bf16[32,4096]{1,0:T(8,128)(2,1)S(1)}, u32[]{:S(2)}, u32[]{:S(2)}) collective-permute-start(bf16[32,4096]{1,0:T(8,128)(2,1)S(1)} %constant_dynamic-update-slice_fusion.7), channel_id=1, source_target_pairs={{0,3},{1,0},{2,1},{3,2},{4,7},{5,4},{6,5},{7,6},{8,11},{9,8},{10,9... | collective-permute-start | bytes 786440 | tf_op jit(solution)/shard_map/ppermute | solution.py:50
  26.0 117.6 %all-to-all-start.3 = ((bf16[4,2,160,1024]{3,2,1,0:T(8,128)(2,1)}), bf16[4,2,160,1024]{3,2,1,0:T(8,128)(2,1)}, u32[]{:S(2)}, u32[]{:S(2)}) async-start(bf16[4,2,160,1024]{3,2,1,0:T(8,128)(2,1)} %pad_maximum_fusion.7), calls=%async_computation.3 | async-start | bytes 5242880 | tf_op jit(solution)/shard_map/all_to_all | solution.py:92
  30.7 216.7 %all-gather.5.cloned.1.call-start = ((), (), s32[]{:S(2)}) async-start(), calls=%async_computation.10 | async-start | bytes 12976128 | tf_op jit(solution)/shard_map/all_gather | solution.py:203
  38.0 25.2 %collective-permute-start.3 = (bf16[1,64,4096]{2,1,0:T(8,128)(2,1)S(1)}, bf16[1,64,4096]{2,1,0:T(8,128)(2,1)S(1)}, u32[]{:S(2)}, u32[]{:S(2)}) collective-permute-start(bf16[1,64,4096]{2,1,0:T(8,128)(2,1)S(1)} %bitcast.487), channel_id=1, source_target_pairs={{0,8},{4,12},{8,0},{12,4},{16,24},{20,28},{24,16},{28,20},{1,9},{5... | collective-permute-start | bytes 1572872 | tf_op jit(solution)/shard_map/ppermute | solution.py:46
  43.8 22.5 %collective-permute-start.6 = (bf16[1,64,4096]{2,1,0:T(8,128)(2,1)S(1)}, bf16[1,64,4096]{2,1,0:T(8,128)(2,1)S(1)}, u32[]{:S(2)}, u32[]{:S(2)}) collective-permute-start(bf16[1,64,4096]{2,1,0:T(8,128)(2,1)S(1)} %bitcast.483), channel_id=1, source_target_pairs={{0,16},{4,20},{8,24},{12,28},{16,0},{20,4},{24,8},{28,12},{1,17},{... | collective-permute-start | bytes 1572872 | tf_op jit(solution)/shard_map/ppermute | solution.py:46
  45.3 61.8 %copy-start.103 = (f32[256]{0:T(256)}, f32[256]{0:T(256)S(1)}, u32[]{:S(2)}) copy-start(f32[256]{0:T(256)S(1)} %get-tuple-element.136) | copy-start | bytes 3076
  45.4 76.1 %copy-start.111 = (f32[256]{0:T(256)}, f32[256]{0:T(256)S(1)}, u32[]{:S(2)}) copy-start(f32[256]{0:T(256)S(1)} %get-tuple-element.135) | copy-start | bytes 3076
  63.3 33.5 %collective-permute-start.4 = (bf16[2,64,4096]{2,1,0:T(8,128)(2,1)S(1)}, bf16[2,64,4096]{2,1,0:T(8,128)(2,1)S(1)}, u32[]{:S(2)}, u32[]{:S(2)}) collective-permute-start(bf16[2,64,4096]{2,1,0:T(8,128)(2,1)S(1)} %pad_maximum_fusion.14), channel_id=1, source_target_pairs={{0,16},{4,20},{8,24},{12,28},{16,0},{20,4},{24,8},{28,12},{1,17},{... | collective-permute-start | bytes 3145736 | tf_op jit(solution)/shard_map/ppermute | solution.py:46
  66.4 36.2 %collective-permute-start.7 = (bf16[2,64,4096]{2,1,0:T(8,128)(2,1)S(1)}, bf16[2,64,4096]{2,1,0:T(8,128)(2,1)S(1)}, u32[]{:S(2)}, u32[]{:S(2)}) collective-permute-start(bf16[2,64,4096]{2,1,0:T(8,128)(2,1)S(1)} %pad_maximum_fusion.15), channel_id=1, source_target_pairs={{0,8},{4,12},{8,0},{12,4},{16,24},{20,28},{24,16},{28,20},{1,9},{5... | collective-permute-start | bytes 3145736 | tf_op jit(solution)/shard_map/ppermute | solution.py:46
  97.0 6.0 collective-permute-start.5
  102.8 4.2 collective-permute-start.8
  142.1 54.1 %copy-start.35 = (bf16[256,1024]{1,0:T(8,128)(2,1)}, bf16[256,1024]{1,0:T(8,128)(2,1)S(1)}, u32[]{:S(2)}) copy-start(bf16[256,1024]{1,0:T(8,128)(2,1)S(1)} %get-tuple-element.98) | copy-start | bytes 1572868
  143.7 47.9 %all-to-all-start = ((bf16[4,160,1024]{2,1,0:T(8,128)(2,1)}), bf16[4,160,1024]{2,1,0:T(8,128)(2,1)S(1)}, u32[]{:S(2)}, u32[]{:S(2)}) async-start(bf16[4,160,1024]{2,1,0:T(8,128)(2,1)} %bitcast.508), calls=%async_computation | async-start | bytes 2621440 | tf_op jit(solution)/shard_map/all_to_all | solution.py:92
  159.9 35.6 %copy-start.94 = (s32[2,256,2]{1,2,0:T(2,128)S(1)}, s32[2,256,2]{1,2,0:T(2,128)}, u32[]{:S(2)}) copy-start(s32[2,256,2]{1,2,0:T(2,128)} %param.17) | copy-start | bytes 12292
  159.9 36.2 %copy-start.84 = (bf16[1024,4]{0,1:T(4,128)(2,1)S(1)}, bf16[1024,4]{0,1:T(4,128)(2,1)}, u32[]{:S(2)}) copy-start(bf16[1024,4]{0,1:T(4,128)(2,1)} %param.23) | copy-start | bytes 24580
  191.6 35.0 %all-to-all-start.1 = ((bf16[4,160,1024]{2,1,0:T(8,128)(2,1)}), bf16[4,160,1024]{2,1,0:T(8,128)(2,1)S(1)}, u32[]{:S(2)}, u32[]{:S(2)}) async-start(bf16[4,160,1024]{2,1,0:T(8,128)(2,1)} %bitcast.507), calls=%async_computation.1 | async-start | bytes 2621440 | tf_op jit(solution)/shard_map/all_to_all | solution.py:92
  317.0 87.7 %collective-permute-start.9 = (f32[1,2,160]{2,1,0:T(2,128)S(1)}, f32[1,2,160]{2,1,0:T(2,128)S(1)}, u32[]{:S(2)}, u32[]{:S(2)}) collective-permute-start(f32[1,2,160]{2,1,0:T(2,128)S(1)} %get-tuple-element.89), channel_id=1, source_target_pairs={{0,1},{1,2},{2,3},{3,0},{4,5},{5,6},{6,7},{7,4},{8,9},{9,10},{10,1... | collective-permute-start | bytes 3848 | tf_op jit(solution)/shard_map/ppermute | solution.py:50
  317.1 87.7 %collective-permute-start.10 = (f32[1,2,160]{2,1,0:T(2,128)S(1)}, f32[1,2,160]{2,1,0:T(2,128)S(1)}, u32[]{:S(2)}, u32[]{:S(2)}) collective-permute-start(f32[1,2,160]{2,1,0:T(2,128)S(1)} %get-tuple-element.90), channel_id=1, source_target_pairs={{0,2},{1,3},{2,0},{3,1},{4,6},{5,7},{6,4},{7,5},{8,10},{9,11},{10,... | collective-permute-start | bytes 3848 | tf_op jit(solution)/shard_map/ppermute | solution.py:50
  319.1 85.7 %collective-permute-start.11 = (f32[1,2,160]{2,1,0:T(2,128)S(1)}, f32[1,2,160]{2,1,0:T(2,128)S(1)}, u32[]{:S(2)}, u32[]{:S(2)}) collective-permute-start(f32[1,2,160]{2,1,0:T(2,128)S(1)} %get-tuple-element.88), channel_id=1, source_target_pairs={{0,3},{1,0},{2,1},{3,2},{4,7},{5,4},{6,5},{7,6},{8,11},{9,8},{10,9... | collective-permute-start | bytes 3848 | tf_op jit(solution)/shard_map/ppermute | solution.py:50
  334.4 70.7 %all-to-all-start.5 = ((bf16[4,160,1024]{2,1,0:T(8,128)(2,1)}), bf16[4,160,1024]{2,1,0:T(8,128)(2,1)}, u32[]{:S(2)}, u32[]{:S(2)}) async-start(bf16[4,160,1024]{2,1,0:T(8,128)(2,1)} %bitcast.525), calls=%async_computation.5 | async-start | bytes 2621440 | tf_op jit(solution)/shard_map/all_to_all | solution.py:92
  338.7 315.0 %reduce-scatter.2.cloned.1.call-start = ((), (), s32[]{:S(2)}) async-start(), calls=%async_computation.9 | async-start | bytes 12976128 | tf_op jit(solution)/shard_map/reduce_scatter | solution.py:263
  385.4 156.3 %collective-permute-start.27 = (bf16[4,352,1024]{2,1,0:T(8,128)(2,1)}, bf16[4,352,1024]{2,1,0:T(8,128)(2,1)}, u32[]{:S(2)}, u32[]{:S(2)}) collective-permute-start(bf16[4,352,1024]{2,1,0:T(8,128)(2,1)} %dynamic-slice_bitcast_fusion.1), channel_id=1, source_target_pairs={{0,4},{4,0},{8,12},{12,8},{16,20},{20,16},{24,28},{28,24},{1,5},{5... | collective-permute-start | bytes 8650760 | tf_op jit(solution)/shard_map/ppermute | solution.py:46
  405.0 35.4 %all-to-all-start.4 = ((bf16[4,160,1024]{2,1,0:T(8,128)(2,1)}), bf16[4,160,1024]{2,1,0:T(8,128)(2,1)}, u32[]{:S(2)}, u32[]{:S(2)}) async-start(bf16[4,160,1024]{2,1,0:T(8,128)(2,1)} %bitcast.524), calls=%async_computation.4 | async-start | bytes 2621440 | tf_op jit(solution)/shard_map/all_to_all | solution.py:92
  479.8 4.4 collective-permute-start.22
  485.5 8.5 %collective-permute-start.25 = (bf16[1,2,64,1024]{3,2,1,0:T(8,128)(2,1)S(1)}, bf16[1,2,64,1024]{3,2,1,0:T(8,128)(2,1)}, u32[]{:S(2)}, u32[]{:S(2)}) collective-permute-start(bf16[1,2,64,1024]{3,2,1,0:T(8,128)(2,1)S(1)} %dynamic-slice_bitcast_fusion.7), channel_id=1, source_target_pairs={{0,16},{4,20},{8,24},{12,28},{16,0},{20,4},{24,8},{28,12},{1,17},{... | collective-permute-start | bytes 786440 | tf_op jit(solution)/shard_map/ppermute | solution.py:46
  488.8 43.0 %collective-permute-start.12 = (f32[52,128]{1,0:T(8,128)S(1)}, f32[52,128]{1,0:T(8,128)S(1)}, u32[]{:S(2)}, u32[]{:S(2)}) collective-permute-start(f32[52,128]{1,0:T(8,128)S(1)} %maximum_bitcast_fusion.1), channel_id=1, source_target_pairs={{0,4},{4,0},{8,12},{12,8},{16,20},{20,16},{24,28},{28,24},{1,5},{5... | collective-permute-start | bytes 79880 | tf_op jit(solution)/shard_map/ppermute | solution.py:46
  489.9 9.2 %collective-permute-start.23 = (bf16[2,1,64,1024]{3,2,1,0:T(8,128)(2,1)S(1)}, bf16[2,1,64,1024]{3,2,1,0:T(8,128)(2,1)S(1)}, u32[]{:S(2)}, u32[]{:S(2)}) collective-permute-start(bf16[2,1,64,1024]{3,2,1,0:T(8,128)(2,1)S(1)} %dynamic-slice_bitcast_fusion.8), channel_id=1, source_target_pairs={{0,8},{4,12},{8,0},{12,4},{16,24},{20,28},{24,16},{28,20},{1,9},{5... | collective-permute-start | bytes 786440 | tf_op jit(solution)/shard_map/ppermute | solution.py:46
  495.1 6.3 collective-permute-start.26
  500.1 5.0 collective-permute-start.24
  505.9 11.5 %all-to-all-start.7 = ((bf16[4,32,1024]{2,1,0:T(8,128)(2,1)}), bf16[4,32,1024]{2,1,0:T(8,128)(2,1)S(1)}, u32[]{:S(2)}, u32[]{:S(2)}) async-start(bf16[4,32,1024]{2,1,0:T(8,128)(2,1)} %bitcast.122), calls=%async_computation.7 | async-start | bytes 524288 | tf_op jit(solution)/shard_map/all_to_all | solution.py:92
  517.4 73.3 %all-to-all-start.2 = ((bf16[4,2,160,1024]{3,2,1,0:T(8,128)(2,1)}), bf16[4,2,160,1024]{3,2,1,0:T(8,128)(2,1)}, u32[]{:S(2)}, u32[]{:S(2)}) async-start(bf16[4,2,160,1024]{3,2,1,0:T(8,128)(2,1)} %pad_maximum_fusion.6), calls=%async_computation.2 | async-start | bytes 5242880 | tf_op jit(solution)/shard_map/all_to_all | solution.py:92
  531.8 3.9 collective-permute-start.13
  532.0 60.6 %collective-permute-start.17 = (bf16[4,128,3072]{2,1,0:T(8,128)(2,1)}, bf16[4,128,3072]{2,1,0:T(8,128)(2,1)}, u32[]{:S(2)}, u32[]{:S(2)}) collective-permute-start(bf16[4,128,3072]{2,1,0:T(8,128)(2,1)} %dynamic-slice_bitcast_fusion), channel_id=1, source_target_pairs={{0,4},{4,0},{8,12},{12,8},{16,20},{20,16},{24,28},{28,24},{1,5},{5... | collective-permute-start | bytes 9437192 | tf_op jit(solution)/shard_map/ppermute | solution.py:46
  535.8 3.9 collective-permute-start.14
  539.7 23.8 %collective-permute-start.15 = (f32[52,128]{1,0:T(8,128)S(1)}, f32[52,128]{1,0:T(8,128)S(1)}, u32[]{:S(2)}, u32[]{:S(2)}) collective-permute-start(f32[52,128]{1,0:T(8,128)S(1)} %add.524), channel_id=1, source_target_pairs={{0,1},{1,0},{2,3},{3,2},{4,5},{5,4},{6,7},{7,6},{8,9},{9,8},{10,11... | collective-permute-start | bytes 79880 | tf_op jit(solution)/shard_map/ppermute | solution.py:46
  547.1 36.8 %collective-permute-start.30 = (bf16[1,2,176,1024]{3,2,1,0:T(8,128)(2,1)}, bf16[1,2,176,1024]{3,2,1,0:T(8,128)(2,1)}, u32[]{:S(2)}, u32[]{:S(2)}) collective-permute-start(bf16[1,2,176,1024]{3,2,1,0:T(8,128)(2,1)} %dynamic-slice_bitcast_fusion.5), channel_id=1, source_target_pairs={{0,16},{4,20},{8,24},{12,28},{16,0},{20,4},{24,8},{28,12},{1,17},{... | collective-permute-start | bytes 2162696 | tf_op jit(solution)/shard_map/ppermute | solution.py:46
  563.6 17.7 %collective-permute-start.16 = (f32[52,128]{1,0:T(8,128)S(1)}, f32[52,128]{1,0:T(8,128)S(1)}, u32[]{:S(2)}, u32[]{:S(2)}) collective-permute-start(f32[52,128]{1,0:T(8,128)S(1)} %add.525), channel_id=1, source_target_pairs={{0,2},{1,3},{2,0},{3,1},{4,6},{5,7},{6,4},{7,5},{8,10},{9,11},{10,... | collective-permute-start | bytes 79880 | tf_op jit(solution)/shard_map/ppermute | solution.py:46
  569.4 17.9 %collective-permute-start.28 = (bf16[2,1,176,1024]{3,2,0,1:T(8,128)(2,1)}, bf16[2,1,176,1024]{3,2,0,1:T(8,128)(2,1)}, u32[]{:S(2)}, u32[]{:S(2)}) collective-permute-start(bf16[2,1,176,1024]{3,2,0,1:T(8,128)(2,1)} %dynamic-slice_bitcast_fusion.6), channel_id=1, source_target_pairs={{0,8},{4,12},{8,0},{12,4},{16,24},{20,28},{24,16},{28,20},{1,9},{5... | collective-permute-start | bytes 2162696 | tf_op jit(solution)/shard_map/ppermute | solution.py:46
  586.4 55.0 %collective-permute-start.31 = (bf16[1,1,176,1024]{3,2,1,0:T(8,128)(2,1)}, bf16[1,1,176,1024]{3,2,1,0:T(8,128)(2,1)}, u32[]{:S(2)}, u32[]{:S(2)}) collective-permute-start(bf16[1,1,176,1024]{3,2,1,0:T(8,128)(2,1)} %constant_dynamic-slice_fusion.3), channel_id=1, source_target_pairs={{0,8},{4,12},{8,0},{12,4},{16,24},{20,28},{24,16},{28,20},{1,9},{5... | collective-permute-start | bytes 1081352 | tf_op jit(solution)/shard_map/ppermute | solution.py:46
  589.6 52.9 %collective-permute-start.29 = (bf16[1,1,176,1024]{3,2,0,1:T(8,128)(2,1)}, bf16[1,1,176,1024]{3,2,0,1:T(8,128)(2,1)}, u32[]{:S(2)}, u32[]{:S(2)}) collective-permute-start(bf16[1,1,176,1024]{3,2,0,1:T(8,128)(2,1)} %constant_dynamic-slice_fusion.4), channel_id=1, source_target_pairs={{0,16},{4,20},{8,24},{12,28},{16,0},{20,4},{24,8},{28,12},{1,17},{... | collective-permute-start | bytes 1081352 | tf_op jit(solution)/shard_map/ppermute | solution.py:46
  598.0 18.1 %collective-permute-start.20 = (bf16[1,2,64,3072]{3,2,1,0:T(8,128)(2,1)S(1)}, bf16[1,2,64,3072]{3,2,1,0:T(8,128)(2,1)S(1)}, u32[]{:S(2)}, u32[]{:S(2)}) collective-permute-start(bf16[1,2,64,3072]{3,2,1,0:T(8,128)(2,1)S(1)} %dynamic-slice_bitcast_fusion.3), channel_id=1, source_target_pairs={{0,16},{4,20},{8,24},{12,28},{16,0},{20,4},{24,8},{28,12},{1,17},{... | collective-permute-start | bytes 2359304 | tf_op jit(solution)/shard_map/ppermute | solution.py:46
  602.0 20.5 %collective-permute-start.18 = (bf16[2,1,64,3072]{3,2,1,0:T(8,128)(2,1)S(1)}, bf16[2,1,64,3072]{3,2,1,0:T(8,128)(2,1)S(1)}, u32[]{:S(2)}, u32[]{:S(2)}) collective-permute-start(bf16[2,1,64,3072]{3,2,1,0:T(8,128)(2,1)S(1)} %dynamic-slice_bitcast_fusion.4), channel_id=1, source_target_pairs={{0,8},{4,12},{8,0},{12,4},{16,24},{20,28},{24,16},{28,20},{1,9},{5... | collective-permute-start | bytes 2359304 | tf_op jit(solution)/shard_map/ppermute | solution.py:46
  616.4 11.9 %collective-permute-start.21 = (bf16[1,1,64,3072]{3,2,1,0:T(8,128)(2,1)S(1)}, bf16[1,1,64,3072]{3,2,1,0:T(8,128)(2,1)S(1)}, u32[]{:S(2)}, u32[]{:S(2)}) collective-permute-start(bf16[1,1,64,3072]{3,2,1,0:T(8,128)(2,1)S(1)} %constant_dynamic-slice_fusion.7), channel_id=1, source_target_pairs={{0,8},{4,12},{8,0},{12,4},{16,24},{20,28},{24,16},{28,20},{1,9},{5... | collective-permute-start | bytes 1179656 | tf_op jit(solution)/shard_map/ppermute | solution.py:46
  622.8 7.8 %collective-permute-start.19 = (bf16[1,1,64,3072]{3,2,1,0:T(8,128)(2,1)S(1)}, bf16[1,1,64,3072]{3,2,1,0:T(8,128)(2,1)S(1)}, u32[]{:S(2)}, u32[]{:S(2)}) collective-permute-start(bf16[1,1,64,3072]{3,2,1,0:T(8,128)(2,1)S(1)} %constant_dynamic-slice_fusion.8), channel_id=1, source_target_pairs={{0,16},{4,20},{8,24},{12,28},{16,0},{20,4},{24,8},{28,12},{1,17},{... | collective-permute-start | bytes 1179656 | tf_op jit(solution)/shard_map/ppermute | solution.py:46
  631.7 19.9 %all-to-all-start.6 = ((bf16[4,32,3072]{2,1,0:T(8,128)(2,1)}), bf16[4,32,3072]{2,1,0:T(8,128)(2,1)}, u32[]{:S(2)}, u32[]{:S(2)}) async-start(bf16[4,32,3072]{2,1,0:T(8,128)(2,1)} %bitcast.513), calls=%async_computation.6 | async-start | bytes 1572864 | tf_op jit(solution)/shard_map/all_to_all | solution.py:92
  (116 other events, 953.2 us)
Sparse Core Ops, SparseCore 0:
  9.9 57.0 all-gather.6
  68.9 80.3 all-gather.4
  373.7 90.8 reduce-scatter.1

commit v3 on v2

v3 whole, which is shorter than its diff:
```python
from functools import partial

import jax
import jax.numpy as jnp
from jax import lax
from jax.experimental import pallas as pl
from jax.experimental.pallas import tpu as pltpu
from jax.sharding import PartitionSpec as P

EPSILON = 1e-06
NEG_BIG = -1e30
LIMITS = (12, 16, 23, 32, 46, 64, 91)
F32 = jnp.float32
BF16 = jnp.bfloat16


def bucket_of(offset):
    distance = jnp.abs(offset)
    far_part = 8 + sum(((distance >= limit).astype(jnp.int32) for limit in LIMITS))
    near_far = jnp.where(distance < 8, distance, far_part)
    return jnp.where(offset > 0, 16, 0) + near_far


def slot_positions(routes, experts):
    order = jnp.concatenate([routes[:, 0], routes[:, 1]])
    chosen = (order[:, None] == jnp.arange(experts, dtype=jnp.int32)[None, :]).astype(jnp.int32)
    before = jnp.cumsum(chosen, axis=0) - chosen
    place = jnp.sum(before * chosen, axis=1)
    return place.reshape(2, -1).T


def tree_mask(segment, parent):
    same = segment[None, :] == segment[:, None]
    upward = segment[None, :] == parent[:, None]
    downward = parent[None, :] == segment[:, None]
    return same | upward | downward


def rms_scale(values):
    return lax.rsqrt(jnp.mean(values * values, axis=-1, keepdims=True) + EPSILON)


def gelu_product(gate_part, up_part):
    return jax.nn.gelu(gate_part, approximate=True) * up_part


def after(value, *others):
    return lax.optimization_barrier((value, others))[0]


def flip(value, axis, size, bit):
    return lax.ppermute(value, axis, [(i, i ^ bit) for i in range(size)])


def shift(value, axis, size, step):
    return lax.ppermute(value, axis, [(i, (i + step) % size) for i in range(size)])


def halving_orders(size):
    bits = [1 << k for k in range(1, size.bit_length() - 1)]
    return (bits, bits[::-1])


def gather_dp(block, size, hold):
    rows = block.shape[0]
    half = rows // 2
    columns = []
    for part, order in enumerate(halving_orders(size)):
        have = block[None, part * half : (part + 1) * half]
        rels = [0]
        for bit in order:
            if len(rels) == 2:
                have = after(have, hold)
            have = jnp.concatenate([have, flip(have, "dp", size, bit)], axis=0)
            rels = rels + [rel ^ bit for rel in rels]
        columns.append((have, rels))
    near = [columns[0][0], columns[1][0]]
    far = [flip(have, "dp", size, 1) for have in near]
    return near + far, [columns[0][1], columns[1][1]]


def gather_expert(block, size):
    me = lax.axis_index("expert")
    full = jnp.zeros((size,) + block.shape, block.dtype)
    for step in range(size):
        piece = shift(block, "expert", size, step) if step else block
        full = lax.dynamic_update_slice(full, piece[None], ((me - step) % size, 0, 0))
    return full.reshape(size * block.shape[0], block.shape[1])


def all_to_all(value):
    return lax.all_to_all(value, "expert", split_axis=0, concat_axis=0, tiled=True)


def split_bit(value, me, bit):
    mine = (me // bit) % 2
    kept = lax.dynamic_index_in_dim(value, mine, 0, keepdims=False)
    sent = lax.dynamic_index_in_dim(value, 1 - mine, 0, keepdims=False)
    return kept, sent


def scatter_core(total, size):
    me = lax.axis_index("dp")
    rows, width = total.shape[0] // size, total.shape[1]
    kept, sent = split_bit(jnp.moveaxis(total.reshape(size // 2, 2, rows, width), 1, 0), me, 1)
    return kept.astype(F32) + flip(sent, "dp", size, 1).astype(F32)


def scatter_dp(summed, size):
    me = lax.axis_index("dp")
    _, rows, width = summed.shape
    half = rows // 2
    outs = []
    for part, order in enumerate(halving_orders(size)):
        value = summed[:, part * half : (part + 1) * half]
        left = [1 << k for k in range(1, size.bit_length() - 1)]
        for bit in order:
            place = left.index(bit)
            high, low = 1 << (len(left) - 1 - place), 1 << place
            shaped = value.astype(BF16).reshape(high, 2, low, half, width)
            kept, sent = split_bit(jnp.moveaxis(shaped, 1, 0), me, bit)
            value = kept.astype(F32) + flip(sent, "dp", size, bit).astype(F32)
            left.remove(bit)
        outs.append(value.reshape(half, width))
    return jnp.concatenate(outs, axis=0)


def scatter_expert(total, size):
    rows = total.shape[0] // size
    low = total.astype(BF16).reshape(size, rows, total.shape[1])
    return jnp.sum(all_to_all(low).astype(F32), axis=0)


def sum_all(value, sizes):
    for axis in ("dp", "expert"):
        bit = 1
        while bit < sizes[axis]:
            value = value + flip(value, axis, sizes[axis], bit)
            bit *= 2
    return value


def dot(left, right):
    return jnp.dot(left, right, preferred_element_type=F32)


def dot_t(left, right):
    return lax.dot_general(left, right, (((1,), (1,)), ((), ())), preferred_element_type=F32)


def t_dot(left, right):
    return lax.dot_general(left, right, (((0,), (0,)), ((), ())), preferred_element_type=F32)

LIGHT = pl.CostEstimate(flops=1, bytes_accessed=1, transcendentals=0)


GELU_C = 0.7978845608028654
GELU_A = 0.044715


def expert_body(
    mine, x_ref, go_ref, wr_ref, wg_ref, wu_ref, wo_ref, *refs
):
    y_ref, dx_ref, gt_ref, du_ref, dy_ref, y_acc, dx_acc = refs[-7:]
    step, last = pl.program_id(0), pl.num_programs(0) - 1

    @pl.when(step == 0)
    def _():
        logits = dot(x_ref[...], wr_ref[...])
        lane = lax.broadcasted_iota(jnp.int32, logits.shape, 1)
        logits = jnp.where(lane < mine[1], logits, NEG_BIG)
        top = jnp.max(logits, axis=-1, keepdims=True)
        weights = jnp.exp(logits - top)
        total = jnp.sum(weights, axis=-1, keepdims=True)
        gate = jnp.sum(jnp.where(lane == mine[0], weights, 0.0), axis=-1, keepdims=True) / total
        dy_ref[...] = (gate * go_ref[...].astype(F32)).astype(BF16)
        y_acc[...] = jnp.zeros_like(y_acc)
        dx_acc[...] = jnp.zeros_like(dx_acc)

    x = x_ref[...]
    wg, wu, wo = wg_ref[...], wu_ref[...], wo_ref[...]
    a, b = dot(x, wg), dot(x, wu)
    dg = dot_t(dy_ref[...], wo)
    square = a * a
    t = jnp.tanh(GELU_C * (a + GELU_A * (a * square)))
    half = 0.5 + 0.5 * t
    act = a * half
    slope = half + (0.5 * GELU_C) * a * (1.0 - t * t) * (1.0 + (3.0 * GELU_A) * square)
    g = (act * b).astype(BF16)
    da = (dg * b * slope).astype(BF16)
    db = (dg * act).astype(BF16)
    gt_ref[...] = g.T
    du_ref[0] = da
    du_ref[1] = db
    y_acc[...] += dot(g, wo)
    dx_acc[...] += dot_t(jnp.concatenate([da, db], axis=1), jnp.concatenate([wg, wu], axis=1))

    @pl.when(step == last)
    def _():
        y = y_acc[...].astype(BF16)
        y_ref[...] = y
        width = y.shape[1]
        dx_ref[:, :width] = dx_acc[...].astype(BF16)
        product = go_ref[...].astype(F32) * y.astype(F32)
        rest = jnp.sum(product, axis=-1, keepdims=True)
        lane = lax.broadcasted_iota(jnp.int32, (y.shape[0], 128), 1)
        terms = jnp.zeros(lane.shape, F32)
        for place in range(3):
            term = rest.astype(BF16).astype(F32)
            terms = jnp.where(lane == place, term, terms)
            rest = rest - term
        dx_ref[:, width:] = terms.astype(BF16)


def tile_of(size, most):
    return max(t for t in range(128, most + 1, 128) if size % t == 0)


def expert_call(batch, batches, mine, x, go, w_router, w_in, w_out, held):
    rows, width = x.shape
    inner = w_out.shape[0]
    tile = tile_of(inner, 256)
    tiles = inner // tile
    whole = lambda shape: pl.BlockSpec(shape, lambda j: (0,) * len(shape))
    in_specs = [
        pl.BlockSpec(memory_space=pltpu.SMEM),
        whole((rows, width)),
        whole((rows, width)),
        whole(w_router.shape),
        pl.BlockSpec((width, tile), lambda j: (0, j)),
        pl.BlockSpec((width, tile), lambda j: (0, tiles + j)),
        pl.BlockSpec((tile, width), lambda j: (j, 0)),
    ]
    args = [mine, x, go, w_router, w_in, w_in, w_out]
    aliases = {}
    if held is not None:
        in_specs += [pl.BlockSpec(memory_space=pl.ANY)] * 3
        aliases = {len(args): 2, len(args) + 1: 3, len(args) + 2: 4}
        args += list(held)
    flops = 12 * rows * width * inner
    return pl.pallas_call(
        expert_body,
        grid=(tiles,),
        in_specs=in_specs,
        out_specs=[
            whole((rows, width)),
            whole((rows, width + 128)),
            pl.BlockSpec((tile, rows), lambda j: (j, batch)),
            pl.BlockSpec((2, rows, tile), lambda j: (0, batch, j)),
            pl.BlockSpec((rows, width), lambda j: (batch, 0)),
        ],
        out_shape=[
            jax.ShapeDtypeStruct((rows, width), BF16),
            jax.ShapeDtypeStruct((rows, width + 128), BF16),
            jax.ShapeDtypeStruct((inner, batches * rows), BF16),
            jax.ShapeDtypeStruct((2, batches * rows, inner), BF16),
            jax.ShapeDtypeStruct((batches * rows, width), BF16),
        ],
        scratch_shapes=[pltpu.VMEM((rows, width), F32), pltpu.VMEM((rows, width), F32)],
        input_output_aliases=aliases,
        compiler_params=pltpu.CompilerParams(vmem_limit_bytes=56 << 20),
        cost_estimate=LIGHT,
        name="expert",
    )(*args)


def weight_in_body(*refs):
    xs, du_ref, out_ref, flipped = refs[:-3], refs[-3], refs[-2], refs[-1]
    rows = xs[0].shape[0]

    @pl.when(pl.program_id(0) == 0)
    def _():
        for n, x_ref in enumerate(xs):
            flipped[:, n * rows : (n + 1) * rows] = x_ref[...].T

    out_ref[...] = dot(flipped[...], du_ref[0]).astype(BF16).reshape(out_ref.shape)


def weight_in_call(size, xs, du):
    rows, width = xs[0].shape
    _, total, inner = du.shape
    tile = tile_of(inner, 256)
    tiles = inner // tile
    part = width // size
    space = 2 * tiles * part + (inner // size) * (width // tile)
    return pl.pallas_call(
        weight_in_body,
        grid=(2 * tiles,),
        in_specs=[pl.BlockSpec((rows, width), lambda j: (0, 0)) for _ in xs]
        + [pl.BlockSpec((1, total, tile), lambda j: (j // tiles, 0, j % tiles))],
        out_specs=pl.BlockSpec((size, part, tile), lambda j: (0, j, 0)),
        out_shape=jax.ShapeDtypeStruct((size, space, tile), BF16),
        scratch_shapes=[pltpu.VMEM((width, total), BF16)],
        compiler_params=pltpu.CompilerParams(vmem_limit_bytes=56 << 20),
        cost_estimate=LIGHT,
        name="weight_in",
    )(*xs, du)


def weight_out_body(gt_ref, dy_ref, _, out_ref):
    out_ref[...] = dot(gt_ref[...], dy_ref[...]).astype(BF16).reshape(out_ref.shape)


def weight_out_call(gt, dy, joined):
    inner, total = gt.shape
    width = dy.shape[1]
    size, space, tile = joined.shape
    part = inner // size
    first = (space - part * (width // tile)) // part
    assert first * part + part * (width // tile) == space
    return pl.pallas_call(
        weight_out_body,
        grid=(width // tile,),
        in_specs=[
            pl.BlockSpec((inner, total), lambda j: (0, 0)),
            pl.BlockSpec((total, tile), lambda j: (0, j)),
            pl.BlockSpec(memory_space=pl.ANY),
        ],
        out_specs=pl.BlockSpec((size, part, tile), lambda j: (0, first + j, 0)),
        out_shape=jax.ShapeDtypeStruct(joined.shape, BF16),
        input_output_aliases={2: 0},
        compiler_params=pltpu.CompilerParams(vmem_limit_bytes=56 << 20),
        cost_estimate=LIGHT,
        name="weight_out",
    )(gt, dy, joined)


def lane_below(shape, limit):
    return lax.broadcasted_iota(jnp.int32, shape, 1) < limit


def allowed_keys(rows, columns):
    segment_q, parent_q = rows[0:1], rows[1:2]
    segment_k, parent_k = columns[:, 0:1], columns[:, 1:2]
    return (segment_k == segment_q) | (segment_k == parent_q) | (parent_k == segment_q)


def pair_scores(h, head_size, scale, q, k, bias, allowed):
    low = lane_below(k.shape, head_size)
    mine = low if h % 2 == 0 else ~low
    raw = dot_t(jnp.where(mine, k, jnp.zeros_like(k)), q) * scale + bias
    return jnp.where(allowed, raw, NEG_BIG)


def piece_moves(me, pieces, rels, whole, arrived):
    moves = []
    for number, piece in enumerate(pieces):
        part, other = number % 2, number // 2
        half = piece.shape[1]
        for place, rel in enumerate(rels[part]):
            row = pl.multiple_of((me ^ rel ^ other) * (2 * half) + part * half, half)
            moves.append(
                pltpu.make_async_copy(
                    piece.at[place], whole.at[pl.ds(row, half)], arrived.at[len(moves)]
                )
            )
            moves[-1].start()
    return moves


def join_body(rels, me_ref, *refs):
    pieces, whole, arrived = refs[:-2], refs[-2], refs[-1]
    for move in piece_moves(me_ref[0], pieces, rels, whole, arrived):
        move.wait()


def join_call(me, pieces, rels):
    outside = pl.BlockSpec(memory_space=pl.ANY)
    count = 4 * len(rels[0])
    return pl.pallas_call(
        partial(join_body, rels),
        in_specs=[pl.BlockSpec(memory_space=pltpu.SMEM)] + [outside] * len(pieces),
        out_specs=pl.BlockSpec(memory_space=pltpu.VMEM),
        out_shape=jax.ShapeDtypeStruct((count * pieces[0].shape[1], pieces[0].shape[2]), BF16),
        scratch_shapes=[pltpu.SemaphoreType.DMA((count,))],
        cost_estimate=LIGHT,
        name="join",
    )(me, *pieces)


def forward_body(heads, experts, rels, *refs):
    if rels is None:
        weights_ref, refs = refs[0], refs[1:]
    else:
        me_ref, pieces, refs = refs[0], refs[1:5], refs[5:]
        refs, (full_ref, weights_ref, arrived, written) = refs[:-4], refs[-4:]
        moves = piece_moves(me_ref[0], pieces, rels, weights_ref, arrived)
    (
        tokens_ref,
        gain1_ref,
        bias_ref,
        rows_ref,
        columns_ref,
        gain2_ref,
        router_ref,
        targets_ref,
        x_ref,
        n1_ref,
        qkv_ref,
        lse_ref,
        o_ref,
        h1_ref,
        probs_ref,
    ) = refs
    length, width = tokens_ref.shape
    head_size = width // heads
    scale = head_size ** (-0.5)
    h0 = tokens_ref[...].astype(F32)
    n1 = (h0 * rms_scale(h0) * gain1_ref[...]).astype(BF16)
    n1_ref[...] = n1
    if rels is not None:
        for move in moves:
            move.wait()
        keep = pltpu.make_async_copy(weights_ref, full_ref, written)
        keep.start()
    for part in range(3):
        columns = slice(part * width, (part + 1) * width)
        qkv_ref[:, columns] = dot(n1, weights_ref[:, columns]).astype(BF16)
    allowed = allowed_keys(rows_ref[...], columns_ref[...])
    span = 2 * head_size
    for pair in range(heads // 2):
        at = pair * span
        q = qkv_ref[:, at : at + span]
        k = qkv_ref[:, width + at : width + at + span]
        flipped = qkv_ref[:, 2 * width + at : 2 * width + at + span].T
        parts = []
        for half in range(2):
            h = 2 * pair + half
            s = pair_scores(h, head_size, scale, q, k, bias_ref[h], allowed)
            top = jnp.max(s, axis=0, keepdims=True)
            e = jnp.exp(s - top)
            total = jnp.sum(e, axis=0, keepdims=True)
            lse_ref[h : h + 1] = top + jnp.log(total)
            p = (e * (1.0 / total)).astype(BF16)
            parts.append(dot(flipped[half * head_size : (half + 1) * head_size], p))
        o_ref[:, at : at + span] = jnp.concatenate(parts, axis=0).T.astype(BF16)
    h1 = h0 + dot(o_ref[...], weights_ref[:, 3 * width :])
    h1_ref[...] = h1
    n2 = (h1 * rms_scale(h1) * gain2_ref[...]).astype(BF16)
    logits = dot(n2, router_ref[...])
    logits = jnp.where(lane_below(logits.shape, experts), logits, NEG_BIG)
    top = jnp.max(logits, axis=-1, keepdims=True)
    e = jnp.exp(logits - top)
    probs_ref[...] = e / jnp.sum(e, axis=-1, keepdims=True)
    slots = lax.broadcasted_iota(jnp.int32, (x_ref.shape[0], length), 0)
    place = (slots == targets_ref[0:1]) | (slots == targets_ref[1:2])
    x_ref[...] = dot(place.astype(F32).astype(BF16), n2).astype(BF16)
    if rels is not None:
        keep.wait()


def forward_call(heads, experts, slot_count, weights, rels, *args):
    length, width = args[0].shape
    shapes = [
        ((slot_count, width), BF16),
        ((length, width), BF16),
        ((length, 3 * width), BF16),
        ((heads, length), F32),
        ((length, width), BF16),
        ((length, width), F32),
        ((length, 128), F32),
    ]
    inside = pl.BlockSpec(memory_space=pltpu.VMEM)
    outside = pl.BlockSpec(memory_space=pl.ANY)
    in_specs = [inside] * len(args)
    out_specs = [inside] * len(shapes)
    scratch = []
    if rels is None:
        args, in_specs = (weights,) + args, [inside] + in_specs
    else:
        me, pieces = weights
        args = (me, *pieces) + args
        in_specs = [pl.BlockSpec(memory_space=pltpu.SMEM)] + [outside] * len(pieces) + in_specs
        shapes.append(((width, 4 * width), BF16))
        out_specs.append(outside)
        scratch = [
            pltpu.VMEM((width, 4 * width), BF16),
            pltpu.SemaphoreType.DMA((4 * len(rels[0]),)),
            pltpu.SemaphoreType.DMA,
        ]
    return pl.pallas_call(
        partial(forward_body, heads, experts, rels),
        in_specs=in_specs,
        out_specs=out_specs,
        out_shape=[jax.ShapeDtypeStruct(*s) for s in shapes],
        scratch_shapes=scratch,
        compiler_params=pltpu.CompilerParams(vmem_limit_bytes=56 << 20),
        cost_estimate=LIGHT,
        name="attention_forward",
    )(*args)


def backward_body(
    heads,
    experts,
    dx_ref,
    targets_ref,
    routes_ref,
    probs_ref,
    h1_ref,
    go_ref,
    gain2_ref,
    router_ref,
    proj_ref,
    qkv_ref,
    lse_ref,
    bias_ref,
    rows_ref,
    columns_ref,
    dh1_ref,
    dbranch_ref,
    dqkv_ref,
    ds_ref,
    router_grad_ref,
    gain_grad_ref,
    do_ref,
):
    length, width = h1_ref.shape
    head_size = width // heads
    scale = head_size ** (-0.5)
    slots = lax.broadcasted_iota(jnp.int32, (length, dx_ref.shape[0]), 1)
    hot = [slots == targets_ref[:, j : j + 1] for j in range(2)]
    pick = [m.astype(F32).astype(BF16) for m in hot]
    dgate = [jnp.sum(dot(m, dx_ref[:, width:]), axis=-1, keepdims=True) for m in pick]
    probs = probs_ref[...]
    lane = lax.broadcasted_iota(jnp.int32, probs.shape, 1)
    dprobs = sum(jnp.where(lane == routes_ref[:, j : j + 1], dgate[j], 0.0) for j in range(2))
    dlogits = probs * (dprobs - jnp.sum(probs * dprobs, axis=-1, keepdims=True))
    dlogits = dlogits.astype(BF16)
    dn2 = dot(pick[0] + pick[1], dx_ref[:, :width]) + dot_t(dlogits, router_ref[...])
    h1 = h1_ref[...]
    r2 = rms_scale(h1)
    n2_hat = h1 * r2
    gain2 = gain2_ref[...]
    n2 = (n2_hat * gain2).astype(BF16)
    router_grad_ref[...] = t_dot(dlogits, n2)
    gain_grad_ref[...] = jnp.sum(dn2 * n2_hat, axis=0, keepdims=True)
    scaled = dn2 * gain2
    mean = jnp.mean(scaled * n2_hat, axis=-1, keepdims=True)
    dh1 = go_ref[...].astype(F32) + r2 * (scaled - n2_hat * mean)
    dh1_ref[...] = dh1
    dbranch = dh1.astype(BF16)
    dbranch_ref[...] = dbranch
    do_ref[...] = dot_t(dbranch, proj_ref[...]).astype(BF16)
    allowed = allowed_keys(rows_ref[...], columns_ref[...])
    span = 2 * head_size
    low = lane_below((length, span), head_size)
    for pair in range(heads // 2):
        at = pair * span
        q = qkv_ref[:, at : at + span]
        k = qkv_ref[:, width + at : width + at + span]
        v = qkv_ref[:, 2 * width + at : 2 * width + at + span]
        do = do_ref[:, at : at + span]
        flipped = k.T
        dq, dk, dv = [], [], []
        for half in range(2):
            h = 2 * pair + half
            s = pair_scores(h, head_size, scale, q, k, bias_ref[h], allowed)
            p = jnp.exp(s - lse_ref[h : h + 1])
            mine = low if half == 0 else ~low
            dp = dot_t(jnp.where(mine, v, jnp.zeros_like(v)), do)
            inner = jnp.sum(p * dp, axis=0, keepdims=True)
            ds = (p * (dp - inner)).astype(BF16)
            ds_ref[h] = ds
            dv.append(dot(p.astype(BF16), do))
            dk.append(dot(ds, q))
            dq.append(dot(flipped[half * head_size : (half + 1) * head_size], ds))
        dqkv_ref[:, at : at + span] = (jnp.concatenate(dq, axis=0).T * scale).astype(BF16)
        dqkv_ref[:, width + at : width + at + span] = (jnp.where(low, *dk) * scale).astype(BF16)
        dqkv_ref[:, 2 * width + at : 2 * width + at + span] = jnp.where(low, *dv).astype(BF16)


def backward_call(heads, experts, dx, targets, routes, probs, h1, go, gain2, router, proj, *rest):
    length, width = h1.shape
    shapes = [
        ((length, width), F32),
        ((length, width), BF16),
        ((length, 3 * width), BF16),
        ((heads, length, length), BF16),
        ((128, width), F32),
        ((1, width), F32),
    ]
    args = (dx, targets, routes, probs, h1, go, gain2, router, proj) + rest
    in_specs = [pl.BlockSpec(a.shape, lambda i, n=a.ndim: (0,) * n) for a in args]
    in_specs[8] = pl.BlockSpec((width, width), lambda i: (0, 3))
    return pl.pallas_call(
        partial(backward_body, heads, experts),
        grid=(1,),
        in_specs=in_specs,
        out_specs=[pl.BlockSpec(s, lambda i, n=len(s): (0,) * n) for s, _ in shapes],
        out_shape=[jax.ShapeDtypeStruct(*s) for s in shapes],
        scratch_shapes=[pltpu.VMEM((length, width), BF16)],
        compiler_params=pltpu.CompilerParams(vmem_limit_bytes=56 << 20),
        cost_estimate=LIGHT,
        name="attention_backward",
    )(*args)


def on_device(
    sizes,
    tokens,
    cotangent,
    segment_ids,
    parent_ids,
    routes,
    gain_attn,
    w_qkv,
    w_proj,
    rel_bias,
    gain_moe,
    w_router,
    w_in,
    w_out,
):
    dp, experts = sizes["dp"], sizes["expert"]
    batches, length, width = tokens.shape
    heads = rel_bias.shape[1]
    head_size = width // heads
    inner = w_in.shape[2] // 2
    capacity = (10 * length + 4 * experts - 1) // (4 * experts)
    slot_count = experts * capacity
    scale = head_size ** (-0.5)
    me_e = lax.axis_index("expert")

    attn_block = gather_expert(jnp.concatenate([w_qkv, w_proj], axis=1), experts)
    places = jax.vmap(partial(slot_positions, experts=experts))(routes)
    targets = routes * capacity + places
    hot = targets[..., None] == jnp.arange(slot_count, dtype=jnp.int32)
    select = hot.astype(BF16)
    both = select[:, :, 0] + select[:, :, 1]
    out_grads = [cotangent[n] for n in range(batches)]
    outgoing = [
        t_dot(both[n], out_grads[n]).astype(BF16).reshape(experts, capacity, width)
        for n in range(batches)
    ]
    go_slots = [all_to_all(after(v, attn_block)) for v in outgoing]

    positions = jnp.arange(length, dtype=jnp.int32)
    buckets = bucket_of(positions[:, None] - positions[None, :])
    bucket_hot = (buckets[:, :, None] == jnp.arange(rel_bias.shape[0], dtype=jnp.int32)).astype(F32)
    bias = jnp.einsum("kqc,ch->hkq", bucket_hot, rel_bias, precision=lax.Precision.HIGHEST)

    me_d = lax.axis_index("dp").astype(jnp.int32)[None]
    out_pieces, rels = gather_dp(w_out[0], dp, ())
    wout_full = join_call(me_d, out_pieces, rels)
    pieces, _ = gather_dp(after(attn_block, out_pieces[:2]), dp, (bias, outgoing))
    win_full = lax.all_gather(
        after(w_in[0], pieces[:2], go_slots[0]), "dp", axis=0, tiled=True
    )

    router_wide = jnp.pad(w_router, ((0, 0), (0, 128 - experts)))
    gain1, gain2 = gain_attn[None], gain_moe[None]
    saved = []
    for n in range(batches):
        id_rows = jnp.stack([segment_ids[n], parent_ids[n]])
        target_columns = targets[n]
        weights = attn_w if n else (me_d, pieces)
        outs = forward_call(
            heads,
            experts,
            slot_count,
            weights,
            None if n else rels,
            tokens[n],
            gain1,
            bias,
            id_rows,
            id_rows.T,
            gain2,
            router_wide,
            target_columns.T,
        )
        if n == 0:
            *outs, attn_w = outs
        x_slots = all_to_all(after(outs[0], go_slots).reshape(experts, capacity, width))
        saved.append((id_rows,) + tuple(outs[1:]) + (x_slots,))

    mine = jnp.stack([me_e, jnp.int32(experts)]).astype(jnp.int32)
    held, grads = [], None
    for n in range(batches):
        x = saved[n][-1].reshape(slot_count, width)
        go = go_slots[n].reshape(slot_count, width)
        y, dx, *grads = expert_call(
            n, batches, mine, x, go, router_wide, win_full, wout_full, grads
        )
        dx_back = all_to_all(dx.reshape(experts, capacity, width + 128))
        held.append((x, dx_back.reshape(slot_count, width + 128), y))
    y_back = all_to_all(
        jnp.stack([h[2].reshape(experts, capacity, width) for h in held], axis=1)
    )

    def backward(n, dx_back):
        id_rows, _, qkv, lse, _, h1, probs, _ = saved[n]
        return backward_call(
            heads,
            experts,
            dx_back,
            targets[n],
            routes[n],
            probs,
            h1,
            out_grads[n],
            gain2,
            router_wide,
            attn_w,
            qkv,
            lse,
            bias,
            id_rows,
            id_rows.T,
        )

    gt, du, dy = grads
    joined = weight_in_call(dp, [h[0] for h in held], after(du, held[0][1]))
    backs = []
    for n in range(batches):
        backs.append(backward(n, after(held[n][1], joined)))
        if n == 0:
            joined = weight_out_call(after(gt, held[-1][1], backs[0]), dy, joined)
    space, tile = joined.shape[1:]
    summed = lax.psum_scatter(
        joined.reshape(dp * space, tile), "dp", scatter_dimension=0, tiled=True
    )
    part_in, part_out = w_in.shape[1], w_out.shape[1]
    cut = (w_in.shape[2] // tile) * part_in
    in_total = summed[:cut].reshape(-1, part_in, tile).transpose(1, 0, 2)
    in_total = in_total.reshape(part_in, -1).astype(F32)
    out_total = summed[cut:].reshape(-1, part_out, tile).transpose(1, 0, 2)
    out_total = out_total.reshape(part_out, -1).astype(F32)

    outputs, input_grads = [], []
    full_qkv = attn_w[:, : 3 * width]
    n1_all, o_all, dbranch_all, dqkv_all = (
        jnp.concatenate(parts, axis=0)
        for parts in (
            [v[1] for v in saved],
            [v[4] for v in saved],
            [v[1] for v in backs],
            [v[2] for v in backs],
        )
    )
    qkv_part = t_dot(n1_all, dqkv_all)
    proj_part = t_dot(o_all, dbranch_all)
    attn_part = jnp.concatenate([qkv_part, proj_part], axis=1).astype(BF16)
    attn_core = scatter_core(attn_part, dp)
    attn_sum = scatter_dp(attn_core, dp)
    router_grad = sum(v[4] for v in backs)[:experts].T
    gain_moe_grad = sum(v[5] for v in backs)[0]
    table_grad = jnp.einsum(
        "nhkq,kqc->ch",
        after(jnp.stack([v[3] for v in backs]), attn_core),
        bucket_hot.astype(BF16),
        preferred_element_type=F32,
    )
    gain_attn_grad = 0.0
    for n in range(batches):
        _, n1, _, _, _, h1, probs, _ = saved[n]
        dh1, _, dqkv, _, _, _ = backs[n]
        y_n = after(y_back, attn_sum)[:, n].reshape(slot_count, width)
        route_hot = (routes[n][:, :, None] == jnp.arange(experts, dtype=jnp.int32)).astype(F32)
        gates = jnp.sum(probs[:, None, :experts] * route_hot, axis=-1)
        picked0, picked1 = dot(select[n][:, 0], y_n), dot(select[n][:, 1], y_n)
        moe = gates[:, :1] * picked0 + gates[:, 1:] * picked1
        outputs.append((h1 + moe).astype(BF16))
        h0 = tokens[n].astype(F32)
        r1 = rms_scale(h0)
        n1_hat = h0 * r1
        dn1 = dot_t(after(dqkv, attn_core), full_qkv)
        gain_attn_grad = gain_attn_grad + jnp.sum(dn1 * n1_hat, axis=0)
        scaled = dn1 * gain_attn
        input_grad = dh1 + r1 * (
            scaled - n1_hat * jnp.mean(scaled * n1_hat, axis=-1, keepdims=True)
        )
        input_grads.append(input_grad.astype(BF16))

    attn_total = scatter_expert(attn_sum, experts)
    qkv_total, proj_total = attn_total[:, : 3 * width], attn_total[:, 3 * width :]
    small = jnp.concatenate(
        [gain_attn_grad, table_grad.reshape(-1), gain_moe_grad, router_grad.reshape(-1)]
    )
    small = sum_all(after(small.reshape(-1, 128), attn_sum), sizes).reshape(-1)
    cuts = (width, width + table_grad.size, 2 * width + table_grad.size)
    return (
        jnp.stack(outputs),
        jnp.stack(input_grads),
        small[: cuts[0]],
        qkv_total,
        proj_total,
        small[cuts[0] : cuts[1]].reshape(table_grad.shape),
        small[cuts[1] : cuts[2]],
        small[cuts[2] :].reshape(router_grad.shape),
        in_total[None],
        out_total[None],
    )


def solution(mesh):
    rows = P(None, ("dp", "expert"), None)
    in_specs = (
        rows,
        rows,
        P(None, ("dp", "expert")),
        P(None, ("dp", "expert")),
        rows,
        P(),
        P(("dp", "expert"), None),
        P(("dp", "expert"), None),
        P(),
        P(),
        P(),
        P("expert", "dp", None),
        P("expert", "dp", None),
    )
    out_specs = (
        rows,
        rows,
        P(),
        P(("dp", "expert"), None),
        P(("dp", "expert"), None),
        P(),
        P(),
        P(),
        P("expert", "dp", None),
        P("expert", "dp", None),
    )
    return jax.shard_map(
        partial(on_device, dict(mesh.shape)),
        mesh=mesh,
        in_specs=in_specs,
        out_specs=out_specs,
        check_vma=False,
    )
```

time: 669 us -> 516 us (0.77)
  matrix products: 250 us -> 24.6 us
  Pallas kernels: 0 us -> 172 us
  waiting for transfers between devices: 208 us -> 134 us
  other arithmetic: 50.3 us -> 33 us
  starting transfers between devices: 82.9 us -> 68.4 us
    pallas_call x0 -> x9, Pallas kernels: none -> 172 us  [the longest x2 67.4 us: expert_call(): pl.pallas_call(expert_body, grid=(tiles,), in_specs=in_specs, out_specs=[...]
    dot_general x20 -> x4, matrix products: 86.4 us -> 2.46 us  [dot(): return jnp.dot(left, right, preferred_element_type=F32)]
    dot_general x14 -> x4, matrix products: 72.3 us -> 9.45 us  [t_dot(): lax.dot_general(left, right, (((0,), (0,)), ((), ())), preferred_element_...]
    all_to_all x8, waiting for transfers between devices: 83 us -> 30.1 us  [all_to_all(): lax.all_to_all(value, 'expert', split_axis=0, concat_axis=0, tiled=True)]
    dot_general x10 -> x2, matrix products: 55.5 us -> 7.2 us  [dot_t(): lax.dot_general(left, right, (((1,), (1,)), ((), ())), preferred_element_...]
    dot_general x15 -> x2, matrix products: 36.1 us -> 5.48 us  [the longest x1 4.13 us: on_device(): jnp.einsum('kqc,ch->hkq', bucket_hot, rel_bias, precision=lax.Precision.H...]
    ppermute x26 -> x22, waiting for transfers between devices: 123 us -> 103 us  [flip(): return lax.ppermute(value, axis, [(i, i ^ bit) for i in range(size)])]
    all_to_all x8, starting transfers between devices: 47.2 us -> 38.6 us  [all_to_all(): lax.all_to_all(value, 'expert', split_axis=0, concat_axis=0, tiled=True)]
  transfers between devices with their start and end apart: 43 -> 35, of which waited for: 21 -> 17; matrix products, arithmetic and copies ran while one was open for 40% -> 19% of each run, Pallas kernels for 0% -> 31%
where the time goes in v3:
time: 516 us; the launch traced here: 507 us
  Pallas kernels  172 us (33%)
  waiting for transfers between devices  134 us (26%)
  starting transfers between devices  68.4 us (13%)
  local copies, waits for them, and re-layouts  60.1 us (12%)
  other arithmetic  33 us (6%)
  matrix products  24.6 us (5%)
  between operations  15.3 us (3%)
    ppermute x22, waiting for transfers between devices, flip(): return lax.ppermute(value, axis, [(i, i ^ bit) for i in range(size)])  103 us
    pallas_call x2, Pallas kernels, expert_call(): pl.pallas_call(expert_body, grid=(tiles,), in_specs=in_specs, out_specs=[...  67.4 us
    all_to_all x8, starting transfers between devices, all_to_all(): lax.all_to_all(value, 'expert', split_axis=0, concat_axis=0, tiled=True)  38.6 us
    pallas_call x2, Pallas kernels, forward_call(): pl.pallas_call(partial(forward_body, heads, experts, rels), in_specs=in_s...  31.4 us
    all_to_all x8, waiting for transfers between devices, all_to_all(): lax.all_to_all(value, 'expert', split_axis=0, concat_axis=0, tiled=True)  30.1 us
    pallas_call x2, Pallas kernels, backward_call(): pl.pallas_call(partial(backward_body, heads, experts), grid=(1,), in_spec...  27.5 us
    pallas_call x1, Pallas kernels, weight_in_call(): pl.pallas_call(weight_in_body, grid=(2 * tiles,), in_specs=[pl.BlockSpec(...  27.2 us
    ppermute x22, starting transfers between devices, flip(): return lax.ppermute(value, axis, [(i, i ^ bit) for i in range(size)])  22.8 us
  transfers between devices with their start and end apart: 35, of which 17 were waited for; matrix products, arithmetic and copies ran while one was open for 19% of the time, Pallas kernels for 31%

profile of v3, /device:TPU:0, one launch (start us, length us, event | category | flops | bytes accessed | tf_op | source)
XLA Modules:
  0.0 507.0 jit_solution(3243940102642220124)
XLA Ops:
  10.3 3.0 collective-permute-start
  13.3 2.6 collective-permute-start.1
  23.2 2.4 reduce-window.6
  28.0 4.1 fusion
  40.5 12.9 %collective-permute-done.4 = bf16[2,176,1024]{2,1,0:T(8,128)(2,1)S(1)} collective-permute-done((bf16[2,176,1024]{2,1,0:T(8,128)(2,1)S(1)}, bf16[2,176,1024]{2,1,0:T(8,128)(2,1)S(1)}, u32[]{:S(2)}, u32[]{:S(2)}) %collective-permute-start.4) | collective-permute-done | bytes 720928 | tf_op jit(solution)/shard_map/ppermute | solution.py:52
  63.1 4.4 copy.193
  67.5 7.4 %all-to-all-start = ((bf16[4,160,1024]{2,1,0:T(8,128)(2,1)}), bf16[4,160,1024]{2,1,0:T(8,128)(2,1)S(1)}, u32[]{:S(2)}, u32[]{:S(2)}) async-start(bf16[4,160,1024]{2,1,0:T(8,128)(2,1)} %bitcast.15), calls=%async_computation | async-start | bytes 2621440 | tf_op jit(solution)/shard_map/all_to_all | solution.py:92
  81.5 16.8 %collective-permute-done.10 = bf16[2,64,4096]{2,1,0:T(8,128)(2,1)S(1)} collective-permute-done((bf16[2,64,4096]{2,1,0:T(8,128)(2,1)S(1)}, bf16[2,64,4096]{2,1,0:T(8,128)(2,1)S(1)}, u32[]{:S(2)}, u32[]{:S(2)}) %collective-permute-start.10) | collective-permute-done | bytes 1048608 | tf_op jit(solution)/shard_map/ppermute | solution.py:52
  100.8 3.0 all-to-all-done
  105.5 3.8 all-to-all-start.1
  113.6 16.8 %attention_forward.2 = (bf16[640,1024]{1,0:T(8,128)(2,1)}, bf16[256,1024]{1,0:T(8,128)(2,1)}, bf16[256,3072]{1,0:T(8,128)(2,1)}, f32[16,256]{1,0:T(8,128)}, bf16...) custom-call(s32[1]{0:T(128)} %bitcast.refs_0_.me_ref, ...), custom_call_target="tpu_custom_call" | custom-call | flops 1 | bytes 1 | tf_op jit(solution)/shard_map/attention_forward/pallas_call | solution.py:481
  130.4 10.8 %all-to-all-done.1 = bf16[4,160,1024]{2,1,0:T(8,128)(2,1)S(1)} async-done(((bf16[4,160,1024]{2,1,0:T(8,128)(2,1)}), bf16[4,160,1024]{2,1,0:T(8,128)(2,1)S(1)}, u32[]{:S(2)}, u32[]{:S(2)}) %all-to-all-start.1) | async-done | bytes 1310752 | tf_op jit(solution)/shard_map/all_to_all | solution.py:92
  142.2 4.1 all-to-all-start.2
  147.8 14.6 %attention_forward.3 = (bf16[640,1024]{1,0:T(8,128)(2,1)}, bf16[256,1024]{1,0:T(8,128)(2,1)}, bf16[256,3072]{1,0:T(8,128)(2,1)}, f32[16,256]{1,0:T(8,128)}, bf16...) custom-call(bf16[1024,4096]{1,0:T(8,128)(2,1)} %get-tuple-element.75.refs_0_.proj_ref, ...), custom_call_target="tpu_custom_call" | custom-call | flops 1 | bytes 1 | tf_op jit(solution)/shard_map/attention_forward/pallas_call | solution.py:481
  162.4 14.9 %all-to-all-done.2 = bf16[4,160,1024]{2,1,0:T(8,128)(2,1)S(1)} async-done(((bf16[4,160,1024]{2,1,0:T(8,128)(2,1)}), bf16[4,160,1024]{2,1,0:T(8,128)(2,1)S(1)}, u32[]{:S(2)}, u32[]{:S(2)}) %all-to-all-start.2) | async-done | bytes 1310752 | tf_op jit(solution)/shard_map/all_to_all | solution.py:92
  177.3 3.5 all-to-all-start.3
  182.0 2.5 collective-permute-done.13.refs_2_
  186.5 5.2 %join.1.wo_ref = bf16[2816,1024]{1,0:T(8,128)(2,1)} custom-call(s32[1]{0:T(128)} %bitcast.refs_0_.me_ref, bf16[4,176,1024]{2,1,0:T(8,128)(2,1)} %pad_maximum_fusion.3.refs_0_, bf16[4,176,1024]{2,1,0:T(8,128)(2,1)} %pad_maximum_fusion.4.refs_1_, bf16[4,176,1024]{2,1,0:T(8,128)(2,1)} %collective-permute-done.13.refs_2_, ...), custom_call_target="tpu_custom_call" | custom-call | flops 1 | bytes 1 | tf_op jit(solution)/shard_map/join/pallas_call | solution.py:370
  191.7 33.7 %expert.2 = (bf16[640,1024]{1,0:T(8,128)(2,1)}, bf16[640,1152]{1,0:T(8,128)(2,1)}, bf16[2816,1280]{1,0:T(8,128)(2,1)}, bf16[2,1280,2816]{2,1,0:T(8,128)(2,1)}, bf16[1280,1024]{1,0:T(8,128)(2,1)}) custom-call(s32[2]{0:T(128)} %pad_add_fusion.4.mine, bf16[640,1024]{1,0:T(8,128)(2,1)} %bitcast.203, bf16[640,1024]{1,0:T(8,128)(2,1)} %bitcast.221, ...), custom_call_target="tpu_custom_call" | custom-call | flops 1 | bytes 1 | tf_op jit(solution)/shard_map/expert/pallas_call | solution.py:241
  225.5 5.2 %all-to-all-start.5 = ((bf16[4,160,1152]{2,1,0:T(8,128)(2,1)}), bf16[4,160,1152]{2,1,0:T(8,128)(2,1)}, u32[]{:S(2)}, u32[]{:S(2)}) async-start(bf16[4,160,1152]{2,1,0:T(8,128)(2,1)} %bitcast.228), calls=%async_computation.5 | async-start | bytes 2949120 | tf_op jit(solution)/shard_map/all_to_all | solution.py:92
  230.7 33.7 %expert.3 = (bf16[640,1024]{1,0:T(8,128)(2,1)}, bf16[640,1152]{1,0:T(8,128)(2,1)}, bf16[2816,1280]{1,0:T(8,128)(2,1)}, bf16[2,1280,2816]{2,1,0:T(8,128)(2,1)}, bf16[1280,1024]{1,0:T(8,128)(2,1)}) custom-call(s32[2]{0:T(128)} %pad_add_fusion.4.mine, bf16[640,1024]{1,0:T(8,128)(2,1)} %bitcast.205, ...), custom_call_target="tpu_custom_call", output_to_operand_aliasing={{2}: (7, {}), {3}: (8, {}), {4}: (9, {})} | custom-call | flops 1 | bytes 1 | tf_op jit(solution)/shard_map/expert/pallas_call | solution.py:241
  265.9 3.8 all-to-all-start.6
  271.5 27.2 %weight_in.1._ = bf16[8,4224,256]{2,1,0:T(8,128)(2,1)} custom-call(bf16[640,1024]{1,0:T(8,128)(2,1)} %bitcast.204, bf16[640,1024]{1,0:T(8,128)(2,1)} %bitcast.206, bf16[2,1280,2816]{2,1,0:T(8,128)(2,1)} %get-tuple-element.86.refs_2_), custom_call_target="tpu_custom_call" | custom-call | flops 1 | bytes 1 | tf_op jit(solution)/shard_map/weight_in/pallas_call | solution.py:286
  298.7 13.6 %attention_backward.2 = (f32[256,1024]{1,0:T(8,128)}, bf16[256,1024]{1,0:T(8,128)(2,1)}, bf16[256,3072]{1,0:T(8,128)(2,1)}, bf16[16,256,256]{2,1,0:T(8,128)(2,1)...) custom-call(bf16[640,1152]{1,0:T(8,128)(2,1)} %bitcast.47.dx_ref, s32[256,2]{1,0:T(8,128)} %get-tuple-element.197.targets_ref, ...), custom_call_target="tpu_custom_call" | custom-call | flops 1 | bytes 1 | tf_op jit(solution)/shard_map/attention_backward/pallas_call | solution.py:586
  312.3 13.4 %weight_out.1 = bf16[8,4224,256]{2,1,0:T(8,128)(2,1)} custom-call(bf16[2816,1280]{1,0:T(8,128)(2,1)} %get-tuple-element.98.gt_ref, bf16[1280,1024]{1,0:T(8,128)(2,1)} %get-tuple-element.99.dy_ref, bf16[8,4224,256]{2,1,0:T(8,128)(2,1)} %weight_in.1._), custom_call_target="tpu_custom_call", output_to_operand_aliasing={{}: (2, {})} | custom-call | flops 1 | bytes 1 | tf_op jit(solution)/shard_map/weight_out/pallas_call | solution.py:311
  326.5 13.9 %attention_backward.3 = (f32[256,1024]{1,0:T(8,128)}, bf16[256,1024]{1,0:T(8,128)(2,1)}, bf16[256,3072]{1,0:T(8,128)(2,1)}, bf16[16,256,256]{2,1,0:T(8,128)(2,1)...) custom-call(bf16[640,1152]{1,0:T(8,128)(2,1)} %bitcast.218, s32[256,2]{1,0:T(8,128)} %get-tuple-element.194.targets_ref, ...), custom_call_target="tpu_custom_call" | custom-call | flops 1 | bytes 1 | tf_op jit(solution)/shard_map/attention_backward/pallas_call | solution.py:586
  340.5 2.5 convolution_convert_fusion.1
  343.6 3.7 convolution_convert_fusion
  347.4 2.6 fusion.7
  350.0 2.8 copy-done.2
  356.6 3.1 pad_maximum_fusion.1
  359.6 5.5 %all-to-all-start.4 = ((bf16[4,2,160,1024]{3,2,1,0:T(8,128)(2,1)}), bf16[4,2,160,1024]{3,2,1,0:T(8,128)(2,1)}, u32[]{:S(2)}, u32[]{:S(2)}) async-start(bf16[4,2,160,1024]{3,2,1,0:T(8,128)(2,1)} %pad_maximum_fusion.1), calls=%async_computation.4 | async-start | bytes 5242880 | tf_op jit(solution)/shard_map/all_to_all | solution.py:92
  368.3 3.0 pad_maximum_fusion
  372.8 4.4 convert_add_fusion
  379.7 2.9 fusion.79
  385.3 5.0 fusion.1
  390.4 2.2 fusion.40
  394.4 36.7 %collective-permute-done.16 = bf16[2,1,64,4096]{3,2,1,0:T(8,128)(2,1)S(1)} collective-permute-done((bf16[2,1,64,4096]{3,2,1,0:T(8,128)(2,1)S(1)}, bf16[2,1,64,4096]{3,2,1,0:T(8,128)(2,1)S(1)}, u32[]{:S(2)}, u32[]{:S(2)}) %collective-permute-start.16) | collective-permute-done | bytes 1048608 | tf_op jit(solution)/shard_map/ppermute | solution.py:52
  434.0 14.1 %collective-permute-done.17 = bf16[1,1,64,4096]{3,2,1,0:T(8,128)(2,1)S(1)} collective-permute-done((bf16[1,1,64,4096]{3,2,1,0:T(8,128)(2,1)S(1)}, bf16[1,1,64,4096]{3,2,1,0:T(8,128)(2,1)S(1)}, u32[]{:S(2)}, u32[]{:S(2)}) %collective-permute-start.17) | collective-permute-done | bytes 524320 | tf_op jit(solution)/shard_map/ppermute | solution.py:52
  448.3 2.9 collective-permute-done.19
  452.4 5.3 %all-to-all-start.7 = ((bf16[4,32,4096]{2,1,0:T(8,128)(2,1)}), bf16[4,32,4096]{2,1,0:T(8,128)(2,1)S(1)}, u32[]{:S(2)}, u32[]{:S(2)}) async-start(bf16[4,32,4096]{2,1,0:T(8,128)(2,1)} %bitcast.83), calls=%async_computation.7 | async-start | bytes 2097152 | tf_op jit(solution)/shard_map/all_to_all | solution.py:92
  457.8 2.2 fusion.80
  462.3 3.0 collective-permute-done.21
  466.0 3.2 collective-permute-done.22
  471.9 4.2 collective-permute-done.23
  476.1 4.6 collective-permute-start.24
  481.8 3.6 collective-permute-done.24
  493.6 3.4 copy.178
  (263 shorter events, 93.4 us)
Async XLA Ops:
  7.2 20.8 %copy-start = (f32[32,16]{0,1:T(8,128)S(1)}, f32[32,16]{0,1:T(8,128)}, u32[]{:S(2)}) copy-start(f32[32,16]{0,1:T(8,128)} %param.21) | copy-start | bytes 6148
  10.3 23.3 %collective-permute-start = (bf16[32,4096]{1,0:T(8,128)(2,1)}, bf16[32,4096]{1,0:T(8,128)(2,1)}, u32[]{:S(2)}, u32[]{:S(2)}) collective-permute-start(bf16[32,4096]{1,0:T(8,128)(2,1)} %constant_dynamic-update-slice_fusion), channel_id=1, source_target_pairs={{0,1},{1,2},{2,3},{3,0},{4,5},{5,6},{6,7},{7,4},{8,9},{9,10},{10,1... | collective-permute-start | bytes 786440 | tf_op jit(solution)/shard_map/ppermute | solution.py:56
  13.3 21.3 %collective-permute-start.1 = (bf16[32,4096]{1,0:T(8,128)(2,1)}, bf16[32,4096]{1,0:T(8,128)(2,1)}, u32[]{:S(2)}, u32[]{:S(2)}) collective-permute-start(bf16[32,4096]{1,0:T(8,128)(2,1)} %constant_dynamic-update-slice_fusion), channel_id=1, source_target_pairs={{0,2},{1,3},{2,0},{3,1},{4,6},{5,7},{6,4},{7,5},{8,10},{9,11},{10,... | collective-permute-start | bytes 786440 | tf_op jit(solution)/shard_map/ppermute | solution.py:56
  15.9 23.7 %collective-permute-start.2 = (bf16[32,4096]{1,0:T(8,128)(2,1)}, bf16[32,4096]{1,0:T(8,128)(2,1)}, u32[]{:S(2)}, u32[]{:S(2)}) collective-permute-start(bf16[32,4096]{1,0:T(8,128)(2,1)} %constant_dynamic-update-slice_fusion), channel_id=1, source_target_pairs={{0,3},{1,0},{2,1},{3,2},{4,7},{5,4},{6,5},{7,6},{8,11},{9,8},{10,9... | collective-permute-start | bytes 786440 | tf_op jit(solution)/shard_map/ppermute | solution.py:56
  18.4 17.2 %collective-permute-start.3 = (bf16[1,176,1024]{2,1,0:T(8,128)(2,1)S(1)}, bf16[1,176,1024]{2,1,0:T(8,128)(2,1)}, u32[]{:S(2)}, u32[]{:S(2)}) collective-permute-start(bf16[1,176,1024]{2,1,0:T(8,128)(2,1)S(1)} %get-tuple-element.191), channel_id=1, source_target_pairs={{0,8},{4,12},{8,0},{12,4},{16,24},{20,28},{24,16},{28,20},{1,9},{5... | collective-permute-start | bytes 1081352 | tf_op jit(solution)/shard_map/ppermute | solution.py:52
  19.9 17.2 %collective-permute-start.5 = (bf16[1,176,1024]{2,1,0:T(8,128)(2,1)S(1)}, bf16[1,176,1024]{2,1,0:T(8,128)(2,1)}, u32[]{:S(2)}, u32[]{:S(2)}) collective-permute-start(bf16[1,176,1024]{2,1,0:T(8,128)(2,1)S(1)} %get-tuple-element.190), channel_id=1, source_target_pairs={{0,16},{4,20},{8,24},{12,28},{16,0},{20,4},{24,8},{28,12},{1,17},{... | collective-permute-start | bytes 1081352 | tf_op jit(solution)/shard_map/ppermute | solution.py:52
  36.6 16.8 %collective-permute-start.4 = (bf16[2,176,1024]{2,1,0:T(8,128)(2,1)S(1)}, bf16[2,176,1024]{2,1,0:T(8,128)(2,1)S(1)}, u32[]{:S(2)}, u32[]{:S(2)}) collective-permute-start(bf16[2,176,1024]{2,1,0:T(8,128)(2,1)S(1)} %pad_maximum_fusion.9), channel_id=1, source_target_pairs={{0,16},{4,20},{8,24},{12,28},{16,0},{20,4},{24,8},{28,12},{1,17},{... | collective-permute-start | bytes 2162696 | tf_op jit(solution)/shard_map/ppermute | solution.py:52
  38.2 17.5 %collective-permute-start.6 = (bf16[2,176,1024]{2,1,0:T(8,128)(2,1)S(1)}, bf16[2,176,1024]{2,1,0:T(8,128)(2,1)S(1)}, u32[]{:S(2)}, u32[]{:S(2)}) collective-permute-start(bf16[2,176,1024]{2,1,0:T(8,128)(2,1)S(1)} %pad_maximum_fusion.10), channel_id=1, source_target_pairs={{0,8},{4,12},{8,0},{12,4},{16,24},{20,28},{24,16},{28,20},{1,9},{5... | collective-permute-start | bytes 2162696 | tf_op jit(solution)/shard_map/ppermute | solution.py:52
  57.9 17.0 %collective-permute-start.9 = (bf16[1,64,4096]{2,1,0:T(8,128)(2,1)}, bf16[1,64,4096]{2,1,0:T(8,128)(2,1)S(1)}, u32[]{:S(2)}, u32[]{:S(2)}) collective-permute-start(bf16[1,64,4096]{2,1,0:T(8,128)(2,1)} %get-tuple-element.188), channel_id=1, source_target_pairs={{0,16},{4,20},{8,24},{12,28},{16,0},{20,4},{24,8},{28,12},{1,17},{... | collective-permute-start | bytes 1572872 | tf_op jit(solution)/shard_map/ppermute | solution.py:52
  60.0 16.7 %collective-permute-start.7 = (bf16[1,64,4096]{2,1,0:T(8,128)(2,1)S(1)}, bf16[1,64,4096]{2,1,0:T(8,128)(2,1)}, u32[]{:S(2)}, u32[]{:S(2)}) collective-permute-start(bf16[1,64,4096]{2,1,0:T(8,128)(2,1)S(1)} %get-tuple-element.189), channel_id=1, source_target_pairs={{0,8},{4,12},{8,0},{12,4},{16,24},{20,28},{24,16},{28,20},{1,9},{5... | collective-permute-start | bytes 1572872 | tf_op jit(solution)/shard_map/ppermute | solution.py:52
  67.5 36.3 %all-to-all-start = ((bf16[4,160,1024]{2,1,0:T(8,128)(2,1)}), bf16[4,160,1024]{2,1,0:T(8,128)(2,1)S(1)}, u32[]{:S(2)}, u32[]{:S(2)}) async-start(bf16[4,160,1024]{2,1,0:T(8,128)(2,1)} %bitcast.15), calls=%async_computation | async-start | bytes 2621440 | tf_op jit(solution)/shard_map/all_to_all | solution.py:92
  74.9 116.8 %all-gather.2.cloned.1.call-start = ((), (), s32[]{:S(2)}) async-start(), calls=%async_computation.9 | async-start | bytes 12976128 | tf_op jit(solution)/shard_map/all_gather | solution.py:647
  76.0 22.2 %collective-permute-start.10 = (bf16[2,64,4096]{2,1,0:T(8,128)(2,1)S(1)}, bf16[2,64,4096]{2,1,0:T(8,128)(2,1)S(1)}, u32[]{:S(2)}, u32[]{:S(2)}) collective-permute-start(bf16[2,64,4096]{2,1,0:T(8,128)(2,1)S(1)} %pad_maximum_fusion.6), channel_id=1, source_target_pairs={{0,8},{4,12},{8,0},{12,4},{16,24},{20,28},{24,16},{28,20},{1,9},{5... | collective-permute-start | bytes 3145736 | tf_op jit(solution)/shard_map/ppermute | solution.py:52
  77.8 21.9 %collective-permute-start.8 = (bf16[2,64,4096]{2,1,0:T(8,128)(2,1)S(1)}, bf16[2,64,4096]{2,1,0:T(8,128)(2,1)S(1)}, u32[]{:S(2)}, u32[]{:S(2)}) collective-permute-start(bf16[2,64,4096]{2,1,0:T(8,128)(2,1)S(1)} %pad_maximum_fusion.5), channel_id=1, source_target_pairs={{0,16},{4,20},{8,24},{12,28},{16,0},{20,4},{24,8},{28,12},{1,17},{... | collective-permute-start | bytes 3145736 | tf_op jit(solution)/shard_map/ppermute | solution.py:52
  104.9 6.7 %copy-start.30 = (bf16[1024,4]{0,1:T(4,128)(2,1)S(1)}, bf16[1024,4]{0,1:T(4,128)(2,1)}, u32[]{:S(2)}) copy-start(bf16[1024,4]{0,1:T(4,128)(2,1)} %param.23) | copy-start | bytes 24580
  104.9 7.6 %copy-start.6 = (bf16[2,256,1024]{2,1,0:T(8,128)(2,1)S(1)}, bf16[2,256,1024]{2,1,0:T(8,128)(2,1)}, u32[]{:S(2)}) copy-start(bf16[2,256,1024]{2,1,0:T(8,128)(2,1)} %param.13) | copy-start | bytes 3145732
  104.9 8.7 %collective-permute-start.12 = (bf16[4,64,4096]{2,1,0:T(8,128)(2,1)}, bf16[4,64,4096]{2,1,0:T(8,128)(2,1)}, u32[]{:S(2)}, u32[]{:S(2)}) collective-permute-start(bf16[4,64,4096]{2,1,0:T(8,128)(2,1)} %constant_dynamic-update-slice_fusion.4.refs_2_), channel_id=1, source_target_pairs={{0,4},{4,0},{8,12},{12,8},{16,20},{20,16},{24,28},{28,24},{1,5},{5... | collective-permute-start | bytes 6291464 | tf_op jit(solution)/shard_map/ppermute | solution.py:52
  105.0 8.6 %collective-permute-start.11 = (bf16[4,64,4096]{2,1,0:T(8,128)(2,1)}, bf16[4,64,4096]{2,1,0:T(8,128)(2,1)}, u32[]{:S(2)}, u32[]{:S(2)}) collective-permute-start(bf16[4,64,4096]{2,1,0:T(8,128)(2,1)} %constant_dynamic-update-slice_fusion.2.refs_1_), channel_id=1, source_target_pairs={{0,4},{4,0},{8,12},{12,8},{16,20},{20,16},{24,28},{28,24},{1,5},{5... | collective-permute-start | bytes 6291464 | tf_op jit(solution)/shard_map/ppermute | solution.py:52
  105.5 35.7 %all-to-all-start.1 = ((bf16[4,160,1024]{2,1,0:T(8,128)(2,1)}), bf16[4,160,1024]{2,1,0:T(8,128)(2,1)S(1)}, u32[]{:S(2)}, u32[]{:S(2)}) async-start(bf16[4,160,1024]{2,1,0:T(8,128)(2,1)} %bitcast.223), calls=%async_computation.1 | async-start | bytes 2621440 | tf_op jit(solution)/shard_map/all_to_all | solution.py:92
  142.2 35.1 %all-to-all-start.2 = ((bf16[4,160,1024]{2,1,0:T(8,128)(2,1)}), bf16[4,160,1024]{2,1,0:T(8,128)(2,1)S(1)}, u32[]{:S(2)}, u32[]{:S(2)}) async-start(bf16[4,160,1024]{2,1,0:T(8,128)(2,1)} %bitcast.233), calls=%async_computation.2 | async-start | bytes 2621440 | tf_op jit(solution)/shard_map/all_to_all | solution.py:92
  177.3 14.4 %copy-start.4 = (bf16[4,160,1024]{2,1,0:T(8,128)(2,1)}, bf16[4,160,1024]{2,1,0:T(8,128)(2,1)S(1)}, u32[]{:S(2)}) copy-start(bf16[4,160,1024]{2,1,0:T(8,128)(2,1)S(1)} %all-to-all-done.2) | copy-start | bytes 3932164
  177.3 48.2 %all-to-all-start.3 = ((bf16[4,160,1024]{2,1,0:T(8,128)(2,1)}), bf16[4,160,1024]{2,1,0:T(8,128)(2,1)S(1)}, u32[]{:S(2)}, u32[]{:S(2)}) async-start(bf16[4,160,1024]{2,1,0:T(8,128)(2,1)} %bitcast.232), calls=%async_computation.3 | async-start | bytes 2621440 | tf_op jit(solution)/shard_map/all_to_all | solution.py:92
  180.8 3.6 collective-permute-start.13
  180.9 5.6 %collective-permute-start.14 = (bf16[4,176,1024]{2,1,0:T(8,128)(2,1)}, bf16[4,176,1024]{2,1,0:T(8,128)(2,1)}, u32[]{:S(2)}, u32[]{:S(2)}) collective-permute-start(bf16[4,176,1024]{2,1,0:T(8,128)(2,1)} %pad_maximum_fusion.4.refs_1_), channel_id=1, source_target_pairs={{0,4},{4,0},{8,12},{12,8},{16,20},{20,16},{24,28},{28,24},{1,5},{5... | collective-permute-start | bytes 4325384 | tf_op jit(solution)/shard_map/ppermute | solution.py:52
  225.5 40.4 %all-to-all-start.5 = ((bf16[4,160,1152]{2,1,0:T(8,128)(2,1)}), bf16[4,160,1152]{2,1,0:T(8,128)(2,1)}, u32[]{:S(2)}, u32[]{:S(2)}) async-start(bf16[4,160,1152]{2,1,0:T(8,128)(2,1)} %bitcast.228), calls=%async_computation.5 | async-start | bytes 2949120 | tf_op jit(solution)/shard_map/all_to_all | solution.py:92
  265.9 46.4 %all-to-all-start.6 = ((bf16[4,160,1152]{2,1,0:T(8,128)(2,1)}), bf16[4,160,1152]{2,1,0:T(8,128)(2,1)S(1)}, u32[]{:S(2)}, u32[]{:S(2)}) async-start(bf16[4,160,1152]{2,1,0:T(8,128)(2,1)} %bitcast.227), calls=%async_computation.6 | async-start | bytes 2949120 | tf_op jit(solution)/shard_map/all_to_all | solution.py:92
  269.7 220.1 %reduce-scatter.2.cloned.1.call-start = ((), (), s32[]{:S(2)}) async-start(), calls=%async_computation.10 | async-start | bytes 19464192 | tf_op jit(solution)/shard_map/reduce_scatter | solution.py:721
  312.3 13.4 %copy-start.10 = (bf16[4,160,1152]{2,1,0:T(8,128)(2,1)}, bf16[4,160,1152]{2,1,0:T(8,128)(2,1)S(1)}, u32[]{:S(2)}) copy-start(bf16[4,160,1152]{2,1,0:T(8,128)(2,1)S(1)} %all-to-all-done.6) | copy-start | bytes 4423684
  326.5 13.9 %copy-start.40 = (bf16[256,1024]{1,0:T(8,128)(2,1)S(1)}, bf16[256,1024]{1,0:T(8,128)(2,1)}, u32[]{:S(2)}) copy-start(bf16[256,1024]{1,0:T(8,128)(2,1)} %get-tuple-element.106) | copy-start | bytes 1572868
  326.5 13.9 %copy-start.42 = (bf16[256,1024]{1,0:T(8,128)(2,1)S(1)}, bf16[256,1024]{1,0:T(8,128)(2,1)}, u32[]{:S(2)}) copy-start(bf16[256,1024]{1,0:T(8,128)(2,1)} %get-tuple-element.107) | copy-start | bytes 1572868
  326.5 13.9 %copy-start.43 = (bf16[256,1024]{1,0:T(8,128)(2,1)S(1)}, bf16[256,1024]{1,0:T(8,128)(2,1)}, u32[]{:S(2)}) copy-start(bf16[256,1024]{1,0:T(8,128)(2,1)} %get-tuple-element.94) | copy-start | bytes 1572868
  352.9 18.5 %collective-permute-start.15 = (bf16[4,128,4096]{2,1,0:T(8,128)(2,1)}, bf16[4,128,4096]{2,1,0:T(8,128)(2,1)}, u32[]{:S(2)}, u32[]{:S(2)}) collective-permute-start(bf16[4,128,4096]{2,1,0:T(8,128)(2,1)} %fusion.7), channel_id=1, source_target_pairs={{0,4},{4,0},{8,12},{12,8},{16,20},{20,16},{24,28},{28,24},{1,5},{5... | collective-permute-start | bytes 12582920 | tf_op jit(solution)/shard_map/ppermute | solution.py:52
  359.6 11.7 %slice-start.2 = ((s8[6291456]{0:T(1024)(128)(4,1)}), s8[2097152]{0:T(1024)(128)(4,1)S(1)}, s32[]{:S(2)}) async-start(s8[6291456]{0:T(1024)(128)(4,1)} %bitcast.200), calls=%async_computation.13 | async-start | bytes 4194304
  359.6 92.8 %all-to-all-start.4 = ((bf16[4,2,160,1024]{3,2,1,0:T(8,128)(2,1)}), bf16[4,2,160,1024]{3,2,1,0:T(8,128)(2,1)}, u32[]{:S(2)}, u32[]{:S(2)}) async-start(bf16[4,2,160,1024]{3,2,1,0:T(8,128)(2,1)} %pad_maximum_fusion.1), calls=%async_computation.4 | async-start | bytes 5242880 | tf_op jit(solution)/shard_map/all_to_all | solution.py:92
  379.7 10.6 %slice-start = ((s8[8388608]{0:T(1024)(128)(4,1)}), s8[4194304]{0:T(1024)(128)(4,1)S(1)}, s32[]{:S(2)}) async-start(s8[8388608]{0:T(1024)(128)(4,1)} %bitcast.197), calls=%async_computation.11 | async-start | bytes 8388608
  382.7 48.3 %collective-permute-start.16 = (bf16[2,1,64,4096]{3,2,1,0:T(8,128)(2,1)S(1)}, bf16[2,1,64,4096]{3,2,1,0:T(8,128)(2,1)S(1)}, u32[]{:S(2)}, u32[]{:S(2)}) collective-permute-start(bf16[2,1,64,4096]{3,2,1,0:T(8,128)(2,1)S(1)} %dynamic-slice_bitcast_fusion.1), channel_id=1, source_target_pairs={{0,8},{4,12},{8,0},{12,4},{16,24},{20,28},{24,16},{28,20},{1,9},{5... | collective-permute-start | bytes 3145736 | tf_op jit(solution)/shard_map/ppermute | solution.py:52
  383.6 6.8 %slice-start.1 = ((s8[8388608]{0:T(1024)(128)(4,1)}), s8[4194304]{0:T(1024)(128)(4,1)S(1)}, s32[]{:S(2)}) async-start(s8[8388608]{0:T(1024)(128)(4,1)} %bitcast.197), calls=%async_computation.12 | async-start | bytes 8388608
  383.6 6.8 %copy-start.26 = (f32[1024]{0:T(1024)S(1)}, f32[1024]{0:T(1024)}, u32[]{:S(2)}) copy-start(f32[1024]{0:T(1024)} %param.18) | copy-start | bytes 12292
  383.6 6.8 %copy-start.36 = (bf16[256,3072]{1,0:T(8,128)(2,1)S(1)}, bf16[256,3072]{1,0:T(8,128)(2,1)}, u32[]{:S(2)}) copy-start(bf16[256,3072]{1,0:T(8,128)(2,1)} %get-tuple-element.110) | copy-start | bytes 4718596
  383.6 49.2 %collective-permute-start.18 = (bf16[1,2,64,4096]{3,2,1,0:T(8,128)(2,1)S(1)}, bf16[1,2,64,4096]{3,2,1,0:T(8,128)(2,1)S(1)}, u32[]{:S(2)}, u32[]{:S(2)}) collective-permute-start(bf16[1,2,64,4096]{3,2,1,0:T(8,128)(2,1)S(1)} %dynamic-slice_bitcast_fusion), channel_id=1, source_target_pairs={{0,16},{4,20},{8,24},{12,28},{16,0},{20,4},{24,8},{28,12},{1,17},{... | collective-permute-start | bytes 3145736 | tf_op jit(solution)/shard_map/ppermute | solution.py:52
  431.3 16.8 %collective-permute-start.17 = (bf16[1,1,64,4096]{3,2,1,0:T(8,128)(2,1)S(1)}, bf16[1,1,64,4096]{3,2,1,0:T(8,128)(2,1)S(1)}, u32[]{:S(2)}, u32[]{:S(2)}) collective-permute-start(bf16[1,1,64,4096]{3,2,1,0:T(8,128)(2,1)S(1)} %constant_dynamic-slice_fusion.1), channel_id=1, source_target_pairs={{0,16},{4,20},{8,24},{12,28},{16,0},{20,4},{24,8},{28,12},{1,17},{... | collective-permute-start | bytes 1572872 | tf_op jit(solution)/shard_map/ppermute | solution.py:52
  433.1 18.2 %collective-permute-start.19 = (bf16[1,1,64,4096]{3,2,1,0:T(8,128)(2,1)S(1)}, bf16[1,1,64,4096]{3,2,1,0:T(8,128)(2,1)S(1)}, u32[]{:S(2)}, u32[]{:S(2)}) collective-permute-start(bf16[1,1,64,4096]{3,2,1,0:T(8,128)(2,1)S(1)} %constant_dynamic-slice_fusion), channel_id=1, source_target_pairs={{0,8},{4,12},{8,0},{12,4},{16,24},{20,28},{24,16},{28,20},{1,9},{5... | collective-permute-start | bytes 1572872 | tf_op jit(solution)/shard_map/ppermute | solution.py:52
  452.4 8.2 %collective-permute-start.20 = (f32[52,128]{1,0:T(8,128)S(1)}, f32[52,128]{1,0:T(8,128)S(1)}, u32[]{:S(2)}, u32[]{:S(2)}) collective-permute-start(f32[52,128]{1,0:T(8,128)S(1)} %maximum_bitcast_fusion), channel_id=1, source_target_pairs={{0,4},{4,0},{8,12},{12,8},{16,20},{20,16},{24,28},{28,24},{1,5},{5... | collective-permute-start | bytes 79880 | tf_op jit(solution)/shard_map/ppermute | solution.py:52
  452.4 35.7 %all-to-all-start.7 = ((bf16[4,32,4096]{2,1,0:T(8,128)(2,1)}), bf16[4,32,4096]{2,1,0:T(8,128)(2,1)S(1)}, u32[]{:S(2)}, u32[]{:S(2)}) async-start(bf16[4,32,4096]{2,1,0:T(8,128)(2,1)} %bitcast.83), calls=%async_computation.7 | async-start | bytes 2097152 | tf_op jit(solution)/shard_map/all_to_all | solution.py:92
  460.7 4.6 collective-permute-start.21
  465.3 3.9 collective-permute-start.22
  469.2 6.9 %collective-permute-start.23 = (f32[52,128]{1,0:T(8,128)S(1)}, f32[52,128]{1,0:T(8,128)S(1)}, u32[]{:S(2)}, u32[]{:S(2)}) collective-permute-start(f32[52,128]{1,0:T(8,128)S(1)} %add.272), channel_id=1, source_target_pairs={{0,1},{1,0},{2,3},{3,2},{4,5},{5,4},{6,7},{7,6},{8,9},{9,8},{10,11... | collective-permute-start | bytes 79880 | tf_op jit(solution)/shard_map/ppermute | solution.py:52
  476.1 9.3 %collective-permute-start.24 = (f32[52,128]{1,0:T(8,128)S(1)}, f32[52,128]{1,0:T(8,128)S(1)}, u32[]{:S(2)}, u32[]{:S(2)}) collective-permute-start(f32[52,128]{1,0:T(8,128)S(1)} %add.273), channel_id=1, source_target_pairs={{0,2},{1,3},{2,0},{3,1},{4,6},{5,7},{6,4},{7,5},{8,10},{9,11},{10,... | collective-permute-start | bytes 79880 | tf_op jit(solution)/shard_map/ppermute | solution.py:52
  (37 other events, 144.1 us)
Sparse Core Ops, SparseCore 0:
  105.0 65.7 all-gather.1
  325.8 145.5 reduce-scatter.1

commit v4 on v3

--- a/solution.py
+++ b/solution.py
@@ -61,22 +61,27 @@
     return (bits, bits[::-1])
 
 
-def gather_dp(block, size, hold):
-    rows = block.shape[0]
-    half = rows // 2
-    columns = []
+def gather_first(block, size, hold):
+    half = block.shape[0] // 2
+    out = []
     for part, order in enumerate(halving_orders(size)):
-        have = block[None, part * half : (part + 1) * half]
-        rels = [0]
-        for bit in order:
-            if len(rels) == 2:
-                have = after(have, hold)
+        have = after(block[None, part * half : (part + 1) * half], hold)
+        out.append(jnp.concatenate([have, flip(have, "dp", size, order[0])], axis=0))
+    return out
+
+
+def gather_dp(first, size, hold):
+    near, rels = [], []
+    for have, order in zip(first, halving_orders(size)):
+        have = after(have, hold)
+        order_rels = [0, order[0]]
+        for bit in order[1:]:
             have = jnp.concatenate([have, flip(have, "dp", size, bit)], axis=0)
-            rels = rels + [rel ^ bit for rel in rels]
-        columns.append((have, rels))
-    near = [columns[0][0], columns[1][0]]
+            order_rels = order_rels + [rel ^ bit for rel in order_rels]
+        near.append(have)
+        rels.append(order_rels)
     far = [flip(have, "dp", size, 1) for have in near]
-    return near + far, [columns[0][1], columns[1][1]]
+    return near + far, rels
 
 
 def gather_expert(block, size):
@@ -99,14 +104,11 @@
     return kept, sent
 
 
-def scatter_core(total, size):
-    me = lax.axis_index("dp")
-    rows, width = total.shape[0] // size, total.shape[1]
-    kept, sent = split_bit(jnp.moveaxis(total.reshape(size // 2, 2, rows, width), 1, 0), me, 1)
-    return kept.astype(F32) + flip(sent, "dp", size, 1).astype(F32)
-
-
-def scatter_dp(summed, size):
+def scatter_core(keep, send, size):
+    return (keep.astype(F32) + flip(send, "dp", size, 1).astype(F32)).astype(BF16)
+
+
+def scatter_dp(summed, size, hold):
     me = lax.axis_index("dp")
     _, rows, width = summed.shape
     half = rows // 2
@@ -119,7 +121,7 @@
             high, low = 1 << (len(left) - 1 - place), 1 << place
             shaped = value.astype(BF16).reshape(high, 2, low, half, width)
             kept, sent = split_bit(jnp.moveaxis(shaped, 1, 0), me, bit)
-            value = kept.astype(F32) + flip(sent, "dp", size, bit).astype(F32)
+            value = kept.astype(F32) + after(flip(sent, "dp", size, bit), hold).astype(F32)
             left.remove(bit)
         outs.append(value.reshape(half, width))
     return jnp.concatenate(outs, axis=0)
@@ -131,13 +133,20 @@
     return jnp.sum(all_to_all(low).astype(F32), axis=0)
 
 
-def sum_all(value, sizes):
-    for axis in ("dp", "expert"):
-        bit = 1
-        while bit < sizes[axis]:
-            value = value + flip(value, axis, sizes[axis], bit)
-            bit *= 2
+def sum_over(value, axis, size):
+    bit = 1
+    while bit < size:
+        value = value + flip(value, axis, size, bit)
+        bit *= 2
     return value
+
+
+def sum_ring(value, axis, size):
+    terms = [shift(value, axis, size, step) if step else value for step in range(size)]
+    while len(terms) > 1:
+        half = len(terms) // 2
+        terms = [terms[k] + terms[k + half] for k in range(half)]
+    return terms[0]
 
 
 def dot(left, right):
@@ -198,7 +207,7 @@
     @pl.when(step == last)
     def _():
         y = y_acc[...].astype(BF16)
-        y_ref[...] = y
+        y_ref[:, 0] = y.reshape(-1, *y_ref.shape[2:])
         width = y.shape[1]
         dx_ref[:, :width] = dx_acc[...].astype(BF16)
         product = go_ref[...].astype(F32) * y.astype(F32)
@@ -216,7 +225,7 @@
     return max(t for t in range(128, most + 1, 128) if size % t == 0)
 
 
-def expert_call(batch, batches, mine, x, go, w_router, w_in, w_out, held):
+def expert_call(batch, batches, experts, mine, x, go, w_router, w_in, w_out, held):
     rows, width = x.shape
     inner = w_out.shape[0]
     tile = tile_of(inner, 256)
@@ -234,8 +243,8 @@
     args = [mine, x, go, w_router, w_in, w_in, w_out]
     aliases = {}
     if held is not None:
-        in_specs += [pl.BlockSpec(memory_space=pl.ANY)] * 3
-        aliases = {len(args): 2, len(args) + 1: 3, len(args) + 2: 4}
+        in_specs += [pl.BlockSpec(memory_space=pl.ANY)] * 4
+        aliases = {len(args): 0, len(args) + 1: 2, len(args) + 2: 3, len(args) + 3: 4}
         args += list(held)
     flops = 12 * rows * width * inner
     return pl.pallas_call(
@@ -243,14 +252,14 @@
         grid=(tiles,),
         in_specs=in_specs,
         out_specs=[
-            whole((rows, width)),
+            pl.BlockSpec((experts, 1, rows // experts, width), lambda j: (0, batch, 0, 0)),
             whole((rows, width + 128)),
             pl.BlockSpec((tile, rows), lambda j: (j, batch)),
             pl.BlockSpec((2, rows, tile), lambda j: (0, batch, j)),
             pl.BlockSpec((rows, width), lambda j: (batch, 0)),
         ],
         out_shape=[
-            jax.ShapeDtypeStruct((rows, width), BF16),
+            jax.ShapeDtypeStruct((experts, batches, rows // experts, width), BF16),
             jax.ShapeDtypeStruct((rows, width + 128), BF16),
             jax.ShapeDtypeStruct((inner, batches * rows), BF16),
             jax.ShapeDtypeStruct((2, batches * rows, inner), BF16),
@@ -264,6 +273,13 @@
     )(*args)
 
 
+def keep_and_send(value, core, keep_ref, send_ref, place):
+    value = value.reshape((-1, 2) + value.shape[1:])
+    even, odd = value[:, 0], value[:, 1]
+    keep_ref[place] = jnp.where(core == 0, even, odd)
+    send_ref[place] = jnp.where(core == 0, odd, even)
+
+
 def weight_in_body(*refs):
     xs, du_ref, out_ref, flipped = refs[:-3], refs[-3], refs[-2], refs[-1]
     rows = xs[0].shape[0]
@@ -273,7 +289,11 @@
         for n, x_ref in enumerate(xs):
             flipped[:, n * rows : (n + 1) * rows] = x_ref[...].T
 
-    out_ref[...] = dot(flipped[...], du_ref[0]).astype(BF16).reshape(out_ref.shape)
+    tile = out_ref.shape[2]
+    part = flipped.shape[0] // out_ref.shape[0]
+    for place in range(out_ref.shape[1] // part):
+        value = dot(flipped[...], du_ref[0, :, place * tile : (place + 1) * tile]).astype(BF16)
+        out_ref[:, place * part : (place + 1) * part] = value.reshape(-1, part, tile)
 
 
 def weight_in_call(size, xs, du):
@@ -285,10 +305,10 @@
     space = 2 * tiles * part + (inner // size) * (width // tile)
     return pl.pallas_call(
         weight_in_body,
-        grid=(2 * tiles,),
+        grid=(2,),
         in_specs=[pl.BlockSpec((rows, width), lambda j: (0, 0)) for _ in xs]
-        + [pl.BlockSpec((1, total, tile), lambda j: (j // tiles, 0, j % tiles))],
-        out_specs=pl.BlockSpec((size, part, tile), lambda j: (0, j, 0)),
+        + [pl.BlockSpec((1, total, inner), lambda j: (j, 0, 0))],
+        out_specs=pl.BlockSpec((size, tiles * part, tile), lambda j: (0, j, 0)),
         out_shape=jax.ShapeDtypeStruct((size, space, tile), BF16),
         scratch_shapes=[pltpu.VMEM((width, total), BF16)],
         compiler_params=pltpu.CompilerParams(vmem_limit_bytes=56 << 20),
@@ -323,6 +343,81 @@
         cost_estimate=LIGHT,
         name="weight_out",
     )(gt, dy, joined)
+
+
+def spread_body(count, summed_ref, in_ref, out_ref):
+    part, tile = in_ref.shape[0], summed_ref.shape[1]
+    for place in range(count):
+        piece = summed_ref[place * part : (place + 1) * part]
+        in_ref[:, place * tile : (place + 1) * tile] = piece.astype(F32)
+    base, part = count * part, out_ref.shape[0]
+    for place in range(out_ref.shape[1] // tile):
+        piece = summed_ref[base + place * part : base + (place + 1) * part]
+        out_ref[:, place * tile : (place + 1) * tile] = piece.astype(F32)
+
+
+def spread_call(summed, in_shape, out_shape):
+    return pl.pallas_call(
+        partial(spread_body, in_shape[1] // summed.shape[1]),
+        out_shape=[jax.ShapeDtypeStruct(shape, F32) for shape in (in_shape, out_shape)],
+        compiler_params=pltpu.CompilerParams(vmem_limit_bytes=56 << 20),
+        cost_estimate=LIGHT,
+        name="spread",
+    )(summed)
+
+
+def weight_attn_body(count, core_ref, *refs):
+    n1s, os, dqkvs, dbranches = (refs[k * count : (k + 1) * count] for k in range(4))
+    keep_ref, send_ref, flipped, right = refs[4 * count :]
+    step, last = pl.program_id(0), pl.num_programs(0) - 1
+    length = n1s[0].shape[0]
+    blocks = 2 * keep_ref.shape[0]
+
+    def fill(lefts, rights):
+        for n in range(count):
+            if lefts is not None:
+                flipped[:, n * length : (n + 1) * length] = lefts[n][...].T
+            right[n * length : (n + 1) * length] = rights[n][...]
+
+    @pl.when(step == 0)
+    def _():
+        fill(n1s, dqkvs)
+
+    @pl.when((step > 0) & (step < last))
+    def _():
+        fill(None, dqkvs)
+
+    @pl.when(step == last)
+    def _():
+        fill(os, dbranches)
+
+    value = dot(flipped[...], right[...]).astype(BF16)
+    value = value.reshape(blocks, -1, value.shape[1])
+    keep_and_send(value, core_ref[0], keep_ref, send_ref, slice(None))
+
+
+def weight_attn_call(size, core, n1s, os, dqkvs, dbranches):
+    count = len(n1s)
+    length, width = n1s[0].shape
+    whole = pl.BlockSpec((length, width), lambda j: (0, 0))
+    half = pl.BlockSpec((size // 2, width // size, width), lambda j: (0, 0, j))
+    return pl.pallas_call(
+        partial(weight_attn_body, count),
+        grid=(4,),
+        in_specs=[pl.BlockSpec(memory_space=pltpu.SMEM)]
+        + [whole] * (2 * count)
+        + [pl.BlockSpec((length, width), lambda j: (0, jnp.minimum(j, 2)))] * count
+        + [whole] * count,
+        out_specs=[half, half],
+        out_shape=[jax.ShapeDtypeStruct((size // 2, width // size, 4 * width), BF16)] * 2,
+        scratch_shapes=[
+            pltpu.VMEM((width, count * length), BF16),
+            pltpu.VMEM((count * length, width), BF16),
+        ],
+        compiler_params=pltpu.CompilerParams(vmem_limit_bytes=56 << 20),
+        cost_estimate=LIGHT,
+        name="weight_attn",
+    )(core, *n1s, *os, *dqkvs, *dbranches)
 
 
 def lane_below(shape, limit):
@@ -641,9 +736,11 @@
     bias = jnp.einsum("kqc,ch->hkq", bucket_hot, rel_bias, precision=lax.Precision.HIGHEST)
 
     me_d = lax.axis_index("dp").astype(jnp.int32)[None]
-    out_pieces, rels = gather_dp(w_out[0], dp, ())
+    out_first = gather_first(w_out[0], dp, ())
+    attn_first = gather_first(attn_block, dp, (bias, outgoing, out_first))
+    pieces, rels = gather_dp(attn_first, dp, ())
+    out_pieces, _ = gather_dp(out_first, dp, pieces[:2])
     wout_full = join_call(me_d, out_pieces, rels)
-    pieces, _ = gather_dp(after(attn_block, out_pieces[:2]), dp, (bias, outgoing))
     win_full = lax.all_gather(
         after(w_in[0], pieces[:2], go_slots[0]), "dp", axis=0, tiled=True
     )
@@ -661,7 +758,7 @@
             slot_count,
             weights,
             None if n else rels,
-            tokens[n],
+            after(tokens[n], wout_full) if n else tokens[n],
             gain1,
             bias,
             id_rows,
@@ -681,13 +778,11 @@
         x = saved[n][-1].reshape(slot_count, width)
         go = go_slots[n].reshape(slot_count, width)
         y, dx, *grads = expert_call(
-            n, batches, mine, x, go, router_wide, win_full, wout_full, grads
+            n, batches, experts, mine, x, go, router_wide, win_full, wout_full, grads
         )
+        grads = [y] + grads
         dx_back = all_to_all(dx.reshape(experts, capacity, width + 128))
-        held.append((x, dx_back.reshape(slot_count, width + 128), y))
-    y_back = all_to_all(
-        jnp.stack([h[2].reshape(experts, capacity, width) for h in held], axis=1)
-    )
+        held.append((x, dx_back.reshape(slot_count, width + 128)))
 
     def backward(n, dx_back):
         id_rows, _, qkv, lse, _, h1, probs, _ = saved[n]
@@ -710,45 +805,36 @@
             id_rows.T,
         )
 
-    gt, du, dy = grads
+    core = me_d % 2
+    _, gt, du, dy = grads
     joined = weight_in_call(dp, [h[0] for h in held], after(du, held[0][1]))
-    backs = []
-    for n in range(batches):
-        backs.append(backward(n, after(held[n][1], joined)))
-        if n == 0:
-            joined = weight_out_call(after(gt, held[-1][1], backs[0]), dy, joined)
+    backs = [backward(0, after(held[0][1], joined))]
+    joined = weight_out_call(after(gt, held[1][1], backs[0]), dy, joined)
+    backs.append(backward(1, after(held[1][1], joined)))
+    attn_keep, attn_send = weight_attn_call(
+        dp,
+        core,
+        [v[1] for v in saved],
+        [v[4] for v in saved],
+        [v[2] for v in backs],
+        [v[1] for v in backs],
+    )
+    y_back = all_to_all(after(grads[0], attn_keep))
+    attn_core = scatter_core(attn_keep, attn_send, dp)
+    attn_sum = scatter_dp(attn_core, dp, ())
     space, tile = joined.shape[1:]
     summed = lax.psum_scatter(
         joined.reshape(dp * space, tile), "dp", scatter_dimension=0, tiled=True
     )
-    part_in, part_out = w_in.shape[1], w_out.shape[1]
-    cut = (w_in.shape[2] // tile) * part_in
-    in_total = summed[:cut].reshape(-1, part_in, tile).transpose(1, 0, 2)
-    in_total = in_total.reshape(part_in, -1).astype(F32)
-    out_total = summed[cut:].reshape(-1, part_out, tile).transpose(1, 0, 2)
-    out_total = out_total.reshape(part_out, -1).astype(F32)
+    in_total, out_total = spread_call(summed, w_in.shape[1:], w_out.shape[1:])
 
     outputs, input_grads = [], []
     full_qkv = attn_w[:, : 3 * width]
-    n1_all, o_all, dbranch_all, dqkv_all = (
-        jnp.concatenate(parts, axis=0)
-        for parts in (
-            [v[1] for v in saved],
-            [v[4] for v in saved],
-            [v[1] for v in backs],
-            [v[2] for v in backs],
-        )
-    )
-    qkv_part = t_dot(n1_all, dqkv_all)
-    proj_part = t_dot(o_all, dbranch_all)
-    attn_part = jnp.concatenate([qkv_part, proj_part], axis=1).astype(BF16)
-    attn_core = scatter_core(attn_part, dp)
-    attn_sum = scatter_dp(attn_core, dp)
     router_grad = sum(v[4] for v in backs)[:experts].T
     gain_moe_grad = sum(v[5] for v in backs)[0]
     table_grad = jnp.einsum(
         "nhkq,kqc->ch",
-        after(jnp.stack([v[3] for v in backs]), attn_core),
+        after(jnp.stack([v[3] for v in backs]), attn_keep),
         bucket_hot.astype(BF16),
         preferred_element_type=F32,
     )
@@ -765,7 +851,7 @@
         h0 = tokens[n].astype(F32)
         r1 = rms_scale(h0)
         n1_hat = h0 * r1
-        dn1 = dot_t(after(dqkv, attn_core), full_qkv)
+        dn1 = dot_t(after(dqkv, attn_keep), full_qkv)
         gain_attn_grad = gain_attn_grad + jnp.sum(dn1 * n1_hat, axis=0)
         scaled = dn1 * gain_attn
         input_grad = dh1 + r1 * (
@@ -778,7 +864,8 @@
     small = jnp.concatenate(
         [gain_attn_grad, table_grad.reshape(-1), gain_moe_grad, router_grad.reshape(-1)]
     )
-    small = sum_all(after(small.reshape(-1, 128), attn_sum), sizes).reshape(-1)
+    small = sum_over(small.reshape(-1, 128), "dp", dp)
+    small = sum_ring(after(small, attn_sum), "expert", experts).reshape(-1)
     cuts = (width, width + table_grad.size, 2 * width + table_grad.size)
     return (
         jnp.stack(outputs),

time: 516 us -> 488 us (0.946)
  local copies, waits for them, and re-layouts: 60.1 us -> 43.1 us
  Pallas kernels: 172 us -> 183 us
  waiting for transfers between devices: 134 us -> 124 us
    pallas_call x1 -> x3, Pallas kernels: 27.2 us -> 37.8 us  [the longest x1 22.3 us: weight_in_call(): pl.pallas_call(weight_in_body, grid=(2,), in_specs=[pl.BlockSpec((rows, w...]
    ppermute x22 -> x20, waiting for transfers between devices: 103 us -> 93 us  [flip(): return lax.ppermute(value, axis, [(i, i ^ bit) for i in range(size)])]
    unnamed x105 -> x116, local copies, waits for them, and re-layouts: 17.9 us -> 9.97 us
    ppermute x22 -> x20, starting transfers between devices: 22.8 us -> 15.6 us  [flip(): return lax.ppermute(value, axis, [(i, i ^ bit) for i in range(size)])]
    ppermute x3 -> x6, starting transfers between devices: 6.96 us -> 13.7 us  [shift(): lax.ppermute(value, axis, [(i, (i + step) % size) for i in range(size)])]
    dot_general x4 -> x2, matrix products: 9.45 us -> 3.18 us  [t_dot(): lax.dot_general(left, right, (((0,), (0,)), ((), ())), preferred_element_...]
  transfers between devices with their start and end apart: 35 -> 36, of which waited for: 17 -> 15; matrix products, arithmetic and copies ran while one was open for 19% -> 18% of each run, Pallas kernels for 31% -> 35%
where the time goes in v4:
time: 488 us; the launch traced here: 480 us
  Pallas kernels  183 us (38%)
  waiting for transfers between devices  124 us (25%)
  starting transfers between devices  63.9 us (13%)
  local copies, waits for them, and re-layouts  43.1 us (9%)
  other arithmetic  28.7 us (6%)
  matrix products  21.6 us (4%)
  between operations  15.8 us (3%)
    ppermute x20, waiting for transfers between devices, flip(): return lax.ppermute(value, axis, [(i, i ^ bit) for i in range(size)])  93 us
    pallas_call x2, Pallas kernels, expert_call(): pl.pallas_call(expert_body, grid=(tiles,), in_specs=in_specs, out_specs=[...  67.5 us
    all_to_all x8, starting transfers between devices, all_to_all(): lax.all_to_all(value, 'expert', split_axis=0, concat_axis=0, tiled=True)  34.5 us
    pallas_call x2, Pallas kernels, forward_call(): pl.pallas_call(partial(forward_body, heads, experts, rels), in_specs=in_s...  31.4 us
    pallas_call x2, Pallas kernels, backward_call(): pl.pallas_call(partial(backward_body, heads, experts), grid=(1,), in_spec...  27.4 us
    all_to_all x8, waiting for transfers between devices, all_to_all(): lax.all_to_all(value, 'expert', split_axis=0, concat_axis=0, tiled=True)  27.1 us
    pallas_call x1, Pallas kernels, weight_in_call(): pl.pallas_call(weight_in_body, grid=(2,), in_specs=[pl.BlockSpec((rows, w...  22.3 us
    ppermute x20, starting transfers between devices, flip(): return lax.ppermute(value, axis, [(i, i ^ bit) for i in range(size)])  15.6 us
  transfers between devices with their start and end apart: 36, of which 15 were waited for; matrix products, arithmetic and copies ran while one was open for 18% of the time, Pallas kernels for 35%

profile of v4, /device:TPU:0, one launch (start us, length us, event | category | flops | bytes accessed | tf_op | source)
XLA Modules:
  0.0 479.6 jit_solution(9795526607177917233)
XLA Ops:
  7.2 1.6 constant_dynamic-update-slice_fusion.1
  10.3 3.0 collective-permute-start
  13.3 2.6 collective-permute-start.1
  23.2 2.4 reduce-window.6
  28.4 2.8 fusion
  31.2 4.4 copy.148
  42.9 1.9 pad_maximum_fusion.8
  44.8 1.9 pad_maximum_fusion.9
  47.8 11.2 %collective-permute-done.7 = bf16[1,64,4096]{2,1,0:T(8,128)(2,1)S(1)} collective-permute-done((bf16[1,64,4096]{2,1,0:T(8,128)(2,1)S(1)}, bf16[1,64,4096]{2,1,0:T(8,128)(2,1)S(1)}, u32[]{:S(2)}, u32[]{:S(2)}) %collective-permute-start.7) | collective-permute-done | bytes 524320 | tf_op jit(solution)/shard_map/ppermute | solution.py:52
  59.7 3.5 all-to-all-start
  64.0 17.8 %collective-permute-done.8 = bf16[2,64,4096]{2,1,0:T(8,128)(2,1)} collective-permute-done((bf16[2,64,4096]{2,1,0:T(8,128)(2,1)S(1)}, bf16[2,64,4096]{2,1,0:T(8,128)(2,1)}, u32[]{:S(2)}, u32[]{:S(2)}) %collective-permute-start.8) | collective-permute-done | bytes 1048608 | tf_op jit(solution)/shard_map/ppermute | solution.py:52
  81.9 1.7 pad_maximum_fusion.2.refs_2_
  83.6 2.2 collective-permute-done.6
  87.3 4.9 %all-to-all-done = bf16[4,160,1024]{2,1,0:T(8,128)(2,1)S(1)} async-done(((bf16[4,160,1024]{2,1,0:T(8,128)(2,1)}), bf16[4,160,1024]{2,1,0:T(8,128)(2,1)S(1)}, u32[]{:S(2)}, u32[]{:S(2)}) %all-to-all-start) | async-done | bytes 1310752 | tf_op jit(solution)/shard_map/all_to_all | solution.py:97
  94.0 4.5 all-to-all-start.1
  106.1 16.8 %attention_forward.2 = (bf16[640,1024]{1,0:T(8,128)(2,1)}, bf16[256,1024]{1,0:T(8,128)(2,1)}, bf16[256,3072]{1,0:T(8,128)(2,1)}, f32[16,256]{1,0:T(8,128)}, bf16...) custom-call(s32[1]{0:T(128)} %bitcast.refs_0_.me_ref, ...), custom_call_target="tpu_custom_call" | custom-call | flops 1 | bytes 1 | tf_op jit(solution)/shard_map/attention_forward/pallas_call | solution.py:576
  122.8 7.5 %all-to-all-done.1 = bf16[4,160,1024]{2,1,0:T(8,128)(2,1)} async-done(((bf16[4,160,1024]{2,1,0:T(8,128)(2,1)}), bf16[4,160,1024]{2,1,0:T(8,128)(2,1)}, u32[]{:S(2)}, u32[]{:S(2)}) %all-to-all-start.1) | async-done | bytes 1310752 | tf_op jit(solution)/shard_map/all_to_all | solution.py:97
  130.4 3.8 all-to-all-start.3
  135.1 2.1 constant_dynamic-update-slice_fusion.4.refs_1_
  140.7 3.9 collective-permute-done.13.refs_2_
  144.7 5.2 %join.1.wo_ref = bf16[2816,1024]{1,0:T(8,128)(2,1)} custom-call(s32[1]{0:T(128)} %bitcast.refs_0_.me_ref, bf16[4,176,1024]{2,1,0:T(8,128)(2,1)} %copy-done.19, bf16[4,176,1024]{2,1,0:T(8,128)(2,1)} %constant_dynamic-update-slice_fusion.4.refs_1_, bf16[4,176,1024]{2,1,0:T(8,128)(2,1)} %collective-permute-done.13.refs_2_, ...), custom_call_target="tpu_custom_call" | custom-call | flops 1 | bytes 1 | tf_op jit(solution)/shard_map/join/pallas_call | solution.py:465
  149.9 14.6 %attention_forward.3 = (bf16[640,1024]{1,0:T(8,128)(2,1)}, bf16[256,1024]{1,0:T(8,128)(2,1)}, bf16[256,3072]{1,0:T(8,128)(2,1)}, f32[16,256]{1,0:T(8,128)}, bf16...) custom-call(bf16[1024,4096]{1,0:T(8,128)(2,1)} %get-tuple-element.75.refs_0_.proj_ref, ...), custom_call_target="tpu_custom_call" | custom-call | flops 1 | bytes 1 | tf_op jit(solution)/shard_map/attention_forward/pallas_call | solution.py:576
  165.1 4.5 all-to-all-start.2
  170.2 3.6 all-gather.2.cloned.1.call-done.wg_ref.wu_ref
  173.9 33.8 %expert.2 = (bf16[4,2,160,1024]{3,2,1,0:T(8,128)(2,1)}, bf16[640,1152]{1,0:T(8,128)(2,1)}, bf16[2816,1280]{1,0:T(8,128)(2,1)}, bf16[2,1280,2816]{2,1,0:T(8,128)(2,1)}, bf16[1280,1024]{1,0:T(8,128)(2,1)}) custom-call(s32[2]{0:T(128)} %pad_add_fusion.4.mine, bf16[640,1024]{1,0:T(8,128)(2,1)} %bitcast.177, bf16[640,1024]{1,0:T(8,128)(2,1)} %bitcast.190, ...), custom_call_target="tpu_custom_call" | custom-call | flops 1 | bytes 1 | tf_op jit(solution)/shard_map/expert/pallas_call | solution.py:250
  207.7 5.0 %all-to-all-start.4 = ((bf16[4,160,1152]{2,1,0:T(8,128)(2,1)}), bf16[4,160,1152]{2,1,0:T(8,128)(2,1)}, u32[]{:S(2)}, u32[]{:S(2)}) async-start(bf16[4,160,1152]{2,1,0:T(8,128)(2,1)} %bitcast.200), calls=%async_computation.4 | async-start | bytes 2949120 | tf_op jit(solution)/shard_map/all_to_all | solution.py:97
  212.7 33.8 %expert.3 = (bf16[4,2,160,1024]{3,2,1,0:T(8,128)(2,1)}, bf16[640,1152]{1,0:T(8,128)(2,1)}, bf16[2816,1280]{1,0:T(8,128)(2,1)}, bf16[2,1280,2816]{2,1,0:T(8,128)(2,1)}, bf16[1280,1024]{1,0:T(8,128)(2,1)}) custom-call(s32[2]{0:T(128)} %pad_add_fusion.4.mine, ...), custom_call_target="tpu_custom_call", output_to_operand_aliasing={{0}: (7, {}), {2}: (8, {}), {3}: (9, {}), {4}: (10, {})} | custom-call | flops 1 | bytes 1 | tf_op jit(solution)/shard_map/expert/pallas_call | solution.py:250
  248.0 3.7 all-to-all-start.5
  253.6 22.3 %weight_in.1._ = bf16[8,4224,256]{2,1,0:T(8,128)(2,1)} custom-call(bf16[640,1024]{1,0:T(8,128)(2,1)} %bitcast.178, bf16[640,1024]{1,0:T(8,128)(2,1)} %bitcast.184, bf16[2,1280,2816]{2,1,0:T(8,128)(2,1)} %get-tuple-element.97.refs_2_), custom_call_target="tpu_custom_call" | custom-call | flops 1 | bytes 1 | tf_op jit(solution)/shard_map/weight_in/pallas_call | solution.py:306
  275.9 13.6 %attention_backward.2 = (f32[256,1024]{1,0:T(8,128)}, bf16[256,1024]{1,0:T(8,128)(2,1)}, bf16[256,3072]{1,0:T(8,128)(2,1)}, bf16[16,256,256]{2,1,0:T(8,128)(2,1)...) custom-call(bf16[640,1152]{1,0:T(8,128)(2,1)} %bitcast.43.dx_ref, s32[256,2]{1,0:T(8,128)} %get-tuple-element.201.targets_ref, ...), custom_call_target="tpu_custom_call" | custom-call | flops 1 | bytes 1 | tf_op jit(solution)/shard_map/attention_backward/pallas_call | solution.py:681
  289.5 13.4 %weight_out.1 = bf16[8,4224,256]{2,1,0:T(8,128)(2,1)} custom-call(bf16[2816,1280]{1,0:T(8,128)(2,1)} %get-tuple-element.109.gt_ref, bf16[1280,1024]{1,0:T(8,128)(2,1)} %get-tuple-element.110.dy_ref, bf16[8,4224,256]{2,1,0:T(8,128)(2,1)} %weight_in.1._), custom_call_target="tpu_custom_call", output_to_operand_aliasing={{}: (2, {})} | custom-call | flops 1 | bytes 1 | tf_op jit(solution)/shard_map/weight_out/pallas_call | solution.py:331
  303.7 13.9 %attention_backward.3 = (f32[256,1024]{1,0:T(8,128)}, bf16[256,1024]{1,0:T(8,128)(2,1)}, bf16[256,3072]{1,0:T(8,128)(2,1)}, bf16[16,256,256]{2,1,0:T(8,128)(2,1)...) custom-call(bf16[640,1152]{1,0:T(8,128)(2,1)} %bitcast.189, s32[256,2]{1,0:T(8,128)} %get-tuple-element.198.targets_ref, ...), custom_call_target="tpu_custom_call" | custom-call | flops 1 | bytes 1 | tf_op jit(solution)/shard_map/attention_backward/pallas_call | solution.py:681
  317.6 11.6 %weight_attn.1 = (bf16[4,128,4096]{2,1,0:T(8,128)(2,1)}, bf16[4,128,4096]{2,1,0:T(8,128)(2,1)}) custom-call(s32[1]{0:T(128)S(6)} %select_n.107.core_ref, bf16[256,1024]{1,0:T(8,128)(2,1)} %get-tuple-element.91.refs_0_, bf16[256,1024]{1,0:T(8,128)(2,1)} %get-tuple-element.92.refs_1_, bf16[256,1024]{1,0:T(8,128)(2,1)} %get-tuple-element.93.refs_2_, ...), custom_call_target="tpu_custom_call" | custom-call | flops 1 | bytes 1 | tf_op jit(solution)/shard_map/weight_attn/pallas_call | solution.py:404
  331.9 2.7 pad_maximum_fusion
  338.3 4.7 fusion.1
  343.1 7.1 %fusion.33 = (f32[1024]{0:T(1024)S(1)}, f32[256]{0:T(256)S(1)}, f32[256]{0:T(256)S(1)}, f32[1024]{0:T(1024)S(1)}, f32[256,1024]{1,0:T(8,128)}) fusion(f32[256]{0:T(256)S(1)} %get-tuple-element.224, bf16[2,256,1024]{2,1,0:T(8,128)(2,1)S(1)} %copy-done.5, f32[1024]{0:T(1024)S(1)} %copy-done.40, f32[256]{0:T(256)S(1)} %get-tuple-element.223, ...), kind=kOutput, calls=%fused_computation.56 | convolution fusion | flops 1614280192 | bytes 11026432 | tf_op jit(solution)/shard_map/dot_general | solution.py:157
  350.7 3.7 add_convert_fusion
  359.8 5.2 %all-to-all-start.6 = ((bf16[4,2,160,1024]{3,2,1,0:T(8,128)(2,1)}), bf16[4,2,160,1024]{3,2,1,0:T(8,128)(2,1)S(1)}, u32[]{:S(2)}, u32[]{:S(2)}) async-start(bf16[4,2,160,1024]{3,2,1,0:T(8,128)(2,1)} %get-tuple-element.119), calls=%async_computation.6 | async-start | bytes 5242880 | tf_op jit(solution)/shard_map/all_to_all | solution.py:97
  368.2 39.0 %collective-permute-done.16 = bf16[2,1,64,4096]{3,2,1,0:T(8,128)(2,1)} collective-permute-done((bf16[2,1,64,4096]{3,2,1,0:T(8,128)(2,1)}, bf16[2,1,64,4096]{3,2,1,0:T(8,128)(2,1)}, u32[]{:S(2)}, u32[]{:S(2)}) %collective-permute-start.16) | collective-permute-done | bytes 1048608 | tf_op jit(solution)/shard_map/ppermute | solution.py:52
  409.9 5.6 %collective-permute-done.18 = bf16[1,2,64,4096]{3,2,1,0:T(8,128)(2,1)S(1)} collective-permute-done((bf16[1,2,64,4096]{3,2,1,0:T(8,128)(2,1)S(1)}, bf16[1,2,64,4096]{3,2,1,0:T(8,128)(2,1)S(1)}, u32[]{:S(2)}, u32[]{:S(2)}) %collective-permute-start.18) | collective-permute-done | bytes 1048608 | tf_op jit(solution)/shard_map/ppermute | solution.py:52
  415.8 1.7 collective-permute-start.19
  419.9 10.0 %collective-permute-done.22 = f32[52,128]{1,0:T(8,128)S(1)} collective-permute-done((f32[52,128]{1,0:T(8,128)S(1)}, f32[52,128]{1,0:T(8,128)S(1)}, u32[]{:S(2)}, u32[]{:S(2)}) %collective-permute-start.22) | collective-permute-done | bytes 26656 | tf_op jit(solution)/shard_map/ppermute | solution.py:52
  429.9 2.8 collective-permute-done.19
  434.0 3.0 collective-permute-start.23
  438.4 2.4 collective-permute-start.25
  440.8 4.3 all-to-all-start.7
  453.0 12.5 %all-to-all-done.7 = bf16[4,32,4096]{2,1,0:T(8,128)(2,1)} async-done(((bf16[4,32,4096]{2,1,0:T(8,128)(2,1)}), bf16[4,32,4096]{2,1,0:T(8,128)(2,1)}, u32[]{:S(2)}, u32[]{:S(2)}) %all-to-all-start.7) | async-done | bytes 1048608 | tf_op jit(solution)/shard_map/all_to_all | solution.py:97
  468.4 3.8 spread.1
  (262 shorter events, 75.6 us)
Async XLA Ops:
  7.2 21.2 %copy-start = (f32[32,16]{0,1:T(8,128)S(1)}, f32[32,16]{0,1:T(8,128)}, u32[]{:S(2)}) copy-start(f32[32,16]{0,1:T(8,128)} %param.21) | copy-start | bytes 6148
  10.3 29.6 %collective-permute-start = (bf16[32,4096]{1,0:T(8,128)(2,1)}, bf16[32,4096]{1,0:T(8,128)(2,1)}, u32[]{:S(2)}, u32[]{:S(2)}) collective-permute-start(bf16[32,4096]{1,0:T(8,128)(2,1)} %constant_dynamic-update-slice_fusion), channel_id=1, source_target_pairs={{0,1},{1,2},{2,3},{3,0},{4,5},{5,6},{6,7},{7,4},{8,9},{9,10},{10,1... | collective-permute-start | bytes 786440 | tf_op jit(solution)/shard_map/ppermute | solution.py:56
  13.3 27.5 %collective-permute-start.1 = (bf16[32,4096]{1,0:T(8,128)(2,1)}, bf16[32,4096]{1,0:T(8,128)(2,1)}, u32[]{:S(2)}, u32[]{:S(2)}) collective-permute-start(bf16[32,4096]{1,0:T(8,128)(2,1)} %constant_dynamic-update-slice_fusion), channel_id=1, source_target_pairs={{0,2},{1,3},{2,0},{3,1},{4,6},{5,7},{6,4},{7,5},{8,10},{9,11},{10,... | collective-permute-start | bytes 786440 | tf_op jit(solution)/shard_map/ppermute | solution.py:56
  15.9 25.9 %collective-permute-start.2 = (bf16[32,4096]{1,0:T(8,128)(2,1)}, bf16[32,4096]{1,0:T(8,128)(2,1)}, u32[]{:S(2)}, u32[]{:S(2)}) collective-permute-start(bf16[32,4096]{1,0:T(8,128)(2,1)} %constant_dynamic-update-slice_fusion), channel_id=1, source_target_pairs={{0,3},{1,0},{2,1},{3,2},{4,7},{5,4},{6,5},{7,6},{8,11},{9,8},{10,9... | collective-permute-start | bytes 786440 | tf_op jit(solution)/shard_map/ppermute | solution.py:56
  18.4 24.5 %collective-permute-start.3 = (bf16[1,176,1024]{2,1,0:T(8,128)(2,1)S(1)}, bf16[1,176,1024]{2,1,0:T(8,128)(2,1)}, u32[]{:S(2)}, u32[]{:S(2)}) collective-permute-start(bf16[1,176,1024]{2,1,0:T(8,128)(2,1)S(1)} %get-tuple-element.195), channel_id=1, source_target_pairs={{0,8},{4,12},{8,0},{12,4},{16,24},{20,28},{24,16},{28,20},{1,9},{5... | collective-permute-start | bytes 1081352 | tf_op jit(solution)/shard_map/ppermute | solution.py:52
  19.9 24.9 %collective-permute-start.4 = (bf16[1,176,1024]{2,1,0:T(8,128)(2,1)S(1)}, bf16[1,176,1024]{2,1,0:T(8,128)(2,1)}, u32[]{:S(2)}, u32[]{:S(2)}) collective-permute-start(bf16[1,176,1024]{2,1,0:T(8,128)(2,1)S(1)} %get-tuple-element.194), channel_id=1, source_target_pairs={{0,16},{4,20},{8,24},{12,28},{16,0},{20,4},{24,8},{28,12},{1,17},{... | collective-permute-start | bytes 1081352 | tf_op jit(solution)/shard_map/ppermute | solution.py:52
  46.8 12.3 %collective-permute-start.7 = (bf16[1,64,4096]{2,1,0:T(8,128)(2,1)S(1)}, bf16[1,64,4096]{2,1,0:T(8,128)(2,1)S(1)}, u32[]{:S(2)}, u32[]{:S(2)}) collective-permute-start(bf16[1,64,4096]{2,1,0:T(8,128)(2,1)S(1)} %bitcast.197), channel_id=1, source_target_pairs={{0,16},{4,20},{8,24},{12,28},{16,0},{20,4},{24,8},{28,12},{1,17},{... | collective-permute-start | bytes 1572872 | tf_op jit(solution)/shard_map/ppermute | solution.py:52
  47.3 16.1 %collective-permute-start.5 = (bf16[1,64,4096]{2,1,0:T(8,128)(2,1)S(1)}, bf16[1,64,4096]{2,1,0:T(8,128)(2,1)S(1)}, u32[]{:S(2)}, u32[]{:S(2)}) collective-permute-start(bf16[1,64,4096]{2,1,0:T(8,128)(2,1)S(1)} %bitcast.195), channel_id=1, source_target_pairs={{0,8},{4,12},{8,0},{12,4},{16,24},{20,28},{24,16},{28,20},{1,9},{5... | collective-permute-start | bytes 1572872 | tf_op jit(solution)/shard_map/ppermute | solution.py:52
  59.1 22.7 %collective-permute-start.8 = (bf16[2,64,4096]{2,1,0:T(8,128)(2,1)S(1)}, bf16[2,64,4096]{2,1,0:T(8,128)(2,1)}, u32[]{:S(2)}, u32[]{:S(2)}) collective-permute-start(bf16[2,64,4096]{2,1,0:T(8,128)(2,1)S(1)} %pad_maximum_fusion.5), channel_id=1, source_target_pairs={{0,8},{4,12},{8,0},{12,4},{16,24},{20,28},{24,16},{28,20},{1,9},{5... | collective-permute-start | bytes 3145736 | tf_op jit(solution)/shard_map/ppermute | solution.py:52
  59.7 32.5 %all-to-all-start = ((bf16[4,160,1024]{2,1,0:T(8,128)(2,1)}), bf16[4,160,1024]{2,1,0:T(8,128)(2,1)S(1)}, u32[]{:S(2)}, u32[]{:S(2)}) async-start(bf16[4,160,1024]{2,1,0:T(8,128)(2,1)} %bitcast.14), calls=%async_computation | async-start | bytes 2621440 | tf_op jit(solution)/shard_map/all_to_all | solution.py:97
  63.3 110.6 %all-gather.2.cloned.1.call-start = ((), (), s32[]{:S(2)}) async-start(), calls=%async_computation.9 | async-start | bytes 12976128 | tf_op jit(solution)/shard_map/all_gather | solution.py:744
  63.5 22.4 %collective-permute-start.6 = (bf16[2,64,4096]{2,1,0:T(8,128)(2,1)S(1)}, bf16[2,64,4096]{2,1,0:T(8,128)(2,1)S(1)}, u32[]{:S(2)}, u32[]{:S(2)}) collective-permute-start(bf16[2,64,4096]{2,1,0:T(8,128)(2,1)S(1)} %pad_maximum_fusion.4), channel_id=1, source_target_pairs={{0,16},{4,20},{8,24},{12,28},{16,0},{20,4},{24,8},{28,12},{1,17},{... | collective-permute-start | bytes 3145736 | tf_op jit(solution)/shard_map/ppermute | solution.py:52
  93.4 12.7 %collective-permute-start.10 = (bf16[4,64,4096]{2,1,0:T(8,128)(2,1)S(1)}, bf16[4,64,4096]{2,1,0:T(8,128)(2,1)}, u32[]{:S(2)}, u32[]{:S(2)}) collective-permute-start(bf16[4,64,4096]{2,1,0:T(8,128)(2,1)S(1)} %pad_maximum_fusion.2.refs_2_), channel_id=1, source_target_pairs={{0,4},{4,0},{8,12},{12,8},{16,20},{20,16},{24,28},{28,24},{1,5},{5... | collective-permute-start | bytes 6291464 | tf_op jit(solution)/shard_map/ppermute | solution.py:52
  93.5 12.6 %collective-permute-start.9 = (bf16[4,64,4096]{2,1,0:T(8,128)(2,1)}, bf16[4,64,4096]{2,1,0:T(8,128)(2,1)}, u32[]{:S(2)}, u32[]{:S(2)}) collective-permute-start(bf16[4,64,4096]{2,1,0:T(8,128)(2,1)} %pad_maximum_fusion.1.refs_1_), channel_id=1, source_target_pairs={{0,4},{4,0},{8,12},{12,8},{16,20},{20,16},{24,28},{28,24},{1,5},{5... | collective-permute-start | bytes 6291464 | tf_op jit(solution)/shard_map/ppermute | solution.py:52
  94.0 36.4 %all-to-all-start.1 = ((bf16[4,160,1024]{2,1,0:T(8,128)(2,1)}), bf16[4,160,1024]{2,1,0:T(8,128)(2,1)}, u32[]{:S(2)}, u32[]{:S(2)}) async-start(bf16[4,160,1024]{2,1,0:T(8,128)(2,1)} %bitcast.191), calls=%async_computation.1 | async-start | bytes 2621440 | tf_op jit(solution)/shard_map/all_to_all | solution.py:97
  99.2 35.9 %collective-permute-start.12 = (bf16[2,176,1024]{2,1,0:T(8,128)(2,1)}, bf16[2,176,1024]{2,1,0:T(8,128)(2,1)}, u32[]{:S(2)}, u32[]{:S(2)}) collective-permute-start(bf16[2,176,1024]{2,1,0:T(8,128)(2,1)} %pad_maximum_fusion.9), channel_id=1, source_target_pairs={{0,8},{4,12},{8,0},{12,4},{16,24},{20,28},{24,16},{28,20},{1,9},{5... | collective-permute-start | bytes 2162696 | tf_op jit(solution)/shard_map/ppermute | solution.py:52
  102.7 34.5 %collective-permute-start.11 = (bf16[2,176,1024]{2,1,0:T(8,128)(2,1)}, bf16[2,176,1024]{2,1,0:T(8,128)(2,1)}, u32[]{:S(2)}, u32[]{:S(2)}) collective-permute-start(bf16[2,176,1024]{2,1,0:T(8,128)(2,1)} %pad_maximum_fusion.8), channel_id=1, source_target_pairs={{0,16},{4,20},{8,24},{12,28},{16,0},{20,4},{24,8},{28,12},{1,17},{... | collective-permute-start | bytes 2162696 | tf_op jit(solution)/shard_map/ppermute | solution.py:52
  122.8 12.2 %copy-start.20 = (bf16[2,176,1024]{2,1,0:T(8,128)(2,1)S(1)}, bf16[2,176,1024]{2,1,0:T(8,128)(2,1)}, u32[]{:S(2)}) copy-start(bf16[2,176,1024]{2,1,0:T(8,128)(2,1)} %pad_maximum_fusion.8) | copy-start | bytes 2162692
  130.4 34.7 %all-to-all-start.3 = ((bf16[4,160,1024]{2,1,0:T(8,128)(2,1)}), bf16[4,160,1024]{2,1,0:T(8,128)(2,1)S(1)}, u32[]{:S(2)}, u32[]{:S(2)}) async-start(bf16[4,160,1024]{2,1,0:T(8,128)(2,1)} %bitcast.202), calls=%async_computation.3 | async-start | bytes 2621440 | tf_op jit(solution)/shard_map/all_to_all | solution.py:97
  137.2 3.6 collective-permute-start.14
  138.4 6.3 %collective-permute-start.13 = (bf16[4,176,1024]{2,1,0:T(8,128)(2,1)S(1)}, bf16[4,176,1024]{2,1,0:T(8,128)(2,1)}, u32[]{:S(2)}, u32[]{:S(2)}) collective-permute-start(bf16[4,176,1024]{2,1,0:T(8,128)(2,1)S(1)} %constant_dynamic-update-slice_fusion.2.refs_0_), channel_id=1, source_target_pairs={{0,4},{4,0},{8,12},{12,8},{16,20},{20,16},{24,28},{28,24},{1,5},{5... | collective-permute-start | bytes 4325384 | tf_op jit(solution)/shard_map/ppermute | solution.py:52
  165.1 42.5 %all-to-all-start.2 = ((bf16[4,160,1024]{2,1,0:T(8,128)(2,1)}), bf16[4,160,1024]{2,1,0:T(8,128)(2,1)S(1)}, u32[]{:S(2)}, u32[]{:S(2)}) async-start(bf16[4,160,1024]{2,1,0:T(8,128)(2,1)} %bitcast.203), calls=%async_computation.2 | async-start | bytes 2621440 | tf_op jit(solution)/shard_map/all_to_all | solution.py:97
  207.7 40.4 %all-to-all-start.4 = ((bf16[4,160,1152]{2,1,0:T(8,128)(2,1)}), bf16[4,160,1152]{2,1,0:T(8,128)(2,1)}, u32[]{:S(2)}, u32[]{:S(2)}) async-start(bf16[4,160,1152]{2,1,0:T(8,128)(2,1)} %bitcast.200), calls=%async_computation.4 | async-start | bytes 2949120 | tf_op jit(solution)/shard_map/all_to_all | solution.py:97
  248.0 41.5 %all-to-all-start.5 = ((bf16[4,160,1152]{2,1,0:T(8,128)(2,1)}), bf16[4,160,1152]{2,1,0:T(8,128)(2,1)S(1)}, u32[]{:S(2)}, u32[]{:S(2)}) async-start(bf16[4,160,1152]{2,1,0:T(8,128)(2,1)} %bitcast.199), calls=%async_computation.5 | async-start | bytes 2949120 | tf_op jit(solution)/shard_map/all_to_all | solution.py:97
  251.7 216.7 %reduce-scatter.2.cloned.1.call-start = ((), (), s32[]{:S(2)}) async-start(), calls=%async_computation.10 | async-start | bytes 19464192 | tf_op jit(solution)/shard_map/reduce_scatter | solution.py:826
  289.5 13.4 %copy-start.11 = (bf16[4,160,1152]{2,1,0:T(8,128)(2,1)}, bf16[4,160,1152]{2,1,0:T(8,128)(2,1)S(1)}, u32[]{:S(2)}) copy-start(bf16[4,160,1152]{2,1,0:T(8,128)(2,1)S(1)} %all-to-all-done.5) | copy-start | bytes 4423684
  317.6 11.8 %copy-start.28 = (s32[1,256,2]{2,1,0:T(8,128)S(1)}, s32[1,256,2]{2,1,0:T(8,128)}, u32[]{:S(2)}) copy-start(s32[1,256,2]{2,1,0:T(8,128)} %copy.138) | copy-start | bytes 6148
  317.6 11.9 %copy-start.29 = (s32[1,256,2]{2,1,0:T(8,128)S(1)}, s32[1,256,2]{2,1,0:T(8,128)}, u32[]{:S(2)}) copy-start(s32[1,256,2]{2,1,0:T(8,128)} %copy.139) | copy-start | bytes 6148
  317.6 12.0 %copy-start.5 = (bf16[2,256,1024]{2,1,0:T(8,128)(2,1)S(1)}, bf16[2,256,1024]{2,1,0:T(8,128)(2,1)}, u32[]{:S(2)}) copy-start(bf16[2,256,1024]{2,1,0:T(8,128)(2,1)} %param.13) | copy-start | bytes 3145732
  317.6 12.3 %copy-start.22 = (pred[2,256,2,640]{3,1,2,0:T(32,128)(4,1)S(1)}, pred[2,256,2,640]{3,1,2,0:T(32,128)(4,1)}, u32[]{:S(2)}) copy-start(pred[2,256,2,640]{3,1,2,0:T(32,128)(4,1)} %get-tuple-element.204) | copy-start | bytes 1966084
  329.3 21.5 %collective-permute-start.15 = (bf16[4,128,4096]{2,1,0:T(8,128)(2,1)}, bf16[4,128,4096]{2,1,0:T(8,128)(2,1)}, u32[]{:S(2)}, u32[]{:S(2)}) collective-permute-start(bf16[4,128,4096]{2,1,0:T(8,128)(2,1)} %get-tuple-element.120), channel_id=1, source_target_pairs={{0,4},{4,0},{8,12},{12,8},{16,20},{20,16},{24,28},{28,24},{1,5},{5... | collective-permute-start | bytes 12582920 | tf_op jit(solution)/shard_map/ppermute | solution.py:52
  329.9 13.2 %copy-start.46 = (f32[256]{0:T(256)}, f32[256]{0:T(256)S(1)}, u32[]{:S(2)}) copy-start(f32[256]{0:T(256)S(1)} %get-tuple-element.223) | copy-start | bytes 3076
  329.9 13.2 %copy-start.48 = (f32[256]{0:T(256)}, f32[256]{0:T(256)S(1)}, u32[]{:S(2)}) copy-start(f32[256]{0:T(256)S(1)} %get-tuple-element.224) | copy-start | bytes 3076
  350.2 14.8 %collective-permute-start.20 = (f32[52,128]{1,0:T(8,128)S(1)}, f32[52,128]{1,0:T(8,128)S(1)}, u32[]{:S(2)}, u32[]{:S(2)}) collective-permute-start(f32[52,128]{1,0:T(8,128)S(1)} %maximum_bitcast_fusion), channel_id=1, source_target_pairs={{0,4},{4,0},{8,12},{12,8},{16,20},{20,16},{24,28},{28,24},{1,5},{5... | collective-permute-start | bytes 79880 | tf_op jit(solution)/shard_map/ppermute | solution.py:52
  358.4 48.7 %collective-permute-start.16 = (bf16[2,1,64,4096]{3,2,1,0:T(8,128)(2,1)}, bf16[2,1,64,4096]{3,2,1,0:T(8,128)(2,1)}, u32[]{:S(2)}, u32[]{:S(2)}) collective-permute-start(bf16[2,1,64,4096]{3,2,1,0:T(8,128)(2,1)} %dynamic-slice_bitcast_fusion.1), channel_id=1, source_target_pairs={{0,8},{4,12},{8,0},{12,4},{16,24},{20,28},{24,16},{28,20},{1,9},{5... | collective-permute-start | bytes 3145736 | tf_op jit(solution)/shard_map/ppermute | solution.py:52
  359.8 81.0 %all-to-all-start.6 = ((bf16[4,2,160,1024]{3,2,1,0:T(8,128)(2,1)}), bf16[4,2,160,1024]{3,2,1,0:T(8,128)(2,1)S(1)}, u32[]{:S(2)}, u32[]{:S(2)}) async-start(bf16[4,2,160,1024]{3,2,1,0:T(8,128)(2,1)} %get-tuple-element.119), calls=%async_computation.6 | async-start | bytes 5242880 | tf_op jit(solution)/shard_map/all_to_all | solution.py:97
  365.0 42.2 %copy-start.10 = (bf16[4,64,4096]{2,1,0:T(8,128)(2,1)S(1)}, bf16[4,64,4096]{2,1,0:T(8,128)(2,1)}, u32[]{:S(2)}) copy-start(bf16[4,64,4096]{2,1,0:T(8,128)(2,1)} %copy-done.9) | copy-start | bytes 6291460
  365.1 53.1 %collective-permute-start.21 = (f32[52,128]{1,0:T(8,128)S(1)}, f32[52,128]{1,0:T(8,128)S(1)}, u32[]{:S(2)}, u32[]{:S(2)}) collective-permute-start(f32[52,128]{1,0:T(8,128)S(1)} %fusion.60), channel_id=1, source_target_pairs={{0,8},{4,12},{8,0},{12,4},{16,24},{20,28},{24,16},{28,20},{1,9},{5... | collective-permute-start | bytes 79880 | tf_op jit(solution)/shard_map/ppermute | solution.py:52
  367.0 48.5 %copy-start.8 = (bf16[4,64,4096]{2,1,0:T(8,128)(2,1)S(1)}, bf16[4,64,4096]{2,1,0:T(8,128)(2,1)}, u32[]{:S(2)}) copy-start(bf16[4,64,4096]{2,1,0:T(8,128)(2,1)} %get-tuple-element.181) | copy-start | bytes 6291460
  367.0 48.5 %collective-permute-start.18 = (bf16[1,2,64,4096]{3,2,1,0:T(8,128)(2,1)S(1)}, bf16[1,2,64,4096]{3,2,1,0:T(8,128)(2,1)S(1)}, u32[]{:S(2)}, u32[]{:S(2)}) collective-permute-start(bf16[1,2,64,4096]{3,2,1,0:T(8,128)(2,1)S(1)} %dynamic-slice_bitcast_fusion), channel_id=1, source_target_pairs={{0,16},{4,20},{8,24},{12,28},{16,0},{20,4},{24,8},{28,12},{1,17},{... | collective-permute-start | bytes 3145736 | tf_op jit(solution)/shard_map/ppermute | solution.py:52
  408.8 21.1 %collective-permute-start.17 = (bf16[1,1,64,4096]{3,2,1,0:T(8,128)(2,1)S(1)}, bf16[1,1,64,4096]{3,2,1,0:T(8,128)(2,1)S(1)}, u32[]{:S(2)}, u32[]{:S(2)}) collective-permute-start(bf16[1,1,64,4096]{3,2,1,0:T(8,128)(2,1)S(1)} %constant_dynamic-slice_fusion.1), channel_id=1, source_target_pairs={{0,16},{4,20},{8,24},{12,28},{16,0},{20,4},{24,8},{28,12},{1,17},{... | collective-permute-start | bytes 1572872 | tf_op jit(solution)/shard_map/ppermute | solution.py:52
  415.8 16.9 %collective-permute-start.19 = (bf16[1,1,64,4096]{3,2,1,0:T(8,128)(2,1)S(1)}, bf16[1,1,64,4096]{3,2,1,0:T(8,128)(2,1)S(1)}, u32[]{:S(2)}, u32[]{:S(2)}) collective-permute-start(bf16[1,1,64,4096]{3,2,1,0:T(8,128)(2,1)S(1)} %constant_dynamic-slice_fusion), channel_id=1, source_target_pairs={{0,8},{4,12},{8,0},{12,4},{16,24},{20,28},{24,16},{28,20},{1,9},{5... | collective-permute-start | bytes 1572872 | tf_op jit(solution)/shard_map/ppermute | solution.py:52
  418.2 11.7 %collective-permute-start.22 = (f32[52,128]{1,0:T(8,128)S(1)}, f32[52,128]{1,0:T(8,128)S(1)}, u32[]{:S(2)}, u32[]{:S(2)}) collective-permute-start(f32[52,128]{1,0:T(8,128)S(1)} %fusion.78), channel_id=1, source_target_pairs={{0,16},{4,20},{8,24},{12,28},{16,0},{20,4},{24,8},{28,12},{1,17},{... | collective-permute-start | bytes 79880 | tf_op jit(solution)/shard_map/ppermute | solution.py:52
  434.0 16.2 %collective-permute-start.23 = (f32[52,128]{1,0:T(8,128)S(1)}, f32[52,128]{1,0:T(8,128)S(1)}, u32[]{:S(2)}, u32[]{:S(2)}) collective-permute-start(f32[52,128]{1,0:T(8,128)S(1)} %add.267), channel_id=1, source_target_pairs={{0,2},{1,3},{2,0},{3,1},{4,6},{5,7},{6,4},{7,5},{8,10},{9,11},{10,... | collective-permute-start | bytes 79880 | tf_op jit(solution)/shard_map/ppermute | solution.py:56
  437.0 13.3 %collective-permute-start.24 = (f32[52,128]{1,0:T(8,128)S(1)}, f32[52,128]{1,0:T(8,128)S(1)}, u32[]{:S(2)}, u32[]{:S(2)}) collective-permute-start(f32[52,128]{1,0:T(8,128)S(1)} %add.267), channel_id=1, source_target_pairs={{0,1},{1,2},{2,3},{3,0},{4,5},{5,6},{6,7},{7,4},{8,9},{9,10},{10,1... | collective-permute-start | bytes 79880 | tf_op jit(solution)/shard_map/ppermute | solution.py:56
  438.4 11.9 %collective-permute-start.25 = (f32[52,128]{1,0:T(8,128)S(1)}, f32[52,128]{1,0:T(8,128)S(1)}, u32[]{:S(2)}, u32[]{:S(2)}) collective-permute-start(f32[52,128]{1,0:T(8,128)S(1)} %add.267), channel_id=1, source_target_pairs={{0,3},{1,0},{2,1},{3,2},{4,7},{5,4},{6,5},{7,6},{8,11},{9,8},{10,9... | collective-permute-start | bytes 79880 | tf_op jit(solution)/shard_map/ppermute | solution.py:56
  440.8 24.7 %all-to-all-start.7 = ((bf16[4,32,4096]{2,1,0:T(8,128)(2,1)}), bf16[4,32,4096]{2,1,0:T(8,128)(2,1)}, u32[]{:S(2)}, u32[]{:S(2)}) async-start(bf16[4,32,4096]{2,1,0:T(8,128)(2,1)} %bitcast.192), calls=%async_computation.7 | async-start | bytes 2097152 | tf_op jit(solution)/shard_map/all_to_all | solution.py:97
  452.4 19.9 %copy-start.1 = (f32[32,16]{0,1:T(8,128)S(1)}, f32[32,16]{0,1:T(8,128)}, u32[]{:S(2)}) copy-start(f32[32,16]{0,1:T(8,128)} %param.21) | copy-start | bytes 6148
  (42 other events, 230.5 us)
Sparse Core Ops, SparseCore 0:
  93.5 80.3 all-gather.1
  303.0 149.3 reduce-scatter.1

commit v5 on v4

--- a/solution.py
+++ b/solution.py
@@ -121,7 +121,8 @@
             high, low = 1 << (len(left) - 1 - place), 1 << place
             shaped = value.astype(BF16).reshape(high, 2, low, half, width)
             kept, sent = split_bit(jnp.moveaxis(shaped, 1, 0), me, bit)
-            value = kept.astype(F32) + after(flip(sent, "dp", size, bit), hold).astype(F32)
+            got = flip(sent, "dp", size, bit)
+            value = kept.astype(F32) + after(got, hold).astype(F32)
             left.remove(bit)
         outs.append(value.reshape(half, width))
     return jnp.concatenate(outs, axis=0)
@@ -691,6 +692,74 @@
     )(*args)
 
 
+def finish_body(count, tokens_ref, gain_ref, weights_ref, *refs):
+    dqkvs, dh1s = refs[:count], refs[count : 2 * count]
+    out_ref, gain_grad_ref = refs[2 * count :]
+    gain = gain_ref[...]
+    total = jnp.zeros(gain.shape, F32)
+    for n in range(count):
+        h0 = tokens_ref[n].astype(F32)
+        r1 = rms_scale(h0)
+        n1_hat = h0 * r1
+        dn1 = dot_t(dqkvs[n][...], weights_ref[...])
+        total = total + jnp.sum(dn1 * n1_hat, axis=0, keepdims=True)
+        scaled = dn1 * gain
+        mean = jnp.mean(scaled * n1_hat, axis=-1, keepdims=True)
+        out_ref[n] = (dh1s[n][...] + r1 * (scaled - n1_hat * mean)).astype(BF16)
+    gain_grad_ref[...] = total
+
+
+def finish_call(tokens, gain, weights, dqkvs, dh1s):
+    args = (tokens, gain, weights, *dqkvs, *dh1s)
+    in_specs = [pl.BlockSpec(a.shape, lambda i, n=a.ndim: (0,) * n) for a in args]
+    in_specs[2] = pl.BlockSpec((tokens.shape[2], 3 * tokens.shape[2]), lambda i: (0, 0))
+    return pl.pallas_call(
+        partial(finish_body, len(dqkvs)),
+        grid=(1,),
+        in_specs=in_specs,
+        out_specs=[
+            pl.BlockSpec(tokens.shape, lambda i: (0, 0, 0)),
+            pl.BlockSpec(gain.shape, lambda i: (0, 0)),
+        ],
+        out_shape=[
+            jax.ShapeDtypeStruct(tokens.shape, BF16),
+            jax.ShapeDtypeStruct(gain.shape, F32),
+        ],
+        compiler_params=pltpu.CompilerParams(vmem_limit_bytes=56 << 20),
+        cost_estimate=LIGHT,
+        name="finish",
+    )(*args)
+
+
+def output_body(count, y_ref, targets_ref, routes_ref, *refs):
+    probs, h1s, out_ref = refs[:count], refs[count : 2 * count], refs[-1]
+    width = out_ref.shape[2]
+    for n in range(count):
+        y = y_ref[:, n].reshape(-1, width)
+        slots = lax.broadcasted_iota(jnp.int32, (out_ref.shape[1], y.shape[0]), 1)
+        total = h1s[n][...]
+        moe = 0.0
+        for j in range(2):
+            weights = probs[n][...]
+            lane = lax.broadcasted_iota(jnp.int32, weights.shape, 1)
+            mine = lane == routes_ref[n, :, j : j + 1]
+            gate = jnp.sum(jnp.where(mine, weights, 0.0), axis=-1, keepdims=True)
+            pick = (slots == targets_ref[n, :, j : j + 1]).astype(F32).astype(BF16)
+            moe = moe + gate * dot(pick, y)
+        out_ref[n] = (total + moe).astype(BF16)
+
+
+def output_call(y, targets, routes, probs, h1s):
+    length, width = h1s[0].shape
+    return pl.pallas_call(
+        partial(output_body, len(h1s)),
+        out_shape=jax.ShapeDtypeStruct((len(h1s), length, width), BF16),
+        compiler_params=pltpu.CompilerParams(vmem_limit_bytes=56 << 20),
+        cost_estimate=LIGHT,
+        name="output",
+    )(y, targets, routes, *probs, *h1s)
+
+
 def on_device(
     sizes,
     tokens,
@@ -728,7 +797,8 @@
         t_dot(both[n], out_grads[n]).astype(BF16).reshape(experts, capacity, width)
         for n in range(batches)
     ]
-    go_slots = [all_to_all(after(v, attn_block)) for v in outgoing]
+    go_joint = all_to_all(after(jnp.stack(outgoing, axis=1), attn_block))
+    go_slots = [go_joint[:, n] for n in range(batches)]
 
     positions = jnp.arange(length, dtype=jnp.int32)
     buckets = bucket_of(positions[:, None] - positions[None, :])
@@ -736,11 +806,9 @@
     bias = jnp.einsum("kqc,ch->hkq", bucket_hot, rel_bias, precision=lax.Precision.HIGHEST)
 
     me_d = lax.axis_index("dp").astype(jnp.int32)[None]
-    out_first = gather_first(w_out[0], dp, ())
-    attn_first = gather_first(attn_block, dp, (bias, outgoing, out_first))
-    pieces, rels = gather_dp(attn_first, dp, ())
-    out_pieces, _ = gather_dp(out_first, dp, pieces[:2])
-    wout_full = join_call(me_d, out_pieces, rels)
+    attn_first = gather_first(attn_block, dp, outgoing)
+    pieces, rels = gather_dp(attn_first, dp, bias)
+    wout_full = lax.all_gather(w_out[0], "dp", axis=0, tiled=True)
     win_full = lax.all_gather(
         after(w_in[0], pieces[:2], go_slots[0]), "dp", axis=0, tiled=True
     )
@@ -758,7 +826,7 @@
             slot_count,
             weights,
             None if n else rels,
-            after(tokens[n], wout_full) if n else tokens[n],
+            tokens[n],
             gain1,
             bias,
             id_rows,
@@ -821,55 +889,38 @@
     )
     y_back = all_to_all(after(grads[0], attn_keep))
     attn_core = scatter_core(attn_keep, attn_send, dp)
-    attn_sum = scatter_dp(attn_core, dp, ())
     space, tile = joined.shape[1:]
     summed = lax.psum_scatter(
         joined.reshape(dp * space, tile), "dp", scatter_dimension=0, tiled=True
     )
     in_total, out_total = spread_call(summed, w_in.shape[1:], w_out.shape[1:])
 
-    outputs, input_grads = [], []
-    full_qkv = attn_w[:, : 3 * width]
     router_grad = sum(v[4] for v in backs)[:experts].T
     gain_moe_grad = sum(v[5] for v in backs)[0]
     table_grad = jnp.einsum(
         "nhkq,kqc->ch",
-        after(jnp.stack([v[3] for v in backs]), attn_keep),
+        after(jnp.stack([v[3] for v in backs]), attn_core),
         bucket_hot.astype(BF16),
         preferred_element_type=F32,
     )
-    gain_attn_grad = 0.0
-    for n in range(batches):
-        _, n1, _, _, _, h1, probs, _ = saved[n]
-        dh1, _, dqkv, _, _, _ = backs[n]
-        y_n = after(y_back, attn_sum)[:, n].reshape(slot_count, width)
-        route_hot = (routes[n][:, :, None] == jnp.arange(experts, dtype=jnp.int32)).astype(F32)
-        gates = jnp.sum(probs[:, None, :experts] * route_hot, axis=-1)
-        picked0, picked1 = dot(select[n][:, 0], y_n), dot(select[n][:, 1], y_n)
-        moe = gates[:, :1] * picked0 + gates[:, 1:] * picked1
-        outputs.append((h1 + moe).astype(BF16))
-        h0 = tokens[n].astype(F32)
-        r1 = rms_scale(h0)
-        n1_hat = h0 * r1
-        dn1 = dot_t(after(dqkv, attn_keep), full_qkv)
-        gain_attn_grad = gain_attn_grad + jnp.sum(dn1 * n1_hat, axis=0)
-        scaled = dn1 * gain_attn
-        input_grad = dh1 + r1 * (
-            scaled - n1_hat * jnp.mean(scaled * n1_hat, axis=-1, keepdims=True)
-        )
-        input_grads.append(input_grad.astype(BF16))
-
+    input_grads, gain_attn_grad = finish_call(
+        tokens, gain1, attn_w, [after(v[2], attn_core) for v in backs], [v[0] for v in backs]
+    )
+    small = jnp.concatenate(
+        [gain_attn_grad[0], table_grad.reshape(-1), gain_moe_grad, router_grad.reshape(-1)]
+    )
+    small = sum_over(small.reshape(-1, 128), "dp", dp)
+    attn_sum = scatter_dp(attn_core, dp, (input_grads, table_grad))
+    small = sum_ring(after(small, attn_sum), "expert", experts).reshape(-1)
     attn_total = scatter_expert(attn_sum, experts)
     qkv_total, proj_total = attn_total[:, : 3 * width], attn_total[:, 3 * width :]
-    small = jnp.concatenate(
-        [gain_attn_grad, table_grad.reshape(-1), gain_moe_grad, router_grad.reshape(-1)]
-    )
-    small = sum_over(small.reshape(-1, 128), "dp", dp)
-    small = sum_ring(after(small, attn_sum), "expert", experts).reshape(-1)
+    outputs = output_call(
+        after(y_back, attn_sum), targets, routes, [v[6] for v in saved], [v[5] for v in saved]
+    )
     cuts = (width, width + table_grad.size, 2 * width + table_grad.size)
     return (
-        jnp.stack(outputs),
-        jnp.stack(input_grads),
+        outputs,
+        input_grads,
         small[: cuts[0]],
         qkv_total,
         proj_total,

time: 488 us -> 465 us (0.953)
  matrix products: 21.6 us -> 5.2 us
  Pallas kernels: 183 us -> 195 us
  other arithmetic: 28.7 us -> 20.4 us
  starting transfers between devices: 63.9 us -> 55.8 us
  waiting for transfers between devices: 124 us -> 129 us
    dot_general x7 -> x1, matrix products: 15.6 us -> 1.34 us  [on_device(): jnp.einsum('nhkq,kqc->ch', after(jnp.stack([v[3] for v in backs]), attn_c...]
    ppermute x20 -> x14, waiting for transfers between devices: 93 us -> 106 us  [flip(): return lax.ppermute(value, axis, [(i, i ^ bit) for i in range(size)])]
    pallas_call x1 -> x2, Pallas kernels: 5.24 us -> 15.4 us  [the longest x1 9.63 us: finish_call(): pl.pallas_call(partial(finish_body, len(dqkvs)), grid=(1,), in_specs=in_s...]
    all_to_all x8 -> x7, waiting for transfers between devices: 27.1 us -> 17.6 us  [all_to_all(): lax.all_to_all(value, 'expert', split_axis=0, concat_axis=0, tiled=True)]
    ppermute x20 -> x14, starting transfers between devices: 15.6 us -> 9.76 us  [flip(): return lax.ppermute(value, axis, [(i, i ^ bit) for i in range(size)])]
    all_to_all x8 -> x7, starting transfers between devices: 34.5 us -> 31.5 us  [all_to_all(): lax.all_to_all(value, 'expert', split_axis=0, concat_axis=0, tiled=True)]
    unnamed x116 -> x65, local copies, waits for them, and re-layouts: 9.97 us -> 7.98 us
  transfers between devices with their start and end apart: 36 -> 30, of which waited for: 15 -> 17; matrix products, arithmetic and copies ran while one was open for 18% -> 13% of each run, Pallas kernels for 35% -> 39%
where the time goes in v5:
time: 465 us; the launch traced here: 461 us
  Pallas kernels  195 us (42%)
  waiting for transfers between devices  129 us (28%)
  starting transfers between devices  55.8 us (12%)
  local copies, waits for them, and re-layouts  40.3 us (9%)
  other arithmetic  20.4 us (4%)
  between operations  15 us (3%)
  matrix products  5.2 us (1%)
    ppermute x14, waiting for transfers between devices, flip(): return lax.ppermute(value, axis, [(i, i ^ bit) for i in range(size)])  106 us
    pallas_call x2, Pallas kernels, expert_call(): pl.pallas_call(expert_body, grid=(tiles,), in_specs=in_specs, out_specs=[...  67.5 us
    pallas_call x2, Pallas kernels, forward_call(): pl.pallas_call(partial(forward_body, heads, experts, rels), in_specs=in_s...  34 us
    all_to_all x7, starting transfers between devices, all_to_all(): lax.all_to_all(value, 'expert', split_axis=0, concat_axis=0, tiled=True)  31.5 us
    pallas_call x2, Pallas kernels, backward_call(): pl.pallas_call(partial(backward_body, heads, experts), grid=(1,), in_spec...  27.4 us
    pallas_call x1, Pallas kernels, weight_in_call(): pl.pallas_call(weight_in_body, grid=(2,), in_specs=[pl.BlockSpec((rows, w...  22.4 us
    all_to_all x7, waiting for transfers between devices, all_to_all(): lax.all_to_all(value, 'expert', split_axis=0, concat_axis=0, tiled=True)  17.6 us
    ppermute x6, starting transfers between devices, shift(): lax.ppermute(value, axis, [(i, (i + step) % size) for i in range(size)])  14.2 us
  transfers between devices with their start and end apart: 30, of which 17 were waited for; matrix products, arithmetic and copies ran while one was open for 13% of the time, Pallas kernels for 39%

profile of v5, /device:TPU:0, one launch (start us, length us, event | category | flops | bytes accessed | tf_op | source)
XLA Modules:
  0.0 461.3 jit_solution(18419869143488573000)
XLA Ops:
  9.0 3.0 collective-permute-start
  12.1 2.6 collective-permute-start.1
  16.8 2.4 reduce-window.6
  23.6 1.7 pad_maximum_fusion.1
  25.3 3.7 all-to-all-start
  31.0 1.7 bitcast_dynamic-update-slice_fusion.2
  32.7 1.7 bitcast_dynamic-update-slice_fusion.1
  39.7 2.8 fusion
  42.5 4.4 copy.125
  46.9 13.2 %collective-permute-done.5 = bf16[1,64,4096]{2,1,0:T(8,128)(2,1)S(1)} collective-permute-done((bf16[1,64,4096]{2,1,0:T(8,128)(2,1)S(1)}, bf16[1,64,4096]{2,1,0:T(8,128)(2,1)S(1)}, u32[]{:S(2)}, u32[]{:S(2)}) %collective-permute-start.5) | collective-permute-done | bytes 524320 | tf_op jit(solution)/shard_map/ppermute | solution.py:52
  61.8 2.1 collective-permute-done.3
  65.2 23.6 %collective-permute-done.6 = bf16[2,64,4096]{2,1,0:T(8,128)(2,1)S(1)} collective-permute-done((bf16[2,64,4096]{2,1,0:T(8,128)(2,1)S(1)}, bf16[2,64,4096]{2,1,0:T(8,128)(2,1)S(1)}, u32[]{:S(2)}, u32[]{:S(2)}) %collective-permute-start.6) | collective-permute-done | bytes 1048608 | tf_op jit(solution)/shard_map/ppermute | solution.py:52
  91.2 2.2 all-to-all-done
  93.5 1.9 fusion.29
  96.7 1.6 copy.101.refs_12_
  103.8 17.6 %attention_forward.2 = (bf16[640,1024]{1,0:T(8,128)(2,1)}, bf16[256,1024]{1,0:T(8,128)(2,1)}, bf16[256,3072]{1,0:T(8,128)(2,1)}, f32[16,256]{1,0:T(8,128)}, bf16...) custom-call(s32[1]{0:T(128)} %bitcast.1.refs_0_, ...), custom_call_target="tpu_custom_call" | custom-call | flops 1 | bytes 1 | tf_op jit(solution)/shard_map/attention_forward/pallas_call | solution.py:577
  121.4 4.7 %all-to-all-start.2 = ((bf16[4,160,1024]{2,1,0:T(8,128)(2,1)}), bf16[4,160,1024]{2,1,0:T(8,128)(2,1)S(1)}, u32[]{:S(2)}, u32[]{:S(2)}) async-start(bf16[4,160,1024]{2,1,0:T(8,128)(2,1)} %bitcast.161), calls=%async_computation.2 | async-start | bytes 2621440 | tf_op jit(solution)/shard_map/all_to_all | solution.py:97
  127.7 16.4 %attention_forward.3 = (bf16[640,1024]{1,0:T(8,128)(2,1)}, bf16[256,1024]{1,0:T(8,128)(2,1)}, bf16[256,3072]{1,0:T(8,128)(2,1)}, f32[16,256]{1,0:T(8,128)}, bf16...) custom-call(bf16[1024,4096]{1,0:T(8,128)(2,1)} %get-tuple-element.78.refs_0_.proj_ref.weights_ref, ...), custom_call_target="tpu_custom_call" | custom-call | flops 1 | bytes 1 | tf_op jit(solution)/shard_map/attention_forward/pallas_call | solution.py:577
  144.0 13.8 %all-to-all-done.2 = bf16[4,160,1024]{2,1,0:T(8,128)(2,1)S(1)} async-done(((bf16[4,160,1024]{2,1,0:T(8,128)(2,1)}), bf16[4,160,1024]{2,1,0:T(8,128)(2,1)S(1)}, u32[]{:S(2)}, u32[]{:S(2)}) %all-to-all-start.2) | async-done | bytes 1310752 | tf_op jit(solution)/shard_map/all_to_all | solution.py:97
  157.8 4.0 all-to-all-start.1
  163.6 33.7 %expert.2 = (bf16[4,2,160,1024]{3,2,1,0:T(8,128)(2,1)}, bf16[640,1152]{1,0:T(8,128)(2,1)}, bf16[2816,1280]{1,0:T(8,128)(2,1)}, bf16[2,1280,2816]{2,1,0:T(8,128)(2,1)}, bf16[1280,1024]{1,0:T(8,128)(2,1)}) custom-call(s32[2]{0:T(128)} %pad_add_fusion.4.mine, bf16[640,1024]{1,0:T(8,128)(2,1)} %bitcast.138, bf16[640,1024]{1,0:T(8,128)(2,1)} %bitcast.147, ...), custom_call_target="tpu_custom_call" | custom-call | flops 1 | bytes 1 | tf_op jit(solution)/shard_map/expert/pallas_call | solution.py:251
  197.4 4.6 all-to-all-start.3
  202.0 33.8 %expert.3 = (bf16[4,2,160,1024]{3,2,1,0:T(8,128)(2,1)}, bf16[640,1152]{1,0:T(8,128)(2,1)}, bf16[2816,1280]{1,0:T(8,128)(2,1)}, bf16[2,1280,2816]{2,1,0:T(8,128)(2,1)}, bf16[1280,1024]{1,0:T(8,128)(2,1)}) custom-call(s32[2]{0:T(128)} %pad_add_fusion.4.mine, ...), custom_call_target="tpu_custom_call", output_to_operand_aliasing={{0}: (7, {}), {2}: (8, {}), {3}: (9, {}), {4}: (10, {})} | custom-call | flops 1 | bytes 1 | tf_op jit(solution)/shard_map/expert/pallas_call | solution.py:251
  235.8 1.6 all-to-all-done.3
  237.4 3.7 all-to-all-start.4
  243.1 22.4 %weight_in.1._ = bf16[8,4224,256]{2,1,0:T(8,128)(2,1)} custom-call(bf16[640,1024]{1,0:T(8,128)(2,1)} %bitcast.139, bf16[640,1024]{1,0:T(8,128)(2,1)} %bitcast.141, bf16[2,1280,2816]{2,1,0:T(8,128)(2,1)} %get-tuple-element.95.refs_2_), custom_call_target="tpu_custom_call" | custom-call | flops 1 | bytes 1 | tf_op jit(solution)/shard_map/weight_in/pallas_call | solution.py:307
  265.5 13.5 %attention_backward.2 = (f32[256,1024]{1,0:T(8,128)}, bf16[256,1024]{1,0:T(8,128)(2,1)}, bf16[256,3072]{1,0:T(8,128)(2,1)}, bf16[16,256,256]{2,1,0:T(8,128)(2,1)...) custom-call(bf16[640,1152]{1,0:T(8,128)(2,1)} %bitcast.45.dx_ref, s32[256,2]{1,0:T(8,128)} %get-tuple-element.187.targets_ref, ...), custom_call_target="tpu_custom_call" | custom-call | flops 1 | bytes 1 | tf_op jit(solution)/shard_map/attention_backward/pallas_call | solution.py:682
  279.1 13.4 %weight_out.1 = bf16[8,4224,256]{2,1,0:T(8,128)(2,1)} custom-call(bf16[2816,1280]{1,0:T(8,128)(2,1)} %get-tuple-element.109.gt_ref, bf16[1280,1024]{1,0:T(8,128)(2,1)} %get-tuple-element.110.dy_ref, bf16[8,4224,256]{2,1,0:T(8,128)(2,1)} %weight_in.1._), custom_call_target="tpu_custom_call", output_to_operand_aliasing={{}: (2, {})} | custom-call | flops 1 | bytes 1 | tf_op jit(solution)/shard_map/weight_out/pallas_call | solution.py:332
  292.6 13.8 %attention_backward.3 = (f32[256,1024]{1,0:T(8,128)}, bf16[256,1024]{1,0:T(8,128)(2,1)}, bf16[256,3072]{1,0:T(8,128)(2,1)}, bf16[16,256,256]{2,1,0:T(8,128)(2,1)...) custom-call(bf16[640,1152]{1,0:T(8,128)(2,1)} %bitcast.146, s32[256,2]{1,0:T(8,128)} %get-tuple-element.184.targets_ref, ...), custom_call_target="tpu_custom_call" | custom-call | flops 1 | bytes 1 | tf_op jit(solution)/shard_map/attention_backward/pallas_call | solution.py:682
  306.4 11.2 %weight_attn.1 = (bf16[4,128,4096]{2,1,0:T(8,128)(2,1)}, bf16[4,128,4096]{2,1,0:T(8,128)(2,1)}) custom-call(s32[1]{0:T(128)S(6)} %select_n.107.core_ref, bf16[256,1024]{1,0:T(8,128)(2,1)} %get-tuple-element.89.refs_0_, bf16[256,1024]{1,0:T(8,128)(2,1)} %get-tuple-element.90.refs_1_, bf16[256,1024]{1,0:T(8,128)(2,1)} %get-tuple-element.91.refs_2_, ...), custom_call_target="tpu_custom_call" | custom-call | flops 1 | bytes 1 | tf_op jit(solution)/shard_map/weight_attn/pallas_call | solution.py:405
  317.7 5.4 %all-to-all-start.5 = ((bf16[4,2,160,1024]{3,2,1,0:T(8,128)(2,1)}), bf16[4,2,160,1024]{3,2,1,0:T(8,128)(2,1)S(1)}, u32[]{:S(2)}, u32[]{:S(2)}) async-start(bf16[4,2,160,1024]{3,2,1,0:T(8,128)(2,1)} %get-tuple-element.119), calls=%async_computation.5 | async-start | bytes 5242880 | tf_op jit(solution)/shard_map/all_to_all | solution.py:97
  323.1 2.8 pad_maximum_fusion
  326.8 3.5 add_convert_fusion
  334.9 9.6 %finish.1 = (bf16[2,256,1024]{2,1,0:T(8,128)(2,1)}, f32[1,1024]{1,0:T(1,128)}) custom-call(bf16[2,256,1024]{2,1,0:T(8,128)(2,1)} %tokens_ref.1, f32[1,1024]{1,0:T(1,128)} %bitcast.179, bf16[1024,4096]{1,0:T(8,128)(2,1)} %get-tuple-element.78.refs_0_.proj_ref.weights_ref, bf16[256,3072]{1,0:T(8,128)(2,1)} %get-tuple-element.121.refs_4_.refs_0_, ...), custom_call_target="tpu_custom_call" | custom-call | flops 1 | bytes 1 | tf_op jit(solution)/shard_map/finish/pallas_call | solution.py:716
  346.8 32.0 %collective-permute-done.10 = bf16[2,1,64,4096]{3,2,1,0:T(8,128)(2,1)} collective-permute-done((bf16[2,1,64,4096]{3,2,1,0:T(8,128)(2,1)}, bf16[2,1,64,4096]{3,2,1,0:T(8,128)(2,1)}, u32[]{:S(2)}, u32[]{:S(2)}) %collective-permute-start.10) | collective-permute-done | bytes 1048608 | tf_op jit(solution)/shard_map/ppermute | solution.py:52
  378.8 1.6 fusion.7
  380.8 1.6 collective-permute-done.12
  384.8 21.1 %collective-permute-done.11 = bf16[1,1,64,4096]{3,2,1,0:T(8,128)(2,1)S(1)} collective-permute-done((bf16[1,1,64,4096]{3,2,1,0:T(8,128)(2,1)S(1)}, bf16[1,1,64,4096]{3,2,1,0:T(8,128)(2,1)S(1)}, u32[]{:S(2)}, u32[]{:S(2)}) %collective-permute-start.11) | collective-permute-done | bytes 524320 | tf_op jit(solution)/shard_map/ppermute | solution.py:52
  405.9 3.5 collective-permute-done.13
  410.7 5.3 %all-to-all-start.6 = ((bf16[4,32,4096]{2,1,0:T(8,128)(2,1)}), bf16[4,32,4096]{2,1,0:T(8,128)(2,1)}, u32[]{:S(2)}, u32[]{:S(2)}) async-start(bf16[4,32,4096]{2,1,0:T(8,128)(2,1)} %bitcast.151), calls=%async_computation.6 | async-start | bytes 2097152 | tf_op jit(solution)/shard_map/all_to_all | solution.py:97
  419.3 3.5 collective-permute-done.15
  423.5 3.5 collective-permute-done.16
  427.0 3.1 collective-permute-start.17
  431.6 2.7 collective-permute-start.19
  434.3 5.8 %output.1 = bf16[2,256,1024]{2,1,0:T(8,128)(2,1)} custom-call(bf16[4,2,160,1024]{3,2,1,0:T(8,128)(2,1)} %copy-done.4, s32[2,256,2]{2,1,0:T(8,128)} %copy-done.12, s32[2,256,2]{2,1,0:T(8,128)} %copy-done.16, f32[256,128]{1,0:T(8,128)} %get-tuple-element.97.probs_ref.refs_0_, f32[256,128]{1,0:T(8,128)} %get-tuple-element.112.probs_ref.refs_1_, ...), custom_call_target="tpu_custom_call" | custom-call | flops 1 | bytes 1 | tf_op jit(solution)/shard_map/output/pallas_call | solution.py:754
  440.0 1.8 collective-permute-done.17
  447.5 2.8 reduce-scatter.2.cloned.1.call-done.summed_ref
  450.3 3.8 spread.1
  (175 shorter events, 55.9 us)
Async XLA Ops:
  7.2 32.5 %copy-start = (f32[32,16]{0,1:T(8,128)S(1)}, f32[32,16]{0,1:T(8,128)}, u32[]{:S(2)}) copy-start(f32[32,16]{0,1:T(8,128)} %param.21) | copy-start | bytes 6148
  7.2 155.2 %all-gather.6.cloned.1.call-start = ((), (), s32[]{:S(2)}) async-start(), calls=%async_computation.10 | async-start | bytes 6488064 | tf_op jit(solution)/shard_map/all_gather | solution.py:811
  9.0 22.0 %collective-permute-start = (bf16[32,4096]{1,0:T(8,128)(2,1)S(1)}, bf16[32,4096]{1,0:T(8,128)(2,1)}, u32[]{:S(2)}, u32[]{:S(2)}) collective-permute-start(bf16[32,4096]{1,0:T(8,128)(2,1)S(1)} %constant_dynamic-update-slice_fusion), channel_id=1, source_target_pairs={{0,1},{1,2},{2,3},{3,0},{4,5},{5,6},{6,7},{7,4},{8,9},{9,10},{10,1... | collective-permute-start | bytes 786440 | tf_op jit(solution)/shard_map/ppermute | solution.py:56
  12.1 20.7 %collective-permute-start.1 = (bf16[32,4096]{1,0:T(8,128)(2,1)S(1)}, bf16[32,4096]{1,0:T(8,128)(2,1)}, u32[]{:S(2)}, u32[]{:S(2)}) collective-permute-start(bf16[32,4096]{1,0:T(8,128)(2,1)S(1)} %constant_dynamic-update-slice_fusion), channel_id=1, source_target_pairs={{0,2},{1,3},{2,0},{3,1},{4,6},{5,7},{6,4},{7,5},{8,10},{9,11},{10,... | collective-permute-start | bytes 786440 | tf_op jit(solution)/shard_map/ppermute | solution.py:56
  14.6 19.7 %collective-permute-start.2 = (bf16[32,4096]{1,0:T(8,128)(2,1)S(1)}, bf16[32,4096]{1,0:T(8,128)(2,1)S(1)}, u32[]{:S(2)}, u32[]{:S(2)}) collective-permute-start(bf16[32,4096]{1,0:T(8,128)(2,1)S(1)} %constant_dynamic-update-slice_fusion), channel_id=1, source_target_pairs={{0,3},{1,0},{2,1},{3,2},{4,7},{5,4},{6,5},{7,6},{8,11},{9,8},{10,9... | collective-permute-start | bytes 786440 | tf_op jit(solution)/shard_map/ppermute | solution.py:56
  21.1 74.9 %copy-start.12 = (s32[2,256,2]{2,1,0:T(8,128)}, s32[2,256,2]{2,1,0:T(8,128)S(1)}, u32[]{:S(2)}) copy-start(s32[2,256,2]{2,1,0:T(8,128)S(1)} %bitcast_add_fusion.targets_ref) | copy-start | bytes 12292
  25.3 68.2 %all-to-all-start = ((bf16[4,2,160,1024]{3,2,1,0:T(8,128)(2,1)}), bf16[4,2,160,1024]{3,2,1,0:T(8,128)(2,1)S(1)}, u32[]{:S(2)}, u32[]{:S(2)}) async-start(bf16[4,2,160,1024]{3,2,1,0:T(8,128)(2,1)} %pad_maximum_fusion.1), calls=%async_computation | async-start | bytes 5242880 | tf_op jit(solution)/shard_map/all_to_all | solution.py:97
  29.0 134.6 %all-gather.4.cloned.1.call-start = ((), (), s32[]{:S(2)}) async-start(), calls=%async_computation.8 | async-start | bytes 12976128 | tf_op jit(solution)/shard_map/all_gather | solution.py:812
  36.4 23.7 %collective-permute-start.5 = (bf16[1,64,4096]{2,1,0:T(8,128)(2,1)S(1)}, bf16[1,64,4096]{2,1,0:T(8,128)(2,1)S(1)}, u32[]{:S(2)}, u32[]{:S(2)}) collective-permute-start(bf16[1,64,4096]{2,1,0:T(8,128)(2,1)S(1)} %bitcast.156), channel_id=1, source_target_pairs={{0,16},{4,20},{8,24},{12,28},{16,0},{20,4},{24,8},{28,12},{1,17},{... | collective-permute-start | bytes 1572872 | tf_op jit(solution)/shard_map/ppermute | solution.py:52
  38.1 25.7 %collective-permute-start.3 = (bf16[1,64,4096]{2,1,0:T(8,128)(2,1)S(1)}, bf16[1,64,4096]{2,1,0:T(8,128)(2,1)S(1)}, u32[]{:S(2)}, u32[]{:S(2)}) collective-permute-start(bf16[1,64,4096]{2,1,0:T(8,128)(2,1)S(1)} %bitcast.154), channel_id=1, source_target_pairs={{0,8},{4,12},{8,0},{12,4},{16,24},{20,28},{24,16},{28,20},{1,9},{5... | collective-permute-start | bytes 1572872 | tf_op jit(solution)/shard_map/ppermute | solution.py:52
  60.2 28.5 %collective-permute-start.6 = (bf16[2,64,4096]{2,1,0:T(8,128)(2,1)S(1)}, bf16[2,64,4096]{2,1,0:T(8,128)(2,1)S(1)}, u32[]{:S(2)}, u32[]{:S(2)}) collective-permute-start(bf16[2,64,4096]{2,1,0:T(8,128)(2,1)S(1)} %pad_maximum_fusion.4), channel_id=1, source_target_pairs={{0,8},{4,12},{8,0},{12,4},{16,24},{20,28},{24,16},{28,20},{1,9},{5... | collective-permute-start | bytes 3145736 | tf_op jit(solution)/shard_map/ppermute | solution.py:52
  63.9 24.9 %collective-permute-start.4 = (bf16[2,64,4096]{2,1,0:T(8,128)(2,1)S(1)}, bf16[2,64,4096]{2,1,0:T(8,128)(2,1)S(1)}, u32[]{:S(2)}, u32[]{:S(2)}) collective-permute-start(bf16[2,64,4096]{2,1,0:T(8,128)(2,1)S(1)} %pad_maximum_fusion.3), channel_id=1, source_target_pairs={{0,16},{4,20},{8,24},{12,28},{16,0},{20,4},{24,8},{28,12},{1,17},{... | collective-permute-start | bytes 3145736 | tf_op jit(solution)/shard_map/ppermute | solution.py:52
  95.4 5.1 %copy-start.24 = (bf16[1024,4]{0,1:T(4,128)(2,1)S(1)}, bf16[1024,4]{0,1:T(4,128)(2,1)}, u32[]{:S(2)}) copy-start(bf16[1024,4]{0,1:T(4,128)(2,1)} %param.23) | copy-start | bytes 24580
  95.4 6.0 %copy-start.15 = (bf16[2,256,1024]{2,1,0:T(8,128)(2,1)S(1)}, bf16[2,256,1024]{2,1,0:T(8,128)(2,1)}, u32[]{:S(2)}) copy-start(bf16[2,256,1024]{2,1,0:T(8,128)(2,1)} %tokens_ref.1) | copy-start | bytes 3145732
  95.4 7.0 %collective-permute-start.8 = (bf16[4,64,4096]{2,1,0:T(8,128)(2,1)}, bf16[4,64,4096]{2,1,0:T(8,128)(2,1)S(1)}, u32[]{:S(2)}, u32[]{:S(2)}) collective-permute-start(bf16[4,64,4096]{2,1,0:T(8,128)(2,1)} %copy-done.10), channel_id=1, source_target_pairs={{0,4},{4,0},{8,12},{12,8},{16,20},{20,16},{24,28},{28,24},{1,5},{5... | collective-permute-start | bytes 6291464 | tf_op jit(solution)/shard_map/ppermute | solution.py:52
  95.5 7.5 %collective-permute-start.7 = (bf16[4,64,4096]{2,1,0:T(8,128)(2,1)}, bf16[4,64,4096]{2,1,0:T(8,128)(2,1)}, u32[]{:S(2)}, u32[]{:S(2)}) collective-permute-start(bf16[4,64,4096]{2,1,0:T(8,128)(2,1)} %constant_dynamic-update-slice_fusion.2.refs_1_), channel_id=1, source_target_pairs={{0,4},{4,0},{8,12},{12,8},{16,20},{20,16},{24,28},{28,24},{1,5},{5... | collective-permute-start | bytes 6291464 | tf_op jit(solution)/shard_map/ppermute | solution.py:52
  121.4 5.4 %copy-start.27 = (s32[1,256]{1,0:T(1,128)S(1)}, s32[1,256]{1,0:T(1,128)}, u32[]{:S(2)}) copy-start(s32[1,256]{1,0:T(1,128)} %get-tuple-element.199) | copy-start | bytes 3076
  121.4 36.4 %all-to-all-start.2 = ((bf16[4,160,1024]{2,1,0:T(8,128)(2,1)}), bf16[4,160,1024]{2,1,0:T(8,128)(2,1)S(1)}, u32[]{:S(2)}, u32[]{:S(2)}) async-start(bf16[4,160,1024]{2,1,0:T(8,128)(2,1)} %bitcast.161), calls=%async_computation.2 | async-start | bytes 2621440 | tf_op jit(solution)/shard_map/all_to_all | solution.py:97
  157.8 5.8 %copy-start.2 = (bf16[4,160,1024]{2,1,0:T(8,128)(2,1)}, bf16[4,160,1024]{2,1,0:T(8,128)(2,1)S(1)}, u32[]{:S(2)}) copy-start(bf16[4,160,1024]{2,1,0:T(8,128)(2,1)S(1)} %all-to-all-done.2) | copy-start | bytes 3932164
  157.8 39.5 %all-to-all-start.1 = ((bf16[4,160,1024]{2,1,0:T(8,128)(2,1)}), bf16[4,160,1024]{2,1,0:T(8,128)(2,1)S(1)}, u32[]{:S(2)}, u32[]{:S(2)}) async-start(bf16[4,160,1024]{2,1,0:T(8,128)(2,1)} %bitcast.162), calls=%async_computation.1 | async-start | bytes 2621440 | tf_op jit(solution)/shard_map/all_to_all | solution.py:97
  197.3 4.6 %copy-start.3 = (bf16[4,160,1024]{2,1,0:T(8,128)(2,1)}, bf16[4,160,1024]{2,1,0:T(8,128)(2,1)S(1)}, u32[]{:S(2)}) copy-start(bf16[4,160,1024]{2,1,0:T(8,128)(2,1)S(1)} %all-to-all-done.1) | copy-start | bytes 3932164
  197.4 40.0 %all-to-all-start.3 = ((bf16[4,160,1152]{2,1,0:T(8,128)(2,1)}), bf16[4,160,1152]{2,1,0:T(8,128)(2,1)}, u32[]{:S(2)}, u32[]{:S(2)}) async-start(bf16[4,160,1152]{2,1,0:T(8,128)(2,1)} %bitcast.159), calls=%async_computation.3 | async-start | bytes 2949120 | tf_op jit(solution)/shard_map/all_to_all | solution.py:97
  235.7 5.5 %copy-start.20 = (s32[2,256,2]{1,2,0:T(2,128)S(1)}, s32[2,256,2]{1,2,0:T(2,128)}, u32[]{:S(2)}) copy-start(s32[2,256,2]{1,2,0:T(2,128)} %param.17) | copy-start | bytes 12292
  235.8 6.4 %copy-start.14 = (bf16[2,256,1024]{2,1,0:T(8,128)(2,1)S(1)}, bf16[2,256,1024]{2,1,0:T(8,128)(2,1)}, u32[]{:S(2)}) copy-start(bf16[2,256,1024]{2,1,0:T(8,128)(2,1)} %param.14) | copy-start | bytes 3145732
  237.4 41.7 %all-to-all-start.4 = ((bf16[4,160,1152]{2,1,0:T(8,128)(2,1)}), bf16[4,160,1152]{2,1,0:T(8,128)(2,1)S(1)}, u32[]{:S(2)}, u32[]{:S(2)}) async-start(bf16[4,160,1152]{2,1,0:T(8,128)(2,1)} %bitcast.158), calls=%async_computation.4 | async-start | bytes 2949120 | tf_op jit(solution)/shard_map/all_to_all | solution.py:97
  241.0 209.3 %reduce-scatter.2.cloned.1.call-start = ((), (), s32[]{:S(2)}) async-start(), calls=%async_computation.9 | async-start | bytes 19464192 | tf_op jit(solution)/shard_map/reduce_scatter | solution.py:893
  241.3 24.2 %copy-start.16 = (s32[2,256,2]{2,1,0:T(8,128)}, s32[2,256,2]{2,1,0:T(8,128)S(1)}, u32[]{:S(2)}) copy-start(s32[2,256,2]{2,1,0:T(8,128)S(1)} %copy.106.routes_ref) | copy-start | bytes 12292
  279.1 13.4 %copy-start.9 = (bf16[4,160,1152]{2,1,0:T(8,128)(2,1)}, bf16[4,160,1152]{2,1,0:T(8,128)(2,1)S(1)}, u32[]{:S(2)}) copy-start(bf16[4,160,1152]{2,1,0:T(8,128)(2,1)S(1)} %all-to-all-done.4) | copy-start | bytes 4423684
  317.6 8.4 %collective-permute-start.9 = (bf16[4,128,4096]{2,1,0:T(8,128)(2,1)}, bf16[4,128,4096]{2,1,0:T(8,128)(2,1)}, u32[]{:S(2)}, u32[]{:S(2)}) collective-permute-start(bf16[4,128,4096]{2,1,0:T(8,128)(2,1)} %get-tuple-element.120), channel_id=1, source_target_pairs={{0,4},{4,0},{8,12},{12,8},{16,20},{20,16},{24,28},{28,24},{1,5},{5... | collective-permute-start | bytes 12582920 | tf_op jit(solution)/shard_map/ppermute | solution.py:52
  317.7 93.1 %all-to-all-start.5 = ((bf16[4,2,160,1024]{3,2,1,0:T(8,128)(2,1)}), bf16[4,2,160,1024]{3,2,1,0:T(8,128)(2,1)S(1)}, u32[]{:S(2)}, u32[]{:S(2)}) async-start(bf16[4,2,160,1024]{3,2,1,0:T(8,128)(2,1)} %get-tuple-element.119), calls=%async_computation.5 | async-start | bytes 5242880 | tf_op jit(solution)/shard_map/all_to_all | solution.py:97
  323.1 3.6 copy-start.11
  331.7 47.1 %collective-permute-start.10 = (bf16[2,1,64,4096]{3,2,1,0:T(8,128)(2,1)}, bf16[2,1,64,4096]{3,2,1,0:T(8,128)(2,1)}, u32[]{:S(2)}, u32[]{:S(2)}) collective-permute-start(bf16[2,1,64,4096]{3,2,1,0:T(8,128)(2,1)} %dynamic-slice_bitcast_fusion.1), channel_id=1, source_target_pairs={{0,8},{4,12},{8,0},{12,4},{16,24},{20,28},{24,16},{28,20},{1,9},{5... | collective-permute-start | bytes 3145736 | tf_op jit(solution)/shard_map/ppermute | solution.py:52
  334.1 48.3 %collective-permute-start.12 = (bf16[1,2,64,4096]{3,2,1,0:T(8,128)(2,1)}, bf16[1,2,64,4096]{3,2,1,0:T(8,128)(2,1)}, u32[]{:S(2)}, u32[]{:S(2)}) collective-permute-start(bf16[1,2,64,4096]{3,2,1,0:T(8,128)(2,1)} %dynamic-slice_bitcast_fusion), channel_id=1, source_target_pairs={{0,16},{4,20},{8,24},{12,28},{16,0},{20,4},{24,8},{28,12},{1,17},{... | collective-permute-start | bytes 3145736 | tf_op jit(solution)/shard_map/ppermute | solution.py:52
  345.5 33.4 %copy-start.8 = (bf16[4,64,4096]{2,1,0:T(8,128)(2,1)S(1)}, bf16[4,64,4096]{2,1,0:T(8,128)(2,1)}, u32[]{:S(2)}) copy-start(bf16[4,64,4096]{2,1,0:T(8,128)(2,1)} %copy-done.7) | copy-start | bytes 6291460
  380.5 25.4 %collective-permute-start.11 = (bf16[1,1,64,4096]{3,2,1,0:T(8,128)(2,1)S(1)}, bf16[1,1,64,4096]{3,2,1,0:T(8,128)(2,1)S(1)}, u32[]{:S(2)}, u32[]{:S(2)}) collective-permute-start(bf16[1,1,64,4096]{3,2,1,0:T(8,128)(2,1)S(1)} %constant_dynamic-slice_fusion.1), channel_id=1, source_target_pairs={{0,16},{4,20},{8,24},{12,28},{16,0},{20,4},{24,8},{28,12},{1,17},{... | collective-permute-start | bytes 1572872 | tf_op jit(solution)/shard_map/ppermute | solution.py:52
  383.9 25.5 %collective-permute-start.13 = (bf16[1,1,64,4096]{3,2,1,0:T(8,128)(2,1)S(1)}, bf16[1,1,64,4096]{3,2,1,0:T(8,128)(2,1)S(1)}, u32[]{:S(2)}, u32[]{:S(2)}) collective-permute-start(bf16[1,1,64,4096]{3,2,1,0:T(8,128)(2,1)S(1)} %constant_dynamic-slice_fusion), channel_id=1, source_target_pairs={{0,8},{4,12},{8,0},{12,4},{16,24},{20,28},{24,16},{28,20},{1,9},{5... | collective-permute-start | bytes 1572872 | tf_op jit(solution)/shard_map/ppermute | solution.py:52
  409.6 6.4 %copy-start.25 = (f32[1,1024]{1,0:T(1,128)S(1)}, f32[1,1024]{1,0:T(1,128)}, u32[]{:S(2)}) copy-start(f32[1,1024]{1,0:T(1,128)} %get-tuple-element.108) | copy-start | bytes 12292
  409.7 6.4 %copy-start.26 = (f32[1,1024]{1,0:T(1,128)S(1)}, f32[1,1024]{1,0:T(1,128)}, u32[]{:S(2)}) copy-start(f32[1,1024]{1,0:T(1,128)} %get-tuple-element.133) | copy-start | bytes 12292
  410.7 6.8 %copy-start.21 = (f32[1,1024]{1,0:T(1,128)S(1)}, f32[1,1024]{1,0:T(1,128)}, u32[]{:S(2)}) copy-start(f32[1,1024]{1,0:T(1,128)} %get-tuple-element.132) | copy-start | bytes 12292
  410.7 23.5 %copy-start.4 = (bf16[4,2,160,1024]{3,2,1,0:T(8,128)(2,1)}, bf16[4,2,160,1024]{3,2,1,0:T(8,128)(2,1)S(1)}, u32[]{:S(2)}) copy-start(bf16[4,2,160,1024]{3,2,1,0:T(8,128)(2,1)S(1)} %all-to-all-done.5.y_ref) | copy-start | bytes 7864324
  410.7 33.9 %all-to-all-start.6 = ((bf16[4,32,4096]{2,1,0:T(8,128)(2,1)}), bf16[4,32,4096]{2,1,0:T(8,128)(2,1)}, u32[]{:S(2)}, u32[]{:S(2)}) async-start(bf16[4,32,4096]{2,1,0:T(8,128)(2,1)} %bitcast.151), calls=%async_computation.6 | async-start | bytes 2097152 | tf_op jit(solution)/shard_map/all_to_all | solution.py:97
  417.6 1.3 collective-permute-start.14
  418.8 3.9 collective-permute-start.15
  422.8 4.3 collective-permute-start.16
  427.0 14.8 %collective-permute-start.17 = (f32[52,128]{1,0:T(8,128)S(1)}, f32[52,128]{1,0:T(8,128)S(1)}, u32[]{:S(2)}, u32[]{:S(2)}) collective-permute-start(f32[52,128]{1,0:T(8,128)S(1)} %add.221), channel_id=1, source_target_pairs={{0,2},{1,3},{2,0},{3,1},{4,6},{5,7},{6,4},{7,5},{8,10},{9,11},{10,... | collective-permute-start | bytes 79880 | tf_op jit(solution)/shard_map/ppermute | solution.py:56
  430.1 11.8 %collective-permute-start.18 = (f32[52,128]{1,0:T(8,128)S(1)}, f32[52,128]{1,0:T(8,128)S(1)}, u32[]{:S(2)}, u32[]{:S(2)}) collective-permute-start(f32[52,128]{1,0:T(8,128)S(1)} %add.221), channel_id=1, source_target_pairs={{0,1},{1,2},{2,3},{3,0},{4,5},{5,6},{6,7},{7,4},{8,9},{9,10},{10,1... | collective-permute-start | bytes 79880 | tf_op jit(solution)/shard_map/ppermute | solution.py:56
  431.6 10.3 %collective-permute-start.19 = (f32[52,128]{1,0:T(8,128)S(1)}, f32[52,128]{1,0:T(8,128)S(1)}, u32[]{:S(2)}, u32[]{:S(2)}) collective-permute-start(f32[52,128]{1,0:T(8,128)S(1)} %add.221), channel_id=1, source_target_pairs={{0,3},{1,0},{2,1},{3,2},{4,7},{5,4},{6,5},{7,6},{8,11},{9,8},{10,9... | collective-permute-start | bytes 79880 | tf_op jit(solution)/shard_map/ppermute | solution.py:56
  444.0 10.2 %copy-start.1 = (f32[32,16]{0,1:T(8,128)S(1)}, f32[32,16]{0,1:T(8,128)}, u32[]{:S(2)}) copy-start(f32[32,16]{0,1:T(8,128)} %param.21) | copy-start | bytes 6148
  (11 other events, 24.4 us)
Sparse Core Ops, SparseCore 0:
  16.1 56.6 all-gather.5
  95.5 68.0 all-gather.3
  292.7 157.5 reduce-scatter.1

commit v6 on v5

--- a/solution.py
+++ b/solution.py
@@ -876,9 +876,8 @@
     core = me_d % 2
     _, gt, du, dy = grads
     joined = weight_in_call(dp, [h[0] for h in held], after(du, held[0][1]))
-    backs = [backward(0, after(held[0][1], joined))]
-    joined = weight_out_call(after(gt, held[1][1], backs[0]), dy, joined)
-    backs.append(backward(1, after(held[1][1], joined)))
+    joined = after(weight_out_call(gt, dy, joined), held[1][1])
+    backs = [backward(n, after(held[n][1], joined)) for n in range(batches)]
     attn_keep, attn_send = weight_attn_call(
         dp,
         core,

time: 465 us -> 459 us (0.987)
  waiting for transfers between devices: 129 us -> 119 us
    ppermute x14, waiting for transfers between devices: 106 us -> 99.8 us  [flip(): return lax.ppermute(value, axis, [(i, i ^ bit) for i in range(size)])]
  transfers between devices with their start and end apart: 30 -> 30, of which waited for: 17 -> 14; matrix products, arithmetic and copies ran while one was open for 13% -> 13% of each run, Pallas kernels for 39% -> 42%
where the time goes in v6:
time: 459 us; the launch traced here: 455 us
  Pallas kernels  196 us (43%)
  waiting for transfers between devices  119 us (26%)
  starting transfers between devices  57.6 us (13%)
  local copies, waits for them, and re-layouts  41.3 us (9%)
  other arithmetic  20.6 us (4%)
  between operations  14.9 us (3%)
  matrix products  5.2 us (1%)
    ppermute x14, waiting for transfers between devices, flip(): return lax.ppermute(value, axis, [(i, i ^ bit) for i in range(size)])  99.8 us
    pallas_call x2, Pallas kernels, expert_call(): pl.pallas_call(expert_body, grid=(tiles,), in_specs=in_specs, out_specs=[...  67.5 us
    pallas_call x2, Pallas kernels, forward_call(): pl.pallas_call(partial(forward_body, heads, experts, rels), in_specs=in_s...  34.1 us
    all_to_all x7, starting transfers between devices, all_to_all(): lax.all_to_all(value, 'expert', split_axis=0, concat_axis=0, tiled=True)  30.8 us
    pallas_call x2, Pallas kernels, backward_call(): pl.pallas_call(partial(backward_body, heads, experts), grid=(1,), in_spec...  30.5 us
    pallas_call x1, Pallas kernels, weight_in_call(): pl.pallas_call(weight_in_body, grid=(2,), in_specs=[pl.BlockSpec((rows, w...  22.2 us
    all_to_all x7, waiting for transfers between devices, all_to_all(): lax.all_to_all(value, 'expert', split_axis=0, concat_axis=0, tiled=True)  17.5 us
    ppermute x6, starting transfers between devices, shift(): lax.ppermute(value, axis, [(i, (i + step) % size) for i in range(size)])  14 us
  transfers between devices with their start and end apart: 30, of which 14 were waited for; matrix products, arithmetic and copies ran while one was open for 13% of the time, Pallas kernels for 42%

profile of v6, /device:TPU:0, one launch (start us, length us, event | category | flops | bytes accessed | tf_op | source)
XLA Modules:
  0.0 454.7 jit_solution(1009231006141640239)
XLA Ops:
  9.0 3.0 collective-permute-start
  12.1 2.6 collective-permute-start.1
  16.8 2.4 reduce-window.6
  23.6 1.7 pad_maximum_fusion.1
  25.3 3.7 all-to-all-start
  31.0 1.7 bitcast_dynamic-update-slice_fusion.2
  32.7 1.7 bitcast_dynamic-update-slice_fusion.1
  36.4 1.6 collective-permute-start.5
  38.1 1.6 collective-permute-start.3
  39.7 2.8 fusion
  42.5 4.4 copy.125
  46.9 13.2 %collective-permute-done.5 = bf16[1,64,4096]{2,1,0:T(8,128)(2,1)S(1)} collective-permute-done((bf16[1,64,4096]{2,1,0:T(8,128)(2,1)S(1)}, bf16[1,64,4096]{2,1,0:T(8,128)(2,1)S(1)}, u32[]{:S(2)}, u32[]{:S(2)}) %collective-permute-start.5) | collective-permute-done | bytes 524320 | tf_op jit(solution)/shard_map/ppermute | solution.py:52
  61.8 2.1 collective-permute-done.3
  65.2 23.6 %collective-permute-done.6 = bf16[2,64,4096]{2,1,0:T(8,128)(2,1)S(1)} collective-permute-done((bf16[2,64,4096]{2,1,0:T(8,128)(2,1)S(1)}, bf16[2,64,4096]{2,1,0:T(8,128)(2,1)S(1)}, u32[]{:S(2)}, u32[]{:S(2)}) %collective-permute-start.6) | collective-permute-done | bytes 1048608 | tf_op jit(solution)/shard_map/ppermute | solution.py:52
  91.2 2.2 all-to-all-done
  93.5 1.9 fusion.29
  96.7 1.6 copy.101.refs_12_
  103.8 17.6 %attention_forward.2 = (bf16[640,1024]{1,0:T(8,128)(2,1)}, bf16[256,1024]{1,0:T(8,128)(2,1)}, bf16[256,3072]{1,0:T(8,128)(2,1)}, f32[16,256]{1,0:T(8,128)}, bf16...) custom-call(s32[1]{0:T(128)} %bitcast.1.refs_0_, ...), custom_call_target="tpu_custom_call" | custom-call | flops 1 | bytes 1 | tf_op jit(solution)/shard_map/attention_forward/pallas_call | solution.py:577
  121.4 4.7 %all-to-all-start.2 = ((bf16[4,160,1024]{2,1,0:T(8,128)(2,1)}), bf16[4,160,1024]{2,1,0:T(8,128)(2,1)S(1)}, u32[]{:S(2)}, u32[]{:S(2)}) async-start(bf16[4,160,1024]{2,1,0:T(8,128)(2,1)} %bitcast.161), calls=%async_computation.2 | async-start | bytes 2621440 | tf_op jit(solution)/shard_map/all_to_all | solution.py:97
  127.6 16.4 %attention_forward.3 = (bf16[640,1024]{1,0:T(8,128)(2,1)}, bf16[256,1024]{1,0:T(8,128)(2,1)}, bf16[256,3072]{1,0:T(8,128)(2,1)}, f32[16,256]{1,0:T(8,128)}, bf16...) custom-call(bf16[1024,4096]{1,0:T(8,128)(2,1)} %get-tuple-element.78.refs_0_.proj_ref.weights_ref, ...), custom_call_target="tpu_custom_call" | custom-call | flops 1 | bytes 1 | tf_op jit(solution)/shard_map/attention_forward/pallas_call | solution.py:577
  144.1 13.7 %all-to-all-done.2 = bf16[4,160,1024]{2,1,0:T(8,128)(2,1)S(1)} async-done(((bf16[4,160,1024]{2,1,0:T(8,128)(2,1)}), bf16[4,160,1024]{2,1,0:T(8,128)(2,1)S(1)}, u32[]{:S(2)}, u32[]{:S(2)}) %all-to-all-start.2) | async-done | bytes 1310752 | tf_op jit(solution)/shard_map/all_to_all | solution.py:97
  157.8 4.0 all-to-all-start.1
  163.5 33.7 %expert.2 = (bf16[4,2,160,1024]{3,2,1,0:T(8,128)(2,1)}, bf16[640,1152]{1,0:T(8,128)(2,1)}, bf16[2816,1280]{1,0:T(8,128)(2,1)}, bf16[2,1280,2816]{2,1,0:T(8,128)(2,1)}, bf16[1280,1024]{1,0:T(8,128)(2,1)}) custom-call(s32[2]{0:T(128)} %pad_add_fusion.4.mine, bf16[640,1024]{1,0:T(8,128)(2,1)} %bitcast.138, bf16[640,1024]{1,0:T(8,128)(2,1)} %bitcast.147, ...), custom_call_target="tpu_custom_call" | custom-call | flops 1 | bytes 1 | tf_op jit(solution)/shard_map/expert/pallas_call | solution.py:251
  197.3 4.6 %all-to-all-start.3 = ((bf16[4,160,1152]{2,1,0:T(8,128)(2,1)}), bf16[4,160,1152]{2,1,0:T(8,128)(2,1)}, u32[]{:S(2)}, u32[]{:S(2)}) async-start(bf16[4,160,1152]{2,1,0:T(8,128)(2,1)} %bitcast.159), calls=%async_computation.3 | async-start | bytes 2949120 | tf_op jit(solution)/shard_map/all_to_all | solution.py:97
  201.9 33.8 %expert.3 = (bf16[4,2,160,1024]{3,2,1,0:T(8,128)(2,1)}, bf16[640,1152]{1,0:T(8,128)(2,1)}, bf16[2816,1280]{1,0:T(8,128)(2,1)}, bf16[2,1280,2816]{2,1,0:T(8,128)(2,1)}, bf16[1280,1024]{1,0:T(8,128)(2,1)}) custom-call(s32[2]{0:T(128)} %pad_add_fusion.4.mine, ...), custom_call_target="tpu_custom_call", output_to_operand_aliasing={{0}: (7, {}), {2}: (8, {}), {3}: (9, {}), {4}: (10, {})} | custom-call | flops 1 | bytes 1 | tf_op jit(solution)/shard_map/expert/pallas_call | solution.py:251
  235.7 1.6 all-to-all-done.3
  237.3 3.6 all-to-all-start.4
  241.1 22.2 %weight_in.1._ = bf16[8,4224,256]{2,1,0:T(8,128)(2,1)} custom-call(bf16[640,1024]{1,0:T(8,128)(2,1)} %bitcast.139, bf16[640,1024]{1,0:T(8,128)(2,1)} %bitcast.141, bf16[2,1280,2816]{2,1,0:T(8,128)(2,1)} %get-tuple-element.97.refs_2_), custom_call_target="tpu_custom_call" | custom-call | flops 1 | bytes 1 | tf_op jit(solution)/shard_map/weight_in/pallas_call | solution.py:307
  263.3 12.8 %weight_out.1 = bf16[8,4224,256]{2,1,0:T(8,128)(2,1)} custom-call(bf16[2816,1280]{1,0:T(8,128)(2,1)} %get-tuple-element.94.gt_ref, bf16[1280,1024]{1,0:T(8,128)(2,1)} %get-tuple-element.95.dy_ref, bf16[8,4224,256]{2,1,0:T(8,128)(2,1)} %weight_in.1._), custom_call_target="tpu_custom_call", output_to_operand_aliasing={{}: (2, {})} | custom-call | flops 1 | bytes 1 | tf_op jit(solution)/shard_map/weight_out/pallas_call | solution.py:332
  279.3 14.5 %attention_backward.3 = (f32[256,1024]{1,0:T(8,128)}, bf16[256,1024]{1,0:T(8,128)(2,1)}, bf16[256,3072]{1,0:T(8,128)(2,1)}, bf16[16,256,256]{2,1,0:T(8,128)(2,1)...) custom-call(bf16[640,1152]{1,0:T(8,128)(2,1)} %bitcast.146, s32[256,2]{1,0:T(8,128)} %get-tuple-element.184.targets_ref, ...), custom_call_target="tpu_custom_call" | custom-call | flops 1 | bytes 1 | tf_op jit(solution)/shard_map/attention_backward/pallas_call | solution.py:682
  293.8 15.9 %attention_backward.2 = (f32[256,1024]{1,0:T(8,128)}, bf16[256,1024]{1,0:T(8,128)(2,1)}, bf16[256,3072]{1,0:T(8,128)(2,1)}, bf16[16,256,256]{2,1,0:T(8,128)(2,1)...) custom-call(bf16[640,1152]{1,0:T(8,128)(2,1)} %bitcast.45.dx_ref, s32[256,2]{1,0:T(8,128)} %get-tuple-element.187.targets_ref, ...), custom_call_target="tpu_custom_call" | custom-call | flops 1 | bytes 1 | tf_op jit(solution)/shard_map/attention_backward/pallas_call | solution.py:682
  309.8 10.2 %weight_attn.1 = (bf16[4,128,4096]{2,1,0:T(8,128)(2,1)}, bf16[4,128,4096]{2,1,0:T(8,128)(2,1)}) custom-call(s32[1]{0:T(128)S(6)} %select_n.107.core_ref, bf16[256,1024]{1,0:T(8,128)(2,1)} %get-tuple-element.89.refs_0_, bf16[256,1024]{1,0:T(8,128)(2,1)} %get-tuple-element.90.refs_1_, bf16[256,1024]{1,0:T(8,128)(2,1)} %get-tuple-element.91.refs_2_, ...), custom_call_target="tpu_custom_call" | custom-call | flops 1 | bytes 1 | tf_op jit(solution)/shard_map/weight_attn/pallas_call | solution.py:405
  320.0 5.1 %all-to-all-start.5 = ((bf16[4,2,160,1024]{3,2,1,0:T(8,128)(2,1)}), bf16[4,2,160,1024]{3,2,1,0:T(8,128)(2,1)S(1)}, u32[]{:S(2)}, u32[]{:S(2)}) async-start(bf16[4,2,160,1024]{3,2,1,0:T(8,128)(2,1)} %get-tuple-element.115), calls=%async_computation.5 | async-start | bytes 5242880 | tf_op jit(solution)/shard_map/all_to_all | solution.py:97
  325.1 2.9 pad_maximum_fusion
  328.8 3.5 add_convert_fusion
  336.8 9.8 %finish.1 = (bf16[2,256,1024]{2,1,0:T(8,128)(2,1)}, f32[1,1024]{1,0:T(1,128)}) custom-call(bf16[2,256,1024]{2,1,0:T(8,128)(2,1)} %tokens_ref.1, f32[1,1024]{1,0:T(1,128)} %bitcast.179, bf16[1024,4096]{1,0:T(8,128)(2,1)} %get-tuple-element.78.refs_0_.proj_ref.weights_ref, bf16[256,3072]{1,0:T(8,128)(2,1)} %get-tuple-element.117.refs_4_.refs_0_, ...), custom_call_target="tpu_custom_call" | custom-call | flops 1 | bytes 1 | tf_op jit(solution)/shard_map/finish/pallas_call | solution.py:716
  348.9 33.4 %collective-permute-done.10 = bf16[2,1,64,4096]{3,2,1,0:T(8,128)(2,1)} collective-permute-done((bf16[2,1,64,4096]{3,2,1,0:T(8,128)(2,1)}, bf16[2,1,64,4096]{3,2,1,0:T(8,128)(2,1)}, u32[]{:S(2)}, u32[]{:S(2)}) %collective-permute-start.10) | collective-permute-done | bytes 1048608 | tf_op jit(solution)/shard_map/ppermute | solution.py:52
  382.3 1.6 fusion.7
  387.6 15.4 %collective-permute-done.11 = bf16[1,1,64,4096]{3,2,1,0:T(8,128)(2,1)S(1)} collective-permute-done((bf16[1,1,64,4096]{3,2,1,0:T(8,128)(2,1)S(1)}, bf16[1,1,64,4096]{3,2,1,0:T(8,128)(2,1)S(1)}, u32[]{:S(2)}, u32[]{:S(2)}) %collective-permute-start.11) | collective-permute-done | bytes 524320 | tf_op jit(solution)/shard_map/ppermute | solution.py:52
  403.0 4.9 %collective-permute-done.13 = bf16[1,1,64,4096]{3,2,1,0:T(8,128)(2,1)S(1)} collective-permute-done((bf16[1,1,64,4096]{3,2,1,0:T(8,128)(2,1)S(1)}, bf16[1,1,64,4096]{3,2,1,0:T(8,128)(2,1)S(1)}, u32[]{:S(2)}, u32[]{:S(2)}) %collective-permute-start.13) | collective-permute-done | bytes 524320 | tf_op jit(solution)/shard_map/ppermute | solution.py:52
  409.3 5.2 %all-to-all-start.6 = ((bf16[4,32,4096]{2,1,0:T(8,128)(2,1)}), bf16[4,32,4096]{2,1,0:T(8,128)(2,1)}, u32[]{:S(2)}, u32[]{:S(2)}) async-start(bf16[4,32,4096]{2,1,0:T(8,128)(2,1)} %bitcast.151), calls=%async_computation.6 | async-start | bytes 2097152 | tf_op jit(solution)/shard_map/all_to_all | solution.py:97
  417.2 1.6 collective-permute-start.15
  418.8 2.9 collective-permute-done.15
  423.2 2.5 collective-permute-done.16
  425.7 2.9 collective-permute-start.17
  430.1 2.6 collective-permute-start.19
  432.7 5.5 %output.1 = bf16[2,256,1024]{2,1,0:T(8,128)(2,1)} custom-call(bf16[4,2,160,1024]{3,2,1,0:T(8,128)(2,1)} %copy-done.4, s32[2,256,2]{2,1,0:T(8,128)} %copy-done.12, s32[2,256,2]{2,1,0:T(8,128)} %copy-done.16, f32[256,128]{1,0:T(8,128)} %get-tuple-element.101.probs_ref.refs_0_, f32[256,128]{1,0:T(8,128)} %get-tuple-element.107.probs_ref.refs_1_, ...), custom_call_target="tpu_custom_call" | custom-call | flops 1 | bytes 1 | tf_op jit(solution)/shard_map/output/pallas_call | solution.py:754
  443.9 3.8 spread.1
  (175 shorter events, 54.9 us)
Async XLA Ops:
  7.2 32.5 %copy-start = (f32[32,16]{0,1:T(8,128)S(1)}, f32[32,16]{0,1:T(8,128)}, u32[]{:S(2)}) copy-start(f32[32,16]{0,1:T(8,128)} %param.21) | copy-start | bytes 6148
  7.2 155.2 %all-gather.6.cloned.1.call-start = ((), (), s32[]{:S(2)}) async-start(), calls=%async_computation.10 | async-start | bytes 6488064 | tf_op jit(solution)/shard_map/all_gather | solution.py:811
  9.0 22.0 %collective-permute-start = (bf16[32,4096]{1,0:T(8,128)(2,1)S(1)}, bf16[32,4096]{1,0:T(8,128)(2,1)}, u32[]{:S(2)}, u32[]{:S(2)}) collective-permute-start(bf16[32,4096]{1,0:T(8,128)(2,1)S(1)} %constant_dynamic-update-slice_fusion), channel_id=1, source_target_pairs={{0,1},{1,2},{2,3},{3,0},{4,5},{5,6},{6,7},{7,4},{8,9},{9,10},{10,1... | collective-permute-start | bytes 786440 | tf_op jit(solution)/shard_map/ppermute | solution.py:56
  12.1 20.7 %collective-permute-start.1 = (bf16[32,4096]{1,0:T(8,128)(2,1)S(1)}, bf16[32,4096]{1,0:T(8,128)(2,1)}, u32[]{:S(2)}, u32[]{:S(2)}) collective-permute-start(bf16[32,4096]{1,0:T(8,128)(2,1)S(1)} %constant_dynamic-update-slice_fusion), channel_id=1, source_target_pairs={{0,2},{1,3},{2,0},{3,1},{4,6},{5,7},{6,4},{7,5},{8,10},{9,11},{10,... | collective-permute-start | bytes 786440 | tf_op jit(solution)/shard_map/ppermute | solution.py:56
  14.6 19.7 %collective-permute-start.2 = (bf16[32,4096]{1,0:T(8,128)(2,1)S(1)}, bf16[32,4096]{1,0:T(8,128)(2,1)S(1)}, u32[]{:S(2)}, u32[]{:S(2)}) collective-permute-start(bf16[32,4096]{1,0:T(8,128)(2,1)S(1)} %constant_dynamic-update-slice_fusion), channel_id=1, source_target_pairs={{0,3},{1,0},{2,1},{3,2},{4,7},{5,4},{6,5},{7,6},{8,11},{9,8},{10,9... | collective-permute-start | bytes 786440 | tf_op jit(solution)/shard_map/ppermute | solution.py:56
  21.1 74.8 %copy-start.12 = (s32[2,256,2]{2,1,0:T(8,128)}, s32[2,256,2]{2,1,0:T(8,128)S(1)}, u32[]{:S(2)}) copy-start(s32[2,256,2]{2,1,0:T(8,128)S(1)} %bitcast_add_fusion.targets_ref) | copy-start | bytes 12292
  25.3 68.2 %all-to-all-start = ((bf16[4,2,160,1024]{3,2,1,0:T(8,128)(2,1)}), bf16[4,2,160,1024]{3,2,1,0:T(8,128)(2,1)S(1)}, u32[]{:S(2)}, u32[]{:S(2)}) async-start(bf16[4,2,160,1024]{3,2,1,0:T(8,128)(2,1)} %pad_maximum_fusion.1), calls=%async_computation | async-start | bytes 5242880 | tf_op jit(solution)/shard_map/all_to_all | solution.py:97
  29.0 134.6 %all-gather.4.cloned.1.call-start = ((), (), s32[]{:S(2)}) async-start(), calls=%async_computation.8 | async-start | bytes 12976128 | tf_op jit(solution)/shard_map/all_gather | solution.py:812
  36.4 23.7 %collective-permute-start.5 = (bf16[1,64,4096]{2,1,0:T(8,128)(2,1)S(1)}, bf16[1,64,4096]{2,1,0:T(8,128)(2,1)S(1)}, u32[]{:S(2)}, u32[]{:S(2)}) collective-permute-start(bf16[1,64,4096]{2,1,0:T(8,128)(2,1)S(1)} %bitcast.156), channel_id=1, source_target_pairs={{0,16},{4,20},{8,24},{12,28},{16,0},{20,4},{24,8},{28,12},{1,17},{... | collective-permute-start | bytes 1572872 | tf_op jit(solution)/shard_map/ppermute | solution.py:52
  38.1 25.7 %collective-permute-start.3 = (bf16[1,64,4096]{2,1,0:T(8,128)(2,1)S(1)}, bf16[1,64,4096]{2,1,0:T(8,128)(2,1)S(1)}, u32[]{:S(2)}, u32[]{:S(2)}) collective-permute-start(bf16[1,64,4096]{2,1,0:T(8,128)(2,1)S(1)} %bitcast.154), channel_id=1, source_target_pairs={{0,8},{4,12},{8,0},{12,4},{16,24},{20,28},{24,16},{28,20},{1,9},{5... | collective-permute-start | bytes 1572872 | tf_op jit(solution)/shard_map/ppermute | solution.py:52
  60.2 28.5 %collective-permute-start.6 = (bf16[2,64,4096]{2,1,0:T(8,128)(2,1)S(1)}, bf16[2,64,4096]{2,1,0:T(8,128)(2,1)S(1)}, u32[]{:S(2)}, u32[]{:S(2)}) collective-permute-start(bf16[2,64,4096]{2,1,0:T(8,128)(2,1)S(1)} %pad_maximum_fusion.4), channel_id=1, source_target_pairs={{0,8},{4,12},{8,0},{12,4},{16,24},{20,28},{24,16},{28,20},{1,9},{5... | collective-permute-start | bytes 3145736 | tf_op jit(solution)/shard_map/ppermute | solution.py:52
  63.9 24.9 %collective-permute-start.4 = (bf16[2,64,4096]{2,1,0:T(8,128)(2,1)S(1)}, bf16[2,64,4096]{2,1,0:T(8,128)(2,1)S(1)}, u32[]{:S(2)}, u32[]{:S(2)}) collective-permute-start(bf16[2,64,4096]{2,1,0:T(8,128)(2,1)S(1)} %pad_maximum_fusion.3), channel_id=1, source_target_pairs={{0,16},{4,20},{8,24},{12,28},{16,0},{20,4},{24,8},{28,12},{1,17},{... | collective-permute-start | bytes 3145736 | tf_op jit(solution)/shard_map/ppermute | solution.py:52
  95.3 5.1 %copy-start.24 = (bf16[1024,4]{0,1:T(4,128)(2,1)S(1)}, bf16[1024,4]{0,1:T(4,128)(2,1)}, u32[]{:S(2)}) copy-start(bf16[1024,4]{0,1:T(4,128)(2,1)} %param.23) | copy-start | bytes 24580
  95.3 6.1 %copy-start.15 = (bf16[2,256,1024]{2,1,0:T(8,128)(2,1)S(1)}, bf16[2,256,1024]{2,1,0:T(8,128)(2,1)}, u32[]{:S(2)}) copy-start(bf16[2,256,1024]{2,1,0:T(8,128)(2,1)} %tokens_ref.1) | copy-start | bytes 3145732
  95.4 7.1 %collective-permute-start.8 = (bf16[4,64,4096]{2,1,0:T(8,128)(2,1)}, bf16[4,64,4096]{2,1,0:T(8,128)(2,1)S(1)}, u32[]{:S(2)}, u32[]{:S(2)}) collective-permute-start(bf16[4,64,4096]{2,1,0:T(8,128)(2,1)} %copy-done.10), channel_id=1, source_target_pairs={{0,4},{4,0},{8,12},{12,8},{16,20},{20,16},{24,28},{28,24},{1,5},{5... | collective-permute-start | bytes 6291464 | tf_op jit(solution)/shard_map/ppermute | solution.py:52
  95.4 7.5 %collective-permute-start.7 = (bf16[4,64,4096]{2,1,0:T(8,128)(2,1)}, bf16[4,64,4096]{2,1,0:T(8,128)(2,1)}, u32[]{:S(2)}, u32[]{:S(2)}) collective-permute-start(bf16[4,64,4096]{2,1,0:T(8,128)(2,1)} %constant_dynamic-update-slice_fusion.2.refs_1_), channel_id=1, source_target_pairs={{0,4},{4,0},{8,12},{12,8},{16,20},{20,16},{24,28},{28,24},{1,5},{5... | collective-permute-start | bytes 6291464 | tf_op jit(solution)/shard_map/ppermute | solution.py:52
  99.6 3.3 copy-start.22
  121.4 5.4 %copy-start.27 = (s32[1,256]{1,0:T(1,128)S(1)}, s32[1,256]{1,0:T(1,128)}, u32[]{:S(2)}) copy-start(s32[1,256]{1,0:T(1,128)} %get-tuple-element.199) | copy-start | bytes 3076
  121.4 36.4 %all-to-all-start.2 = ((bf16[4,160,1024]{2,1,0:T(8,128)(2,1)}), bf16[4,160,1024]{2,1,0:T(8,128)(2,1)S(1)}, u32[]{:S(2)}, u32[]{:S(2)}) async-start(bf16[4,160,1024]{2,1,0:T(8,128)(2,1)} %bitcast.161), calls=%async_computation.2 | async-start | bytes 2621440 | tf_op jit(solution)/shard_map/all_to_all | solution.py:97
  157.8 5.8 %copy-start.2 = (bf16[4,160,1024]{2,1,0:T(8,128)(2,1)}, bf16[4,160,1024]{2,1,0:T(8,128)(2,1)S(1)}, u32[]{:S(2)}) copy-start(bf16[4,160,1024]{2,1,0:T(8,128)(2,1)S(1)} %all-to-all-done.2) | copy-start | bytes 3932164
  157.8 39.5 %all-to-all-start.1 = ((bf16[4,160,1024]{2,1,0:T(8,128)(2,1)}), bf16[4,160,1024]{2,1,0:T(8,128)(2,1)S(1)}, u32[]{:S(2)}, u32[]{:S(2)}) async-start(bf16[4,160,1024]{2,1,0:T(8,128)(2,1)} %bitcast.162), calls=%async_computation.1 | async-start | bytes 2621440 | tf_op jit(solution)/shard_map/all_to_all | solution.py:97
  197.3 4.6 %copy-start.3 = (bf16[4,160,1024]{2,1,0:T(8,128)(2,1)}, bf16[4,160,1024]{2,1,0:T(8,128)(2,1)S(1)}, u32[]{:S(2)}) copy-start(bf16[4,160,1024]{2,1,0:T(8,128)(2,1)S(1)} %all-to-all-done.1) | copy-start | bytes 3932164
  197.3 40.0 %all-to-all-start.3 = ((bf16[4,160,1152]{2,1,0:T(8,128)(2,1)}), bf16[4,160,1152]{2,1,0:T(8,128)(2,1)}, u32[]{:S(2)}, u32[]{:S(2)}) async-start(bf16[4,160,1152]{2,1,0:T(8,128)(2,1)} %bitcast.159), calls=%async_computation.3 | async-start | bytes 2949120 | tf_op jit(solution)/shard_map/all_to_all | solution.py:97
  237.3 38.8 %all-to-all-start.4 = ((bf16[4,160,1152]{2,1,0:T(8,128)(2,1)}), bf16[4,160,1152]{2,1,0:T(8,128)(2,1)S(1)}, u32[]{:S(2)}, u32[]{:S(2)}) async-start(bf16[4,160,1152]{2,1,0:T(8,128)(2,1)} %bitcast.158), calls=%async_computation.4 | async-start | bytes 2949120 | tf_op jit(solution)/shard_map/all_to_all | solution.py:97
  240.9 203.0 %reduce-scatter.2.cloned.1.call-start = ((), (), s32[]{:S(2)}) async-start(), calls=%async_computation.9 | async-start | bytes 19464192 | tf_op jit(solution)/shard_map/reduce_scatter | solution.py:892
  277.4 16.4 %copy-start.16 = (s32[2,256,2]{2,1,0:T(8,128)}, s32[2,256,2]{2,1,0:T(8,128)S(1)}, u32[]{:S(2)}) copy-start(s32[2,256,2]{2,1,0:T(8,128)S(1)} %copy.106.routes_ref) | copy-start | bytes 12292
  320.0 8.1 %collective-permute-start.9 = (bf16[4,128,4096]{2,1,0:T(8,128)(2,1)}, bf16[4,128,4096]{2,1,0:T(8,128)(2,1)}, u32[]{:S(2)}, u32[]{:S(2)}) collective-permute-start(bf16[4,128,4096]{2,1,0:T(8,128)(2,1)} %get-tuple-element.116), channel_id=1, source_target_pairs={{0,4},{4,0},{8,12},{12,8},{16,20},{20,16},{24,28},{28,24},{1,5},{5... | collective-permute-start | bytes 12582920 | tf_op jit(solution)/shard_map/ppermute | solution.py:52
  320.0 89.2 %all-to-all-start.5 = ((bf16[4,2,160,1024]{3,2,1,0:T(8,128)(2,1)}), bf16[4,2,160,1024]{3,2,1,0:T(8,128)(2,1)S(1)}, u32[]{:S(2)}, u32[]{:S(2)}) async-start(bf16[4,2,160,1024]{3,2,1,0:T(8,128)(2,1)} %get-tuple-element.115), calls=%async_computation.5 | async-start | bytes 5242880 | tf_op jit(solution)/shard_map/all_to_all | solution.py:97
  325.1 3.7 copy-start.11
  332.6 3.7 copy-start.5
  332.6 3.7 copy-start.7
  333.8 48.5 %collective-permute-start.10 = (bf16[2,1,64,4096]{3,2,1,0:T(8,128)(2,1)}, bf16[2,1,64,4096]{3,2,1,0:T(8,128)(2,1)}, u32[]{:S(2)}, u32[]{:S(2)}) collective-permute-start(bf16[2,1,64,4096]{3,2,1,0:T(8,128)(2,1)} %dynamic-slice_bitcast_fusion.1), channel_id=1, source_target_pairs={{0,8},{4,12},{8,0},{12,4},{16,24},{20,28},{24,16},{28,20},{1,9},{5... | collective-permute-start | bytes 3145736 | tf_op jit(solution)/shard_map/ppermute | solution.py:52
  336.3 48.8 %collective-permute-start.12 = (bf16[1,2,64,4096]{3,2,1,0:T(8,128)(2,1)}, bf16[1,2,64,4096]{3,2,1,0:T(8,128)(2,1)}, u32[]{:S(2)}, u32[]{:S(2)}) collective-permute-start(bf16[1,2,64,4096]{3,2,1,0:T(8,128)(2,1)} %dynamic-slice_bitcast_fusion), channel_id=1, source_target_pairs={{0,16},{4,20},{8,24},{12,28},{16,0},{20,4},{24,8},{28,12},{1,17},{... | collective-permute-start | bytes 3145736 | tf_op jit(solution)/shard_map/ppermute | solution.py:52
  347.6 34.8 %copy-start.8 = (bf16[4,64,4096]{2,1,0:T(8,128)(2,1)S(1)}, bf16[4,64,4096]{2,1,0:T(8,128)(2,1)}, u32[]{:S(2)}) copy-start(bf16[4,64,4096]{2,1,0:T(8,128)(2,1)} %copy-done.7) | copy-start | bytes 6291460
  384.0 19.0 %collective-permute-start.11 = (bf16[1,1,64,4096]{3,2,1,0:T(8,128)(2,1)S(1)}, bf16[1,1,64,4096]{3,2,1,0:T(8,128)(2,1)S(1)}, u32[]{:S(2)}, u32[]{:S(2)}) collective-permute-start(bf16[1,1,64,4096]{3,2,1,0:T(8,128)(2,1)S(1)} %constant_dynamic-slice_fusion.1), channel_id=1, source_target_pairs={{0,16},{4,20},{8,24},{12,28},{16,0},{20,4},{24,8},{28,12},{1,17},{... | collective-permute-start | bytes 1572872 | tf_op jit(solution)/shard_map/ppermute | solution.py:52
  386.7 21.2 %collective-permute-start.13 = (bf16[1,1,64,4096]{3,2,1,0:T(8,128)(2,1)S(1)}, bf16[1,1,64,4096]{3,2,1,0:T(8,128)(2,1)S(1)}, u32[]{:S(2)}, u32[]{:S(2)}) collective-permute-start(bf16[1,1,64,4096]{3,2,1,0:T(8,128)(2,1)S(1)} %constant_dynamic-slice_fusion), channel_id=1, source_target_pairs={{0,8},{4,12},{8,0},{12,4},{16,24},{20,28},{24,16},{28,20},{1,9},{5... | collective-permute-start | bytes 1572872 | tf_op jit(solution)/shard_map/ppermute | solution.py:52
  409.2 6.5 %copy-start.25 = (f32[1,1024]{1,0:T(1,128)S(1)}, f32[1,1024]{1,0:T(1,128)}, u32[]{:S(2)}) copy-start(f32[1,1024]{1,0:T(1,128)} %get-tuple-element.132) | copy-start | bytes 12292
  409.2 6.5 %copy-start.26 = (f32[1,1024]{1,0:T(1,128)S(1)}, f32[1,1024]{1,0:T(1,128)}, u32[]{:S(2)}) copy-start(f32[1,1024]{1,0:T(1,128)} %get-tuple-element.131) | copy-start | bytes 12292
  409.2 6.7 %copy-start.21 = (f32[1,1024]{1,0:T(1,128)S(1)}, f32[1,1024]{1,0:T(1,128)}, u32[]{:S(2)}) copy-start(f32[1,1024]{1,0:T(1,128)} %get-tuple-element.130) | copy-start | bytes 12292
  409.3 23.5 %copy-start.4 = (bf16[4,2,160,1024]{3,2,1,0:T(8,128)(2,1)}, bf16[4,2,160,1024]{3,2,1,0:T(8,128)(2,1)S(1)}, u32[]{:S(2)}) copy-start(bf16[4,2,160,1024]{3,2,1,0:T(8,128)(2,1)S(1)} %all-to-all-done.5.y_ref) | copy-start | bytes 7864324
  409.3 31.7 %all-to-all-start.6 = ((bf16[4,32,4096]{2,1,0:T(8,128)(2,1)}), bf16[4,32,4096]{2,1,0:T(8,128)(2,1)}, u32[]{:S(2)}, u32[]{:S(2)}) async-start(bf16[4,32,4096]{2,1,0:T(8,128)(2,1)} %bitcast.151), calls=%async_computation.6 | async-start | bytes 2097152 | tf_op jit(solution)/shard_map/all_to_all | solution.py:97
  415.9 1.3 collective-permute-start.14
  417.2 4.5 collective-permute-start.15
  421.8 3.9 collective-permute-start.16
  425.7 12.5 %collective-permute-start.17 = (f32[52,128]{1,0:T(8,128)S(1)}, f32[52,128]{1,0:T(8,128)S(1)}, u32[]{:S(2)}, u32[]{:S(2)}) collective-permute-start(f32[52,128]{1,0:T(8,128)S(1)} %add.221), channel_id=1, source_target_pairs={{0,2},{1,3},{2,0},{3,1},{4,6},{5,7},{6,4},{7,5},{8,10},{9,11},{10,... | collective-permute-start | bytes 79880 | tf_op jit(solution)/shard_map/ppermute | solution.py:56
  428.6 9.6 %collective-permute-start.18 = (f32[52,128]{1,0:T(8,128)S(1)}, f32[52,128]{1,0:T(8,128)S(1)}, u32[]{:S(2)}, u32[]{:S(2)}) collective-permute-start(f32[52,128]{1,0:T(8,128)S(1)} %add.221), channel_id=1, source_target_pairs={{0,1},{1,2},{2,3},{3,0},{4,5},{5,6},{6,7},{7,4},{8,9},{9,10},{10,1... | collective-permute-start | bytes 79880 | tf_op jit(solution)/shard_map/ppermute | solution.py:56
  430.1 8.2 %collective-permute-start.19 = (f32[52,128]{1,0:T(8,128)S(1)}, f32[52,128]{1,0:T(8,128)S(1)}, u32[]{:S(2)}, u32[]{:S(2)}) collective-permute-start(f32[52,128]{1,0:T(8,128)S(1)} %add.221), channel_id=1, source_target_pairs={{0,3},{1,0},{2,1},{3,2},{4,7},{5,4},{6,5},{7,6},{8,11},{9,8},{10,9... | collective-permute-start | bytes 79880 | tf_op jit(solution)/shard_map/ppermute | solution.py:56
  440.4 7.3 %copy-start.1 = (f32[32,16]{0,1:T(8,128)S(1)}, f32[32,16]{0,1:T(8,128)}, u32[]{:S(2)}) copy-start(f32[32,16]{0,1:T(8,128)} %param.21) | copy-start | bytes 6148
  (11 other events, 17.5 us)
Sparse Core Ops, SparseCore 0:
  16.1 56.6 all-gather.5
  95.5 68.0 all-gather.3
  276.3 148.3 reduce-scatter.1

commit v7 on v6

--- a/solution.py
+++ b/solution.py
@@ -361,7 +361,7 @@
     return pl.pallas_call(
         partial(spread_body, in_shape[1] // summed.shape[1]),
         out_shape=[jax.ShapeDtypeStruct(shape, F32) for shape in (in_shape, out_shape)],
-        compiler_params=pltpu.CompilerParams(vmem_limit_bytes=56 << 20),
+        compiler_params=pltpu.CompilerParams(vmem_limit_bytes=32 << 20),
         cost_estimate=LIGHT,
         name="spread",
     )(summed)
@@ -415,7 +415,7 @@
             pltpu.VMEM((width, count * length), BF16),
             pltpu.VMEM((count * length, width), BF16),
         ],
-        compiler_params=pltpu.CompilerParams(vmem_limit_bytes=56 << 20),
+        compiler_params=pltpu.CompilerParams(vmem_limit_bytes=32 << 20),
         cost_estimate=LIGHT,
         name="weight_attn",
     )(core, *n1s, *os, *dqkvs, *dbranches)
@@ -580,7 +580,7 @@
         out_specs=out_specs,
         out_shape=[jax.ShapeDtypeStruct(*s) for s in shapes],
         scratch_shapes=scratch,
-        compiler_params=pltpu.CompilerParams(vmem_limit_bytes=56 << 20),
+        compiler_params=pltpu.CompilerParams(vmem_limit_bytes=32 << 20),
         cost_estimate=LIGHT,
         name="attention_forward",
     )(*args)
@@ -686,7 +686,7 @@
         out_specs=[pl.BlockSpec(s, lambda i, n=len(s): (0,) * n) for s, _ in shapes],
         out_shape=[jax.ShapeDtypeStruct(*s) for s in shapes],
         scratch_shapes=[pltpu.VMEM((length, width), BF16)],
-        compiler_params=pltpu.CompilerParams(vmem_limit_bytes=56 << 20),
+        compiler_params=pltpu.CompilerParams(vmem_limit_bytes=32 << 20),
         cost_estimate=LIGHT,
         name="attention_backward",
     )(*args)
@@ -725,7 +725,7 @@
             jax.ShapeDtypeStruct(tokens.shape, BF16),
             jax.ShapeDtypeStruct(gain.shape, F32),
         ],
-        compiler_params=pltpu.CompilerParams(vmem_limit_bytes=56 << 20),
+        compiler_params=pltpu.CompilerParams(vmem_limit_bytes=32 << 20),
         cost_estimate=LIGHT,
         name="finish",
     )(*args)
@@ -754,7 +754,7 @@
     return pl.pallas_call(
         partial(output_body, len(h1s)),
         out_shape=jax.ShapeDtypeStruct((len(h1s), length, width), BF16),
-        compiler_params=pltpu.CompilerParams(vmem_limit_bytes=56 << 20),
+        compiler_params=pltpu.CompilerParams(vmem_limit_bytes=32 << 20),
         cost_estimate=LIGHT,
         name="output",
     )(y, targets, routes, *probs, *h1s)

time: 459 us -> 458 us (level)
  Pallas kernels: 196 us -> 163 us
  local copies, waits for them, and re-layouts: 41.3 us -> 65.3 us
  waiting for transfers between devices: 119 us -> 125 us
    unnamed x65 -> x149, local copies, waits for them, and re-layouts: 9.03 us -> 43.8 us
    pallas_call x2, Pallas kernels: 34.1 us -> 21.4 us  [forward_call(): pl.pallas_call(partial(forward_body, heads, experts, rels), in_specs=in_s...]
    pallas_call x2, Pallas kernels: 30.5 us -> 20.2 us  [backward_call(): pl.pallas_call(partial(backward_body, heads, experts), grid=(1,), in_spec...]
    ppermute x14, waiting for transfers between devices: 99.8 us -> 105 us  [flip(): return lax.ppermute(value, axis, [(i, i ^ bit) for i in range(size)])]
    dynamic_update_slice x4, local copies, waits for them, and re-layouts: 4.78 us -> 0.09 us  [gather_expert(): lax.dynamic_update_slice(full, piece[None], ((me - step) % size, 0, 0))]
    pallas_call x1, Pallas kernels: 9.81 us -> 5.16 us  [finish_call(): pl.pallas_call(partial(finish_body, len(dqkvs)), grid=(1,), in_specs=in_s...]
  transfers between devices with their start and end apart: 30 -> 30, of which waited for: 14 -> 16; matrix products, arithmetic and copies ran while one was open for 13% -> 10% of each run, Pallas kernels for 42% -> 36%
where the time goes in v7:
time: 458 us; the launch traced here: 450 us
  Pallas kernels  163 us (36%)
  waiting for transfers between devices  125 us (27%)
  local copies, waits for them, and re-layouts  65.3 us (14%)
  starting transfers between devices  58.3 us (13%)
  other arithmetic  18.4 us (4%)
  between operations  15 us (3%)
  matrix products  5.21 us (1%)
    ppermute x14, waiting for transfers between devices, flip(): return lax.ppermute(value, axis, [(i, i ^ bit) for i in range(size)])  105 us
    pallas_call x2, Pallas kernels, expert_call(): pl.pallas_call(expert_body, grid=(tiles,), in_specs=in_specs, out_specs=[...  67.6 us
    unnamed x149, local copies, waits for them, and re-layouts  43.8 us
    all_to_all x7, starting transfers between devices, all_to_all(): lax.all_to_all(value, 'expert', split_axis=0, concat_axis=0, tiled=True)  31.4 us
    pallas_call x1, Pallas kernels, weight_in_call(): pl.pallas_call(weight_in_body, grid=(2,), in_specs=[pl.BlockSpec((rows, w...  22.2 us
    pallas_call x2, Pallas kernels, forward_call(): pl.pallas_call(partial(forward_body, heads, experts, rels), in_specs=in_s...  21.4 us
    pallas_call x2, Pallas kernels, backward_call(): pl.pallas_call(partial(backward_body, heads, experts), grid=(1,), in_spec...  20.2 us
    all_to_all x7, waiting for transfers between devices, all_to_all(): lax.all_to_all(value, 'expert', split_axis=0, concat_axis=0, tiled=True)  18.1 us
  transfers between devices with their start and end apart: 30, of which 16 were waited for; matrix products, arithmetic and copies ran while one was open for 10% of the time, Pallas kernels for 36%

profile of v7, /device:TPU:0, one launch (start us, length us, event | category | flops | bytes accessed | tf_op | source)
XLA Modules:
  0.0 449.5 jit_solution(8499839136043382962)
XLA Ops:
  9.0 3.0 collective-permute-start
  12.1 2.6 collective-permute-start.1
  16.8 2.4 reduce-window.6
  23.5 1.7 pad_maximum_fusion.1
  25.2 4.5 %all-to-all-start = ((bf16[4,2,160,1024]{3,2,1,0:T(8,128)(2,1)}), bf16[4,2,160,1024]{3,2,1,0:T(8,128)(2,1)}, u32[]{:S(2)}, u32[]{:S(2)}) async-start(bf16[4,2,160,1024]{3,2,1,0:T(8,128)(2,1)} %pad_maximum_fusion.1), calls=%async_computation | async-start | bytes 5242880 | tf_op jit(solution)/shard_map/all_to_all | solution.py:97
  30.0 1.7 collective-permute-done.1
  35.3 2.8 fusion
  38.1 4.4 copy.125
  42.5 9.7 %collective-permute-done.5 = bf16[1,64,4096]{2,1,0:T(8,128)(2,1)S(1)} collective-permute-done((bf16[1,64,4096]{2,1,0:T(8,128)(2,1)S(1)}, bf16[1,64,4096]{2,1,0:T(8,128)(2,1)S(1)}, u32[]{:S(2)}, u32[]{:S(2)}) %collective-permute-start.5) | collective-permute-done | bytes 524320 | tf_op jit(solution)/shard_map/ppermute | solution.py:52
  53.5 3.2 collective-permute-done.3
  57.1 28.1 %collective-permute-done.6 = bf16[2,64,4096]{2,1,0:T(8,128)(2,1)S(1)} collective-permute-done((bf16[2,64,4096]{2,1,0:T(8,128)(2,1)S(1)}, bf16[2,64,4096]{2,1,0:T(8,128)(2,1)S(1)}, u32[]{:S(2)}, u32[]{:S(2)}) %collective-permute-start.6) | collective-permute-done | bytes 1048608 | tf_op jit(solution)/shard_map/ppermute | solution.py:52
  86.7 6.9 %all-to-all-done = bf16[4,2,160,1024]{3,2,1,0:T(8,128)(2,1)} async-done(((bf16[4,2,160,1024]{3,2,1,0:T(8,128)(2,1)}), bf16[4,2,160,1024]{3,2,1,0:T(8,128)(2,1)}, u32[]{:S(2)}, u32[]{:S(2)}) %all-to-all-start) | async-done | bytes 2621472 | tf_op jit(solution)/shard_map/all_to_all | solution.py:97
  93.6 3.4 fusion.29
  100.3 3.5 collective-permute-done.8.refs_4_
  104.4 2.6 copy-done.3
  107.0 11.7 %attention_forward.2 = (bf16[640,1024]{1,0:T(8,128)(2,1)S(1)}, bf16[256,1024]{1,0:T(8,128)(2,1)S(1)}, bf16[256,3072]{1,0:T(8,128)(2,1)S(1)}, f32[16,256]{1,0:T(8...) custom-call(s32[1]{0:T(128)} %bitcast.1.refs_0_, ...), custom_call_target="tpu_custom_call" | custom-call | flops 1 | bytes 1 | tf_op jit(solution)/shard_map/attention_forward/pallas_call | solution.py:577
  124.2 4.1 all-to-all-start.2
  128.6 4.9 %copy-done.2 = bf16[1024,4096]{1,0:T(8,128)(2,1)S(1)} copy-done((bf16[1024,4096]{1,0:T(8,128)(2,1)S(1)}, bf16[1024,4096]{1,0:T(8,128)(2,1)}, u32[]{:S(2)}) %copy-start.2) | copy-done | bytes 8388632
  133.5 2.2 copy-done.4
  135.7 9.7 %attention_forward.3 = (bf16[640,1024]{1,0:T(8,128)(2,1)}, bf16[256,1024]{1,0:T(8,128)(2,1)S(1)}, bf16[256,3072]{1,0:T(8,128)(2,1)S(1)}, f32[16,256]{1,0:T(8,128...) custom-call(bf16[1024,4096]{1,0:T(8,128)(2,1)S(1)} %copy-done.2, ...), custom_call_target="tpu_custom_call" | custom-call | flops 1 | bytes 1 | tf_op jit(solution)/shard_map/attention_forward/pallas_call | solution.py:577
  149.9 10.1 %all-to-all-done.2 = bf16[4,160,1024]{2,1,0:T(8,128)(2,1)S(1)} async-done(((bf16[4,160,1024]{2,1,0:T(8,128)(2,1)}), bf16[4,160,1024]{2,1,0:T(8,128)(2,1)S(1)}, u32[]{:S(2)}, u32[]{:S(2)}) %all-to-all-start.2) | async-done | bytes 1310752 | tf_op jit(solution)/shard_map/all_to_all | solution.py:97
  160.0 3.5 all-to-all-start.1
  164.2 33.8 %expert.2 = (bf16[4,2,160,1024]{3,2,1,0:T(8,128)(2,1)}, bf16[640,1152]{1,0:T(8,128)(2,1)}, bf16[2816,1280]{1,0:T(8,128)(2,1)}, bf16[2,1280,2816]{2,1,0:T(8,128)(2,1)}, bf16[1280,1024]{1,0:T(8,128)(2,1)}) custom-call(s32[2]{0:T(128)} %pad_add_fusion.4.mine, bf16[640,1024]{1,0:T(8,128)(2,1)} %bitcast.159, bf16[640,1024]{1,0:T(8,128)(2,1)} %bitcast.167, ...), custom_call_target="tpu_custom_call" | custom-call | flops 1 | bytes 1 | tf_op jit(solution)/shard_map/expert/pallas_call | solution.py:251
  198.0 5.2 %all-to-all-start.3 = ((bf16[4,160,1152]{2,1,0:T(8,128)(2,1)}), bf16[4,160,1152]{2,1,0:T(8,128)(2,1)S(1)}, u32[]{:S(2)}, u32[]{:S(2)}) async-start(bf16[4,160,1152]{2,1,0:T(8,128)(2,1)} %bitcast.177), calls=%async_computation.3 | async-start | bytes 2949120 | tf_op jit(solution)/shard_map/all_to_all | solution.py:97
  203.2 33.8 %expert.3 = (bf16[4,2,160,1024]{3,2,1,0:T(8,128)(2,1)}, bf16[640,1152]{1,0:T(8,128)(2,1)}, bf16[2816,1280]{1,0:T(8,128)(2,1)}, bf16[2,1280,2816]{2,1,0:T(8,128)(2,1)}, bf16[1280,1024]{1,0:T(8,128)(2,1)}) custom-call(s32[2]{0:T(128)} %pad_add_fusion.4.mine, ...), custom_call_target="tpu_custom_call", output_to_operand_aliasing={{0}: (7, {}), {2}: (8, {}), {3}: (9, {}), {4}: (10, {})} | custom-call | flops 1 | bytes 1 | tf_op jit(solution)/shard_map/expert/pallas_call | solution.py:251
  238.1 4.0 all-to-all-start.4
  242.1 22.2 %weight_in.1._ = bf16[8,4224,256]{2,1,0:T(8,128)(2,1)} custom-call(bf16[640,1024]{1,0:T(8,128)(2,1)} %bitcast.160, bf16[640,1024]{1,0:T(8,128)(2,1)} %bitcast.162, bf16[2,1280,2816]{2,1,0:T(8,128)(2,1)} %get-tuple-element.97.refs_2_), custom_call_target="tpu_custom_call" | custom-call | flops 1 | bytes 1 | tf_op jit(solution)/shard_map/weight_in/pallas_call | solution.py:307
  264.4 13.1 %weight_out.1 = bf16[8,4224,256]{2,1,0:T(8,128)(2,1)} custom-call(bf16[2816,1280]{1,0:T(8,128)(2,1)} %get-tuple-element.94.gt_ref, bf16[1280,1024]{1,0:T(8,128)(2,1)} %get-tuple-element.95.dy_ref, bf16[8,4224,256]{2,1,0:T(8,128)(2,1)} %weight_in.1._), custom_call_target="tpu_custom_call", output_to_operand_aliasing={{}: (2, {})} | custom-call | flops 1 | bytes 1 | tf_op jit(solution)/shard_map/weight_out/pallas_call | solution.py:332
  281.5 2.2 copy-done.5
  286.5 9.8 %attention_backward.3 = (f32[256,1024]{1,0:T(8,128)S(1)}, bf16[256,1024]{1,0:T(8,128)(2,1)S(1)}, bf16[256,3072]{1,0:T(8,128)(2,1)S(1)}, bf16[16,256,256]{2,1,0:T...) custom-call(bf16[640,1152]{1,0:T(8,128)(2,1)S(1)} %bitcast.138, s32[256,2]{1,0:T(8,128)S(1)} %copy-done.47, ...), custom_call_target="tpu_custom_call" | custom-call | flops 1 | bytes 1 | tf_op jit(solution)/shard_map/attention_backward/pallas_call | solution.py:682
  298.6 10.4 %attention_backward.2 = (f32[256,1024]{1,0:T(8,128)S(1)}, bf16[256,1024]{1,0:T(8,128)(2,1)S(1)}, bf16[256,3072]{1,0:T(8,128)(2,1)S(1)}, bf16[16,256,256]{2,1,0:T...) custom-call(bf16[640,1152]{1,0:T(8,128)(2,1)S(1)} %bitcast.137, s32[256,2]{1,0:T(8,128)S(1)} %copy-done.46, ...), custom_call_target="tpu_custom_call" | custom-call | flops 1 | bytes 1 | tf_op jit(solution)/shard_map/attention_backward/pallas_call | solution.py:682
  311.4 7.6 %weight_attn.1 = (bf16[4,128,4096]{2,1,0:T(8,128)(2,1)S(1)}, bf16[4,128,4096]{2,1,0:T(8,128)(2,1)}) custom-call(s32[1]{0:T(128)S(6)} %select_n.107.core_ref, bf16[256,1024]{1,0:T(8,128)(2,1)S(1)} %copy-done.49, bf16[256,1024]{1,0:T(8,128)(2,1)S(1)} %copy-done.53, bf16[256,1024]{1,0:T(8,128)(2,1)S(1)} %copy-done.51, bf16[256,1024]{1,0:T(8,128)(2,1)S(1)} %copy-done.55, ...), custom_call_target="tpu_custom_call" | custom-call | flops 1 | bytes 1 | tf_op jit(solution)/shard_map/weight_attn/pallas_call | solution.py:405
  319.0 2.1 copy-done.14
  321.1 5.0 %all-to-all-start.5 = ((bf16[4,2,160,1024]{3,2,1,0:T(8,128)(2,1)}), bf16[4,2,160,1024]{3,2,1,0:T(8,128)(2,1)S(1)}, u32[]{:S(2)}, u32[]{:S(2)}) async-start(bf16[4,2,160,1024]{3,2,1,0:T(8,128)(2,1)} %get-tuple-element.115), calls=%async_computation.5 | async-start | bytes 5242880 | tf_op jit(solution)/shard_map/all_to_all | solution.py:97
  326.1 3.0 pad_maximum_fusion
  329.9 3.9 add_convert_fusion
  338.2 5.2 %finish.1 = (bf16[2,256,1024]{2,1,0:T(8,128)(2,1)}, f32[1,1024]{1,0:T(1,128)S(1)}) custom-call(bf16[2,256,1024]{2,1,0:T(8,128)(2,1)S(1)} %copy-done.22, f32[1,1024]{1,0:T(1,128)S(1)} %bitcast.155, bf16[1024,4096]{1,0:T(8,128)(2,1)S(1)} %bitcast.132, bf16[256,3072]{1,0:T(8,128)(2,1)S(1)} %copy-done.11, bf16[256,3072]{1,0:T(8,128)(2,1)S(1)} %copy-done.9, ...), custom_call_target="tpu_custom_call" | custom-call | flops 1 | bytes 1 | tf_op jit(solution)/shard_map/finish/pallas_call | solution.py:716
  345.7 37.0 %collective-permute-done.10 = bf16[2,1,64,4096]{3,2,1,0:T(8,128)(2,1)S(1)} collective-permute-done((bf16[2,1,64,4096]{3,2,1,0:T(8,128)(2,1)S(1)}, bf16[2,1,64,4096]{3,2,1,0:T(8,128)(2,1)S(1)}, u32[]{:S(2)}, u32[]{:S(2)}) %collective-permute-start.10) | collective-permute-done | bytes 1048608 | tf_op jit(solution)/shard_map/ppermute | solution.py:52
  386.1 13.4 %collective-permute-done.11 = bf16[1,1,64,4096]{3,2,1,0:T(8,128)(2,1)S(1)} collective-permute-done((bf16[1,1,64,4096]{3,2,1,0:T(8,128)(2,1)S(1)}, bf16[1,1,64,4096]{3,2,1,0:T(8,128)(2,1)S(1)}, u32[]{:S(2)}, u32[]{:S(2)}) %collective-permute-start.11) | collective-permute-done | bytes 524320 | tf_op jit(solution)/shard_map/ppermute | solution.py:52
  402.2 5.0 %all-to-all-start.6 = ((bf16[4,32,4096]{2,1,0:T(8,128)(2,1)}), bf16[4,32,4096]{2,1,0:T(8,128)(2,1)}, u32[]{:S(2)}, u32[]{:S(2)}) async-start(bf16[4,32,4096]{2,1,0:T(8,128)(2,1)} %bitcast.171), calls=%async_computation.6 | async-start | bytes 2097152 | tf_op jit(solution)/shard_map/all_to_all | solution.py:97
  411.7 2.6 collective-permute-start.15
  414.3 2.6 collective-permute-done.15
  417.0 4.4 collective-permute-done.16
  421.4 2.4 collective-permute-start.17
  425.3 2.5 collective-permute-start.19
  430.3 3.0 output.1
  438.9 1.6 copy-done.24
  440.5 2.2 spread.1
  (260 shorter events, 69.9 us)
Async XLA Ops:
  7.2 28.1 %copy-start = (f32[32,16]{0,1:T(8,128)S(1)}, f32[32,16]{0,1:T(8,128)}, u32[]{:S(2)}) copy-start(f32[32,16]{0,1:T(8,128)} %param.21) | copy-start | bytes 6148
  7.2 156.9 %all-gather.6.cloned.1.call-start = ((), (), s32[]{:S(2)}) async-start(), calls=%async_computation.10 | async-start | bytes 6488064 | tf_op jit(solution)/shard_map/all_gather | solution.py:811
  9.0 21.0 %collective-permute-start = (bf16[32,4096]{1,0:T(8,128)(2,1)S(1)}, bf16[32,4096]{1,0:T(8,128)(2,1)S(1)}, u32[]{:S(2)}, u32[]{:S(2)}) collective-permute-start(bf16[32,4096]{1,0:T(8,128)(2,1)S(1)} %constant_dynamic-update-slice_fusion), channel_id=1, source_target_pairs={{0,1},{1,2},{2,3},{3,0},{4,5},{5,6},{6,7},{7,4},{8,9},{9,10},{10,1... | collective-permute-start | bytes 786440 | tf_op jit(solution)/shard_map/ppermute | solution.py:56
  12.1 19.7 %collective-permute-start.1 = (bf16[32,4096]{1,0:T(8,128)(2,1)S(1)}, bf16[32,4096]{1,0:T(8,128)(2,1)S(1)}, u32[]{:S(2)}, u32[]{:S(2)}) collective-permute-start(bf16[32,4096]{1,0:T(8,128)(2,1)S(1)} %constant_dynamic-update-slice_fusion), channel_id=1, source_target_pairs={{0,2},{1,3},{2,0},{3,1},{4,6},{5,7},{6,4},{7,5},{8,10},{9,11},{10,... | collective-permute-start | bytes 786440 | tf_op jit(solution)/shard_map/ppermute | solution.py:56
  14.6 17.1 %collective-permute-start.2 = (bf16[32,4096]{1,0:T(8,128)(2,1)S(1)}, bf16[32,4096]{1,0:T(8,128)(2,1)S(1)}, u32[]{:S(2)}, u32[]{:S(2)}) collective-permute-start(bf16[32,4096]{1,0:T(8,128)(2,1)S(1)} %constant_dynamic-update-slice_fusion), channel_id=1, source_target_pairs={{0,3},{1,0},{2,1},{3,2},{4,7},{5,4},{6,5},{7,6},{8,11},{9,8},{10,9... | collective-permute-start | bytes 786440 | tf_op jit(solution)/shard_map/ppermute | solution.py:56
  25.2 68.4 %all-to-all-start = ((bf16[4,2,160,1024]{3,2,1,0:T(8,128)(2,1)}), bf16[4,2,160,1024]{3,2,1,0:T(8,128)(2,1)}, u32[]{:S(2)}, u32[]{:S(2)}) async-start(bf16[4,2,160,1024]{3,2,1,0:T(8,128)(2,1)} %pad_maximum_fusion.1), calls=%async_computation | async-start | bytes 5242880 | tf_op jit(solution)/shard_map/all_to_all | solution.py:97
  29.7 134.5 %all-gather.4.cloned.1.call-start = ((), (), s32[]{:S(2)}) async-start(), calls=%async_computation.8 | async-start | bytes 12976128 | tf_op jit(solution)/shard_map/all_gather | solution.py:812
  31.9 20.2 %collective-permute-start.5 = (bf16[1,64,4096]{2,1,0:T(8,128)(2,1)S(1)}, bf16[1,64,4096]{2,1,0:T(8,128)(2,1)S(1)}, u32[]{:S(2)}, u32[]{:S(2)}) collective-permute-start(bf16[1,64,4096]{2,1,0:T(8,128)(2,1)S(1)} %bitcast.174), channel_id=1, source_target_pairs={{0,16},{4,20},{8,24},{12,28},{16,0},{20,4},{24,8},{28,12},{1,17},{... | collective-permute-start | bytes 1572872 | tf_op jit(solution)/shard_map/ppermute | solution.py:52
  33.7 23.0 %collective-permute-start.3 = (bf16[1,64,4096]{2,1,0:T(8,128)(2,1)S(1)}, bf16[1,64,4096]{2,1,0:T(8,128)(2,1)S(1)}, u32[]{:S(2)}, u32[]{:S(2)}) collective-permute-start(bf16[1,64,4096]{2,1,0:T(8,128)(2,1)S(1)} %bitcast.172), channel_id=1, source_target_pairs={{0,8},{4,12},{8,0},{12,4},{16,24},{20,28},{24,16},{28,20},{1,9},{5... | collective-permute-start | bytes 1572872 | tf_op jit(solution)/shard_map/ppermute | solution.py:52
  52.2 32.9 %collective-permute-start.6 = (bf16[2,64,4096]{2,1,0:T(8,128)(2,1)S(1)}, bf16[2,64,4096]{2,1,0:T(8,128)(2,1)S(1)}, u32[]{:S(2)}, u32[]{:S(2)}) collective-permute-start(bf16[2,64,4096]{2,1,0:T(8,128)(2,1)S(1)} %pad_maximum_fusion.4), channel_id=1, source_target_pairs={{0,8},{4,12},{8,0},{12,4},{16,24},{20,28},{24,16},{28,20},{1,9},{5... | collective-permute-start | bytes 3145736 | tf_op jit(solution)/shard_map/ppermute | solution.py:52
  56.8 29.8 %collective-permute-start.4 = (bf16[2,64,4096]{2,1,0:T(8,128)(2,1)S(1)}, bf16[2,64,4096]{2,1,0:T(8,128)(2,1)S(1)}, u32[]{:S(2)}, u32[]{:S(2)}) collective-permute-start(bf16[2,64,4096]{2,1,0:T(8,128)(2,1)S(1)} %pad_maximum_fusion.3), channel_id=1, source_target_pairs={{0,16},{4,20},{8,24},{12,28},{16,0},{20,4},{24,8},{28,12},{1,17},{... | collective-permute-start | bytes 3145736 | tf_op jit(solution)/shard_map/ppermute | solution.py:52
  97.0 6.8 %collective-permute-start.8 = (bf16[4,64,4096]{2,1,0:T(8,128)(2,1)}, bf16[4,64,4096]{2,1,0:T(8,128)(2,1)}, u32[]{:S(2)}, u32[]{:S(2)}) collective-permute-start(bf16[4,64,4096]{2,1,0:T(8,128)(2,1)} %copy-done.12), channel_id=1, source_target_pairs={{0,4},{4,0},{8,12},{12,8},{16,20},{20,16},{24,28},{28,24},{1,5},{5... | collective-permute-start | bytes 6291464 | tf_op jit(solution)/shard_map/ppermute | solution.py:52
  97.1 7.3 %collective-permute-start.7 = (bf16[4,64,4096]{2,1,0:T(8,128)(2,1)S(1)}, bf16[4,64,4096]{2,1,0:T(8,128)(2,1)}, u32[]{:S(2)}, u32[]{:S(2)}) collective-permute-start(bf16[4,64,4096]{2,1,0:T(8,128)(2,1)S(1)} %constant_dynamic-update-slice_fusion.2.refs_1_), channel_id=1, source_target_pairs={{0,4},{4,0},{8,12},{12,8},{16,20},{20,16},{24,28},{28,24},{1,5},{5... | collective-permute-start | bytes 6291464 | tf_op jit(solution)/shard_map/ppermute | solution.py:52
  98.6 20.1 %copy-start.32 = (s32[2,256]{0,1:T(8,128)}, s32[2,256]{0,1:T(8,128)S(1)}, u32[]{:S(2)}) copy-start(s32[2,256]{0,1:T(8,128)S(1)} %copy.99) | copy-start | bytes 6148
  98.9 29.7 %copy-start.6 = (bf16[1024,128]{1,0:T(8,128)(2,1)}, bf16[1024,128]{1,0:T(8,128)(2,1)S(1)}, u32[]{:S(2)}) copy-start(bf16[1024,128]{1,0:T(8,128)(2,1)S(1)} %pad.4.refs_11_.refs_7_.wr_ref.router_ref) | copy-start | bytes 786436
  124.2 35.7 %all-to-all-start.2 = ((bf16[4,160,1024]{2,1,0:T(8,128)(2,1)}), bf16[4,160,1024]{2,1,0:T(8,128)(2,1)S(1)}, u32[]{:S(2)}, u32[]{:S(2)}) async-start(bf16[4,160,1024]{2,1,0:T(8,128)(2,1)} %bitcast.141), calls=%async_computation.2 | async-start | bytes 2621440 | tf_op jit(solution)/shard_map/all_to_all | solution.py:97
  128.6 16.9 %copy-start.34 = (s32[2,256]{0,1:T(8,128)}, s32[2,256]{0,1:T(8,128)S(1)}, u32[]{:S(2)}) copy-start(s32[2,256]{0,1:T(8,128)S(1)} %copy.102) | copy-start | bytes 6148
  160.0 38.0 %all-to-all-start.1 = ((bf16[4,160,1024]{2,1,0:T(8,128)(2,1)}), bf16[4,160,1024]{2,1,0:T(8,128)(2,1)S(1)}, u32[]{:S(2)}, u32[]{:S(2)}) async-start(bf16[4,160,1024]{2,1,0:T(8,128)(2,1)} %bitcast.36), calls=%async_computation.1 | async-start | bytes 2621440 | tf_op jit(solution)/shard_map/all_to_all | solution.py:97
  198.0 40.1 %all-to-all-start.3 = ((bf16[4,160,1152]{2,1,0:T(8,128)(2,1)}), bf16[4,160,1152]{2,1,0:T(8,128)(2,1)S(1)}, u32[]{:S(2)}, u32[]{:S(2)}) async-start(bf16[4,160,1152]{2,1,0:T(8,128)(2,1)} %bitcast.177), calls=%async_computation.3 | async-start | bytes 2949120 | tf_op jit(solution)/shard_map/all_to_all | solution.py:97
  238.1 39.4 %all-to-all-start.4 = ((bf16[4,160,1152]{2,1,0:T(8,128)(2,1)}), bf16[4,160,1152]{2,1,0:T(8,128)(2,1)S(1)}, u32[]{:S(2)}, u32[]{:S(2)}) async-start(bf16[4,160,1152]{2,1,0:T(8,128)(2,1)} %bitcast.176), calls=%async_computation.4 | async-start | bytes 2949120 | tf_op jit(solution)/shard_map/all_to_all | solution.py:97
  242.1 196.8 %reduce-scatter.2.cloned.1.call-start = ((), (), s32[]{:S(2)}) async-start(), calls=%async_computation.9 | async-start | bytes 19464192 | tf_op jit(solution)/shard_map/reduce_scatter | solution.py:892
  286.5 12.1 %copy-start.17 = (f32[256,1024]{1,0:T(8,128)S(1)}, f32[256,1024]{1,0:T(8,128)}, u32[]{:S(2)}) copy-start(f32[256,1024]{1,0:T(8,128)} %copy-done.16) | copy-start | bytes 3145732
  286.5 12.1 %copy-start.28 = (bf16[256,3072]{1,0:T(8,128)(2,1)S(1)}, bf16[256,3072]{1,0:T(8,128)(2,1)}, u32[]{:S(2)}) copy-start(bf16[256,3072]{1,0:T(8,128)(2,1)} %copy-done.27) | copy-start | bytes 4718596
  286.5 12.1 %copy-start.33 = (s32[2,256]{0,1:T(8,128)S(1)}, s32[2,256]{0,1:T(8,128)}, u32[]{:S(2)}) copy-start(s32[2,256]{0,1:T(8,128)} %copy-done.32) | copy-start | bytes 6148
  286.5 12.1 %copy-start.41 = (f32[256,128]{1,0:T(8,128)S(1)}, f32[256,128]{1,0:T(8,128)}, u32[]{:S(2)}) copy-start(f32[256,128]{1,0:T(8,128)} %copy-done.40) | copy-start | bytes 393220
  286.5 12.1 %copy-start.46 = (s32[256,2]{1,0:T(8,128)S(1)}, s32[256,2]{1,0:T(8,128)}, u32[]{:S(2)}) copy-start(s32[256,2]{1,0:T(8,128)} %get-tuple-element.187.targets_ref) | copy-start | bytes 6148
  298.6 10.5 %copy-start.58 = (f32[128,1024]{1,0:T(8,128)}, f32[128,1024]{1,0:T(8,128)S(1)}, u32[]{:S(2)}) copy-start(f32[128,1024]{1,0:T(8,128)S(1)} %get-tuple-element.134) | copy-start | bytes 1572868
  298.6 12.8 %copy-start.8 = (bf16[256,3072]{1,0:T(8,128)(2,1)}, bf16[256,3072]{1,0:T(8,128)(2,1)S(1)}, u32[]{:S(2)}) copy-start(bf16[256,3072]{1,0:T(8,128)(2,1)S(1)} %get-tuple-element.118.refs_5_.refs_1_) | copy-start | bytes 4718596
  298.6 12.8 %copy-start.49 = (bf16[256,1024]{1,0:T(8,128)(2,1)S(1)}, bf16[256,1024]{1,0:T(8,128)(2,1)}, u32[]{:S(2)}) copy-start(bf16[256,1024]{1,0:T(8,128)(2,1)} %copy-done.48) | copy-start | bytes 1572868
  298.6 12.8 %copy-start.51 = (bf16[256,1024]{1,0:T(8,128)(2,1)S(1)}, bf16[256,1024]{1,0:T(8,128)(2,1)}, u32[]{:S(2)}) copy-start(bf16[256,1024]{1,0:T(8,128)(2,1)} %copy-done.50) | copy-start | bytes 1572868
  298.6 12.8 %copy-start.53 = (bf16[256,1024]{1,0:T(8,128)(2,1)S(1)}, bf16[256,1024]{1,0:T(8,128)(2,1)}, u32[]{:S(2)}) copy-start(bf16[256,1024]{1,0:T(8,128)(2,1)} %copy-done.52) | copy-start | bytes 1572868
  298.6 12.8 %copy-start.55 = (bf16[256,1024]{1,0:T(8,128)(2,1)S(1)}, bf16[256,1024]{1,0:T(8,128)(2,1)}, u32[]{:S(2)}) copy-start(bf16[256,1024]{1,0:T(8,128)(2,1)} %copy-done.54) | copy-start | bytes 1572868
  321.1 8.0 %collective-permute-start.9 = (bf16[4,128,4096]{2,1,0:T(8,128)(2,1)}, bf16[4,128,4096]{2,1,0:T(8,128)(2,1)}, u32[]{:S(2)}, u32[]{:S(2)}) collective-permute-start(bf16[4,128,4096]{2,1,0:T(8,128)(2,1)} %get-tuple-element.116), channel_id=1, source_target_pairs={{0,4},{4,0},{8,12},{12,8},{16,20},{20,16},{24,28},{28,24},{1,5},{5... | collective-permute-start | bytes 12582920 | tf_op jit(solution)/shard_map/ppermute | solution.py:52
  321.1 81.1 %all-to-all-start.5 = ((bf16[4,2,160,1024]{3,2,1,0:T(8,128)(2,1)}), bf16[4,2,160,1024]{3,2,1,0:T(8,128)(2,1)S(1)}, u32[]{:S(2)}, u32[]{:S(2)}) async-start(bf16[4,2,160,1024]{3,2,1,0:T(8,128)(2,1)} %get-tuple-element.115), calls=%async_computation.5 | async-start | bytes 5242880 | tf_op jit(solution)/shard_map/all_to_all | solution.py:97
  334.5 48.2 %collective-permute-start.10 = (bf16[2,1,64,4096]{3,2,1,0:T(8,128)(2,1)S(1)}, bf16[2,1,64,4096]{3,2,1,0:T(8,128)(2,1)S(1)}, u32[]{:S(2)}, u32[]{:S(2)}) collective-permute-start(bf16[2,1,64,4096]{3,2,1,0:T(8,128)(2,1)S(1)} %dynamic-slice_bitcast_fusion.1), channel_id=1, source_target_pairs={{0,8},{4,12},{8,0},{12,4},{16,24},{20,28},{24,16},{28,20},{1,9},{5... | collective-permute-start | bytes 3145736 | tf_op jit(solution)/shard_map/ppermute | solution.py:52
  336.1 48.4 %collective-permute-start.12 = (bf16[1,2,64,4096]{3,2,1,0:T(8,128)(2,1)S(1)}, bf16[1,2,64,4096]{3,2,1,0:T(8,128)(2,1)S(1)}, u32[]{:S(2)}, u32[]{:S(2)}) collective-permute-start(bf16[1,2,64,4096]{3,2,1,0:T(8,128)(2,1)S(1)} %dynamic-slice_bitcast_fusion), channel_id=1, source_target_pairs={{0,16},{4,20},{8,24},{12,28},{16,0},{20,4},{24,8},{28,12},{1,17},{... | collective-permute-start | bytes 3145736 | tf_op jit(solution)/shard_map/ppermute | solution.py:52
  383.0 16.5 %collective-permute-start.11 = (bf16[1,1,64,4096]{3,2,1,0:T(8,128)(2,1)S(1)}, bf16[1,1,64,4096]{3,2,1,0:T(8,128)(2,1)S(1)}, u32[]{:S(2)}, u32[]{:S(2)}) collective-permute-start(bf16[1,1,64,4096]{3,2,1,0:T(8,128)(2,1)S(1)} %constant_dynamic-slice_fusion.1), channel_id=1, source_target_pairs={{0,16},{4,20},{8,24},{12,28},{16,0},{20,4},{24,8},{28,12},{1,17},{... | collective-permute-start | bytes 1572872 | tf_op jit(solution)/shard_map/ppermute | solution.py:52
  384.7 16.1 %collective-permute-start.13 = (bf16[1,1,64,4096]{3,2,1,0:T(8,128)(2,1)S(1)}, bf16[1,1,64,4096]{3,2,1,0:T(8,128)(2,1)S(1)}, u32[]{:S(2)}, u32[]{:S(2)}) collective-permute-start(bf16[1,1,64,4096]{3,2,1,0:T(8,128)(2,1)S(1)} %constant_dynamic-slice_fusion), channel_id=1, source_target_pairs={{0,8},{4,12},{8,0},{12,4},{16,24},{20,28},{24,16},{28,20},{1,9},{5... | collective-permute-start | bytes 1572872 | tf_op jit(solution)/shard_map/ppermute | solution.py:52
  402.1 25.7 %copy-start.23 = (s32[2,256,2]{2,1,0:T(8,128)S(1)}, s32[2,256,2]{2,1,0:T(8,128)}, u32[]{:S(2)}) copy-start(s32[2,256,2]{2,1,0:T(8,128)} %copy.106.routes_ref) | copy-start | bytes 12292
  402.2 25.7 %copy-start.42 = (f32[256,128]{1,0:T(8,128)S(1)}, f32[256,128]{1,0:T(8,128)}, u32[]{:S(2)}) copy-start(f32[256,128]{1,0:T(8,128)} %copy-done.40) | copy-start | bytes 393220
  402.2 25.7 %copy-start.45 = (f32[256,128]{1,0:T(8,128)S(1)}, f32[256,128]{1,0:T(8,128)}, u32[]{:S(2)}) copy-start(f32[256,128]{1,0:T(8,128)} %copy-done.43) | copy-start | bytes 393220
  402.2 33.9 %all-to-all-start.6 = ((bf16[4,32,4096]{2,1,0:T(8,128)(2,1)}), bf16[4,32,4096]{2,1,0:T(8,128)(2,1)}, u32[]{:S(2)}, u32[]{:S(2)}) async-start(bf16[4,32,4096]{2,1,0:T(8,128)(2,1)} %bitcast.171), calls=%async_computation.6 | async-start | bytes 2097152 | tf_op jit(solution)/shard_map/all_to_all | solution.py:97
  410.4 1.3 collective-permute-start.14
  411.7 5.2 %collective-permute-start.15 = (f32[52,128]{1,0:T(8,128)S(1)}, f32[52,128]{1,0:T(8,128)S(1)}, u32[]{:S(2)}, u32[]{:S(2)}) collective-permute-start(f32[52,128]{1,0:T(8,128)S(1)} %fusion.26), channel_id=1, source_target_pairs={{0,8},{4,12},{8,0},{12,4},{16,24},{20,28},{24,16},{28,20},{1,9},{5... | collective-permute-start | bytes 79880 | tf_op jit(solution)/shard_map/ppermute | solution.py:52
  416.9 4.5 %collective-permute-start.16 = (f32[52,128]{1,0:T(8,128)S(1)}, f32[52,128]{1,0:T(8,128)S(1)}, u32[]{:S(2)}, u32[]{:S(2)}) collective-permute-start(f32[52,128]{1,0:T(8,128)S(1)} %fusion.34), channel_id=1, source_target_pairs={{0,16},{4,20},{8,24},{12,28},{16,0},{20,4},{24,8},{28,12},{1,17},{... | collective-permute-start | bytes 79880 | tf_op jit(solution)/shard_map/ppermute | solution.py:52
  421.4 11.9 %collective-permute-start.17 = (f32[52,128]{1,0:T(8,128)S(1)}, f32[52,128]{1,0:T(8,128)S(1)}, u32[]{:S(2)}, u32[]{:S(2)}) collective-permute-start(f32[52,128]{1,0:T(8,128)S(1)} %add.221), channel_id=1, source_target_pairs={{0,2},{1,3},{2,0},{3,1},{4,6},{5,7},{6,4},{7,5},{8,10},{9,11},{10,... | collective-permute-start | bytes 79880 | tf_op jit(solution)/shard_map/ppermute | solution.py:56
  423.8 9.5 %collective-permute-start.18 = (f32[52,128]{1,0:T(8,128)S(1)}, f32[52,128]{1,0:T(8,128)S(1)}, u32[]{:S(2)}, u32[]{:S(2)}) collective-permute-start(f32[52,128]{1,0:T(8,128)S(1)} %add.221), channel_id=1, source_target_pairs={{0,1},{1,2},{2,3},{3,0},{4,5},{5,6},{6,7},{7,4},{8,9},{9,10},{10,1... | collective-permute-start | bytes 79880 | tf_op jit(solution)/shard_map/ppermute | solution.py:56
  425.3 8.0 %collective-permute-start.19 = (f32[52,128]{1,0:T(8,128)S(1)}, f32[52,128]{1,0:T(8,128)S(1)}, u32[]{:S(2)}, u32[]{:S(2)}) collective-permute-start(f32[52,128]{1,0:T(8,128)S(1)} %add.221), channel_id=1, source_target_pairs={{0,3},{1,0},{2,1},{3,2},{4,7},{5,4},{6,5},{7,6},{8,11},{9,8},{10,9... | collective-permute-start | bytes 79880 | tf_op jit(solution)/shard_map/ppermute | solution.py:56
  (53 other events, 138.4 us)
Sparse Core Ops, SparseCore 0:
  16.1 56.7 all-gather.5
  97.1 67.0 all-gather.3
  277.7 145.2 reduce-scatter.1

commit v8 on v7

--- a/solution.py
+++ b/solution.py
@@ -340,7 +340,7 @@
         out_specs=pl.BlockSpec((size, part, tile), lambda j: (0, first + j, 0)),
         out_shape=jax.ShapeDtypeStruct(joined.shape, BF16),
         input_output_aliases={2: 0},
-        compiler_params=pltpu.CompilerParams(vmem_limit_bytes=56 << 20),
+        compiler_params=pltpu.CompilerParams(vmem_limit_bytes=40 << 20),
         cost_estimate=LIGHT,
         name="weight_out",
     )(gt, dy, joined)

time: 458 us -> 456 us (level)
    unnamed x149 -> x167, local copies, waits for them, and re-layouts: 43.8 us -> 45.1 us
  transfers between devices with their start and end apart: 30 -> 30, of which waited for: 16 -> 17; matrix products, arithmetic and copies ran while one was open for 10% -> 11% of each run, Pallas kernels for 36% -> 35%
where the time goes in v8:
time: 456 us; the launch traced here: 447 us
  Pallas kernels  161 us (35%)
  waiting for transfers between devices  123 us (27%)
  local copies, waits for them, and re-layouts  67.9 us (15%)
  starting transfers between devices  57.5 us (13%)
  other arithmetic  18 us (4%)
  between operations  15 us (3%)
  matrix products  5.21 us (1%)
    ppermute x14, waiting for transfers between devices, flip(): return lax.ppermute(value, axis, [(i, i ^ bit) for i in range(size)])  101 us
    pallas_call x2, Pallas kernels, expert_call(): pl.pallas_call(expert_body, grid=(tiles,), in_specs=in_specs, out_specs=[...  67.6 us
    unnamed x167, local copies, waits for them, and re-layouts  45.1 us
    all_to_all x7, starting transfers between devices, all_to_all(): lax.all_to_all(value, 'expert', split_axis=0, concat_axis=0, tiled=True)  32.2 us
    pallas_call x1, Pallas kernels, weight_in_call(): pl.pallas_call(weight_in_body, grid=(2,), in_specs=[pl.BlockSpec((rows, w...  22.4 us
    pallas_call x2, Pallas kernels, forward_call(): pl.pallas_call(partial(forward_body, heads, experts, rels), in_specs=in_s...  21.4 us
    pallas_call x2, Pallas kernels, backward_call(): pl.pallas_call(partial(backward_body, heads, experts), grid=(1,), in_spec...  20.5 us
    all_to_all x7, waiting for transfers between devices, all_to_all(): lax.all_to_all(value, 'expert', split_axis=0, concat_axis=0, tiled=True)  17.9 us
  transfers between devices with their start and end apart: 30, of which 17 were waited for; matrix products, arithmetic and copies ran while one was open for 11% of the time, Pallas kernels for 35%

profile of v8, /device:TPU:0, one launch (start us, length us, event | category | flops | bytes accessed | tf_op | source)
XLA Modules:
  0.0 446.8 jit_solution(12961489087364804407)
XLA Ops:
  9.0 3.0 collective-permute-start
  12.1 2.6 collective-permute-start.1
  16.8 2.4 reduce-window.6
  23.6 1.7 pad_maximum_fusion.1
  25.3 4.5 %all-to-all-start = ((bf16[4,2,160,1024]{3,2,1,0:T(8,128)(2,1)}), bf16[4,2,160,1024]{3,2,1,0:T(8,128)(2,1)}, u32[]{:S(2)}, u32[]{:S(2)}) async-start(bf16[4,2,160,1024]{3,2,1,0:T(8,128)(2,1)} %pad_maximum_fusion.1), calls=%async_computation | async-start | bytes 5242880 | tf_op jit(solution)/shard_map/all_to_all | solution.py:97
  30.2 1.6 collective-permute-done.1
  31.9 1.6 collective-permute-start.5
  35.3 2.8 fusion
  38.1 4.4 copy.125
  42.4 9.7 %collective-permute-done.5 = bf16[1,64,4096]{2,1,0:T(8,128)(2,1)S(1)} collective-permute-done((bf16[1,64,4096]{2,1,0:T(8,128)(2,1)S(1)}, bf16[1,64,4096]{2,1,0:T(8,128)(2,1)S(1)}, u32[]{:S(2)}, u32[]{:S(2)}) %collective-permute-start.5) | collective-permute-done | bytes 524320 | tf_op jit(solution)/shard_map/ppermute | solution.py:52
  53.5 3.2 collective-permute-done.3
  57.1 28.1 %collective-permute-done.6 = bf16[2,64,4096]{2,1,0:T(8,128)(2,1)S(1)} collective-permute-done((bf16[2,64,4096]{2,1,0:T(8,128)(2,1)S(1)}, bf16[2,64,4096]{2,1,0:T(8,128)(2,1)S(1)}, u32[]{:S(2)}, u32[]{:S(2)}) %collective-permute-start.6) | collective-permute-done | bytes 1048608 | tf_op jit(solution)/shard_map/ppermute | solution.py:52
  86.7 6.9 %all-to-all-done = bf16[4,2,160,1024]{3,2,1,0:T(8,128)(2,1)} async-done(((bf16[4,2,160,1024]{3,2,1,0:T(8,128)(2,1)}), bf16[4,2,160,1024]{3,2,1,0:T(8,128)(2,1)}, u32[]{:S(2)}, u32[]{:S(2)}) %all-to-all-start) | async-done | bytes 2621472 | tf_op jit(solution)/shard_map/all_to_all | solution.py:97
  93.6 3.5 fusion.29
  104.5 2.6 copy-done.3
  107.1 11.7 %attention_forward.2 = (bf16[640,1024]{1,0:T(8,128)(2,1)S(1)}, bf16[256,1024]{1,0:T(8,128)(2,1)S(1)}, bf16[256,3072]{1,0:T(8,128)(2,1)S(1)}, f32[16,256]{1,0:T(8...) custom-call(s32[1]{0:T(128)} %bitcast.1.refs_0_, ...), custom_call_target="tpu_custom_call" | custom-call | flops 1 | bytes 1 | tf_op jit(solution)/shard_map/attention_forward/pallas_call | solution.py:577
  123.3 4.1 all-to-all-start.2
  127.7 5.3 %copy-done.2 = bf16[1024,4096]{1,0:T(8,128)(2,1)S(1)} copy-done((bf16[1024,4096]{1,0:T(8,128)(2,1)S(1)}, bf16[1024,4096]{1,0:T(8,128)(2,1)}, u32[]{:S(2)}) %copy-start.2) | copy-done | bytes 8388632
  133.0 2.2 copy-done.4
  135.1 9.7 %attention_forward.3 = (bf16[640,1024]{1,0:T(8,128)(2,1)}, bf16[256,1024]{1,0:T(8,128)(2,1)S(1)}, bf16[256,3072]{1,0:T(8,128)(2,1)S(1)}, f32[16,256]{1,0:T(8,128...) custom-call(bf16[1024,4096]{1,0:T(8,128)(2,1)S(1)} %copy-done.2, ...), custom_call_target="tpu_custom_call" | custom-call | flops 1 | bytes 1 | tf_op jit(solution)/shard_map/attention_forward/pallas_call | solution.py:577
  149.4 9.7 %all-to-all-done.2 = bf16[4,160,1024]{2,1,0:T(8,128)(2,1)S(1)} async-done(((bf16[4,160,1024]{2,1,0:T(8,128)(2,1)}), bf16[4,160,1024]{2,1,0:T(8,128)(2,1)S(1)}, u32[]{:S(2)}, u32[]{:S(2)}) %all-to-all-start.2) | async-done | bytes 1310752 | tf_op jit(solution)/shard_map/all_to_all | solution.py:97
  159.0 4.3 all-to-all-start.1
  164.3 33.8 %expert.2 = (bf16[4,2,160,1024]{3,2,1,0:T(8,128)(2,1)}, bf16[640,1152]{1,0:T(8,128)(2,1)}, bf16[2816,1280]{1,0:T(8,128)(2,1)}, bf16[2,1280,2816]{2,1,0:T(8,128)(2,1)}, bf16[1280,1024]{1,0:T(8,128)(2,1)}) custom-call(s32[2]{0:T(128)} %pad_add_fusion.4.mine, bf16[640,1024]{1,0:T(8,128)(2,1)} %bitcast.160, bf16[640,1024]{1,0:T(8,128)(2,1)} %bitcast.166, ...), custom_call_target="tpu_custom_call" | custom-call | flops 1 | bytes 1 | tf_op jit(solution)/shard_map/expert/pallas_call | solution.py:251
  198.1 4.9 %all-to-all-start.3 = ((bf16[4,160,1152]{2,1,0:T(8,128)(2,1)}), bf16[4,160,1152]{2,1,0:T(8,128)(2,1)S(1)}, u32[]{:S(2)}, u32[]{:S(2)}) async-start(bf16[4,160,1152]{2,1,0:T(8,128)(2,1)} %bitcast.176), calls=%async_computation.3 | async-start | bytes 2949120 | tf_op jit(solution)/shard_map/all_to_all | solution.py:97
  203.0 33.8 %expert.3 = (bf16[4,2,160,1024]{3,2,1,0:T(8,128)(2,1)}, bf16[640,1152]{1,0:T(8,128)(2,1)}, bf16[2816,1280]{1,0:T(8,128)(2,1)}, bf16[2,1280,2816]{2,1,0:T(8,128)(2,1)}, bf16[1280,1024]{1,0:T(8,128)(2,1)}) custom-call(s32[2]{0:T(128)} %pad_add_fusion.4.mine, ...), custom_call_target="tpu_custom_call", output_to_operand_aliasing={{0}: (7, {}), {2}: (8, {}), {3}: (9, {}), {4}: (10, {})} | custom-call | flops 1 | bytes 1 | tf_op jit(solution)/shard_map/expert/pallas_call | solution.py:251
  238.2 4.4 all-to-all-start.4
  242.6 22.4 %weight_in.1._ = bf16[8,4224,256]{2,1,0:T(8,128)(2,1)} custom-call(bf16[640,1024]{1,0:T(8,128)(2,1)} %bitcast.161, bf16[640,1024]{1,0:T(8,128)(2,1)} %bitcast.37.x_ref.refs_1_, bf16[2,1280,2816]{2,1,0:T(8,128)(2,1)} %get-tuple-element.97.refs_2_), custom_call_target="tpu_custom_call" | custom-call | flops 1 | bytes 1 | tf_op jit(solution)/shard_map/weight_in/pallas_call | solution.py:307
  265.0 1.7 copy-done.8
  266.8 10.7 %weight_out.1 = bf16[8,4224,256]{2,1,0:T(8,128)(2,1)} custom-call(bf16[2816,1280]{1,0:T(8,128)(2,1)S(1)} %bitcast.138, bf16[1280,1024]{1,0:T(8,128)(2,1)S(1)} %copy-done.8, bf16[8,4224,256]{2,1,0:T(8,128)(2,1)} %weight_in.1._), custom_call_target="tpu_custom_call", output_to_operand_aliasing={{}: (2, {})} | custom-call | flops 1 | bytes 1 | tf_op jit(solution)/shard_map/weight_out/pallas_call | solution.py:332
  280.4 2.2 copy-done.5
  284.4 10.1 %attention_backward.3 = (f32[256,1024]{1,0:T(8,128)S(1)}, bf16[256,1024]{1,0:T(8,128)(2,1)S(1)}, bf16[256,3072]{1,0:T(8,128)(2,1)S(1)}, bf16[16,256,256]{2,1,0:T...) custom-call(bf16[640,1152]{1,0:T(8,128)(2,1)} %bitcast.47.dx_ref, s32[256,2]{1,0:T(8,128)S(1)} %copy-done.54, ...), custom_call_target="tpu_custom_call" | custom-call | flops 1 | bytes 1 | tf_op jit(solution)/shard_map/attention_backward/pallas_call | solution.py:682
  296.7 10.4 %attention_backward.2 = (f32[256,1024]{1,0:T(8,128)S(1)}, bf16[256,1024]{1,0:T(8,128)(2,1)S(1)}, bf16[256,3072]{1,0:T(8,128)(2,1)S(1)}, bf16[16,256,256]{2,1,0:T...) custom-call(bf16[640,1152]{1,0:T(8,128)(2,1)S(1)} %bitcast.139, s32[256,2]{1,0:T(8,128)S(1)} %copy-done.53, ...), custom_call_target="tpu_custom_call" | custom-call | flops 1 | bytes 1 | tf_op jit(solution)/shard_map/attention_backward/pallas_call | solution.py:682
  309.4 7.5 %weight_attn.1 = (bf16[4,128,4096]{2,1,0:T(8,128)(2,1)S(1)}, bf16[4,128,4096]{2,1,0:T(8,128)(2,1)}) custom-call(s32[1]{0:T(128)S(6)} %select_n.107.core_ref, bf16[256,1024]{1,0:T(8,128)(2,1)S(1)} %copy-done.56, bf16[256,1024]{1,0:T(8,128)(2,1)S(1)} %copy-done.60, bf16[256,1024]{1,0:T(8,128)(2,1)S(1)} %copy-done.58, bf16[256,1024]{1,0:T(8,128)(2,1)S(1)} %copy-done.62, ...), custom_call_target="tpu_custom_call" | custom-call | flops 1 | bytes 1 | tf_op jit(solution)/shard_map/weight_attn/pallas_call | solution.py:405
  316.9 2.0 copy-done.17
  319.0 5.2 %all-to-all-start.5 = ((bf16[4,2,160,1024]{3,2,1,0:T(8,128)(2,1)}), bf16[4,2,160,1024]{3,2,1,0:T(8,128)(2,1)S(1)}, u32[]{:S(2)}, u32[]{:S(2)}) async-start(bf16[4,2,160,1024]{3,2,1,0:T(8,128)(2,1)} %get-tuple-element.115), calls=%async_computation.5 | async-start | bytes 5242880 | tf_op jit(solution)/shard_map/all_to_all | solution.py:97
  324.2 2.8 pad_maximum_fusion
  327.9 3.6 add_convert_fusion
  335.8 5.2 %finish.1 = (bf16[2,256,1024]{2,1,0:T(8,128)(2,1)}, f32[1,1024]{1,0:T(1,128)S(1)}) custom-call(bf16[2,256,1024]{2,1,0:T(8,128)(2,1)S(1)} %copy-done.27, f32[1,1024]{1,0:T(1,128)S(1)} %bitcast.156, bf16[1024,4096]{1,0:T(8,128)(2,1)S(1)} %bitcast.132, bf16[256,3072]{1,0:T(8,128)(2,1)S(1)} %copy-done.12, bf16[256,3072]{1,0:T(8,128)(2,1)S(1)} %copy-done.10, ...), custom_call_target="tpu_custom_call" | custom-call | flops 1 | bytes 1 | tf_op jit(solution)/shard_map/finish/pallas_call | solution.py:716
  343.3 37.3 %collective-permute-done.10 = bf16[2,1,64,4096]{3,2,1,0:T(8,128)(2,1)S(1)} collective-permute-done((bf16[2,1,64,4096]{3,2,1,0:T(8,128)(2,1)S(1)}, bf16[2,1,64,4096]{3,2,1,0:T(8,128)(2,1)S(1)}, u32[]{:S(2)}, u32[]{:S(2)}) %collective-permute-start.10) | collective-permute-done | bytes 1048608 | tf_op jit(solution)/shard_map/ppermute | solution.py:52
  383.0 13.9 %collective-permute-done.11 = bf16[1,1,64,4096]{3,2,1,0:T(8,128)(2,1)S(1)} collective-permute-done((bf16[1,1,64,4096]{3,2,1,0:T(8,128)(2,1)S(1)}, bf16[1,1,64,4096]{3,2,1,0:T(8,128)(2,1)S(1)}, u32[]{:S(2)}, u32[]{:S(2)}) %collective-permute-start.11) | collective-permute-done | bytes 524320 | tf_op jit(solution)/shard_map/ppermute | solution.py:52
  398.3 4.7 %all-to-all-start.6 = ((bf16[4,32,4096]{2,1,0:T(8,128)(2,1)}), bf16[4,32,4096]{2,1,0:T(8,128)(2,1)}, u32[]{:S(2)}, u32[]{:S(2)}) async-start(bf16[4,32,4096]{2,1,0:T(8,128)(2,1)} %bitcast.170), calls=%async_computation.6 | async-start | bytes 2097152 | tf_op jit(solution)/shard_map/all_to_all | solution.py:97
  409.1 3.0 collective-permute-done.15
  413.7 3.0 collective-permute-done.16
  416.7 2.9 collective-permute-start.17
  421.1 2.6 collective-permute-start.19
  426.1 3.0 output.1
  436.2 1.6 copy-done.30
  437.8 2.2 spread.1
  (279 shorter events, 71.2 us)
Async XLA Ops:
  7.2 28.1 %copy-start = (f32[32,16]{0,1:T(8,128)S(1)}, f32[32,16]{0,1:T(8,128)}, u32[]{:S(2)}) copy-start(f32[32,16]{0,1:T(8,128)} %param.21) | copy-start | bytes 6148
  7.2 156.7 %all-gather.6.cloned.1.call-start = ((), (), s32[]{:S(2)}) async-start(), calls=%async_computation.10 | async-start | bytes 6488064 | tf_op jit(solution)/shard_map/all_gather | solution.py:811
  9.0 21.1 %collective-permute-start = (bf16[32,4096]{1,0:T(8,128)(2,1)S(1)}, bf16[32,4096]{1,0:T(8,128)(2,1)S(1)}, u32[]{:S(2)}, u32[]{:S(2)}) collective-permute-start(bf16[32,4096]{1,0:T(8,128)(2,1)S(1)} %constant_dynamic-update-slice_fusion), channel_id=1, source_target_pairs={{0,1},{1,2},{2,3},{3,0},{4,5},{5,6},{6,7},{7,4},{8,9},{9,10},{10,1... | collective-permute-start | bytes 786440 | tf_op jit(solution)/shard_map/ppermute | solution.py:56
  12.1 19.7 %collective-permute-start.1 = (bf16[32,4096]{1,0:T(8,128)(2,1)S(1)}, bf16[32,4096]{1,0:T(8,128)(2,1)S(1)}, u32[]{:S(2)}, u32[]{:S(2)}) collective-permute-start(bf16[32,4096]{1,0:T(8,128)(2,1)S(1)} %constant_dynamic-update-slice_fusion), channel_id=1, source_target_pairs={{0,2},{1,3},{2,0},{3,1},{4,6},{5,7},{6,4},{7,5},{8,10},{9,11},{10,... | collective-permute-start | bytes 786440 | tf_op jit(solution)/shard_map/ppermute | solution.py:56
  14.6 17.1 %collective-permute-start.2 = (bf16[32,4096]{1,0:T(8,128)(2,1)S(1)}, bf16[32,4096]{1,0:T(8,128)(2,1)S(1)}, u32[]{:S(2)}, u32[]{:S(2)}) collective-permute-start(bf16[32,4096]{1,0:T(8,128)(2,1)S(1)} %constant_dynamic-update-slice_fusion), channel_id=1, source_target_pairs={{0,3},{1,0},{2,1},{3,2},{4,7},{5,4},{6,5},{7,6},{8,11},{9,8},{10,9... | collective-permute-start | bytes 786440 | tf_op jit(solution)/shard_map/ppermute | solution.py:56
  21.1 76.6 %copy-start.24 = (s32[2,256,2]{2,1,0:T(8,128)}, s32[2,256,2]{2,1,0:T(8,128)S(1)}, u32[]{:S(2)}) copy-start(s32[2,256,2]{2,1,0:T(8,128)S(1)} %bitcast_add_fusion.targets_ref) | copy-start | bytes 12292
  25.3 68.3 %all-to-all-start = ((bf16[4,2,160,1024]{3,2,1,0:T(8,128)(2,1)}), bf16[4,2,160,1024]{3,2,1,0:T(8,128)(2,1)}, u32[]{:S(2)}, u32[]{:S(2)}) async-start(bf16[4,2,160,1024]{3,2,1,0:T(8,128)(2,1)} %pad_maximum_fusion.1), calls=%async_computation | async-start | bytes 5242880 | tf_op jit(solution)/shard_map/all_to_all | solution.py:97
  29.9 134.4 %all-gather.4.cloned.1.call-start = ((), (), s32[]{:S(2)}) async-start(), calls=%async_computation.8 | async-start | bytes 12976128 | tf_op jit(solution)/shard_map/all_gather | solution.py:812
  31.9 20.2 %collective-permute-start.5 = (bf16[1,64,4096]{2,1,0:T(8,128)(2,1)S(1)}, bf16[1,64,4096]{2,1,0:T(8,128)(2,1)S(1)}, u32[]{:S(2)}, u32[]{:S(2)}) collective-permute-start(bf16[1,64,4096]{2,1,0:T(8,128)(2,1)S(1)} %bitcast.173), channel_id=1, source_target_pairs={{0,16},{4,20},{8,24},{12,28},{16,0},{20,4},{24,8},{28,12},{1,17},{... | collective-permute-start | bytes 1572872 | tf_op jit(solution)/shard_map/ppermute | solution.py:52
  33.7 23.0 %collective-permute-start.3 = (bf16[1,64,4096]{2,1,0:T(8,128)(2,1)S(1)}, bf16[1,64,4096]{2,1,0:T(8,128)(2,1)S(1)}, u32[]{:S(2)}, u32[]{:S(2)}) collective-permute-start(bf16[1,64,4096]{2,1,0:T(8,128)(2,1)S(1)} %bitcast.171), channel_id=1, source_target_pairs={{0,8},{4,12},{8,0},{12,4},{16,24},{20,28},{24,16},{28,20},{1,9},{5... | collective-permute-start | bytes 1572872 | tf_op jit(solution)/shard_map/ppermute | solution.py:52
  52.2 32.9 %collective-permute-start.6 = (bf16[2,64,4096]{2,1,0:T(8,128)(2,1)S(1)}, bf16[2,64,4096]{2,1,0:T(8,128)(2,1)S(1)}, u32[]{:S(2)}, u32[]{:S(2)}) collective-permute-start(bf16[2,64,4096]{2,1,0:T(8,128)(2,1)S(1)} %pad_maximum_fusion.4), channel_id=1, source_target_pairs={{0,8},{4,12},{8,0},{12,4},{16,24},{20,28},{24,16},{28,20},{1,9},{5... | collective-permute-start | bytes 3145736 | tf_op jit(solution)/shard_map/ppermute | solution.py:52
  56.8 29.7 %collective-permute-start.4 = (bf16[2,64,4096]{2,1,0:T(8,128)(2,1)S(1)}, bf16[2,64,4096]{2,1,0:T(8,128)(2,1)S(1)}, u32[]{:S(2)}, u32[]{:S(2)}) collective-permute-start(bf16[2,64,4096]{2,1,0:T(8,128)(2,1)S(1)} %pad_maximum_fusion.3), channel_id=1, source_target_pairs={{0,16},{4,20},{8,24},{12,28},{16,0},{20,4},{24,8},{28,12},{1,17},{... | collective-permute-start | bytes 3145736 | tf_op jit(solution)/shard_map/ppermute | solution.py:52
  97.1 6.8 %collective-permute-start.8 = (bf16[4,64,4096]{2,1,0:T(8,128)(2,1)}, bf16[4,64,4096]{2,1,0:T(8,128)(2,1)}, u32[]{:S(2)}, u32[]{:S(2)}) collective-permute-start(bf16[4,64,4096]{2,1,0:T(8,128)(2,1)} %copy-done.15), channel_id=1, source_target_pairs={{0,4},{4,0},{8,12},{12,8},{16,20},{20,16},{24,28},{28,24},{1,5},{5... | collective-permute-start | bytes 6291464 | tf_op jit(solution)/shard_map/ppermute | solution.py:52
  97.2 7.3 %collective-permute-start.7 = (bf16[4,64,4096]{2,1,0:T(8,128)(2,1)S(1)}, bf16[4,64,4096]{2,1,0:T(8,128)(2,1)}, u32[]{:S(2)}, u32[]{:S(2)}) collective-permute-start(bf16[4,64,4096]{2,1,0:T(8,128)(2,1)S(1)} %constant_dynamic-update-slice_fusion.2.refs_1_), channel_id=1, source_target_pairs={{0,4},{4,0},{8,12},{12,8},{16,20},{20,16},{24,28},{28,24},{1,5},{5... | collective-permute-start | bytes 6291464 | tf_op jit(solution)/shard_map/ppermute | solution.py:52
  102.4 25.3 %copy-start.6 = (bf16[1024,128]{1,0:T(8,128)(2,1)}, bf16[1024,128]{1,0:T(8,128)(2,1)S(1)}, u32[]{:S(2)}) copy-start(bf16[1024,128]{1,0:T(8,128)(2,1)S(1)} %pad.4.refs_11_.refs_7_.wr_ref.router_ref) | copy-start | bytes 786436
  122.2 174.4 %copy-start.19 = (f32[256,1024]{1,0:T(8,128)}, f32[256,1024]{1,0:T(8,128)S(1)}, u32[]{:S(2)}) copy-start(f32[256,1024]{1,0:T(8,128)S(1)} %get-tuple-element.102.h1_ref.refs_2_) | copy-start | bytes 3145732
  123.3 35.7 %all-to-all-start.2 = ((bf16[4,160,1024]{2,1,0:T(8,128)(2,1)}), bf16[4,160,1024]{2,1,0:T(8,128)(2,1)S(1)}, u32[]{:S(2)}, u32[]{:S(2)}) async-start(bf16[4,160,1024]{2,1,0:T(8,128)(2,1)} %bitcast.142), calls=%async_computation.2 | async-start | bytes 2621440 | tf_op jit(solution)/shard_map/all_to_all | solution.py:97
  127.7 17.2 %copy-start.41 = (s32[2,256]{0,1:T(8,128)}, s32[2,256]{0,1:T(8,128)S(1)}, u32[]{:S(2)}) copy-start(s32[2,256]{0,1:T(8,128)S(1)} %copy.102) | copy-start | bytes 6148
  159.0 39.1 %all-to-all-start.1 = ((bf16[4,160,1024]{2,1,0:T(8,128)(2,1)}), bf16[4,160,1024]{2,1,0:T(8,128)(2,1)}, u32[]{:S(2)}, u32[]{:S(2)}) async-start(bf16[4,160,1024]{2,1,0:T(8,128)(2,1)} %bitcast.36), calls=%async_computation.1 | async-start | bytes 2621440 | tf_op jit(solution)/shard_map/all_to_all | solution.py:97
  198.1 40.1 %all-to-all-start.3 = ((bf16[4,160,1152]{2,1,0:T(8,128)(2,1)}), bf16[4,160,1152]{2,1,0:T(8,128)(2,1)S(1)}, u32[]{:S(2)}, u32[]{:S(2)}) async-start(bf16[4,160,1152]{2,1,0:T(8,128)(2,1)} %bitcast.176), calls=%async_computation.3 | async-start | bytes 2949120 | tf_op jit(solution)/shard_map/all_to_all | solution.py:97
  238.2 39.3 %all-to-all-start.4 = ((bf16[4,160,1152]{2,1,0:T(8,128)(2,1)}), bf16[4,160,1152]{2,1,0:T(8,128)(2,1)}, u32[]{:S(2)}, u32[]{:S(2)}) async-start(bf16[4,160,1152]{2,1,0:T(8,128)(2,1)} %bitcast.175), calls=%async_computation.4 | async-start | bytes 2949120 | tf_op jit(solution)/shard_map/all_to_all | solution.py:97
  242.6 193.7 %reduce-scatter.2.cloned.1.call-start = ((), (), s32[]{:S(2)}) async-start(), calls=%async_computation.9 | async-start | bytes 19464192 | tf_op jit(solution)/shard_map/reduce_scatter | solution.py:892
  242.6 22.4 %slice-start.2 = ((s8[7208960]{0:T(1024)(128)(4,1)}), s8[4194304]{0:T(1024)(128)(4,1)S(1)}, s32[]{:S(2)}) async-start(s8[7208960]{0:T(1024)(128)(4,1)} %bitcast.137), calls=%async_computation.13 | async-start | bytes 8388608
  242.6 22.4 %slice-start.3 = ((s8[7208960]{0:T(1024)(128)(4,1)}), s8[3014656]{0:T(1024)(128)(4,1)S(1)}, s32[]{:S(2)}) async-start(s8[7208960]{0:T(1024)(128)(4,1)} %bitcast.137), calls=%async_computation.14 | async-start | bytes 6029312
  278.3 16.2 %copy-start.28 = (s32[2,256,2]{2,1,0:T(8,128)}, s32[2,256,2]{2,1,0:T(8,128)S(1)}, u32[]{:S(2)}) copy-start(s32[2,256,2]{2,1,0:T(8,128)S(1)} %copy.106.routes_ref) | copy-start | bytes 12292
  284.4 12.2 %copy-start.53 = (s32[256,2]{1,0:T(8,128)S(1)}, s32[256,2]{1,0:T(8,128)}, u32[]{:S(2)}) copy-start(s32[256,2]{1,0:T(8,128)} %get-tuple-element.187.targets_ref) | copy-start | bytes 6148
  295.4 14.0 %copy-start.9 = (bf16[256,3072]{1,0:T(8,128)(2,1)}, bf16[256,3072]{1,0:T(8,128)(2,1)S(1)}, u32[]{:S(2)}) copy-start(bf16[256,3072]{1,0:T(8,128)(2,1)S(1)} %get-tuple-element.118.refs_5_.refs_1_) | copy-start | bytes 4718596
  296.7 12.7 %copy-start.56 = (bf16[256,1024]{1,0:T(8,128)(2,1)S(1)}, bf16[256,1024]{1,0:T(8,128)(2,1)}, u32[]{:S(2)}) copy-start(bf16[256,1024]{1,0:T(8,128)(2,1)} %copy-done.55) | copy-start | bytes 1572868
  296.7 12.6 %copy-start.58 = (bf16[256,1024]{1,0:T(8,128)(2,1)S(1)}, bf16[256,1024]{1,0:T(8,128)(2,1)}, u32[]{:S(2)}) copy-start(bf16[256,1024]{1,0:T(8,128)(2,1)} %copy-done.57) | copy-start | bytes 1572868
  296.7 12.6 %copy-start.60 = (bf16[256,1024]{1,0:T(8,128)(2,1)S(1)}, bf16[256,1024]{1,0:T(8,128)(2,1)}, u32[]{:S(2)}) copy-start(bf16[256,1024]{1,0:T(8,128)(2,1)} %copy-done.59) | copy-start | bytes 1572868
  296.7 12.6 %copy-start.62 = (bf16[256,1024]{1,0:T(8,128)(2,1)S(1)}, bf16[256,1024]{1,0:T(8,128)(2,1)}, u32[]{:S(2)}) copy-start(bf16[256,1024]{1,0:T(8,128)(2,1)} %copy-done.61) | copy-start | bytes 1572868
  319.0 8.0 %collective-permute-start.9 = (bf16[4,128,4096]{2,1,0:T(8,128)(2,1)}, bf16[4,128,4096]{2,1,0:T(8,128)(2,1)}, u32[]{:S(2)}, u32[]{:S(2)}) collective-permute-start(bf16[4,128,4096]{2,1,0:T(8,128)(2,1)} %get-tuple-element.116), channel_id=1, source_target_pairs={{0,4},{4,0},{8,12},{12,8},{16,20},{20,16},{24,28},{28,24},{1,5},{5... | collective-permute-start | bytes 12582920 | tf_op jit(solution)/shard_map/ppermute | solution.py:52
  319.0 79.3 %all-to-all-start.5 = ((bf16[4,2,160,1024]{3,2,1,0:T(8,128)(2,1)}), bf16[4,2,160,1024]{3,2,1,0:T(8,128)(2,1)S(1)}, u32[]{:S(2)}, u32[]{:S(2)}) async-start(bf16[4,2,160,1024]{3,2,1,0:T(8,128)(2,1)} %get-tuple-element.115), calls=%async_computation.5 | async-start | bytes 5242880 | tf_op jit(solution)/shard_map/all_to_all | solution.py:97
  332.2 48.4 %collective-permute-start.10 = (bf16[2,1,64,4096]{3,2,1,0:T(8,128)(2,1)S(1)}, bf16[2,1,64,4096]{3,2,1,0:T(8,128)(2,1)S(1)}, u32[]{:S(2)}, u32[]{:S(2)}) collective-permute-start(bf16[2,1,64,4096]{3,2,1,0:T(8,128)(2,1)S(1)} %dynamic-slice_bitcast_fusion.1), channel_id=1, source_target_pairs={{0,8},{4,12},{8,0},{12,4},{16,24},{20,28},{24,16},{28,20},{1,9},{5... | collective-permute-start | bytes 3145736 | tf_op jit(solution)/shard_map/ppermute | solution.py:52
  333.8 48.3 %collective-permute-start.12 = (bf16[1,2,64,4096]{3,2,1,0:T(8,128)(2,1)S(1)}, bf16[1,2,64,4096]{3,2,1,0:T(8,128)(2,1)S(1)}, u32[]{:S(2)}, u32[]{:S(2)}) collective-permute-start(bf16[1,2,64,4096]{3,2,1,0:T(8,128)(2,1)S(1)} %dynamic-slice_bitcast_fusion), channel_id=1, source_target_pairs={{0,16},{4,20},{8,24},{12,28},{16,0},{20,4},{24,8},{28,12},{1,17},{... | collective-permute-start | bytes 3145736 | tf_op jit(solution)/shard_map/ppermute | solution.py:52
  380.9 16.1 %collective-permute-start.11 = (bf16[1,1,64,4096]{3,2,1,0:T(8,128)(2,1)S(1)}, bf16[1,1,64,4096]{3,2,1,0:T(8,128)(2,1)S(1)}, u32[]{:S(2)}, u32[]{:S(2)}) collective-permute-start(bf16[1,1,64,4096]{3,2,1,0:T(8,128)(2,1)S(1)} %constant_dynamic-slice_fusion.1), channel_id=1, source_target_pairs={{0,16},{4,20},{8,24},{12,28},{16,0},{20,4},{24,8},{28,12},{1,17},{... | collective-permute-start | bytes 1572872 | tf_op jit(solution)/shard_map/ppermute | solution.py:52
  382.4 14.5 %collective-permute-start.13 = (bf16[1,1,64,4096]{3,2,1,0:T(8,128)(2,1)S(1)}, bf16[1,1,64,4096]{3,2,1,0:T(8,128)(2,1)S(1)}, u32[]{:S(2)}, u32[]{:S(2)}) collective-permute-start(bf16[1,1,64,4096]{3,2,1,0:T(8,128)(2,1)S(1)} %constant_dynamic-slice_fusion), channel_id=1, source_target_pairs={{0,8},{4,12},{8,0},{12,4},{16,24},{20,28},{24,16},{28,20},{1,9},{5... | collective-permute-start | bytes 1572872 | tf_op jit(solution)/shard_map/ppermute | solution.py:52
  398.3 25.4 %copy-start.25 = (s32[2,256,2]{2,1,0:T(8,128)S(1)}, s32[2,256,2]{2,1,0:T(8,128)}, u32[]{:S(2)}) copy-start(s32[2,256,2]{2,1,0:T(8,128)} %copy-done.24) | copy-start | bytes 12292
  398.3 25.4 %copy-start.29 = (s32[2,256,2]{2,1,0:T(8,128)S(1)}, s32[2,256,2]{2,1,0:T(8,128)}, u32[]{:S(2)}) copy-start(s32[2,256,2]{2,1,0:T(8,128)} %copy-done.28) | copy-start | bytes 12292
  398.3 25.4 %copy-start.49 = (f32[256,128]{1,0:T(8,128)S(1)}, f32[256,128]{1,0:T(8,128)}, u32[]{:S(2)}) copy-start(f32[256,128]{1,0:T(8,128)} %copy-done.47) | copy-start | bytes 393220
  398.3 25.4 %copy-start.52 = (f32[256,128]{1,0:T(8,128)S(1)}, f32[256,128]{1,0:T(8,128)}, u32[]{:S(2)}) copy-start(f32[256,128]{1,0:T(8,128)} %copy-done.50) | copy-start | bytes 393220
  398.3 35.1 %all-to-all-start.6 = ((bf16[4,32,4096]{2,1,0:T(8,128)(2,1)}), bf16[4,32,4096]{2,1,0:T(8,128)(2,1)}, u32[]{:S(2)}, u32[]{:S(2)}) async-start(bf16[4,32,4096]{2,1,0:T(8,128)(2,1)} %bitcast.170), calls=%async_computation.6 | async-start | bytes 2097152 | tf_op jit(solution)/shard_map/all_to_all | solution.py:97
  406.3 1.3 collective-permute-start.14
  407.6 4.5 %collective-permute-start.15 = (f32[52,128]{1,0:T(8,128)S(1)}, f32[52,128]{1,0:T(8,128)S(1)}, u32[]{:S(2)}, u32[]{:S(2)}) collective-permute-start(f32[52,128]{1,0:T(8,128)S(1)} %fusion.26), channel_id=1, source_target_pairs={{0,8},{4,12},{8,0},{12,4},{16,24},{20,28},{24,16},{28,20},{1,9},{5... | collective-permute-start | bytes 79880 | tf_op jit(solution)/shard_map/ppermute | solution.py:52
  412.2 4.5 %collective-permute-start.16 = (f32[52,128]{1,0:T(8,128)S(1)}, f32[52,128]{1,0:T(8,128)S(1)}, u32[]{:S(2)}, u32[]{:S(2)}) collective-permute-start(f32[52,128]{1,0:T(8,128)S(1)} %fusion.34), channel_id=1, source_target_pairs={{0,16},{4,20},{8,24},{12,28},{16,0},{20,4},{24,8},{28,12},{1,17},{... | collective-permute-start | bytes 79880 | tf_op jit(solution)/shard_map/ppermute | solution.py:52
  416.7 13.9 %collective-permute-start.17 = (f32[52,128]{1,0:T(8,128)S(1)}, f32[52,128]{1,0:T(8,128)S(1)}, u32[]{:S(2)}, u32[]{:S(2)}) collective-permute-start(f32[52,128]{1,0:T(8,128)S(1)} %add.221), channel_id=1, source_target_pairs={{0,2},{1,3},{2,0},{3,1},{4,6},{5,7},{6,4},{7,5},{8,10},{9,11},{10,... | collective-permute-start | bytes 79880 | tf_op jit(solution)/shard_map/ppermute | solution.py:56
  419.6 11.0 %collective-permute-start.18 = (f32[52,128]{1,0:T(8,128)S(1)}, f32[52,128]{1,0:T(8,128)S(1)}, u32[]{:S(2)}, u32[]{:S(2)}) collective-permute-start(f32[52,128]{1,0:T(8,128)S(1)} %add.221), channel_id=1, source_target_pairs={{0,1},{1,2},{2,3},{3,0},{4,5},{5,6},{6,7},{7,4},{8,9},{9,10},{10,1... | collective-permute-start | bytes 79880 | tf_op jit(solution)/shard_map/ppermute | solution.py:56
  421.1 9.6 %collective-permute-start.19 = (f32[52,128]{1,0:T(8,128)S(1)}, f32[52,128]{1,0:T(8,128)S(1)}, u32[]{:S(2)}, u32[]{:S(2)}) collective-permute-start(f32[52,128]{1,0:T(8,128)S(1)} %add.221), channel_id=1, source_target_pairs={{0,3},{1,0},{2,1},{3,2},{4,7},{5,4},{6,5},{7,6},{8,11},{9,8},{10,9... | collective-permute-start | bytes 79880 | tf_op jit(solution)/shard_map/ppermute | solution.py:56
  (62 other events, 218.5 us)
Sparse Core Ops, SparseCore 0:
  16.1 56.7 all-gather.5
  97.2 67.0 all-gather.3
  277.6 144.5 reduce-scatter.1

commit v9 on v8

--- a/solution.py
+++ b/solution.py
@@ -312,7 +312,7 @@
         out_specs=pl.BlockSpec((size, tiles * part, tile), lambda j: (0, j, 0)),
         out_shape=jax.ShapeDtypeStruct((size, space, tile), BF16),
         scratch_shapes=[pltpu.VMEM((width, total), BF16)],
-        compiler_params=pltpu.CompilerParams(vmem_limit_bytes=56 << 20),
+        compiler_params=pltpu.CompilerParams(vmem_limit_bytes=40 << 20),
         cost_estimate=LIGHT,
         name="weight_in",
     )(*xs, du)

time: 456 us -> 463 us (1.015)
  waiting for transfers between devices: 123 us -> 130 us
    ppermute x14, waiting for transfers between devices: 101 us -> 109 us  [flip(): return lax.ppermute(value, axis, [(i, i ^ bit) for i in range(size)])]
    unnamed x167 -> x175, local copies, waits for them, and re-layouts: 45.1 us -> 46 us
  transfers between devices with their start and end apart: 30 -> 30, of which waited for: 17 -> 17; matrix products, arithmetic and copies ran while one was open for 11% -> 10% of each run, Pallas kernels for 35% -> 35%
where the time goes in v9:
time: 463 us; the launch traced here: 455 us
  Pallas kernels  160 us (35%)
  waiting for transfers between devices  130 us (28%)
  local copies, waits for them, and re-layouts  66.6 us (14%)
  starting transfers between devices  58.5 us (13%)
  other arithmetic  19.3 us (4%)
  between operations  15.1 us (3%)
  matrix products  5.2 us (1%)
    ppermute x14, waiting for transfers between devices, flip(): return lax.ppermute(value, axis, [(i, i ^ bit) for i in range(size)])  109 us
    pallas_call x2, Pallas kernels, expert_call(): pl.pallas_call(expert_body, grid=(tiles,), in_specs=in_specs, out_specs=[...  67.6 us
    unnamed x175, local copies, waits for them, and re-layouts  46 us
    all_to_all x7, starting transfers between devices, all_to_all(): lax.all_to_all(value, 'expert', split_axis=0, concat_axis=0, tiled=True)  30.9 us
    pallas_call x1, Pallas kernels, weight_in_call(): pl.pallas_call(weight_in_body, grid=(2,), in_specs=[pl.BlockSpec((rows, w...  21.7 us
    pallas_call x2, Pallas kernels, backward_call(): pl.pallas_call(partial(backward_body, heads, experts), grid=(1,), in_spec...  21.4 us
    pallas_call x2, Pallas kernels, forward_call(): pl.pallas_call(partial(forward_body, heads, experts, rels), in_specs=in_s...  20.4 us
    all_to_all x7, waiting for transfers between devices, all_to_all(): lax.all_to_all(value, 'expert', split_axis=0, concat_axis=0, tiled=True)  19.2 us
  transfers between devices with their start and end apart: 30, of which 17 were waited for; matrix products, arithmetic and copies ran while one was open for 10% of the time, Pallas kernels for 35%

profile of v9, /device:TPU:0, one launch (start us, length us, event | category | flops | bytes accessed | tf_op | source)
XLA Modules:
  0.0 454.6 jit_solution(15111908901591008154)
XLA Ops:
  9.0 3.0 collective-permute-start
  12.1 2.6 collective-permute-start.1
  16.8 2.4 reduce-window.6
  23.5 1.7 pad_maximum_fusion.1
  25.2 4.6 %all-to-all-start = ((bf16[4,2,160,1024]{3,2,1,0:T(8,128)(2,1)}), bf16[4,2,160,1024]{3,2,1,0:T(8,128)(2,1)}, u32[]{:S(2)}, u32[]{:S(2)}) async-start(bf16[4,2,160,1024]{3,2,1,0:T(8,128)(2,1)} %pad_maximum_fusion.1), calls=%async_computation | async-start | bytes 5242880 | tf_op jit(solution)/shard_map/all_to_all | solution.py:97
  35.3 2.8 fusion
  38.1 4.4 copy.125
  42.4 9.7 %collective-permute-done.5 = bf16[1,64,4096]{2,1,0:T(8,128)(2,1)S(1)} collective-permute-done((bf16[1,64,4096]{2,1,0:T(8,128)(2,1)S(1)}, bf16[1,64,4096]{2,1,0:T(8,128)(2,1)S(1)}, u32[]{:S(2)}, u32[]{:S(2)}) %collective-permute-start.5) | collective-permute-done | bytes 524320 | tf_op jit(solution)/shard_map/ppermute | solution.py:52
  53.5 3.2 collective-permute-done.3
  57.1 28.1 %collective-permute-done.6 = bf16[2,64,4096]{2,1,0:T(8,128)(2,1)S(1)} collective-permute-done((bf16[2,64,4096]{2,1,0:T(8,128)(2,1)S(1)}, bf16[2,64,4096]{2,1,0:T(8,128)(2,1)S(1)}, u32[]{:S(2)}, u32[]{:S(2)}) %collective-permute-start.6) | collective-permute-done | bytes 1048608 | tf_op jit(solution)/shard_map/ppermute | solution.py:52
  86.7 6.9 %all-to-all-done = bf16[4,2,160,1024]{3,2,1,0:T(8,128)(2,1)} async-done(((bf16[4,2,160,1024]{3,2,1,0:T(8,128)(2,1)}), bf16[4,2,160,1024]{3,2,1,0:T(8,128)(2,1)}, u32[]{:S(2)}, u32[]{:S(2)}) %all-to-all-start) | async-done | bytes 2621472 | tf_op jit(solution)/shard_map/all_to_all | solution.py:97
  93.6 3.4 fusion.29
  100.3 3.5 collective-permute-done.8.refs_4_
  104.4 2.6 copy-done.3
  107.0 11.7 %attention_forward.2 = (bf16[640,1024]{1,0:T(8,128)(2,1)S(1)}, bf16[256,1024]{1,0:T(8,128)(2,1)S(1)}, bf16[256,3072]{1,0:T(8,128)(2,1)S(1)}, f32[16,256]{1,0:T(8...) custom-call(s32[1]{0:T(128)} %bitcast.1.refs_0_, ...), custom_call_target="tpu_custom_call" | custom-call | flops 1 | bytes 1 | tf_op jit(solution)/shard_map/attention_forward/pallas_call | solution.py:577
  124.8 4.1 all-to-all-start.2
  129.2 4.3 copy-done.2
  133.6 2.2 copy-done.4
  135.8 8.7 %attention_forward.3 = (bf16[640,1024]{1,0:T(8,128)(2,1)S(1)}, bf16[256,1024]{1,0:T(8,128)(2,1)S(1)}, bf16[256,3072]{1,0:T(8,128)(2,1)S(1)}, f32[16,256]{1,0:T(8...) custom-call(bf16[1024,4096]{1,0:T(8,128)(2,1)S(1)} %copy-done.2, ...), custom_call_target="tpu_custom_call" | custom-call | flops 1 | bytes 1 | tf_op jit(solution)/shard_map/attention_forward/pallas_call | solution.py:577
  150.6 10.0 %all-to-all-done.2 = bf16[4,160,1024]{2,1,0:T(8,128)(2,1)S(1)} async-done(((bf16[4,160,1024]{2,1,0:T(8,128)(2,1)}), bf16[4,160,1024]{2,1,0:T(8,128)(2,1)S(1)}, u32[]{:S(2)}, u32[]{:S(2)}) %all-to-all-start.2) | async-done | bytes 1310752 | tf_op jit(solution)/shard_map/all_to_all | solution.py:97
  160.6 3.6 all-to-all-start.1
  164.8 33.8 %expert.2 = (bf16[4,2,160,1024]{3,2,1,0:T(8,128)(2,1)}, bf16[640,1152]{1,0:T(8,128)(2,1)}, bf16[2816,1280]{1,0:T(8,128)(2,1)}, bf16[2,1280,2816]{2,1,0:T(8,128)(2,1)}, bf16[1280,1024]{1,0:T(8,128)(2,1)}) custom-call(s32[2]{0:T(128)} %pad_add_fusion.4.mine, bf16[640,1024]{1,0:T(8,128)(2,1)} %bitcast.139, bf16[640,1024]{1,0:T(8,128)(2,1)} %bitcast.168, ...), custom_call_target="tpu_custom_call" | custom-call | flops 1 | bytes 1 | tf_op jit(solution)/shard_map/expert/pallas_call | solution.py:251
  198.6 5.3 %all-to-all-start.3 = ((bf16[4,160,1152]{2,1,0:T(8,128)(2,1)}), bf16[4,160,1152]{2,1,0:T(8,128)(2,1)}, u32[]{:S(2)}, u32[]{:S(2)}) async-start(bf16[4,160,1152]{2,1,0:T(8,128)(2,1)} %bitcast.178), calls=%async_computation.3 | async-start | bytes 2949120 | tf_op jit(solution)/shard_map/all_to_all | solution.py:97
  203.9 33.8 %expert.3 = (bf16[4,2,160,1024]{3,2,1,0:T(8,128)(2,1)}, bf16[640,1152]{1,0:T(8,128)(2,1)}, bf16[2816,1280]{1,0:T(8,128)(2,1)}, bf16[2,1280,2816]{2,1,0:T(8,128)(2,1)}, bf16[1280,1024]{1,0:T(8,128)(2,1)}) custom-call(s32[2]{0:T(128)} %pad_add_fusion.4.mine, ...), custom_call_target="tpu_custom_call", output_to_operand_aliasing={{0}: (7, {}), {2}: (8, {}), {3}: (9, {}), {4}: (10, {})} | custom-call | flops 1 | bytes 1 | tf_op jit(solution)/shard_map/expert/pallas_call | solution.py:251
  238.3 4.7 %all-to-all-start.4 = ((bf16[4,160,1152]{2,1,0:T(8,128)(2,1)}), bf16[4,160,1152]{2,1,0:T(8,128)(2,1)}, u32[]{:S(2)}, u32[]{:S(2)}) async-start(bf16[4,160,1152]{2,1,0:T(8,128)(2,1)} %bitcast.177), calls=%async_computation.4 | async-start | bytes 2949120 | tf_op jit(solution)/shard_map/all_to_all | solution.py:97
  243.0 21.7 %weight_in.1._ = bf16[8,4224,256]{2,1,0:T(8,128)(2,1)} custom-call(bf16[640,1024]{1,0:T(8,128)(2,1)S(1)} %bitcast.140, bf16[640,1024]{1,0:T(8,128)(2,1)S(1)} %bitcast.142, bf16[2,1280,2816]{2,1,0:T(8,128)(2,1)} %get-tuple-element.97.refs_2_), custom_call_target="tpu_custom_call" | custom-call | flops 1 | bytes 1 | tf_op jit(solution)/shard_map/weight_in/pallas_call | solution.py:307
  264.7 10.7 %weight_out.1 = bf16[8,4224,256]{2,1,0:T(8,128)(2,1)} custom-call(bf16[2816,1280]{1,0:T(8,128)(2,1)S(1)} %bitcast.138, bf16[1280,1024]{1,0:T(8,128)(2,1)S(1)} %copy-done.12, bf16[8,4224,256]{2,1,0:T(8,128)(2,1)} %weight_in.1._), custom_call_target="tpu_custom_call", output_to_operand_aliasing={{}: (2, {})} | custom-call | flops 1 | bytes 1 | tf_op jit(solution)/shard_map/weight_out/pallas_call | solution.py:332
  275.4 1.8 all-to-all-done.4
  280.0 2.3 copy-done.5
  285.1 10.4 %attention_backward.3 = (f32[256,1024]{1,0:T(8,128)S(1)}, bf16[256,1024]{1,0:T(8,128)(2,1)S(1)}, bf16[256,3072]{1,0:T(8,128)(2,1)S(1)}, bf16[16,256,256]{2,1,0:T...) custom-call(bf16[640,1152]{1,0:T(8,128)(2,1)} %bitcast.47.dx_ref, s32[256,2]{1,0:T(8,128)S(1)} %copy-done.50, ...), custom_call_target="tpu_custom_call" | custom-call | flops 1 | bytes 1 | tf_op jit(solution)/shard_map/attention_backward/pallas_call | solution.py:682
  299.3 10.9 %attention_backward.2 = (f32[256,1024]{1,0:T(8,128)S(1)}, bf16[256,1024]{1,0:T(8,128)(2,1)S(1)}, bf16[256,3072]{1,0:T(8,128)(2,1)S(1)}, bf16[16,256,256]{2,1,0:T...) custom-call(bf16[640,1152]{1,0:T(8,128)(2,1)} %bitcast.45.dx_ref, s32[256,2]{1,0:T(8,128)S(1)} %copy-done.49, ...), custom_call_target="tpu_custom_call" | custom-call | flops 1 | bytes 1 | tf_op jit(solution)/shard_map/attention_backward/pallas_call | solution.py:682
  312.6 7.5 %weight_attn.1 = (bf16[4,128,4096]{2,1,0:T(8,128)(2,1)S(1)}, bf16[4,128,4096]{2,1,0:T(8,128)(2,1)}) custom-call(s32[1]{0:T(128)S(6)} %select_n.107.core_ref, bf16[256,1024]{1,0:T(8,128)(2,1)S(1)} %copy-done.52, bf16[256,1024]{1,0:T(8,128)(2,1)S(1)} %copy-done.56, bf16[256,1024]{1,0:T(8,128)(2,1)S(1)} %copy-done.54, bf16[256,1024]{1,0:T(8,128)(2,1)S(1)} %copy-done.58, ...), custom_call_target="tpu_custom_call" | custom-call | flops 1 | bytes 1 | tf_op jit(solution)/shard_map/weight_attn/pallas_call | solution.py:405
  320.1 2.0 copy-done.19
  322.2 3.7 all-to-all-start.5
  325.8 2.8 pad_maximum_fusion
  329.7 3.8 add_convert_fusion
  338.0 5.2 %finish.1 = (bf16[2,256,1024]{2,1,0:T(8,128)(2,1)}, f32[1,1024]{1,0:T(1,128)S(1)}) custom-call(bf16[2,256,1024]{2,1,0:T(8,128)(2,1)S(1)} %copy-done.27, f32[1,1024]{1,0:T(1,128)S(1)} %bitcast.160, bf16[1024,4096]{1,0:T(8,128)(2,1)S(1)} %bitcast.132, bf16[256,3072]{1,0:T(8,128)(2,1)S(1)} %copy-done.16, bf16[256,3072]{1,0:T(8,128)(2,1)S(1)} %copy-done.14, ...), custom_call_target="tpu_custom_call" | custom-call | flops 1 | bytes 1 | tf_op jit(solution)/shard_map/finish/pallas_call | solution.py:716
  345.4 37.2 %collective-permute-done.10 = bf16[2,1,64,4096]{3,2,1,0:T(8,128)(2,1)} collective-permute-done((bf16[2,1,64,4096]{3,2,1,0:T(8,128)(2,1)S(1)}, bf16[2,1,64,4096]{3,2,1,0:T(8,128)(2,1)}, u32[]{:S(2)}, u32[]{:S(2)}) %collective-permute-start.10) | collective-permute-done | bytes 1048608 | tf_op jit(solution)/shard_map/ppermute | solution.py:52
  387.1 16.6 %collective-permute-done.11 = bf16[1,1,64,4096]{3,2,1,0:T(8,128)(2,1)S(1)} collective-permute-done((bf16[1,1,64,4096]{3,2,1,0:T(8,128)(2,1)S(1)}, bf16[1,1,64,4096]{3,2,1,0:T(8,128)(2,1)S(1)}, u32[]{:S(2)}, u32[]{:S(2)}) %collective-permute-start.11) | collective-permute-done | bytes 524320 | tf_op jit(solution)/shard_map/ppermute | solution.py:52
  403.7 2.5 collective-permute-done.13
  407.5 5.0 %all-to-all-start.6 = ((bf16[4,32,4096]{2,1,0:T(8,128)(2,1)}), bf16[4,32,4096]{2,1,0:T(8,128)(2,1)}, u32[]{:S(2)}, u32[]{:S(2)}) async-start(bf16[4,32,4096]{2,1,0:T(8,128)(2,1)} %bitcast.172), calls=%async_computation.6 | async-start | bytes 2097152 | tf_op jit(solution)/shard_map/all_to_all | solution.py:97
  417.1 2.4 collective-permute-start.15
  419.4 2.5 collective-permute-done.15
  422.7 3.2 collective-permute-done.16
  425.9 2.9 collective-permute-start.17
  430.3 2.6 collective-permute-start.19
  435.3 3.0 output.1
  445.6 2.2 spread.1
  (287 shorter events, 75.7 us)
Async XLA Ops:
  7.2 28.1 %copy-start = (f32[32,16]{0,1:T(8,128)S(1)}, f32[32,16]{0,1:T(8,128)}, u32[]{:S(2)}) copy-start(f32[32,16]{0,1:T(8,128)} %param.21) | copy-start | bytes 6148
  7.2 157.6 %all-gather.6.cloned.1.call-start = ((), (), s32[]{:S(2)}) async-start(), calls=%async_computation.10 | async-start | bytes 6488064 | tf_op jit(solution)/shard_map/all_gather | solution.py:811
  9.0 21.0 %collective-permute-start = (bf16[32,4096]{1,0:T(8,128)(2,1)S(1)}, bf16[32,4096]{1,0:T(8,128)(2,1)S(1)}, u32[]{:S(2)}, u32[]{:S(2)}) collective-permute-start(bf16[32,4096]{1,0:T(8,128)(2,1)S(1)} %constant_dynamic-update-slice_fusion), channel_id=1, source_target_pairs={{0,1},{1,2},{2,3},{3,0},{4,5},{5,6},{6,7},{7,4},{8,9},{9,10},{10,1... | collective-permute-start | bytes 786440 | tf_op jit(solution)/shard_map/ppermute | solution.py:56
  12.1 19.7 %collective-permute-start.1 = (bf16[32,4096]{1,0:T(8,128)(2,1)S(1)}, bf16[32,4096]{1,0:T(8,128)(2,1)S(1)}, u32[]{:S(2)}, u32[]{:S(2)}) collective-permute-start(bf16[32,4096]{1,0:T(8,128)(2,1)S(1)} %constant_dynamic-update-slice_fusion), channel_id=1, source_target_pairs={{0,2},{1,3},{2,0},{3,1},{4,6},{5,7},{6,4},{7,5},{8,10},{9,11},{10,... | collective-permute-start | bytes 786440 | tf_op jit(solution)/shard_map/ppermute | solution.py:56
  14.6 17.1 %collective-permute-start.2 = (bf16[32,4096]{1,0:T(8,128)(2,1)S(1)}, bf16[32,4096]{1,0:T(8,128)(2,1)S(1)}, u32[]{:S(2)}, u32[]{:S(2)}) collective-permute-start(bf16[32,4096]{1,0:T(8,128)(2,1)S(1)} %constant_dynamic-update-slice_fusion), channel_id=1, source_target_pairs={{0,3},{1,0},{2,1},{3,2},{4,7},{5,4},{6,5},{7,6},{8,11},{9,8},{10,9... | collective-permute-start | bytes 786440 | tf_op jit(solution)/shard_map/ppermute | solution.py:56
  25.2 68.4 %all-to-all-start = ((bf16[4,2,160,1024]{3,2,1,0:T(8,128)(2,1)}), bf16[4,2,160,1024]{3,2,1,0:T(8,128)(2,1)}, u32[]{:S(2)}, u32[]{:S(2)}) async-start(bf16[4,2,160,1024]{3,2,1,0:T(8,128)(2,1)} %pad_maximum_fusion.1), calls=%async_computation | async-start | bytes 5242880 | tf_op jit(solution)/shard_map/all_to_all | solution.py:97
  29.8 135.1 %all-gather.4.cloned.1.call-start = ((), (), s32[]{:S(2)}) async-start(), calls=%async_computation.8 | async-start | bytes 12976128 | tf_op jit(solution)/shard_map/all_gather | solution.py:812
  31.9 20.2 %collective-permute-start.5 = (bf16[1,64,4096]{2,1,0:T(8,128)(2,1)S(1)}, bf16[1,64,4096]{2,1,0:T(8,128)(2,1)S(1)}, u32[]{:S(2)}, u32[]{:S(2)}) collective-permute-start(bf16[1,64,4096]{2,1,0:T(8,128)(2,1)S(1)} %bitcast.175), channel_id=1, source_target_pairs={{0,16},{4,20},{8,24},{12,28},{16,0},{20,4},{24,8},{28,12},{1,17},{... | collective-permute-start | bytes 1572872 | tf_op jit(solution)/shard_map/ppermute | solution.py:52
  33.7 23.0 %collective-permute-start.3 = (bf16[1,64,4096]{2,1,0:T(8,128)(2,1)S(1)}, bf16[1,64,4096]{2,1,0:T(8,128)(2,1)S(1)}, u32[]{:S(2)}, u32[]{:S(2)}) collective-permute-start(bf16[1,64,4096]{2,1,0:T(8,128)(2,1)S(1)} %bitcast.173), channel_id=1, source_target_pairs={{0,8},{4,12},{8,0},{12,4},{16,24},{20,28},{24,16},{28,20},{1,9},{5... | collective-permute-start | bytes 1572872 | tf_op jit(solution)/shard_map/ppermute | solution.py:52
  52.2 32.9 %collective-permute-start.6 = (bf16[2,64,4096]{2,1,0:T(8,128)(2,1)S(1)}, bf16[2,64,4096]{2,1,0:T(8,128)(2,1)S(1)}, u32[]{:S(2)}, u32[]{:S(2)}) collective-permute-start(bf16[2,64,4096]{2,1,0:T(8,128)(2,1)S(1)} %pad_maximum_fusion.4), channel_id=1, source_target_pairs={{0,8},{4,12},{8,0},{12,4},{16,24},{20,28},{24,16},{28,20},{1,9},{5... | collective-permute-start | bytes 3145736 | tf_op jit(solution)/shard_map/ppermute | solution.py:52
  56.8 29.8 %collective-permute-start.4 = (bf16[2,64,4096]{2,1,0:T(8,128)(2,1)S(1)}, bf16[2,64,4096]{2,1,0:T(8,128)(2,1)S(1)}, u32[]{:S(2)}, u32[]{:S(2)}) collective-permute-start(bf16[2,64,4096]{2,1,0:T(8,128)(2,1)S(1)} %pad_maximum_fusion.3), channel_id=1, source_target_pairs={{0,16},{4,20},{8,24},{12,28},{16,0},{20,4},{24,8},{28,12},{1,17},{... | collective-permute-start | bytes 3145736 | tf_op jit(solution)/shard_map/ppermute | solution.py:52
  97.1 6.8 %collective-permute-start.8 = (bf16[4,64,4096]{2,1,0:T(8,128)(2,1)}, bf16[4,64,4096]{2,1,0:T(8,128)(2,1)}, u32[]{:S(2)}, u32[]{:S(2)}) collective-permute-start(bf16[4,64,4096]{2,1,0:T(8,128)(2,1)} %copy-done.17), channel_id=1, source_target_pairs={{0,4},{4,0},{8,12},{12,8},{16,20},{20,16},{24,28},{28,24},{1,5},{5... | collective-permute-start | bytes 6291464 | tf_op jit(solution)/shard_map/ppermute | solution.py:52
  97.1 7.3 %collective-permute-start.7 = (bf16[4,64,4096]{2,1,0:T(8,128)(2,1)S(1)}, bf16[4,64,4096]{2,1,0:T(8,128)(2,1)}, u32[]{:S(2)}, u32[]{:S(2)}) collective-permute-start(bf16[4,64,4096]{2,1,0:T(8,128)(2,1)S(1)} %constant_dynamic-update-slice_fusion.2.refs_1_), channel_id=1, source_target_pairs={{0,4},{4,0},{8,12},{12,8},{16,20},{20,16},{24,28},{28,24},{1,5},{5... | collective-permute-start | bytes 6291464 | tf_op jit(solution)/shard_map/ppermute | solution.py:52
  98.9 30.3 %copy-start.6 = (bf16[1024,128]{1,0:T(8,128)(2,1)}, bf16[1024,128]{1,0:T(8,128)(2,1)S(1)}, u32[]{:S(2)}) copy-start(bf16[1024,128]{1,0:T(8,128)(2,1)S(1)} %pad.4.refs_11_.refs_7_.wr_ref.router_ref) | copy-start | bytes 786436
  124.8 35.8 %all-to-all-start.2 = ((bf16[4,160,1024]{2,1,0:T(8,128)(2,1)}), bf16[4,160,1024]{2,1,0:T(8,128)(2,1)S(1)}, u32[]{:S(2)}, u32[]{:S(2)}) async-start(bf16[4,160,1024]{2,1,0:T(8,128)(2,1)} %bitcast.145), calls=%async_computation.2 | async-start | bytes 2621440 | tf_op jit(solution)/shard_map/all_to_all | solution.py:97
  129.0 15.4 %copy-start.61 = (s32[2,256]{1,0:T(2,128)}, s32[2,256]{1,0:T(2,128)S(1)}, u32[]{:S(2)}) copy-start(s32[2,256]{1,0:T(2,128)S(1)} %pad_add_fusion.3.refs_4_.rows_ref) | copy-start | bytes 6148
  129.2 15.2 %copy-start.37 = (s32[2,256]{0,1:T(8,128)}, s32[2,256]{0,1:T(8,128)S(1)}, u32[]{:S(2)}) copy-start(s32[2,256]{0,1:T(8,128)S(1)} %copy.102) | copy-start | bytes 6148
  160.6 38.0 %all-to-all-start.1 = ((bf16[4,160,1024]{2,1,0:T(8,128)(2,1)}), bf16[4,160,1024]{2,1,0:T(8,128)(2,1)S(1)}, u32[]{:S(2)}, u32[]{:S(2)}) async-start(bf16[4,160,1024]{2,1,0:T(8,128)(2,1)} %bitcast.146), calls=%async_computation.1 | async-start | bytes 2621440 | tf_op jit(solution)/shard_map/all_to_all | solution.py:97
  198.6 39.7 %all-to-all-start.3 = ((bf16[4,160,1152]{2,1,0:T(8,128)(2,1)}), bf16[4,160,1152]{2,1,0:T(8,128)(2,1)}, u32[]{:S(2)}, u32[]{:S(2)}) async-start(bf16[4,160,1152]{2,1,0:T(8,128)(2,1)} %bitcast.178), calls=%async_computation.3 | async-start | bytes 2949120 | tf_op jit(solution)/shard_map/all_to_all | solution.py:97
  238.3 38.9 %all-to-all-start.4 = ((bf16[4,160,1152]{2,1,0:T(8,128)(2,1)}), bf16[4,160,1152]{2,1,0:T(8,128)(2,1)}, u32[]{:S(2)}, u32[]{:S(2)}) async-start(bf16[4,160,1152]{2,1,0:T(8,128)(2,1)} %bitcast.177), calls=%async_computation.4 | async-start | bytes 2949120 | tf_op jit(solution)/shard_map/all_to_all | solution.py:97
  243.0 201.0 %reduce-scatter.2.cloned.1.call-start = ((), (), s32[]{:S(2)}) async-start(), calls=%async_computation.9 | async-start | bytes 19464192 | tf_op jit(solution)/shard_map/reduce_scatter | solution.py:892
  243.0 21.7 %slice-start.2 = ((s8[7208960]{0:T(1024)(128)(4,1)}), s8[4194304]{0:T(1024)(128)(4,1)S(1)}, s32[]{:S(2)}) async-start(s8[7208960]{0:T(1024)(128)(4,1)} %bitcast.137), calls=%async_computation.13 | async-start | bytes 8388608
  243.0 21.7 %slice-start.3 = ((s8[7208960]{0:T(1024)(128)(4,1)}), s8[3014656]{0:T(1024)(128)(4,1)S(1)}, s32[]{:S(2)}) async-start(s8[7208960]{0:T(1024)(128)(4,1)} %bitcast.137), calls=%async_computation.14 | async-start | bytes 6029312
  243.0 21.7 %copy-start.12 = (bf16[1280,1024]{1,0:T(8,128)(2,1)S(1)}, bf16[1280,1024]{1,0:T(8,128)(2,1)}, u32[]{:S(2)}) copy-start(bf16[1280,1024]{1,0:T(8,128)(2,1)} %get-tuple-element.95.dy_ref) | copy-start | bytes 7864324
  285.1 14.1 %copy-start.22 = (f32[256,1024]{1,0:T(8,128)S(1)}, f32[256,1024]{1,0:T(8,128)}, u32[]{:S(2)}) copy-start(f32[256,1024]{1,0:T(8,128)} %copy-done.21) | copy-start | bytes 3145732
  285.1 14.1 %copy-start.32 = (bf16[256,3072]{1,0:T(8,128)(2,1)S(1)}, bf16[256,3072]{1,0:T(8,128)(2,1)}, u32[]{:S(2)}) copy-start(bf16[256,3072]{1,0:T(8,128)(2,1)} %copy-done.31) | copy-start | bytes 4718596
  285.1 14.1 %copy-start.44 = (f32[256,128]{1,0:T(8,128)S(1)}, f32[256,128]{1,0:T(8,128)}, u32[]{:S(2)}) copy-start(f32[256,128]{1,0:T(8,128)} %copy-done.43) | copy-start | bytes 393220
  285.1 14.1 %copy-start.49 = (s32[256,2]{1,0:T(8,128)S(1)}, s32[256,2]{1,0:T(8,128)}, u32[]{:S(2)}) copy-start(s32[256,2]{1,0:T(8,128)} %get-tuple-element.187.targets_ref) | copy-start | bytes 6148
  285.1 14.1 %copy-start.64 = (f32[16,256]{1,0:T(8,128)S(1)}, f32[16,256]{1,0:T(8,128)}, u32[]{:S(2)}) copy-start(f32[16,256]{1,0:T(8,128)} %copy-done.63) | copy-start | bytes 49156
  299.2 13.3 %copy-start.13 = (bf16[256,3072]{1,0:T(8,128)(2,1)}, bf16[256,3072]{1,0:T(8,128)(2,1)S(1)}, u32[]{:S(2)}) copy-start(bf16[256,3072]{1,0:T(8,128)(2,1)S(1)} %get-tuple-element.118.refs_5_.refs_1_) | copy-start | bytes 4718596
  299.2 13.3 %copy-start.52 = (bf16[256,1024]{1,0:T(8,128)(2,1)S(1)}, bf16[256,1024]{1,0:T(8,128)(2,1)}, u32[]{:S(2)}) copy-start(bf16[256,1024]{1,0:T(8,128)(2,1)} %copy-done.51) | copy-start | bytes 1572868
  299.2 13.3 %copy-start.54 = (bf16[256,1024]{1,0:T(8,128)(2,1)S(1)}, bf16[256,1024]{1,0:T(8,128)(2,1)}, u32[]{:S(2)}) copy-start(bf16[256,1024]{1,0:T(8,128)(2,1)} %copy-done.53) | copy-start | bytes 1572868
  299.2 13.3 %copy-start.56 = (bf16[256,1024]{1,0:T(8,128)(2,1)S(1)}, bf16[256,1024]{1,0:T(8,128)(2,1)}, u32[]{:S(2)}) copy-start(bf16[256,1024]{1,0:T(8,128)(2,1)} %copy-done.55) | copy-start | bytes 1572868
  322.2 7.5 %collective-permute-start.9 = (bf16[4,128,4096]{2,1,0:T(8,128)(2,1)}, bf16[4,128,4096]{2,1,0:T(8,128)(2,1)}, u32[]{:S(2)}, u32[]{:S(2)}) collective-permute-start(bf16[4,128,4096]{2,1,0:T(8,128)(2,1)} %get-tuple-element.116), channel_id=1, source_target_pairs={{0,4},{4,0},{8,12},{12,8},{16,20},{20,16},{24,28},{28,24},{1,5},{5... | collective-permute-start | bytes 12582920 | tf_op jit(solution)/shard_map/ppermute | solution.py:52
  322.2 85.3 %all-to-all-start.5 = ((bf16[4,2,160,1024]{3,2,1,0:T(8,128)(2,1)}), bf16[4,2,160,1024]{3,2,1,0:T(8,128)(2,1)S(1)}, u32[]{:S(2)}, u32[]{:S(2)}) async-start(bf16[4,2,160,1024]{3,2,1,0:T(8,128)(2,1)} %get-tuple-element.115), calls=%async_computation.5 | async-start | bytes 5242880 | tf_op jit(solution)/shard_map/all_to_all | solution.py:97
  334.2 48.5 %collective-permute-start.10 = (bf16[2,1,64,4096]{3,2,1,0:T(8,128)(2,1)S(1)}, bf16[2,1,64,4096]{3,2,1,0:T(8,128)(2,1)}, u32[]{:S(2)}, u32[]{:S(2)}) collective-permute-start(bf16[2,1,64,4096]{3,2,1,0:T(8,128)(2,1)S(1)} %dynamic-slice_bitcast_fusion.1), channel_id=1, source_target_pairs={{0,8},{4,12},{8,0},{12,4},{16,24},{20,28},{24,16},{28,20},{1,9},{5... | collective-permute-start | bytes 3145736 | tf_op jit(solution)/shard_map/ppermute | solution.py:52
  335.7 49.4 %collective-permute-start.12 = (bf16[1,2,64,4096]{3,2,1,0:T(8,128)(2,1)S(1)}, bf16[1,2,64,4096]{3,2,1,0:T(8,128)(2,1)S(1)}, u32[]{:S(2)}, u32[]{:S(2)}) collective-permute-start(bf16[1,2,64,4096]{3,2,1,0:T(8,128)(2,1)S(1)} %dynamic-slice_bitcast_fusion), channel_id=1, source_target_pairs={{0,16},{4,20},{8,24},{12,28},{16,0},{20,4},{24,8},{28,12},{1,17},{... | collective-permute-start | bytes 3145736 | tf_op jit(solution)/shard_map/ppermute | solution.py:52
  384.2 19.5 %collective-permute-start.11 = (bf16[1,1,64,4096]{3,2,1,0:T(8,128)(2,1)S(1)}, bf16[1,1,64,4096]{3,2,1,0:T(8,128)(2,1)S(1)}, u32[]{:S(2)}, u32[]{:S(2)}) collective-permute-start(bf16[1,1,64,4096]{3,2,1,0:T(8,128)(2,1)S(1)} %constant_dynamic-slice_fusion.1), channel_id=1, source_target_pairs={{0,16},{4,20},{8,24},{12,28},{16,0},{20,4},{24,8},{28,12},{1,17},{... | collective-permute-start | bytes 1572872 | tf_op jit(solution)/shard_map/ppermute | solution.py:52
  385.4 20.8 %collective-permute-start.13 = (bf16[1,1,64,4096]{3,2,1,0:T(8,128)(2,1)S(1)}, bf16[1,1,64,4096]{3,2,1,0:T(8,128)(2,1)S(1)}, u32[]{:S(2)}, u32[]{:S(2)}) collective-permute-start(bf16[1,1,64,4096]{3,2,1,0:T(8,128)(2,1)S(1)} %constant_dynamic-slice_fusion), channel_id=1, source_target_pairs={{0,8},{4,12},{8,0},{12,4},{16,24},{20,28},{24,16},{28,20},{1,9},{5... | collective-permute-start | bytes 1572872 | tf_op jit(solution)/shard_map/ppermute | solution.py:52
  407.5 25.4 %copy-start.45 = (f32[256,128]{1,0:T(8,128)S(1)}, f32[256,128]{1,0:T(8,128)}, u32[]{:S(2)}) copy-start(f32[256,128]{1,0:T(8,128)} %copy-done.43) | copy-start | bytes 393220
  407.5 25.4 %copy-start.48 = (f32[256,128]{1,0:T(8,128)S(1)}, f32[256,128]{1,0:T(8,128)}, u32[]{:S(2)}) copy-start(f32[256,128]{1,0:T(8,128)} %copy-done.46) | copy-start | bytes 393220
  407.5 33.6 %all-to-all-start.6 = ((bf16[4,32,4096]{2,1,0:T(8,128)(2,1)}), bf16[4,32,4096]{2,1,0:T(8,128)(2,1)}, u32[]{:S(2)}, u32[]{:S(2)}) async-start(bf16[4,32,4096]{2,1,0:T(8,128)(2,1)} %bitcast.172), calls=%async_computation.6 | async-start | bytes 2097152 | tf_op jit(solution)/shard_map/all_to_all | solution.py:97
  415.8 1.3 collective-permute-start.14
  417.1 4.9 %collective-permute-start.15 = (f32[52,128]{1,0:T(8,128)S(1)}, f32[52,128]{1,0:T(8,128)S(1)}, u32[]{:S(2)}, u32[]{:S(2)}) collective-permute-start(f32[52,128]{1,0:T(8,128)S(1)} %fusion.26), channel_id=1, source_target_pairs={{0,8},{4,12},{8,0},{12,4},{16,24},{20,28},{24,16},{28,20},{1,9},{5... | collective-permute-start | bytes 79880 | tf_op jit(solution)/shard_map/ppermute | solution.py:52
  422.0 3.9 collective-permute-start.16
  425.9 12.4 %collective-permute-start.17 = (f32[52,128]{1,0:T(8,128)S(1)}, f32[52,128]{1,0:T(8,128)S(1)}, u32[]{:S(2)}, u32[]{:S(2)}) collective-permute-start(f32[52,128]{1,0:T(8,128)S(1)} %add.221), channel_id=1, source_target_pairs={{0,2},{1,3},{2,0},{3,1},{4,6},{5,7},{6,4},{7,5},{8,10},{9,11},{10,... | collective-permute-start | bytes 79880 | tf_op jit(solution)/shard_map/ppermute | solution.py:56
  428.9 9.5 %collective-permute-start.18 = (f32[52,128]{1,0:T(8,128)S(1)}, f32[52,128]{1,0:T(8,128)S(1)}, u32[]{:S(2)}, u32[]{:S(2)}) collective-permute-start(f32[52,128]{1,0:T(8,128)S(1)} %add.221), channel_id=1, source_target_pairs={{0,1},{1,2},{2,3},{3,0},{4,5},{5,6},{6,7},{7,4},{8,9},{9,10},{10,1... | collective-permute-start | bytes 79880 | tf_op jit(solution)/shard_map/ppermute | solution.py:56
  430.3 8.0 %collective-permute-start.19 = (f32[52,128]{1,0:T(8,128)S(1)}, f32[52,128]{1,0:T(8,128)S(1)}, u32[]{:S(2)}, u32[]{:S(2)}) collective-permute-start(f32[52,128]{1,0:T(8,128)S(1)} %add.221), channel_id=1, source_target_pairs={{0,3},{1,0},{2,1},{3,2},{4,7},{5,4},{6,5},{7,6},{8,11},{9,8},{10,9... | collective-permute-start | bytes 79880 | tf_op jit(solution)/shard_map/ppermute | solution.py:56
  (66 other events, 190.4 us)
Sparse Core Ops, SparseCore 0:
  16.1 56.7 all-gather.5
  97.1 67.0 all-gather.3
  277.3 146.7 reduce-scatter.1
